TPU v7x, 32 devices: a whole 2x2x4 slice. The times are simulated.
32 devices in a mesh: gx: 4 (over y, core), gy: 8 (over z, x).
Axes of the slice: x: 2, y: 2, z: 4, core: 2. Of those that a mesh axis runs over, the one named last changes fastest.
Arguments:
- field: float32 [8, 2048, 2048], P(None, 'gy', 'gx'), may hold values from -6 to 6
- row_scale: float32 [2048], replicated, may hold values from 0.5 to 2
- col_scale: float32 [2048], P('gx'), may hold values from 0.5 to 2
- row_rate: float32 [2048], replicated, may hold values from 0.2 to 1
- col_shift: float32 [2048], P('gx'), may hold values from -1 to 1
- col_mix: float32 [2048], P('gx'), may hold values from -1 to 1
Outputs:
- latent: float32 [2, 8, 2048, 2048], P(None, 'gy', None, 'gx')
- loglik: float32 [], replicated
All inputs are finite; a program needn't handle non-finite values.
Results may differ from a plain program's by a relative error of at most 0.000075.
Values sent between devices are 32-bit elements; how exact they have to be, the bound alone decides.
No kernel may reach another device: no remote copies, remote signals or barrier semaphores. Data moves between devices by JAX's collectives and lax.ppermute only.
A program may use at most 128 MiB of HBM per device.

v0:
```python
import functools
import math

import jax
import jax.numpy as jnp
from jax import lax
from jax.experimental import pallas as pl
from jax.experimental.pallas import tpu as pltpu
from jax.sharding import PartitionSpec as P

precision_top = lax.Precision.HIGHEST
RADIX = 8
VMEM_BYTES = 40 * 1024 * 1024


def from_partner(value, axis, stride):
    mask = 2**stride
    pairs = [(source, source ^ mask) for source in range(lax.axis_size(axis))]
    return lax.ppermute(value, axis, pairs)


def to_planes(values):
    return lax.all_to_all(values, "gy", split_axis=0, concat_axis=1, tiled=True)


def reverse_bits(value, count):
    result = value * 0
    for place in range(count):
        result = result + (value >> place & 1) * (1 << count - 1 - place)
    return result


def root_table(row_index, freqs, length):
    phase = row_index[:, None] * freqs[None, :] % length
    angle = phase.astype(jnp.float32) * (-2.0 * math.pi / length)
    return (jnp.cos(angle), jnp.sin(angle))


def x_tables(width, devices, position):
    levels = devices.bit_length() - 1
    local_index = jnp.arange(width, dtype=jnp.int32)
    freqs = reverse_bits(position, levels) + devices * local_index
    return root_table(local_index, freqs, devices * width)


def split_table(table):
    high = lax.reduce_precision(table, 8, 7)
    return jnp.stack([high.astype(jnp.bfloat16), (table - high).astype(jnp.bfloat16)])


def split_value(value):
    high = value.astype(jnp.bfloat16)
    return high, (value - high.astype(jnp.float32)).astype(jnp.bfloat16)


def small_fft(values):
    count = len(values)
    if count == 1:
        return values
    even, odd = small_fft(values[0::2]), small_fft(values[1::2])
    first, second = [], []
    root_half = math.sqrt(0.5)
    for place in range(count // 2):
        (er, ei), (re, im) = even[place], odd[place]
        turn = place * 8 // count
        if turn == 1:
            re, im = (re + im) * root_half, (im - re) * root_half
        elif turn == 2:
            re, im = im, -re
        elif turn == 3:
            re, im = (im - re) * root_half, (re + im) * -root_half
        first.append((er + re, ei + im))
        second.append((er - re, ei - im))
    return first + second


def dot(left, right):
    return jnp.dot(left, right, preferred_element_type=jnp.float32)


def dot_split(left_high, left_low, right_high, right_low):
    return dot(left_high, right_high) + (dot(left_high, right_low) + dot(left_low, right_high))


def y_kernel(count, coef_ref, *refs):
    inputs, (table_ref, twist_ref, out_ref, high_ref, low_ref, step_ref) = refs[:count], refs[count:]
    length, width = inputs[0].shape
    inner = length // RADIX
    for s in range(RADIX):
        parts = [ref[pl.ds(s, inner, stride=RADIX), :] for ref in inputs]
        for which in range(2):
            mixed = parts[0] * coef_ref[which, 0]
            for place in range(1, count):
                mixed = mixed + parts[place] * coef_ref[which, place]
            high, low = split_value(mixed)
            rows, cols = pl.ds(which * inner, inner), pl.ds(s * width, width)
            high_ref[rows, cols] = high
            low_ref[rows, cols] = low
    piece = 2 * width

    @pl.loop(0, RADIX * width // piece)
    def _(block):
        cols = pl.ds(pl.multiple_of(block * piece, piece), piece)
        step_ref[:, cols] = dot_split(table_ref[0], table_ref[1], high_ref[:, cols], low_ref[:, cols])

    rows_each = 16

    @pl.loop(0, inner // rows_each)
    def _(block):
        start = pl.multiple_of(block * rows_each, rows_each)
        values = []
        for s in range(RADIX):
            cols = pl.ds(s * width, width)
            re = step_ref[pl.ds(start, rows_each), cols]
            im = step_ref[pl.ds(pl.multiple_of(start + inner, rows_each), rows_each), cols]
            if s:
                cos, sin = twist_ref[0, s, pl.ds(start, rows_each), :], twist_ref[1, s, pl.ds(start, rows_each), :]
                re, im = re * cos - im * sin, re * sin + im * cos
            values.append((re, im))
        for kb, pair in enumerate(small_fft(values)):
            rows = pl.ds(pl.multiple_of(kb * inner + start, rows_each), rows_each)
            for which in range(2):
                high, low = split_value(pair[which])
                out_ref[2 * which, rows, :] = high
                out_ref[2 * which + 1, rows, :] = low


def y_dft(inputs, coefs, table, twist):
    count = len(inputs)
    length, width = inputs[0].shape
    inner = length // RADIX
    whole = pl.BlockSpec(memory_space=pltpu.VMEM)
    return pl.pallas_call(
        functools.partial(y_kernel, count),
        out_shape=jax.ShapeDtypeStruct((4, length, width), jnp.bfloat16),
        in_specs=[pl.BlockSpec(memory_space=pltpu.SMEM)] + [whole] * (count + 2),
        out_specs=whole,
        scratch_shapes=[
            pltpu.VMEM((2 * inner, RADIX * width), jnp.bfloat16),
            pltpu.VMEM((2 * inner, RADIX * width), jnp.bfloat16),
            pltpu.VMEM((2 * inner, RADIX * width), jnp.float32),
        ],
        compiler_params=pltpu.CompilerParams(vmem_limit_bytes=VMEM_BYTES),
        cost_estimate=pl.CostEstimate(
            flops=24 * inner * length * width, bytes_accessed=4 * length * width * (count + 3), transcendentals=0
        ),
        name="y_dft",
    )(coefs, *inputs, table, twist)


def x_product(parts, table_ref):
    high = jnp.concatenate([ref[which] for ref in parts for which in (0, 2)], axis=1)
    low = jnp.concatenate([ref[which] for ref in parts for which in (1, 3)], axis=1)
    return dot_split(high, low, table_ref[0], table_ref[1])


def x_first_kernel(count, *refs):
    parts, (table_ref, out_ref) = refs[:count], refs[count:]
    out_ref[...] = x_product(parts, table_ref)


def x_first(parts, table):
    count = len(parts)
    _, length, width = parts[0].shape
    columns = table.shape[2]
    rows = 256
    return pl.pallas_call(
        functools.partial(x_first_kernel, count),
        out_shape=jax.ShapeDtypeStruct((length, columns), jnp.float32),
        grid=(length // rows,),
        in_specs=[pl.BlockSpec((4, rows, width), lambda i: (0, i, 0))] * count
        + [pl.BlockSpec(table.shape, lambda i: (0, 0, 0))],
        out_specs=pl.BlockSpec((rows, columns), lambda i: (i, 0)),
        compiler_params=pltpu.CompilerParams(vmem_limit_bytes=VMEM_BYTES),
        cost_estimate=pl.CostEstimate(
            flops=12 * count * length * width * columns, bytes_accessed=8 * length * columns, transcendentals=0
        ),
        name="x_first",
    )(*parts, table)


def x_last_kernel(count, *refs):
    parts, (table_ref, sum_ref, row_ref, col_ref, out_ref, total_ref) = refs[:count], refs[count:]
    spec = sum_ref[...] + x_product(parts, table_ref)
    columns = spec.shape[1] // 2
    lanes = row_ref.shape[2]
    total = None
    for tile in range(columns // lanes):
        cols = pl.ds(tile * lanes, lanes)
        col_scale, col_shift, col_mix = col_ref[0:1, cols], col_ref[1:2, cols], col_ref[2:3, cols]
        scale = row_ref[0] * col_scale
        latent_u = spec[:, tile * lanes : (tile + 1) * lanes] * scale
        latent_v = spec[:, columns + tile * lanes : columns + (tile + 1) * lanes] * scale
        log_scale = row_ref[1] * jnp.tanh(latent_u + col_shift)
        latent_w = latent_v * jnp.exp(log_scale) + col_mix * latent_u
        out_ref[0, 0, :, cols] = latent_u
        out_ref[1, 0, :, cols] = latent_w
        terms = log_scale - 0.5 * (latent_u * latent_u + latent_w * latent_w)
        terms = jnp.sum(terms.reshape(-1, 8, lanes), axis=0)
        total = terms if total is None else total + terms

    @pl.when(pl.program_id(0) == 0)
    def _():
        total_ref[...] = jnp.zeros_like(total_ref)

    total_ref[...] += total


def x_last(parts, table, sums, row_pair, col_trio):
    count = len(parts)
    _, length, width = parts[0].shape
    columns = table.shape[2]
    rows = 256
    return pl.pallas_call(
        functools.partial(x_last_kernel, count),
        out_shape=(
            jax.ShapeDtypeStruct((2, 1, length, columns // 2), jnp.float32),
            jax.ShapeDtypeStruct((8, row_pair.shape[2]), jnp.float32),
        ),
        grid=(length // rows,),
        in_specs=[pl.BlockSpec((4, rows, width), lambda i: (0, i, 0))] * count
        + [
            pl.BlockSpec(table.shape, lambda i: (0, 0, 0)),
            pl.BlockSpec((rows, columns), lambda i: (i, 0)),
            pl.BlockSpec((2, rows, row_pair.shape[2]), lambda i: (0, i, 0)),
            pl.BlockSpec(col_trio.shape, lambda i: (0, 0)),
        ],
        out_specs=(
            pl.BlockSpec((2, 1, rows, columns // 2), lambda i: (0, 0, i, 0)),
            pl.BlockSpec((8, row_pair.shape[2]), lambda i: (0, 0)),
        ),
        compiler_params=pltpu.CompilerParams(vmem_limit_bytes=VMEM_BYTES),
        cost_estimate=pl.CostEstimate(
            flops=12 * count * length * width * columns,
            bytes_accessed=12 * length * columns,
            transcendentals=length * columns,
        ),
        name="x_last",
    )(*parts, table, sums, row_pair, col_trio)


def sum_everywhere(tile):
    axes = ("gx", "gy")
    devices = lax.axis_size("gx") * lax.axis_size("gy")
    copies = jnp.broadcast_to(tile[None], (devices,) + tile.shape)
    return jnp.sum(lax.all_to_all(copies, axes, split_axis=0, concat_axis=0, tiled=True))


def four_way(field, row_scale, col_scale, row_rate, col_shift, col_mix):
    position = lax.axis_index("gx")
    planes, rows, columns = field.shape
    length, width = planes * rows, columns // 4
    cuts = lax.optimization_barrier(tuple(field[:, :, c * width : (c + 1) * width] for c in range(4)))
    sign = jnp.where(position < 2, 1.0, -1.0)

    own_real = jnp.where(position == 1, -1.0, jnp.where(position == 3, 0.0, 1.0))
    other_real = jnp.where(position == 2, 0.0, 1.0)
    own_imag = jnp.where(position == 3, 1.0, 0.0)
    other_imag = jnp.where(position == 2, -1.0, 0.0)
    coefs_a = jnp.stack([own_real, other_real, own_imag, other_imag]).reshape(2, 2)
    coefs_b = jnp.concatenate([coefs_a, coefs_a * sign], axis=1)

    inner = length // RADIX
    index = jnp.arange(inner, dtype=jnp.int32)
    cos, sin = root_table(index, index, inner)
    y_table = split_table(jnp.concatenate([jnp.concatenate([cos, -sin], 1), jnp.concatenate([sin, cos], 1)], 0))
    cos, sin = root_table(jnp.arange(RADIX, dtype=jnp.int32), index, length)
    twist = jnp.broadcast_to(jnp.stack([cos, sin])[:, :, :, None], (2, RADIX, inner, width))
    cos, sin = x_tables(columns, 4, position)
    real_rows, imag_rows = jnp.concatenate([cos, sin], 1), jnp.concatenate([-sin, cos], 1)

    def x_table(chunks):
        spans = [slice(c * width, (c + 1) * width) for c in chunks]
        return split_table(jnp.concatenate([rows[s] for s in spans for rows in (real_rows, imag_rows)], 0))

    norm = 1.0 / math.sqrt(length * columns * 4)
    row_pair = jnp.broadcast_to(jnp.stack([row_scale * norm, row_rate])[:, :, None], (2, length, 128))
    col_trio = jnp.stack([col_scale, col_shift, col_mix])
    fixed = 2.0 * (columns * jnp.sum(jnp.log(row_scale)) + length * jnp.sum(jnp.log(col_scale)))
    fixed = fixed - length * columns * math.log(2.0 * math.pi)

    first_a = [from_partner(cuts[c], "gx", 1) + sign * cuts[c] for c in (0, 1)]
    first_b = [to_planes(cuts[c])[0] for c in (2, 3)]
    second_a = [to_planes(value)[0] for value in first_a]
    second_b = [from_partner(value, "gx", 1) for value in first_b]
    parts = []
    for step in range(2):
        own, other = second_a[step], from_partner(second_a[step], "gx", 0)
        parts.append(y_dft([own, other], coefs_a, y_table, twist))
        late, early = second_b[step], first_b[step]
        group = [late, from_partner(late, "gx", 0), early, from_partner(early, "gx", 0)]
        parts.append(y_dft(group, coefs_b, y_table, twist))
    sums = x_first(parts[:2], x_table((0, 2)))
    latent, tile = x_last(parts[2:], x_table((1, 3)), sums, row_pair, col_trio)
    tile = tile + fixed / tile.size
    modes = length * columns * lax.axis_size("gx") * lax.axis_size("gy")
    return (latent, sum_everywhere(tile) / modes)


def complex_einsum(form, real_part, imag_part, cos_part, sin_part):
    first = jnp.einsum(form, real_part, cos_part, precision=precision_top)
    second = jnp.einsum(form, real_part, sin_part, precision=precision_top)
    first = first - jnp.einsum(form, imag_part, sin_part, precision=precision_top)
    second = second + jnp.einsum(form, imag_part, cos_part, precision=precision_top)
    return (first, second)


def x_butterfly(field):
    devices = lax.axis_size("gx")
    levels = devices.bit_length() - 1
    position = lax.axis_index("gx")
    real_part, imag_part = field, jnp.zeros_like(field)
    for level in range(levels - 1, -1, -1):
        half = 1 << level
        lower = position // half % 2 == 0
        offset = position % half
        angle = offset.astype(jnp.float32) * (-math.pi / half)
        cos_twist = jnp.where(lower, 1.0, jnp.cos(angle))
        sin_twist = jnp.where(lower, 0.0, jnp.sin(angle))
        other = from_partner(jnp.stack([real_part, imag_part]), "gx", level)
        diff_real = jnp.where(lower, real_part + other[0], other[0] - real_part)
        diff_imag = jnp.where(lower, imag_part + other[1], other[1] - imag_part)
        real_part = diff_real * cos_twist - diff_imag * sin_twist
        imag_part = diff_real * sin_twist + diff_imag * cos_twist
    cos_part, sin_part = x_tables(field.shape[2], devices, position)
    real_part, imag_part = complex_einsum("zyn,nk->zyk", real_part, imag_part, cos_part, sin_part)
    return (to_planes(real_part), to_planes(imag_part))


def y_transform(real_part, imag_part):
    planes, length, width = real_part.shape
    outer = 1 << (length.bit_length() - 1) // 2
    inner = length // outer
    outer_index = jnp.arange(outer, dtype=jnp.int32)
    inner_index = jnp.arange(inner, dtype=jnp.int32)
    cos_one, sin_one = root_table(outer_index, outer_index, outer)
    cos_two, sin_two = root_table(inner_index, inner_index, inner)
    cos_mid, sin_mid = root_table(outer_index, inner_index, length)
    shaped_real = real_part.reshape(planes, outer, inner, width)
    shaped_imag = imag_part.reshape(planes, outer, inner, width)
    step_real, step_imag = complex_einsum("zabc,ak->zkbc", shaped_real, shaped_imag, cos_one, sin_one)
    twist_cos = cos_mid[None, :, :, None]
    twist_sin = sin_mid[None, :, :, None]
    turned_real = step_real * twist_cos - step_imag * twist_sin
    turned_imag = step_real * twist_sin + step_imag * twist_cos
    final_real, final_imag = complex_einsum("zkbc,bj->zjkc", turned_real, turned_imag, cos_two, sin_two)
    return (final_real.reshape(planes, length, width), final_imag.reshape(planes, length, width))


def any_way(field, row_scale, col_scale, row_rate, col_shift, col_mix):
    spec_real, spec_imag = y_transform(*x_butterfly(field))
    length = spec_real.shape[1]
    total_cols = spec_real.shape[2] * lax.axis_size("gx")
    norm_factor = 1.0 / math.sqrt(length * total_cols)
    scale = row_scale[None, :, None] * col_scale[None, None, :]
    latent_u = spec_real * norm_factor * scale
    latent_v = spec_imag * norm_factor * scale
    log_scale = row_rate[None, :, None] * jnp.tanh(latent_u + col_shift[None, None, :])
    latent_w = latent_v * jnp.exp(log_scale) + col_mix[None, None, :] * latent_u
    terms = (
        -0.5 * (latent_u * latent_u + latent_w * latent_w)
        - math.log(2.0 * math.pi)
        + log_scale
        + 2.0 * jnp.log(scale)
    )
    mode_count = spec_real.size * lax.axis_size("gx") * lax.axis_size("gy")
    loglik = lax.psum(jnp.sum(terms), ("gx", "gy")) / mode_count
    return (jnp.stack([latent_u, latent_w]), loglik)


def per_device(field, *scales):
    return (four_way if lax.axis_size("gx") == 4 else any_way)(field, *scales)


def solution(mesh):
    return jax.shard_map(
        per_device,
        mesh=mesh,
        in_specs=(P(None, "gy", "gx"), P(), P("gx"), P(), P("gx"), P("gx")),
        out_specs=(P(None, "gy", None, "gx"), P()),
        check_vma=False,
    )
```

profile of v0, /device:TPU:0, one launch (start us, length us, event | category | flops | bytes accessed | tf_op | source)
XLA Modules:
  0.0 218.9 jit_solution(994106782676460493)
XLA Ops:
  0.6 3.9 %fusion.43 = (f32[8,256,128]{2,1,0:T(8,128)S(1)}, f32[8,256,128]{2,1,0:T(8,128)S(1)}, f32[8,256,128]{2,1,0:T(8,128)}, f32[8,256,128]{2,1,0:T(8,128)}) fusion(f32[8,256,512]{2,1,0:T(8,128)} %param.6), kind=kLoop, calls=%fused_computation.93 | loop fusion | bytes 8388608 | tf_op jit(solution)/shard_map/slice | solution.py:253
  4.5 32.8 %all_to_all.20 = f32[8,256,128]{2,1,0:T(8,128)S(1)} all-to-all(f32[8,256,128]{2,1,0:T(8,128)S(1)} %get-tuple-element.9), channel_id=1, replica_groups=mesh['gx'=4,'gy'=8] {'gy'}, dimensions={0} | all-to-all | bytes 2097152 | tf_op jit(solution)/shard_map/all_to_all | solution.py:23
  37.3 3.6 %all-to-all-start.3 = ((f32[8,256,128]{2,1,0:T(8,128)}), f32[8,256,128]{2,1,0:T(8,128)S(1)}, u32[]{:S(2)}, u32[]{:S(2)}) async-start(f32[8,256,128]{2,1,0:T(8,128)} %get-tuple-element.11), calls=%async_computation.3 | async-start | bytes 2097152 | tf_op jit(solution)/shard_map/all_to_all | solution.py:23
  40.9 1.6 collective-permute-start
  42.5 22.8 %collective-permute-done = f32[8,256,128]{2,1,0:T(8,128)} collective-permute-done((f32[8,256,128]{2,1,0:T(8,128)S(1)}, f32[8,256,128]{2,1,0:T(8,128)}, u32[]{:S(2)}, u32[]{:S(2)}) %collective-permute-start) | collective-permute-done | bytes 1048608 | tf_op jit(solution)/shard_map/ppermute | solution.py:19
  65.3 2.3 %multiply_add_fusion.1 = f32[8,256,128]{2,1,0:T(8,128)} fusion(f32[8,256,128]{2,1,0:T(8,128)} %collective-permute-done, f32[8,256,128]{2,1,0:T(8,128)S(1)} %get-tuple-element.8, f32[]{:T(128)S(6)} %select_n.63), kind=kLoop, calls=%fused_computation.36 | loop fusion | flops 524288 | bytes 3145732 | tf_op jit(solution)/shard_map/add | solution.py:282
  67.7 5.7 %all-to-all-start = ((f32[8,256,128]{2,1,0:T(8,128)}), f32[8,256,128]{2,1,0:T(8,128)S(1)}, u32[]{:S(2)}, u32[]{:S(2)}) async-start(f32[8,256,128]{2,1,0:T(8,128)} %multiply_add_fusion.1), calls=%async_computation | async-start | bytes 2097152 | tf_op jit(solution)/shard_map/all_to_all | solution.py:23
  73.4 1.5 collective-permute-start.5
  74.9 0.1 pad_maximum_fusion.12
  75.0 0.1 reshape.425.coef_ref
  75.1 1.0 fusion.34
  76.1 20.4 %collective-permute-done.5 = f32[8,256,128]{2,1,0:T(8,128)} collective-permute-done((f32[8,256,128]{2,1,0:T(8,128)}, f32[8,256,128]{2,1,0:T(8,128)}, u32[]{:S(2)}, u32[]{:S(2)}) %collective-permute-start.5) | collective-permute-done | bytes 1048608 | tf_op jit(solution)/shard_map/ppermute | solution.py:19
  96.5 2.6 %multiply_add_fusion = f32[8,256,128]{2,1,0:T(8,128)} fusion(f32[8,256,128]{2,1,0:T(8,128)} %collective-permute-done.5, f32[8,256,128]{2,1,0:T(8,128)} %get-tuple-element.10, f32[]{:T(128)S(6)} %select_n.63), kind=kLoop, calls=%fused_computation.33 | loop fusion | flops 524288 | bytes 3145732 | tf_op jit(solution)/shard_map/add | solution.py:282
  99.1 5.7 %all-to-all-start.2 = ((f32[8,256,128]{2,1,0:T(8,128)}), f32[8,256,128]{2,1,0:T(8,128)}, u32[]{:S(2)}, u32[]{:S(2)}) async-start(f32[8,256,128]{2,1,0:T(8,128)} %multiply_add_fusion), calls=%async_computation.2 | async-start | bytes 2097152 | tf_op jit(solution)/shard_map/all_to_all | solution.py:23
  104.8 1.0 fusion.32
  105.9 0.1 maximum_bitcast_fusion
  106.0 4.1 %fusion.23 = (f32[512,512]{1,0:T(8,128)S(1)}, f32[512,512]{1,0:T(8,128)S(1)}, f32[512,512]{1,0:T(8,128)S(1)}) fusion(s32[512]{0:T(512)S(1)} %multiply_add_fusion.2), kind=kLoop, calls=%fused_computation.56 | loop fusion | flops 3932160 | bytes 3147776 | tf_op jit(solution)/shard_map/sin | solution.py:36
  110.1 0.4 fusion.16
  110.6 1.6 collective-permute-start.7
  112.2 0.6 log_reduce_fusion
  112.8 2.2 %reduce-precision_convert_fusion = (bf16[1,512,1024]{2,1,0:T(8,128)(2,1)}, bf16[1,512,1024]{2,1,0:T(8,128)(2,1)}, bf16[1,512,1024]{2,1,0:T(8,128)(2,1)}, bf16[1,512,1024]{2,1,0:T(8,128)(2,1)}) fusion(f32[1,128,1024]{2,1,0:T(8,128)S(1)} %get-tuple-element.30, f32[1,128,1024]{2,1,0:T(8,128)S(1)} %get-tuple-element.23, ...), kind=kLoop, calls=%fused_computation.1 | loop fusion | flops 7340032 | bytes 8388608 | tf_op jit(solution)/shard_map/convert_element_type | solution.py:48
  115.0 0.5 collective-permute-start.2
  115.6 1.2 reduce-precision_convert_fusion.2
  116.7 10.9 %all-to-all-done.2 = f32[8,256,128]{2,1,0:T(8,128)} async-done(((f32[8,256,128]{2,1,0:T(8,128)}), f32[8,256,128]{2,1,0:T(8,128)}, u32[]{:S(2)}, u32[]{:S(2)}) %all-to-all-start.2) | async-done | bytes 1048608 | tf_op jit(solution)/shard_map/all_to_all | solution.py:23
  127.6 0.7 log_reduce_fusion.1
  128.3 0.5 collective-permute-start.9
  128.8 8.1 %collective-permute-done.7.refs_0_ = f32[2048,128]{1,0:T(8,128)} collective-permute-done((f32[2048,128]{1,0:T(8,128)S(1)}, f32[2048,128]{1,0:T(8,128)}, u32[]{:S(2)}, u32[]{:S(2)}) %collective-permute-start.7) | collective-permute-done | bytes 1048608 | tf_op jit(solution)/shard_map/ppermute | solution.py:19
  136.9 0.1 pad_maximum_fusion.11.coef_ref
  138.3 1.4 pad_maximum_fusion.5.refs_2_.refs_4_
  139.7 0.1 copy-done.2
  139.8 0.3 copy-done.3
  140.1 0.2 pad_maximum_fusion.3.refs_2_
  140.3 1.0 copy-done
  141.4 0.3 copy-done.1
  141.7 0.2 pad_maximum_fusion.1.refs_2_
  141.9 0.5 copy-done.6
  142.4 12.1 %collective-permute-done.2.refs_0_ = f32[2048,128]{1,0:T(8,128)} collective-permute-done((f32[2048,128]{1,0:T(8,128)S(1)}, f32[2048,128]{1,0:T(8,128)}, u32[]{:S(2)}, u32[]{:S(2)}) %collective-permute-start.2) | collective-permute-done | bytes 1048608 | tf_op jit(solution)/shard_map/ppermute | solution.py:19
  154.5 0.5 collective-permute-start.3
  155.1 0.6 broadcast_in_dim.6.refs_3_.refs_5_
  155.6 5.5 %y_dft.4.refs_0_ = bf16[4,2048,128]{2,1,0:T(8,128)(2,1)S(1)} custom-call(f32[2,2]{1,0:T(2,128)S(1)} %reshape.425.coef_ref, f32[2048,128]{1,0:T(8,128)S(1)} %bitcast.40, f32[2048,128]{1,0:T(8,128)} %collective-permute-done.1.refs_1_, bf16[2,512,512]{2,1,0:T(8,128)(2,1)S(1)} %pad_maximum_fusion.5.refs_2_.refs_4_, ...), custom_call_target="tpu_custom_call" | custom-call | flops 1610612736 | bytes 5242880 | tf_op jit(solution)/shard_map/y_dft/pallas_call | solution.py:133
  161.2 6.0 %y_dft.6.refs_0_ = bf16[4,2048,128]{2,1,0:T(8,128)(2,1)S(1)} custom-call(f32[2,2]{1,0:T(2,128)S(1)} %reshape.425.coef_ref, f32[2048,128]{1,0:T(8,128)} %bitcast.12.refs_0_, f32[2048,128]{1,0:T(8,128)} %collective-permute-done.6.refs_1_, bf16[2,512,512]{2,1,0:T(8,128)(2,1)S(1)} %pad_maximum_fusion.5.refs_2_.refs_4_, ...), custom_call_target="tpu_custom_call" | custom-call | flops 1610612736 | bytes 5242880 | tf_op jit(solution)/shard_map/y_dft/pallas_call | solution.py:133
  167.2 6.8 %y_dft.7.refs_1_ = bf16[4,2048,128]{2,1,0:T(8,128)(2,1)S(1)} custom-call(f32[2,4]{1,0:T(2,128)S(1)} %pad_maximum_fusion.11.coef_ref, f32[2048,128]{1,0:T(8,128)} %collective-permute-done.7.refs_0_, f32[2048,128]{1,0:T(8,128)} %collective-permute-done.8.refs_1_, f32[2048,128]{1,0:T(8,128)S(1)} %bitcast.38, f32[2048,128]{1,0:T(8,128)} %collective-permute-done.9.refs_3_, ...), custom_call_target="tpu_custom_call" | custom-call | flops 1610612736 | bytes 7340032 | tf_op jit(solution)/shard_map/y_dft/pallas_call | solution.py:133
  174.0 9.3 %x_first.1.refs_3_ = f32[2048,1024]{1,0:T(8,128)} custom-call(bf16[4,2048,128]{2,1,0:T(8,128)(2,1)S(1)} %y_dft.6.refs_0_, bf16[4,2048,128]{2,1,0:T(8,128)(2,1)S(1)} %y_dft.7.refs_1_, bf16[2,512,1024]{2,1,0:T(8,128)(2,1)S(1)} %pad_maximum_fusion.3.refs_2_), custom_call_target="tpu_custom_call" | custom-call | flops 6442450944 | bytes 16777216 | tf_op jit(solution)/shard_map/x_first/pallas_call | solution.py:167
  183.3 6.1 %y_dft.5.refs_1_ = bf16[4,2048,128]{2,1,0:T(8,128)(2,1)S(1)} custom-call(f32[2,4]{1,0:T(2,128)S(1)} %pad_maximum_fusion.11.coef_ref, f32[2048,128]{1,0:T(8,128)} %collective-permute-done.2.refs_0_, f32[2048,128]{1,0:T(8,128)S(1)} %collective-permute-done.3.refs_1_, f32[2048,128]{1,0:T(8,128)S(1)} %bitcast.35, ...), custom_call_target="tpu_custom_call" | custom-call | flops 1610612736 | bytes 7340032 | tf_op jit(solution)/shard_map/y_dft/pallas_call | solution.py:133
  189.4 0.6 broadcast_in_dim.7.refs_4_
  190.0 13.1 %x_last.1 = (f32[2,1,2048,512]{3,2,1,0:T(8,128)}, f32[8,128]{1,0:T(8,128)S(1)}) custom-call(bf16[4,2048,128]{2,1,0:T(8,128)(2,1)S(1)} %y_dft.4.refs_0_, bf16[4,2048,128]{2,1,0:T(8,128)(2,1)S(1)} %y_dft.5.refs_1_, bf16[2,512,1024]{2,1,0:T(8,128)(2,1)S(1)} %pad_maximum_fusion.1.refs_2_, f32[2048,1024]{1,0:T(8,128)} %x_first.1.refs_3_, ...), custom_call_target="tpu_custom_call" | custom-call | flops 6442450944 | bytes 25165824 | tf_op jit(solution)/shard_map/x_last/pallas_call | solution.py:214
  203.2 13.3 %all_to_all.42 = f32[32,8,128]{2,1,0:T(8,128)S(1)} all-to-all(f32[32,8,128]{2,1,0:T(8,128)S(1)} %broadcast_in_dim.8), channel_id=1, replica_groups=mesh['gx'=4,'gy'=8] {'gx','gy'}, dimensions={0} | all-to-all | bytes 262144 | tf_op jit(solution)/shard_map/all_to_all | solution.py:246
  216.5 0.6 reduce_sum.29
  (33 shorter events, 0.2 us)
Async XLA Ops:
  37.3 30.3 %all-to-all-start.3 = ((f32[8,256,128]{2,1,0:T(8,128)}), f32[8,256,128]{2,1,0:T(8,128)S(1)}, u32[]{:S(2)}, u32[]{:S(2)}) async-start(f32[8,256,128]{2,1,0:T(8,128)} %get-tuple-element.11), calls=%async_computation.3 | async-start | bytes 2097152 | tf_op jit(solution)/shard_map/all_to_all | solution.py:23
  40.9 24.4 %collective-permute-start = (f32[8,256,128]{2,1,0:T(8,128)S(1)}, f32[8,256,128]{2,1,0:T(8,128)}, u32[]{:S(2)}, u32[]{:S(2)}) collective-permute-start(f32[8,256,128]{2,1,0:T(8,128)S(1)} %get-tuple-element.8), channel_id=1, source_target_pairs={{0,16},{8,24},{16,0},{24,8},{1,17},{9,25},{17,1},{25,9},{2,18},{10... | collective-permute-start | bytes 3145736 | tf_op jit(solution)/shard_map/ppermute | solution.py:19
  67.7 31.4 %all-to-all-start = ((f32[8,256,128]{2,1,0:T(8,128)}), f32[8,256,128]{2,1,0:T(8,128)S(1)}, u32[]{:S(2)}, u32[]{:S(2)}) async-start(f32[8,256,128]{2,1,0:T(8,128)} %multiply_add_fusion.1), calls=%async_computation | async-start | bytes 2097152 | tf_op jit(solution)/shard_map/all_to_all | solution.py:23
  73.4 23.1 %collective-permute-start.5 = (f32[8,256,128]{2,1,0:T(8,128)}, f32[8,256,128]{2,1,0:T(8,128)}, u32[]{:S(2)}, u32[]{:S(2)}) collective-permute-start(f32[8,256,128]{2,1,0:T(8,128)} %get-tuple-element.10), channel_id=1, source_target_pairs={{0,16},{8,24},{16,0},{24,8},{1,17},{9,25},{17,1},{25,9},{2,18},{10... | collective-permute-start | bytes 3145736 | tf_op jit(solution)/shard_map/ppermute | solution.py:19
  99.1 28.5 %all-to-all-start.2 = ((f32[8,256,128]{2,1,0:T(8,128)}), f32[8,256,128]{2,1,0:T(8,128)}, u32[]{:S(2)}, u32[]{:S(2)}) async-start(f32[8,256,128]{2,1,0:T(8,128)} %multiply_add_fusion), calls=%async_computation.2 | async-start | bytes 2097152 | tf_op jit(solution)/shard_map/all_to_all | solution.py:23
  110.1 2.1 copy-start.4
  110.1 2.1 copy-start.7
  110.1 2.1 copy-start.8
  110.1 2.1 copy-start.5
  110.6 26.3 %collective-permute-start.7 = (f32[2048,128]{1,0:T(8,128)S(1)}, f32[2048,128]{1,0:T(8,128)}, u32[]{:S(2)}, u32[]{:S(2)}) collective-permute-start(f32[2048,128]{1,0:T(8,128)S(1)} %bitcast.36), channel_id=1, source_target_pairs={{0,16},{8,24},{16,0},{24,8},{1,17},{9,25},{17,1},{25,9},{2,18},{10... | collective-permute-start | bytes 3145736 | tf_op jit(solution)/shard_map/ppermute | solution.py:19
  115.0 39.5 %collective-permute-start.2 = (f32[2048,128]{1,0:T(8,128)S(1)}, f32[2048,128]{1,0:T(8,128)}, u32[]{:S(2)}, u32[]{:S(2)}) collective-permute-start(f32[2048,128]{1,0:T(8,128)S(1)} %bitcast.33), channel_id=1, source_target_pairs={{0,16},{8,24},{16,0},{24,8},{1,17},{9,25},{17,1},{25,9},{2,18},{10... | collective-permute-start | bytes 3145736 | tf_op jit(solution)/shard_map/ppermute | solution.py:19
  115.5 39.0 %collective-permute-start.1 = (f32[2048,128]{1,0:T(8,128)S(1)}, f32[2048,128]{1,0:T(8,128)}, u32[]{:S(2)}, u32[]{:S(2)}) collective-permute-start(f32[2048,128]{1,0:T(8,128)S(1)} %bitcast.39), channel_id=1, source_target_pairs={{0,8},{8,0},{16,24},{24,16},{1,9},{9,1},{17,25},{25,17},{2,10},{10... | collective-permute-start | bytes 3145736 | tf_op jit(solution)/shard_map/ppermute | solution.py:19
  127.6 33.6 %collective-permute-start.6 = (f32[2048,128]{1,0:T(8,128)}, f32[2048,128]{1,0:T(8,128)}, u32[]{:S(2)}, u32[]{:S(2)}) collective-permute-start(f32[2048,128]{1,0:T(8,128)} %bitcast.12.refs_0_), channel_id=1, source_target_pairs={{0,8},{8,0},{16,24},{24,16},{1,9},{9,1},{17,25},{25,17},{2,10},{10... | collective-permute-start | bytes 3145736 | tf_op jit(solution)/shard_map/ppermute | solution.py:19
  128.3 38.9 %collective-permute-start.9 = (f32[2048,128]{1,0:T(8,128)S(1)}, f32[2048,128]{1,0:T(8,128)}, u32[]{:S(2)}, u32[]{:S(2)}) collective-permute-start(f32[2048,128]{1,0:T(8,128)S(1)} %bitcast.37), channel_id=1, source_target_pairs={{0,8},{8,0},{16,24},{24,16},{1,9},{9,1},{17,25},{25,17},{2,10},{10... | collective-permute-start | bytes 3145736 | tf_op jit(solution)/shard_map/ppermute | solution.py:19
  136.9 30.3 %collective-permute-start.8 = (f32[2048,128]{1,0:T(8,128)}, f32[2048,128]{1,0:T(8,128)}, u32[]{:S(2)}, u32[]{:S(2)}) collective-permute-start(f32[2048,128]{1,0:T(8,128)} %collective-permute-done.7.refs_0_), channel_id=1, source_target_pairs={{0,8},{8,0},{16,24},{24,16},{1,9},{9,1},{17,25},{25,17},{2,10},{10... | collective-permute-start | bytes 3145736 | tf_op jit(solution)/shard_map/ppermute | solution.py:19
  138.3 1.5 copy-start.2
  138.3 1.8 copy-start.3
  140.1 1.2 copy-start
  140.1 1.5 copy-start.1
  141.7 0.7 copy-start.6
  154.5 28.7 %collective-permute-start.4 = (f32[2048,128]{1,0:T(8,128)S(1)}, f32[2048,128]{1,0:T(8,128)S(1)}, u32[]{:S(2)}, u32[]{:S(2)}) collective-permute-start(f32[2048,128]{1,0:T(8,128)S(1)} %bitcast.34), channel_id=1, source_target_pairs={{0,8},{8,0},{16,24},{24,16},{1,9},{9,1},{17,25},{25,17},{2,10},{10... | collective-permute-start | bytes 3145736 | tf_op jit(solution)/shard_map/ppermute | solution.py:19
  154.5 28.7 %collective-permute-start.3 = (f32[2048,128]{1,0:T(8,128)}, f32[2048,128]{1,0:T(8,128)S(1)}, u32[]{:S(2)}, u32[]{:S(2)}) collective-permute-start(f32[2048,128]{1,0:T(8,128)} %collective-permute-done.2.refs_0_), channel_id=1, source_target_pairs={{0,8},{8,0},{16,24},{24,16},{1,9},{9,1},{17,25},{25,17},{2,10},{10... | collective-permute-start | bytes 3145736 | tf_op jit(solution)/shard_map/ppermute | solution.py:19
where the time goes:
time: 220 us; the launch traced here: 219 us
  waiting for transfers between devices  74.3 us (34%)
  Pallas kernels  46.8 us (21%)
  blocking collectives  46.1 us (21%)
  starting transfers between devices  21.2 us (10%)
  other arithmetic  19 us (9%)
  local copies, waits for them, and re-layouts  7.46 us (3%)
  between operations  3.96 us (2%)
    ppermute x10, waiting for transfers between devices, from_partner(): return lax.ppermute(value, axis, pairs)  63.4 us
    all_to_all x1, blocking collectives, to_planes(): return lax.all_to_all(values, 'gy', split_axis=0, concat_axis=1, tiled=True)  32.8 us
    pallas_call x4, Pallas kernels, y_dft(): pl.pallas_call(functools.partial(y_kernel, count), out_shape=jax.ShapeDty...  24.4 us
    all_to_all x3, starting transfers between devices, to_planes(): return lax.all_to_all(values, 'gy', split_axis=0, concat_axis=1, tiled=True)  15 us
    all_to_all x1, blocking collectives, sum_everywhere(): lax.all_to_all(copies, axes, split_axis=0, concat_axis=0, tiled=True)  13.3 us
    pallas_call x1, Pallas kernels, x_last(): pl.pallas_call(functools.partial(x_last_kernel, count), out_shape=(jax.Sh...  13.1 us
    all_to_all x3, waiting for transfers between devices, to_planes(): return lax.all_to_all(values, 'gy', split_axis=0, concat_axis=1, tiled=True)  10.9 us
    pallas_call x1, Pallas kernels, x_first(): pl.pallas_call(functools.partial(x_first_kernel, count), out_shape=jax.Sh...  9.29 us
  transfers between devices with their start and end apart: 13, of which 5 were waited for; matrix products, arithmetic and copies ran while one was open for 9% of the time, Pallas kernels for 13%

commit v1 on v0

--- a/solution.py
+++ b/solution.py
@@ -21,6 +21,45 @@
 
 def to_planes(values):
     return lax.all_to_all(values, "gy", split_axis=0, concat_axis=1, tiled=True)
+
+
+def split_kernel(count, me_ref, *refs):
+    inputs, outputs = refs[: len(refs) - count], refs[len(refs) - count :]
+    for place, out_ref in enumerate(outputs):
+        plane = me_ref[0] ^ place
+        if len(inputs) == 1:
+            out_ref[...] = inputs[0][plane]
+        else:
+            sign = (1 - 2 * me_ref[1]).astype(jnp.float32)
+            out_ref[...] = inputs[0][plane] + sign * inputs[1][plane]
+
+
+def split_pieces(numbers, inputs):
+    planes, rows, width = inputs[0].shape
+    whole = pl.BlockSpec(memory_space=pltpu.VMEM)
+    return pl.pallas_call(
+        functools.partial(split_kernel, planes),
+        out_shape=[jax.ShapeDtypeStruct((rows, width), jnp.float32)] * planes,
+        in_specs=[pl.BlockSpec(memory_space=pltpu.SMEM)] + [whole] * len(inputs),
+        out_specs=[whole] * planes,
+        compiler_params=pltpu.CompilerParams(vmem_limit_bytes=VMEM_BYTES),
+        cost_estimate=pl.CostEstimate(
+            flops=planes * rows * width, bytes_accessed=8 * planes * rows * width, transcendentals=0
+        ),
+        name="split_pieces",
+    )(numbers, *inputs)
+
+
+def exchange(pieces, held):
+    devices = lax.axis_size("gy")
+    near = range(1, devices // 2)
+    if held is not None:
+        waited = lax.optimization_barrier((held, [pieces[m] for m in near]))[1]
+        pieces = [pieces[0], *waited, *pieces[devices // 2 :]]
+    received = {0: pieces[0]}
+    for m in (*range(devices // 2, devices), *near):
+        received[m] = lax.ppermute(pieces[m], "gy", [(source, source ^ m) for source in range(devices)])
+    return [received[m] for m in range(devices)]
 
 
 def reverse_bits(value, count):
@@ -240,10 +279,11 @@
 
 
 def sum_everywhere(tile):
-    axes = ("gx", "gy")
-    devices = lax.axis_size("gx") * lax.axis_size("gy")
-    copies = jnp.broadcast_to(tile[None], (devices,) + tile.shape)
-    return jnp.sum(lax.all_to_all(copies, axes, split_axis=0, concat_axis=0, tiled=True))
+    for axis in ("gx", "gy"):
+        devices = lax.axis_size(axis)
+        others = [lax.ppermute(tile, axis, [(s, s ^ m) for s in range(devices)]) for m in range(1, devices)]
+        tile = functools.reduce(jnp.add, others, tile)
+    return jnp.sum(tile)
 
 
 def four_way(field, row_scale, col_scale, row_rate, col_shift, col_mix):
@@ -262,7 +302,9 @@
 
     inner = length // RADIX
     index = jnp.arange(inner, dtype=jnp.int32)
-    cos, sin = root_table(index, index, inner)
+    block = inner // planes
+    arrived = ((index // block) ^ lax.axis_index("gy")) * block + index % block
+    cos, sin = root_table(index, arrived, inner)
     y_table = split_table(jnp.concatenate([jnp.concatenate([cos, -sin], 1), jnp.concatenate([sin, cos], 1)], 0))
     cos, sin = root_table(jnp.arange(RADIX, dtype=jnp.int32), index, length)
     twist = jnp.broadcast_to(jnp.stack([cos, sin])[:, :, :, None], (2, RADIX, inner, width))
@@ -279,10 +321,15 @@
     fixed = 2.0 * (columns * jnp.sum(jnp.log(row_scale)) + length * jnp.sum(jnp.log(col_scale)))
     fixed = fixed - length * columns * math.log(2.0 * math.pi)
 
-    first_a = [from_partner(cuts[c], "gx", 1) + sign * cuts[c] for c in (0, 1)]
-    first_b = [to_planes(cuts[c])[0] for c in (2, 3)]
-    second_a = [to_planes(value)[0] for value in first_a]
+    numbers = jnp.stack([lax.axis_index("gy"), position // 2]).astype(jnp.int32)
+
+    def gather(inputs, held):
+        return jnp.concatenate(exchange(split_pieces(numbers, inputs), held), axis=0)
+
+    first_a = [from_partner(cuts[c], "gx", 1) for c in (0, 1)]
+    first_b = [gather([cuts[2]], None), gather([cuts[3]], first_a[0])]
     second_b = [from_partner(value, "gx", 1) for value in first_b]
+    second_a = [gather([first_a[0], cuts[0]], first_a[1]), gather([first_a[1], cuts[1]], second_b[0])]
     parts = []
     for step in range(2):
         own, other = second_a[step], from_partner(second_a[step], "gx", 0)

time: 220 us -> 220 us (level)
  starting transfers between devices: 21.2 us -> 86.8 us
  blocking collectives: 46.1 us -> 0 us
  waiting for transfers between devices: 74.3 us -> 42.1 us
  local copies, waits for them, and re-layouts: 7.46 us -> 17.2 us
  Pallas kernels: 46.8 us -> 51.8 us
    ppermute x0 -> x38, starting transfers between devices: none -> 80.3 us  [the longest x28 66.9 us: exchange(): lax.ppermute(pieces[m], 'gy', [(source, source ^ m) for source in range(d...]
    ppermute x10, waiting for transfers between devices: 63.4 us -> 2.16 us  [from_partner(): return lax.ppermute(value, axis, pairs)]
    all_to_all x2 -> x0, blocking collectives: 46.1 us -> none  [the longest x1 32.8 us: to_planes(): return lax.all_to_all(values, 'gy', split_axis=0, concat_axis=1, tiled=True)]
    ppermute x0 -> x38, waiting for transfers between devices: none -> 39.9 us  [the longest x28 34.9 us: exchange(): lax.ppermute(pieces[m], 'gy', [(source, source ^ m) for source in range(d...]
    all_to_all x3 -> x0, starting transfers between devices: 15 us -> none  [to_planes(): return lax.all_to_all(values, 'gy', split_axis=0, concat_axis=1, tiled=True)]
    all_to_all x3 -> x0, waiting for transfers between devices: 10.9 us -> none  [to_planes(): return lax.all_to_all(values, 'gy', split_axis=0, concat_axis=1, tiled=True)]
    unnamed x18 -> x52, local copies, waits for them, and re-layouts: 2.27 us -> 11.1 us
    pallas_call x0 -> x4, Pallas kernels: none -> 4.71 us  [split_pieces(): pl.pallas_call(functools.partial(split_kernel, planes), out_shape=[jax.Sh...]
  transfers between devices with their start and end apart: 13 -> 48, of which waited for: 5 -> 19; matrix products, arithmetic and copies ran while one was open for 9% -> 12% of each run, Pallas kernels for 13% -> 14%
where the time goes in v1:
time: 220 us
  starting transfers between devices  86.8 us (39%)
  Pallas kernels  51.8 us (24%)
  waiting for transfers between devices  42.1 us (19%)
  other arithmetic  17.6 us (8%)
  local copies, waits for them, and re-layouts  17.2 us (8%)
  between operations  4.19 us (2%)
    ppermute x28, starting transfers between devices, exchange(): lax.ppermute(pieces[m], 'gy', [(source, source ^ m) for source in range(d...  66.9 us
    ppermute x28, waiting for transfers between devices, exchange(): lax.ppermute(pieces[m], 'gy', [(source, source ^ m) for source in range(d...  34.9 us
    pallas_call x4, Pallas kernels, y_dft(): pl.pallas_call(functools.partial(y_kernel, count), out_shape=jax.ShapeDty...  24.5 us
    ppermute x10, starting transfers between devices, sum_everywhere(): lax.ppermute(tile, axis, [(s, s ^ m) for s in range(devices)])  13.3 us
    pallas_call x1, Pallas kernels, x_last(): pl.pallas_call(functools.partial(x_last_kernel, count), out_shape=(jax.Sh...  13.2 us
    unnamed x52, local copies, waits for them, and re-layouts  11.1 us
    pallas_call x1, Pallas kernels, x_first(): pl.pallas_call(functools.partial(x_first_kernel, count), out_shape=jax.Sh...  9.36 us
    ppermute x10, starting transfers between devices, from_partner(): return lax.ppermute(value, axis, pairs)  6.52 us
  transfers between devices with their start and end apart: 48, of which 19 were waited for; matrix products, arithmetic and copies ran while one was open for 12% of the time, Pallas kernels for 14%

profile of v1, /device:TPU:0, one launch (start us, length us, event | category | flops | bytes accessed | tf_op | source)
XLA Modules:
  0.0 219.6 jit_solution(10476038881395835577)
XLA Ops:
  0.6 3.5 %fusion.48 = (f32[8,256,128]{2,1,0:T(8,128)S(1)}, f32[8,256,128]{2,1,0:T(8,128)S(1)}, f32[8,256,128]{2,1,0:T(8,128)S(1)}, f32[8,256,128]{2,1,0:T(8,128)}) fusion(f32[8,256,512]{2,1,0:T(8,128)} %param.6), kind=kLoop, calls=%fused_computation.136 | loop fusion | bytes 8388608 | tf_op jit(solution)/shard_map/slice | solution.py:293
  8.1 2.9 %collective-permute-start.1 = (f32[256,128]{1,0:T(8,128)}, f32[256,128]{1,0:T(8,128)}, u32[]{:S(2)}, u32[]{:S(2)}) collective-permute-start(f32[256,128]{1,0:T(8,128)} %get-tuple-element.53), channel_id=1, source_target_pairs={{0,1},{1,0},{2,3},{3,2},{4,5},{5,4},{6,7},{7,6},{8,9},{9,8},{10,11... | collective-permute-start | bytes 393224 | tf_op jit(solution)/shard_map/ppermute | solution.py:61
  11.0 1.6 collective-permute-start.2
  12.6 1.9 collective-permute-start
  18.4 1.7 fusion.34
  20.2 4.1 %fusion.23 = (f32[512,512]{1,0:T(8,128)S(1)}, f32[512,512]{1,0:T(8,128)S(1)}, f32[512,512]{1,0:T(8,128)S(1)}) fusion(s32[512]{0:T(512)S(1)} %multiply_add_fusion), kind=kLoop, calls=%fused_computation.54 | loop fusion | flops 3932160 | bytes 3147776 | tf_op jit(solution)/shard_map/sin | solution.py:75
  28.5 1.5 pad_maximum_fusion.3.refs_2_
  30.1 1.5 pad_maximum_fusion.1.refs_2_
  32.3 3.0 %collective-permute-start.4 = (f32[256,128]{1,0:T(8,128)S(1)}, f32[256,128]{1,0:T(8,128)S(1)}, u32[]{:S(2)}, u32[]{:S(2)}) collective-permute-start(f32[256,128]{1,0:T(8,128)S(1)} %copy-done.6), channel_id=1, source_target_pairs={{0,4},{1,5},{2,6},{3,7},{4,0},{5,1},{6,2},{7,3},{8,12},{9,13},{10,... | collective-permute-start | bytes 393224 | tf_op jit(solution)/shard_map/ppermute | solution.py:61
  35.3 1.6 constant_dynamic-update-slice_fusion.6
  38.1 1.6 constant_dynamic-update-slice_fusion.5
  39.7 3.6 %collective-permute-start.6 = (f32[256,128]{1,0:T(8,128)S(1)}, f32[256,128]{1,0:T(8,128)S(1)}, u32[]{:S(2)}, u32[]{:S(2)}) collective-permute-start(f32[256,128]{1,0:T(8,128)S(1)} %get-tuple-element.58), channel_id=1, source_target_pairs={{0,6},{1,7},{2,4},{3,5},{4,2},{5,3},{6,0},{7,1},{8,14},{9,15},{10,... | collective-permute-start | bytes 393224 | tf_op jit(solution)/shard_map/ppermute | solution.py:61
  43.3 1.6 constant_dynamic-update-slice_fusion.4
  44.9 5.6 %collective-permute-start.7 = (f32[256,128]{1,0:T(8,128)S(1)}, f32[256,128]{1,0:T(8,128)S(1)}, u32[]{:S(2)}, u32[]{:S(2)}) collective-permute-start(f32[256,128]{1,0:T(8,128)S(1)} %get-tuple-element.59), channel_id=1, source_target_pairs={{0,7},{1,6},{2,5},{3,4},{4,3},{5,2},{6,1},{7,0},{8,15},{9,14},{10,... | collective-permute-start | bytes 393224 | tf_op jit(solution)/shard_map/ppermute | solution.py:61
  52.2 8.6 %collective-permute-start.22 = (f32[256,128]{1,0:T(8,128)S(1)}, f32[256,128]{1,0:T(8,128)S(1)}, u32[]{:S(2)}, u32[]{:S(2)}) collective-permute-start(f32[256,128]{1,0:T(8,128)S(1)} %get-tuple-element.80), channel_id=1, source_target_pairs={{0,5},{1,4},{2,7},{3,6},{4,1},{5,0},{6,3},{7,2},{8,13},{9,12},{10,... | collective-permute-start | bytes 393224 | tf_op jit(solution)/shard_map/ppermute | solution.py:61
  61.4 2.8 %collective-permute-start.23 = (f32[256,128]{1,0:T(8,128)S(1)}, f32[256,128]{1,0:T(8,128)S(1)}, u32[]{:S(2)}, u32[]{:S(2)}) collective-permute-start(f32[256,128]{1,0:T(8,128)S(1)} %get-tuple-element.81), channel_id=1, source_target_pairs={{0,6},{1,7},{2,4},{3,5},{4,2},{5,3},{6,0},{7,1},{8,14},{9,15},{10,... | collective-permute-start | bytes 393224 | tf_op jit(solution)/shard_map/ppermute | solution.py:61
  66.3 5.6 %collective-permute-start.19 = (f32[256,128]{1,0:T(8,128)S(1)}, f32[256,128]{1,0:T(8,128)S(1)}, u32[]{:S(2)}, u32[]{:S(2)}) collective-permute-start(f32[256,128]{1,0:T(8,128)S(1)} %get-tuple-element.77), channel_id=1, source_target_pairs={{0,2},{1,3},{2,0},{3,1},{4,6},{5,7},{6,4},{7,5},{8,10},{9,11},{10,... | collective-permute-start | bytes 393224 | tf_op jit(solution)/shard_map/ppermute | solution.py:61
  73.3 2.5 %collective-permute-start.20 = (f32[256,128]{1,0:T(8,128)S(1)}, f32[256,128]{1,0:T(8,128)S(1)}, u32[]{:S(2)}, u32[]{:S(2)}) collective-permute-start(f32[256,128]{1,0:T(8,128)S(1)} %get-tuple-element.78), channel_id=1, source_target_pairs={{0,3},{1,2},{2,1},{3,0},{4,7},{5,6},{6,5},{7,4},{8,11},{9,10},{10,... | collective-permute-start | bytes 393224 | tf_op jit(solution)/shard_map/ppermute | solution.py:61
  76.1 1.7 collective-permute-start.8
  79.2 3.0 %collective-permute-start.24 = (f32[256,128]{1,0:T(8,128)S(1)}, f32[256,128]{1,0:T(8,128)S(1)}, u32[]{:S(2)}, u32[]{:S(2)}) collective-permute-start(f32[256,128]{1,0:T(8,128)S(1)} %get-tuple-element.82), channel_id=1, source_target_pairs={{0,7},{1,6},{2,5},{3,4},{4,3},{5,2},{6,1},{7,0},{8,15},{9,14},{10,... | collective-permute-start | bytes 393224 | tf_op jit(solution)/shard_map/ppermute | solution.py:61
  82.2 1.7 collective-permute-start.12
  83.9 1.9 collective-permute-start.13
  88.2 6.0 %collective-permute-start.29 = (f32[256,128]{1,0:T(8,128)S(1)}, f32[256,128]{1,0:T(8,128)S(1)}, u32[]{:S(2)}, u32[]{:S(2)}) collective-permute-start(f32[256,128]{1,0:T(8,128)S(1)} %get-tuple-element.88), channel_id=1, source_target_pairs={{0,2},{1,3},{2,0},{3,1},{4,6},{5,7},{6,4},{7,5},{8,10},{9,11},{10,... | collective-permute-start | bytes 393224 | tf_op jit(solution)/shard_map/ppermute | solution.py:61
  94.3 2.2 collective-permute-start.30
  96.5 4.4 %collective-permute-done.29 = f32[256,128]{1,0:T(8,128)S(1)} collective-permute-done((f32[256,128]{1,0:T(8,128)S(1)}, f32[256,128]{1,0:T(8,128)S(1)}, u32[]{:S(2)}, u32[]{:S(2)}) %collective-permute-start.29) | collective-permute-done | bytes 131104 | tf_op jit(solution)/shard_map/ppermute | solution.py:61
  100.9 2.5 %collective-permute-start.31 = (f32[256,128]{1,0:T(8,128)S(1)}, f32[256,128]{1,0:T(8,128)S(1)}, u32[]{:S(2)}, u32[]{:S(2)}) collective-permute-start(f32[256,128]{1,0:T(8,128)S(1)} %get-tuple-element.90), channel_id=1, source_target_pairs={{0,4},{1,5},{2,6},{3,7},{4,0},{5,1},{6,2},{7,3},{8,12},{9,13},{10,... | collective-permute-start | bytes 393224 | tf_op jit(solution)/shard_map/ppermute | solution.py:61
  106.1 7.0 %collective-permute-done.31 = f32[256,128]{1,0:T(8,128)S(1)} collective-permute-done((f32[256,128]{1,0:T(8,128)S(1)}, f32[256,128]{1,0:T(8,128)S(1)}, u32[]{:S(2)}, u32[]{:S(2)}) %collective-permute-start.31) | collective-permute-done | bytes 131104 | tf_op jit(solution)/shard_map/ppermute | solution.py:61
  113.0 2.9 %collective-permute-start.33 = (f32[256,128]{1,0:T(8,128)S(1)}, f32[256,128]{1,0:T(8,128)S(1)}, u32[]{:S(2)}, u32[]{:S(2)}) collective-permute-start(f32[256,128]{1,0:T(8,128)S(1)} %get-tuple-element.92), channel_id=1, source_target_pairs={{0,6},{1,7},{2,4},{3,5},{4,2},{5,3},{6,0},{7,1},{8,14},{9,15},{10,... | collective-permute-start | bytes 393224 | tf_op jit(solution)/shard_map/ppermute | solution.py:61
  116.0 1.8 collective-permute-start.34
  118.4 2.8 %collective-permute-done.33 = f32[256,128]{1,0:T(8,128)S(1)} collective-permute-done((f32[256,128]{1,0:T(8,128)S(1)}, f32[256,128]{1,0:T(8,128)S(1)}, u32[]{:S(2)}, u32[]{:S(2)}) %collective-permute-start.33) | collective-permute-done | bytes 131104 | tf_op jit(solution)/shard_map/ppermute | solution.py:61
  121.2 2.6 %collective-permute-done.34 = f32[256,128]{1,0:T(8,128)S(1)} collective-permute-done((f32[256,128]{1,0:T(8,128)S(1)}, f32[256,128]{1,0:T(8,128)S(1)}, u32[]{:S(2)}, u32[]{:S(2)}) %collective-permute-start.34) | collective-permute-done | bytes 131104 | tf_op jit(solution)/shard_map/ppermute | solution.py:61
  127.0 2.6 %collective-permute-done.11 = f32[256,128]{1,0:T(8,128)S(1)} collective-permute-done((f32[256,128]{1,0:T(8,128)S(1)}, f32[256,128]{1,0:T(8,128)S(1)}, u32[]{:S(2)}, u32[]{:S(2)}) %collective-permute-start.11) | collective-permute-done | bytes 131104 | tf_op jit(solution)/shard_map/ppermute | solution.py:61
  129.6 1.8 collective-permute-start.14
  131.5 4.9 %collective-permute-done.14 = f32[256,128]{1,0:T(8,128)S(1)} collective-permute-done((f32[256,128]{1,0:T(8,128)S(1)}, f32[256,128]{1,0:T(8,128)S(1)}, u32[]{:S(2)}, u32[]{:S(2)}) %collective-permute-start.14) | collective-permute-done | bytes 131104 | tf_op jit(solution)/shard_map/ppermute | solution.py:61
  136.4 2.6 %collective-permute-start.15 = (f32[256,128]{1,0:T(8,128)S(1)}, f32[256,128]{1,0:T(8,128)S(1)}, u32[]{:S(2)}, u32[]{:S(2)}) collective-permute-start(f32[256,128]{1,0:T(8,128)S(1)} %get-tuple-element.69), channel_id=1, source_target_pairs={{0,7},{1,6},{2,5},{3,4},{4,3},{5,2},{6,1},{7,0},{8,15},{9,14},{10,... | collective-permute-start | bytes 393224 | tf_op jit(solution)/shard_map/ppermute | solution.py:61
  139.1 5.0 %collective-permute-done.15 = f32[256,128]{1,0:T(8,128)S(1)} collective-permute-done((f32[256,128]{1,0:T(8,128)S(1)}, f32[256,128]{1,0:T(8,128)S(1)}, u32[]{:S(2)}, u32[]{:S(2)}) %collective-permute-start.15) | collective-permute-done | bytes 131104 | tf_op jit(solution)/shard_map/ppermute | solution.py:61
  147.4 2.1 collective-permute-done.25.refs_0_
  150.2 5.5 %y_dft.6.refs_0_ = bf16[4,2048,128]{2,1,0:T(8,128)(2,1)S(1)} custom-call(f32[2,2]{1,0:T(2,128)S(1)} %reshape.431.coef_ref, f32[2048,128]{1,0:T(8,128)S(1)} %constant_dynamic-update-slice_fusion.24.refs_0_, f32[2048,128]{1,0:T(8,128)} %collective-permute-done.35.refs_1_, bf16[2,512,512]{2,1,0:T(8,128)(2,1)S(1)} %pad_maximum_fusion.5.refs_2_.refs_4_, ...), custom_call_target="tpu_custom_call" | custom-call | flops 1610612736 | bytes 5242880 | tf_op jit(solution)/shard_map/y_dft/pallas_call | solution.py:172
  155.7 7.2 %y_dft.7.refs_1_ = bf16[4,2048,128]{2,1,0:T(8,128)(2,1)S(1)} custom-call(f32[2,4]{1,0:T(2,128)S(1)} %pad_maximum_fusion.11.coef_ref, f32[2048,128]{1,0:T(8,128)} %collective-permute-done.8.refs_0_, f32[2048,128]{1,0:T(8,128)} %collective-permute-done.36.refs_1_, f32[2048,128]{1,0:T(8,128)} %constant_dynamic-update-slice_fusion.refs_2_, ...), custom_call_target="tpu_custom_call" | custom-call | flops 1610612736 | bytes 7340032 | tf_op jit(solution)/shard_map/y_dft/pallas_call | solution.py:172
  162.9 9.4 %x_first.1.refs_3_ = f32[2048,1024]{1,0:T(8,128)} custom-call(bf16[4,2048,128]{2,1,0:T(8,128)(2,1)S(1)} %y_dft.6.refs_0_, bf16[4,2048,128]{2,1,0:T(8,128)(2,1)S(1)} %y_dft.7.refs_1_, bf16[2,512,1024]{2,1,0:T(8,128)(2,1)S(1)} %copy-done.2), custom_call_target="tpu_custom_call" | custom-call | flops 6442450944 | bytes 16777216 | tf_op jit(solution)/shard_map/x_first/pallas_call | solution.py:206
  172.3 5.5 %y_dft.4.refs_0_ = bf16[4,2048,128]{2,1,0:T(8,128)(2,1)S(1)} custom-call(f32[2,2]{1,0:T(2,128)S(1)} %reshape.431.coef_ref, f32[2048,128]{1,0:T(8,128)S(1)} %constant_dynamic-update-slice_fusion.8.refs_0_, f32[2048,128]{1,0:T(8,128)} %collective-permute-done.16.refs_1_, bf16[2,512,512]{2,1,0:T(8,128)(2,1)S(1)} %pad_maximum_fusion.5.refs_2_.refs_4_, ...), custom_call_target="tpu_custom_call" | custom-call | flops 1610612736 | bytes 5242880 | tf_op jit(solution)/shard_map/y_dft/pallas_call | solution.py:172
  177.8 6.4 %y_dft.5.refs_1_ = bf16[4,2048,128]{2,1,0:T(8,128)(2,1)S(1)} custom-call(f32[2,4]{1,0:T(2,128)S(1)} %pad_maximum_fusion.11.coef_ref, f32[2048,128]{1,0:T(8,128)} %collective-permute-done.25.refs_0_, f32[2048,128]{1,0:T(8,128)S(1)} %collective-permute-done.26.refs_1_, f32[2048,128]{1,0:T(8,128)S(1)} %constant_dynamic-update-slice_fusion.16.refs_2_, ...), custom_call_target="tpu_custom_call" | custom-call | flops 1610612736 | bytes 7340032 | tf_op jit(solution)/shard_map/y_dft/pallas_call | solution.py:172
  185.8 13.2 %x_last.1 = (f32[2,1,2048,512]{3,2,1,0:T(8,128)}, f32[8,128]{1,0:T(8,128)S(1)}) custom-call(bf16[4,2048,128]{2,1,0:T(8,128)(2,1)S(1)} %y_dft.4.refs_0_, bf16[4,2048,128]{2,1,0:T(8,128)(2,1)S(1)} %y_dft.5.refs_1_, bf16[2,512,1024]{2,1,0:T(8,128)(2,1)S(1)} %copy-done.1, f32[2048,1024]{1,0:T(8,128)} %x_first.1.refs_3_, ...), custom_call_target="tpu_custom_call" | custom-call | flops 6442450944 | bytes 25165824 | tf_op jit(solution)/shard_map/x_last/pallas_call | solution.py:253
  198.9 1.5 collective-permute-start.39
  203.5 2.7 %collective-permute-start.47 = (f32[8,128]{1,0:T(8,128)S(1)}, f32[8,128]{1,0:T(8,128)S(1)}, u32[]{:S(2)}, u32[]{:S(2)}) collective-permute-start(f32[8,128]{1,0:T(8,128)S(1)} %add_add_fusion), channel_id=1, source_target_pairs={{0,7},{1,6},{2,5},{3,4},{4,3},{5,2},{6,1},{7,0},{8,15},{9,14},{10,... | collective-permute-start | bytes 12296 | tf_op jit(solution)/shard_map/ppermute | solution.py:284
  206.2 1.6 collective-permute-start.46
  207.8 1.9 collective-permute-start.45
  209.7 1.5 collective-permute-start.44
  (142 shorter events, 44.3 us)
Async XLA Ops:
  8.1 24.2 %collective-permute-start.1 = (f32[256,128]{1,0:T(8,128)}, f32[256,128]{1,0:T(8,128)}, u32[]{:S(2)}, u32[]{:S(2)}) collective-permute-start(f32[256,128]{1,0:T(8,128)} %get-tuple-element.53), channel_id=1, source_target_pairs={{0,1},{1,0},{2,3},{3,2},{4,5},{5,4},{6,7},{7,6},{8,9},{9,8},{10,11... | collective-permute-start | bytes 393224 | tf_op jit(solution)/shard_map/ppermute | solution.py:61
  11.0 25.8 %collective-permute-start.2 = (f32[256,128]{1,0:T(8,128)}, f32[256,128]{1,0:T(8,128)}, u32[]{:S(2)}, u32[]{:S(2)}) collective-permute-start(f32[256,128]{1,0:T(8,128)} %get-tuple-element.54), channel_id=1, source_target_pairs={{0,2},{1,3},{2,0},{3,1},{4,6},{5,7},{6,4},{7,5},{8,10},{9,11},{10,... | collective-permute-start | bytes 393224 | tf_op jit(solution)/shard_map/ppermute | solution.py:61
  12.6 27.1 %collective-permute-start.3 = (f32[256,128]{1,0:T(8,128)}, f32[256,128]{1,0:T(8,128)}, u32[]{:S(2)}, u32[]{:S(2)}) collective-permute-start(f32[256,128]{1,0:T(8,128)} %get-tuple-element.55), channel_id=1, source_target_pairs={{0,3},{1,2},{2,1},{3,0},{4,7},{5,6},{6,5},{7,4},{8,11},{9,10},{10,... | collective-permute-start | bytes 393224 | tf_op jit(solution)/shard_map/ppermute | solution.py:61
  12.6 52.3 %collective-permute-start = (f32[8,256,128]{2,1,0:T(8,128)S(1)}, f32[8,256,128]{2,1,0:T(8,128)}, u32[]{:S(2)}, u32[]{:S(2)}) collective-permute-start(f32[8,256,128]{2,1,0:T(8,128)S(1)} %get-tuple-element.49.refs_1_), channel_id=1, source_target_pairs={{0,16},{8,24},{16,0},{24,8},{1,17},{9,25},{17,1},{25,9},{2,18},{10... | collective-permute-start | bytes 3145736 | tf_op jit(solution)/shard_map/ppermute | solution.py:19
  14.5 50.3 %collective-permute-start.17 = (f32[8,256,128]{2,1,0:T(8,128)S(1)}, f32[8,256,128]{2,1,0:T(8,128)}, u32[]{:S(2)}, u32[]{:S(2)}) collective-permute-start(f32[8,256,128]{2,1,0:T(8,128)S(1)} %get-tuple-element.72.refs_1_), channel_id=1, source_target_pairs={{0,16},{8,24},{16,0},{24,8},{1,17},{9,25},{17,1},{25,9},{2,18},{10... | collective-permute-start | bytes 3145736 | tf_op jit(solution)/shard_map/ppermute | solution.py:19
  32.3 12.6 %collective-permute-start.4 = (f32[256,128]{1,0:T(8,128)S(1)}, f32[256,128]{1,0:T(8,128)S(1)}, u32[]{:S(2)}, u32[]{:S(2)}) collective-permute-start(f32[256,128]{1,0:T(8,128)S(1)} %copy-done.6), channel_id=1, source_target_pairs={{0,4},{1,5},{2,6},{3,7},{4,0},{5,1},{6,2},{7,3},{8,12},{9,13},{10,... | collective-permute-start | bytes 393224 | tf_op jit(solution)/shard_map/ppermute | solution.py:61
  36.9 14.7 %collective-permute-start.5 = (f32[256,128]{1,0:T(8,128)S(1)}, f32[256,128]{1,0:T(8,128)S(1)}, u32[]{:S(2)}, u32[]{:S(2)}) collective-permute-start(f32[256,128]{1,0:T(8,128)S(1)} %copy-done.4), channel_id=1, source_target_pairs={{0,5},{1,4},{2,7},{3,6},{4,1},{5,0},{6,3},{7,2},{8,13},{9,12},{10,... | collective-permute-start | bytes 393224 | tf_op jit(solution)/shard_map/ppermute | solution.py:61
  39.7 12.5 %collective-permute-start.6 = (f32[256,128]{1,0:T(8,128)S(1)}, f32[256,128]{1,0:T(8,128)S(1)}, u32[]{:S(2)}, u32[]{:S(2)}) collective-permute-start(f32[256,128]{1,0:T(8,128)S(1)} %get-tuple-element.58), channel_id=1, source_target_pairs={{0,6},{1,7},{2,4},{3,5},{4,2},{5,3},{6,0},{7,1},{8,14},{9,15},{10,... | collective-permute-start | bytes 393224 | tf_op jit(solution)/shard_map/ppermute | solution.py:61
  44.9 16.6 %collective-permute-start.7 = (f32[256,128]{1,0:T(8,128)S(1)}, f32[256,128]{1,0:T(8,128)S(1)}, u32[]{:S(2)}, u32[]{:S(2)}) collective-permute-start(f32[256,128]{1,0:T(8,128)S(1)} %get-tuple-element.59), channel_id=1, source_target_pairs={{0,7},{1,6},{2,5},{3,4},{4,3},{5,2},{6,1},{7,0},{8,15},{9,14},{10,... | collective-permute-start | bytes 393224 | tf_op jit(solution)/shard_map/ppermute | solution.py:61
  51.5 30.7 %collective-permute-start.21 = (f32[256,128]{1,0:T(8,128)S(1)}, f32[256,128]{1,0:T(8,128)S(1)}, u32[]{:S(2)}, u32[]{:S(2)}) collective-permute-start(f32[256,128]{1,0:T(8,128)S(1)} %get-tuple-element.79), channel_id=1, source_target_pairs={{0,4},{1,5},{2,6},{3,7},{4,0},{5,1},{6,2},{7,3},{8,12},{9,13},{10,... | collective-permute-start | bytes 393224 | tf_op jit(solution)/shard_map/ppermute | solution.py:61
  52.2 31.7 %collective-permute-start.22 = (f32[256,128]{1,0:T(8,128)S(1)}, f32[256,128]{1,0:T(8,128)S(1)}, u32[]{:S(2)}, u32[]{:S(2)}) collective-permute-start(f32[256,128]{1,0:T(8,128)S(1)} %get-tuple-element.80), channel_id=1, source_target_pairs={{0,5},{1,4},{2,7},{3,6},{4,1},{5,0},{6,3},{7,2},{8,13},{9,12},{10,... | collective-permute-start | bytes 393224 | tf_op jit(solution)/shard_map/ppermute | solution.py:61
  61.4 24.4 %collective-permute-start.23 = (f32[256,128]{1,0:T(8,128)S(1)}, f32[256,128]{1,0:T(8,128)S(1)}, u32[]{:S(2)}, u32[]{:S(2)}) collective-permute-start(f32[256,128]{1,0:T(8,128)S(1)} %get-tuple-element.81), channel_id=1, source_target_pairs={{0,6},{1,7},{2,4},{3,5},{4,2},{5,3},{6,0},{7,1},{8,14},{9,15},{10,... | collective-permute-start | bytes 393224 | tf_op jit(solution)/shard_map/ppermute | solution.py:61
  64.9 8.4 %collective-permute-start.18 = (f32[256,128]{1,0:T(8,128)S(1)}, f32[256,128]{1,0:T(8,128)S(1)}, u32[]{:S(2)}, u32[]{:S(2)}) collective-permute-start(f32[256,128]{1,0:T(8,128)S(1)} %get-tuple-element.76), channel_id=1, source_target_pairs={{0,1},{1,0},{2,3},{3,2},{4,5},{5,4},{6,7},{7,6},{8,9},{9,8},{10,11... | collective-permute-start | bytes 393224 | tf_op jit(solution)/shard_map/ppermute | solution.py:61
  66.3 9.8 %collective-permute-start.19 = (f32[256,128]{1,0:T(8,128)S(1)}, f32[256,128]{1,0:T(8,128)S(1)}, u32[]{:S(2)}, u32[]{:S(2)}) collective-permute-start(f32[256,128]{1,0:T(8,128)S(1)} %get-tuple-element.77), channel_id=1, source_target_pairs={{0,2},{1,3},{2,0},{3,1},{4,6},{5,7},{6,4},{7,5},{8,10},{9,11},{10,... | collective-permute-start | bytes 393224 | tf_op jit(solution)/shard_map/ppermute | solution.py:61
  73.3 5.9 %collective-permute-start.20 = (f32[256,128]{1,0:T(8,128)S(1)}, f32[256,128]{1,0:T(8,128)S(1)}, u32[]{:S(2)}, u32[]{:S(2)}) collective-permute-start(f32[256,128]{1,0:T(8,128)S(1)} %get-tuple-element.78), channel_id=1, source_target_pairs={{0,3},{1,2},{2,1},{3,0},{4,7},{5,6},{6,5},{7,4},{8,11},{9,10},{10,... | collective-permute-start | bytes 393224 | tf_op jit(solution)/shard_map/ppermute | solution.py:61
  76.1 39.8 %collective-permute-start.8 = (f32[2048,128]{1,0:T(8,128)}, f32[2048,128]{1,0:T(8,128)}, u32[]{:S(2)}, u32[]{:S(2)}) collective-permute-start(f32[2048,128]{1,0:T(8,128)} %constant_dynamic-update-slice_fusion.refs_2_), channel_id=1, source_target_pairs={{0,16},{8,24},{16,0},{24,8},{1,17},{9,25},{17,1},{25,9},{2,18},{10... | collective-permute-start | bytes 3145736 | tf_op jit(solution)/shard_map/ppermute | solution.py:19
  79.2 9.0 %collective-permute-start.24 = (f32[256,128]{1,0:T(8,128)S(1)}, f32[256,128]{1,0:T(8,128)S(1)}, u32[]{:S(2)}, u32[]{:S(2)}) collective-permute-start(f32[256,128]{1,0:T(8,128)S(1)} %get-tuple-element.82), channel_id=1, source_target_pairs={{0,7},{1,6},{2,5},{3,4},{4,3},{5,2},{6,1},{7,0},{8,15},{9,14},{10,... | collective-permute-start | bytes 393224 | tf_op jit(solution)/shard_map/ppermute | solution.py:61
  82.2 41.6 %collective-permute-start.12 = (f32[256,128]{1,0:T(8,128)S(1)}, f32[256,128]{1,0:T(8,128)S(1)}, u32[]{:S(2)}, u32[]{:S(2)}) collective-permute-start(f32[256,128]{1,0:T(8,128)S(1)} %get-tuple-element.66), channel_id=1, source_target_pairs={{0,4},{1,5},{2,6},{3,7},{4,0},{5,1},{6,2},{7,3},{8,12},{9,13},{10,... | collective-permute-start | bytes 393224 | tf_op jit(solution)/shard_map/ppermute | solution.py:61
  83.9 42.5 %collective-permute-start.13 = (f32[256,128]{1,0:T(8,128)S(1)}, f32[256,128]{1,0:T(8,128)S(1)}, u32[]{:S(2)}, u32[]{:S(2)}) collective-permute-start(f32[256,128]{1,0:T(8,128)S(1)} %get-tuple-element.67), channel_id=1, source_target_pairs={{0,5},{1,4},{2,7},{3,6},{4,1},{5,0},{6,3},{7,2},{8,13},{9,12},{10,... | collective-permute-start | bytes 393224 | tf_op jit(solution)/shard_map/ppermute | solution.py:61
  85.9 8.4 %collective-permute-start.28 = (f32[256,128]{1,0:T(8,128)S(1)}, f32[256,128]{1,0:T(8,128)S(1)}, u32[]{:S(2)}, u32[]{:S(2)}) collective-permute-start(f32[256,128]{1,0:T(8,128)S(1)} %get-tuple-element.87), channel_id=1, source_target_pairs={{0,1},{1,0},{2,3},{3,2},{4,5},{5,4},{6,7},{7,6},{8,9},{9,8},{10,11... | collective-permute-start | bytes 393224 | tf_op jit(solution)/shard_map/ppermute | solution.py:61
  88.2 12.6 %collective-permute-start.29 = (f32[256,128]{1,0:T(8,128)S(1)}, f32[256,128]{1,0:T(8,128)S(1)}, u32[]{:S(2)}, u32[]{:S(2)}) collective-permute-start(f32[256,128]{1,0:T(8,128)S(1)} %get-tuple-element.88), channel_id=1, source_target_pairs={{0,2},{1,3},{2,0},{3,1},{4,6},{5,7},{6,4},{7,5},{8,10},{9,11},{10,... | collective-permute-start | bytes 393224 | tf_op jit(solution)/shard_map/ppermute | solution.py:61
  94.3 10.3 %collective-permute-start.30 = (f32[256,128]{1,0:T(8,128)S(1)}, f32[256,128]{1,0:T(8,128)S(1)}, u32[]{:S(2)}, u32[]{:S(2)}) collective-permute-start(f32[256,128]{1,0:T(8,128)S(1)} %get-tuple-element.89), channel_id=1, source_target_pairs={{0,3},{1,2},{2,1},{3,0},{4,7},{5,6},{6,5},{7,4},{8,11},{9,10},{10,... | collective-permute-start | bytes 393224 | tf_op jit(solution)/shard_map/ppermute | solution.py:61
  100.9 12.1 %collective-permute-start.31 = (f32[256,128]{1,0:T(8,128)S(1)}, f32[256,128]{1,0:T(8,128)S(1)}, u32[]{:S(2)}, u32[]{:S(2)}) collective-permute-start(f32[256,128]{1,0:T(8,128)S(1)} %get-tuple-element.90), channel_id=1, source_target_pairs={{0,4},{1,5},{2,6},{3,7},{4,0},{5,1},{6,2},{7,3},{8,12},{9,13},{10,... | collective-permute-start | bytes 393224 | tf_op jit(solution)/shard_map/ppermute | solution.py:61
  104.6 13.3 %collective-permute-start.32 = (f32[256,128]{1,0:T(8,128)S(1)}, f32[256,128]{1,0:T(8,128)S(1)}, u32[]{:S(2)}, u32[]{:S(2)}) collective-permute-start(f32[256,128]{1,0:T(8,128)S(1)} %get-tuple-element.91), channel_id=1, source_target_pairs={{0,5},{1,4},{2,7},{3,6},{4,1},{5,0},{6,3},{7,2},{8,13},{9,12},{10,... | collective-permute-start | bytes 393224 | tf_op jit(solution)/shard_map/ppermute | solution.py:61
  113.0 8.2 %collective-permute-start.33 = (f32[256,128]{1,0:T(8,128)S(1)}, f32[256,128]{1,0:T(8,128)S(1)}, u32[]{:S(2)}, u32[]{:S(2)}) collective-permute-start(f32[256,128]{1,0:T(8,128)S(1)} %get-tuple-element.92), channel_id=1, source_target_pairs={{0,6},{1,7},{2,4},{3,5},{4,2},{5,3},{6,0},{7,1},{8,14},{9,15},{10,... | collective-permute-start | bytes 393224 | tf_op jit(solution)/shard_map/ppermute | solution.py:61
  116.0 7.8 %collective-permute-start.34 = (f32[256,128]{1,0:T(8,128)S(1)}, f32[256,128]{1,0:T(8,128)S(1)}, u32[]{:S(2)}, u32[]{:S(2)}) collective-permute-start(f32[256,128]{1,0:T(8,128)S(1)} %get-tuple-element.93), channel_id=1, source_target_pairs={{0,7},{1,6},{2,5},{3,4},{4,3},{5,2},{6,1},{7,0},{8,15},{9,14},{10,... | collective-permute-start | bytes 393224 | tf_op jit(solution)/shard_map/ppermute | solution.py:61
  117.8 7.1 %collective-permute-start.9 = (f32[256,128]{1,0:T(8,128)S(1)}, f32[256,128]{1,0:T(8,128)S(1)}, u32[]{:S(2)}, u32[]{:S(2)}) collective-permute-start(f32[256,128]{1,0:T(8,128)S(1)} %get-tuple-element.63), channel_id=1, source_target_pairs={{0,1},{1,0},{2,3},{3,2},{4,5},{5,4},{6,7},{7,6},{8,9},{9,8},{10,11... | collective-permute-start | bytes 393224 | tf_op jit(solution)/shard_map/ppermute | solution.py:61
  121.2 5.3 %collective-permute-start.10 = (f32[256,128]{1,0:T(8,128)S(1)}, f32[256,128]{1,0:T(8,128)S(1)}, u32[]{:S(2)}, u32[]{:S(2)}) collective-permute-start(f32[256,128]{1,0:T(8,128)S(1)} %get-tuple-element.64), channel_id=1, source_target_pairs={{0,2},{1,3},{2,0},{3,1},{4,6},{5,7},{6,4},{7,5},{8,10},{9,11},{10,... | collective-permute-start | bytes 393224 | tf_op jit(solution)/shard_map/ppermute | solution.py:61
  123.8 5.9 %collective-permute-start.11 = (f32[256,128]{1,0:T(8,128)S(1)}, f32[256,128]{1,0:T(8,128)S(1)}, u32[]{:S(2)}, u32[]{:S(2)}) collective-permute-start(f32[256,128]{1,0:T(8,128)S(1)} %get-tuple-element.65), channel_id=1, source_target_pairs={{0,3},{1,2},{2,1},{3,0},{4,7},{5,6},{6,5},{7,4},{8,11},{9,10},{10,... | collective-permute-start | bytes 393224 | tf_op jit(solution)/shard_map/ppermute | solution.py:61
  123.8 23.0 %collective-permute-start.35 = (f32[2048,128]{1,0:T(8,128)S(1)}, f32[2048,128]{1,0:T(8,128)}, u32[]{:S(2)}, u32[]{:S(2)}) collective-permute-start(f32[2048,128]{1,0:T(8,128)S(1)} %constant_dynamic-update-slice_fusion.24.refs_0_), channel_id=1, source_target_pairs={{0,8},{8,0},{16,24},{24,16},{1,9},{9,1},{17,25},{25,17},{2,10},{10... | collective-permute-start | bytes 3145736 | tf_op jit(solution)/shard_map/ppermute | solution.py:19
  124.9 24.7 %collective-permute-start.25 = (f32[2048,128]{1,0:T(8,128)S(1)}, f32[2048,128]{1,0:T(8,128)}, u32[]{:S(2)}, u32[]{:S(2)}) collective-permute-start(f32[2048,128]{1,0:T(8,128)S(1)} %constant_dynamic-update-slice_fusion.16.refs_2_), channel_id=1, source_target_pairs={{0,16},{8,24},{16,0},{24,8},{1,17},{9,25},{17,1},{25,9},{2,18},{10... | collective-permute-start | bytes 3145736 | tf_op jit(solution)/shard_map/ppermute | solution.py:19
  126.4 29.3 %collective-permute-start.37 = (f32[2048,128]{1,0:T(8,128)}, f32[2048,128]{1,0:T(8,128)}, u32[]{:S(2)}, u32[]{:S(2)}) collective-permute-start(f32[2048,128]{1,0:T(8,128)} %constant_dynamic-update-slice_fusion.refs_2_), channel_id=1, source_target_pairs={{0,8},{8,0},{16,24},{24,16},{1,9},{9,1},{17,25},{25,17},{2,10},{10... | collective-permute-start | bytes 3145736 | tf_op jit(solution)/shard_map/ppermute | solution.py:19
  126.5 29.2 %collective-permute-start.36 = (f32[2048,128]{1,0:T(8,128)}, f32[2048,128]{1,0:T(8,128)}, u32[]{:S(2)}, u32[]{:S(2)}) collective-permute-start(f32[2048,128]{1,0:T(8,128)} %collective-permute-done.8.refs_0_), channel_id=1, source_target_pairs={{0,8},{8,0},{16,24},{24,16},{1,9},{9,1},{17,25},{25,17},{2,10},{10... | collective-permute-start | bytes 3145736 | tf_op jit(solution)/shard_map/ppermute | solution.py:19
  129.6 6.8 %collective-permute-start.14 = (f32[256,128]{1,0:T(8,128)S(1)}, f32[256,128]{1,0:T(8,128)S(1)}, u32[]{:S(2)}, u32[]{:S(2)}) collective-permute-start(f32[256,128]{1,0:T(8,128)S(1)} %get-tuple-element.68), channel_id=1, source_target_pairs={{0,6},{1,7},{2,4},{3,5},{4,2},{5,3},{6,0},{7,1},{8,14},{9,15},{10,... | collective-permute-start | bytes 393224 | tf_op jit(solution)/shard_map/ppermute | solution.py:61
  136.4 7.7 %collective-permute-start.15 = (f32[256,128]{1,0:T(8,128)S(1)}, f32[256,128]{1,0:T(8,128)S(1)}, u32[]{:S(2)}, u32[]{:S(2)}) collective-permute-start(f32[256,128]{1,0:T(8,128)S(1)} %get-tuple-element.69), channel_id=1, source_target_pairs={{0,7},{1,6},{2,5},{3,4},{4,3},{5,2},{6,1},{7,0},{8,15},{9,14},{10,... | collective-permute-start | bytes 393224 | tf_op jit(solution)/shard_map/ppermute | solution.py:61
  144.1 28.2 %collective-permute-start.16 = (f32[2048,128]{1,0:T(8,128)S(1)}, f32[2048,128]{1,0:T(8,128)}, u32[]{:S(2)}, u32[]{:S(2)}) collective-permute-start(f32[2048,128]{1,0:T(8,128)S(1)} %constant_dynamic-update-slice_fusion.8.refs_0_), channel_id=1, source_target_pairs={{0,8},{8,0},{16,24},{24,16},{1,9},{9,1},{17,25},{25,17},{2,10},{10... | collective-permute-start | bytes 3145736 | tf_op jit(solution)/shard_map/ppermute | solution.py:19
  146.9 30.9 %collective-permute-start.27 = (f32[2048,128]{1,0:T(8,128)S(1)}, f32[2048,128]{1,0:T(8,128)S(1)}, u32[]{:S(2)}, u32[]{:S(2)}) collective-permute-start(f32[2048,128]{1,0:T(8,128)S(1)} %constant_dynamic-update-slice_fusion.16.refs_2_), channel_id=1, source_target_pairs={{0,8},{8,0},{16,24},{24,16},{1,9},{9,1},{17,25},{25,17},{2,10},{10... | collective-permute-start | bytes 3145736 | tf_op jit(solution)/shard_map/ppermute | solution.py:19
  149.6 28.2 %collective-permute-start.26 = (f32[2048,128]{1,0:T(8,128)}, f32[2048,128]{1,0:T(8,128)S(1)}, u32[]{:S(2)}, u32[]{:S(2)}) collective-permute-start(f32[2048,128]{1,0:T(8,128)} %collective-permute-done.25.refs_0_), channel_id=1, source_target_pairs={{0,8},{8,0},{16,24},{24,16},{1,9},{9,1},{17,25},{25,17},{2,10},{10... | collective-permute-start | bytes 3145736 | tf_op jit(solution)/shard_map/ppermute | solution.py:19
  198.9 3.6 %collective-permute-start.39 = (f32[8,128]{1,0:T(8,128)S(1)}, f32[8,128]{1,0:T(8,128)S(1)}, u32[]{:S(2)}, u32[]{:S(2)}) collective-permute-start(f32[8,128]{1,0:T(8,128)S(1)} %broadcast_add_fusion), channel_id=1, source_target_pairs={{0,16},{8,24},{16,0},{24,8},{1,17},{9,25},{17,1},{25,9},{2,18},{10... | collective-permute-start | bytes 12296 | tf_op jit(solution)/shard_map/ppermute | solution.py:284
  200.4 3.0 %collective-permute-start.40 = (f32[8,128]{1,0:T(8,128)S(1)}, f32[8,128]{1,0:T(8,128)S(1)}, u32[]{:S(2)}, u32[]{:S(2)}) collective-permute-start(f32[8,128]{1,0:T(8,128)S(1)} %broadcast_add_fusion), channel_id=1, source_target_pairs={{0,24},{8,16},{16,8},{24,0},{1,25},{9,17},{17,9},{25,1},{2,26},{10... | collective-permute-start | bytes 12296 | tf_op jit(solution)/shard_map/ppermute | solution.py:284
  200.8 2.7 %collective-permute-start.38 = (f32[8,128]{1,0:T(8,128)S(1)}, f32[8,128]{1,0:T(8,128)S(1)}, u32[]{:S(2)}, u32[]{:S(2)}) collective-permute-start(f32[8,128]{1,0:T(8,128)S(1)} %broadcast_add_fusion), channel_id=1, source_target_pairs={{0,8},{8,0},{16,24},{24,16},{1,9},{9,1},{17,25},{25,17},{2,10},{10... | collective-permute-start | bytes 12296 | tf_op jit(solution)/shard_map/ppermute | solution.py:284
  203.5 8.8 %collective-permute-start.47 = (f32[8,128]{1,0:T(8,128)S(1)}, f32[8,128]{1,0:T(8,128)S(1)}, u32[]{:S(2)}, u32[]{:S(2)}) collective-permute-start(f32[8,128]{1,0:T(8,128)S(1)} %add_add_fusion), channel_id=1, source_target_pairs={{0,7},{1,6},{2,5},{3,4},{4,3},{5,2},{6,1},{7,0},{8,15},{9,14},{10,... | collective-permute-start | bytes 12296 | tf_op jit(solution)/shard_map/ppermute | solution.py:284
  206.2 7.5 %collective-permute-start.46 = (f32[8,128]{1,0:T(8,128)S(1)}, f32[8,128]{1,0:T(8,128)S(1)}, u32[]{:S(2)}, u32[]{:S(2)}) collective-permute-start(f32[8,128]{1,0:T(8,128)S(1)} %add_add_fusion), channel_id=1, source_target_pairs={{0,6},{1,7},{2,4},{3,5},{4,2},{5,3},{6,0},{7,1},{8,14},{9,15},{10,... | collective-permute-start | bytes 12296 | tf_op jit(solution)/shard_map/ppermute | solution.py:284
  207.8 6.9 %collective-permute-start.45 = (f32[8,128]{1,0:T(8,128)S(1)}, f32[8,128]{1,0:T(8,128)S(1)}, u32[]{:S(2)}, u32[]{:S(2)}) collective-permute-start(f32[8,128]{1,0:T(8,128)S(1)} %add_add_fusion), channel_id=1, source_target_pairs={{0,5},{1,4},{2,7},{3,6},{4,1},{5,0},{6,3},{7,2},{8,13},{9,12},{10,... | collective-permute-start | bytes 12296 | tf_op jit(solution)/shard_map/ppermute | solution.py:284
  209.7 5.0 %collective-permute-start.44 = (f32[8,128]{1,0:T(8,128)S(1)}, f32[8,128]{1,0:T(8,128)S(1)}, u32[]{:S(2)}, u32[]{:S(2)}) collective-permute-start(f32[8,128]{1,0:T(8,128)S(1)} %add_add_fusion), channel_id=1, source_target_pairs={{0,4},{1,5},{2,6},{3,7},{4,0},{5,1},{6,2},{7,3},{8,12},{9,13},{10,... | collective-permute-start | bytes 12296 | tf_op jit(solution)/shard_map/ppermute | solution.py:284
  211.2 4.5 %collective-permute-start.43 = (f32[8,128]{1,0:T(8,128)S(1)}, f32[8,128]{1,0:T(8,128)S(1)}, u32[]{:S(2)}, u32[]{:S(2)}) collective-permute-start(f32[8,128]{1,0:T(8,128)S(1)} %add_add_fusion), channel_id=1, source_target_pairs={{0,3},{1,2},{2,1},{3,0},{4,7},{5,6},{6,5},{7,4},{8,11},{9,10},{10,... | collective-permute-start | bytes 12296 | tf_op jit(solution)/shard_map/ppermute | solution.py:284
  212.3 3.6 %collective-permute-start.42 = (f32[8,128]{1,0:T(8,128)S(1)}, f32[8,128]{1,0:T(8,128)S(1)}, u32[]{:S(2)}, u32[]{:S(2)}) collective-permute-start(f32[8,128]{1,0:T(8,128)S(1)} %add_add_fusion), channel_id=1, source_target_pairs={{0,2},{1,3},{2,0},{3,1},{4,6},{5,7},{6,4},{7,5},{8,10},{9,11},{10,... | collective-permute-start | bytes 12296 | tf_op jit(solution)/shard_map/ppermute | solution.py:284
  213.7 3.6 %collective-permute-start.41 = (f32[8,128]{1,0:T(8,128)S(1)}, f32[8,128]{1,0:T(8,128)S(1)}, u32[]{:S(2)}, u32[]{:S(2)}) collective-permute-start(f32[8,128]{1,0:T(8,128)S(1)} %add_add_fusion), channel_id=1, source_target_pairs={{0,1},{1,0},{2,3},{3,2},{4,5},{5,4},{6,7},{7,6},{8,9},{9,8},{10,11... | collective-permute-start | bytes 12296 | tf_op jit(solution)/shard_map/ppermute | solution.py:284
  (12 other events, 31.9 us)

commit v2 on v0

--- a/solution.py
+++ b/solution.py
@@ -240,17 +240,14 @@
 
 
 def sum_everywhere(tile):
-    axes = ("gx", "gy")
-    devices = lax.axis_size("gx") * lax.axis_size("gy")
-    copies = jnp.broadcast_to(tile[None], (devices,) + tile.shape)
-    return jnp.sum(lax.all_to_all(copies, axes, split_axis=0, concat_axis=0, tiled=True))
+    return jnp.sum(lax.all_gather(jnp.sum(tile, axis=0, keepdims=True), ("gx", "gy")))
 
 
 def four_way(field, row_scale, col_scale, row_rate, col_shift, col_mix):
     position = lax.axis_index("gx")
     planes, rows, columns = field.shape
     length, width = planes * rows, columns // 4
-    cuts = lax.optimization_barrier(tuple(field[:, :, c * width : (c + 1) * width] for c in range(4)))
+    field_a, field_b = lax.optimization_barrier((field[:, :, : 2 * width], field[:, :, 2 * width :]))
     sign = jnp.where(position < 2, 1.0, -1.0)
 
     own_real = jnp.where(position == 1, -1.0, jnp.where(position == 3, 0.0, 1.0))
@@ -279,10 +276,14 @@
     fixed = 2.0 * (columns * jnp.sum(jnp.log(row_scale)) + length * jnp.sum(jnp.log(col_scale)))
     fixed = fixed - length * columns * math.log(2.0 * math.pi)
 
-    first_a = [from_partner(cuts[c], "gx", 1) + sign * cuts[c] for c in (0, 1)]
-    first_b = [to_planes(cuts[c])[0] for c in (2, 3)]
-    second_a = [to_planes(value)[0] for value in first_a]
-    second_b = [from_partner(value, "gx", 1) for value in first_b]
+    first_a, first_b = lax.optimization_barrier((from_partner(field_a, "gx", 1), to_planes(field_b)[0]))
+    first_a = [first_a[:, :, span] + sign * field_a[:, :, span] for span in (slice(0, width), slice(width, None))]
+    first_b = [first_b[:, :width], first_b[:, width:]]
+    first_a, first_b = lax.optimization_barrier((first_a, first_b))
+    second_b, second_a = [from_partner(first_b[0], "gx", 1)], [to_planes(first_a[0])[0]]
+    first_a[1], second_b[0] = lax.optimization_barrier((first_a[1], second_b[0]))
+    second_b.append(from_partner(first_b[1], "gx", 1))
+    second_a.append(to_planes(first_a[1])[0])
     parts = []
     for step in range(2):
         own, other = second_a[step], from_partner(second_a[step], "gx", 0)

time: 220 us -> 247 us (1.12)
  blocking collectives: 46.1 us -> 68.4 us
  other arithmetic: 19 us -> 25.2 us
  waiting for transfers between devices: 74.3 us -> 69.7 us
    all_gather x0 -> x1, blocking collectives: none -> 68.4 us  [sum_everywhere(): lax.all_gather(jnp.sum(tile, axis=0, keepdims=True), ('gx', 'gy'))]
    all_to_all x2 -> x0, blocking collectives: 46.1 us -> none  [the longest x1 32.8 us: to_planes(): return lax.all_to_all(values, 'gy', split_axis=0, concat_axis=1, tiled=True)]
    all_to_all x3, waiting for transfers between devices: 10.9 us -> 1.08 us  [to_planes(): return lax.all_to_all(values, 'gy', split_axis=0, concat_axis=1, tiled=True)]
    ppermute x10 -> x9, waiting for transfers between devices: 63.4 us -> 68.7 us  [from_partner(): return lax.ppermute(value, axis, pairs)]
    another operation x3, other arithmetic: 1.83 us -> 6.02 us  [split_table(): jnp.stack([high.astype(jnp.bfloat16), (table - high).astype(jnp.bfloat16)])]
    all_to_all x3, starting transfers between devices: 15 us -> 17.8 us  [to_planes(): return lax.all_to_all(values, 'gy', split_axis=0, concat_axis=1, tiled=True)]
    add x3 -> x1, other arithmetic: 4.96 us -> 3.19 us  [four_way(): first_a[:, :, span] + sign * field_a[:, :, span]]
    slice x1 -> x2, local copies, waits for them, and re-layouts: 3.91 us -> 5.64 us  [the longest x1 3.81 us: four_way(): field[:, :, 2 * width:]]
  transfers between devices with their start and end apart: 13 -> 12, of which waited for: 5 -> 4; matrix products, arithmetic and copies ran while one was open for 9% -> 9% of each run, Pallas kernels for 13% -> 12%
where the time goes in v2:
time: 247 us; the launch traced here: 246 us
  waiting for transfers between devices  69.7 us (28%)
  blocking collectives  68.4 us (28%)
  Pallas kernels  47.4 us (19%)
  other arithmetic  25.2 us (10%)
  starting transfers between devices  22.8 us (9%)
  local copies, waits for them, and re-layouts  8.34 us (3%)
  between operations  3.95 us (2%)
    ppermute x9, waiting for transfers between devices, from_partner(): return lax.ppermute(value, axis, pairs)  68.7 us
    all_gather x1, blocking collectives, sum_everywhere(): lax.all_gather(jnp.sum(tile, axis=0, keepdims=True), ('gx', 'gy'))  68.4 us
    pallas_call x4, Pallas kernels, y_dft(): pl.pallas_call(functools.partial(y_kernel, count), out_shape=jax.ShapeDty...  25 us
    all_to_all x3, starting transfers between devices, to_planes(): return lax.all_to_all(values, 'gy', split_axis=0, concat_axis=1, tiled=True)  17.8 us
    pallas_call x1, Pallas kernels, x_last(): pl.pallas_call(functools.partial(x_last_kernel, count), out_shape=(jax.Sh...  13.1 us
    pallas_call x1, Pallas kernels, x_first(): pl.pallas_call(functools.partial(x_first_kernel, count), out_shape=jax.Sh...  9.3 us
    another operation x3, other arithmetic, split_table(): jnp.stack([high.astype(jnp.bfloat16), (table - high).astype(jnp.bfloat16)])  6.02 us
    sin x3, other arithmetic, root_table(): return (jnp.cos(angle), jnp.sin(angle))  5.22 us
  transfers between devices with their start and end apart: 12, of which 4 were waited for; matrix products, arithmetic and copies ran while one was open for 9% of the time, Pallas kernels for 12%

profile of v2, /device:TPU:0, one launch (start us, length us, event | category | flops | bytes accessed | tf_op | source)
XLA Modules:
  0.0 245.8 jit_solution(17846180001232290118)
XLA Ops:
  0.6 3.8 %fusion.43 = (f32[8,256,256]{2,1,0:T(8,128)}, f32[8,256,256]{2,1,0:T(8,128)S(1)}) fusion(f32[8,256,512]{2,1,0:T(8,128)} %param.6), kind=kLoop, calls=%fused_computation.93 | loop fusion | bytes 8388608 | tf_op jit(solution)/shard_map/slice | solution.py:250
  4.4 7.3 %all-to-all-start = ((f32[8,256,256]{2,1,0:T(8,128)}), f32[8,256,256]{2,1,0:T(8,128)}, u32[]{:S(2)}, u32[]{:S(2)}) async-start(f32[8,256,256]{2,1,0:T(8,128)} %get-tuple-element.15), calls=%async_computation | async-start | bytes 4194304 | tf_op jit(solution)/shard_map/all_to_all | solution.py:23
  11.7 1.6 collective-permute-start
  13.3 45.7 %collective-permute-done = f32[8,256,256]{2,1,0:T(8,128)} collective-permute-done((f32[8,256,256]{2,1,0:T(8,128)S(1)}, f32[8,256,256]{2,1,0:T(8,128)}, u32[]{:S(2)}, u32[]{:S(2)}) %collective-permute-start) | collective-permute-done | bytes 2097184 | tf_op jit(solution)/shard_map/ppermute | solution.py:19
  59.0 1.1 all-to-all-done
  60.0 1.8 fusion.44
  61.9 0.4 copy-done.3
  62.3 3.2 %multiply_add_fusion = (f32[8,256,128]{2,1,0:T(8,128)}, f32[8,256,128]{2,1,0:T(8,128)}) fusion(f32[8,256,256]{2,1,0:T(8,128)S(1)} %copy-done.3, f32[8,256,256]{2,1,0:T(8,128)} %collective-permute-done, f32[]{:T(128)S(6)} %select_n.63), kind=kLoop, calls=%fused_computation.35 | loop fusion | flops 1048576 | bytes 6291460 | tf_op jit(solution)/shard_map/add | solution.py:280
  65.5 4.6 %all-to-all-start.2 = ((f32[8,256,128]{2,1,0:T(8,128)}), f32[8,256,128]{2,1,0:T(8,128)}, u32[]{:S(2)}, u32[]{:S(2)}) async-start(f32[8,256,128]{2,1,0:T(8,128)} %get-tuple-element.22), calls=%async_computation.2 | async-start | bytes 2097152 | tf_op jit(solution)/shard_map/all_to_all | solution.py:23
  70.0 0.1 fusion.41
  70.1 1.6 collective-permute-start.1
  71.7 0.1 pad_maximum_fusion.12
  71.8 0.1 reshape.420.coef_ref
  71.8 1.0 fusion.34
  72.8 1.0 fusion.32
  73.9 1.1 maximum_bitcast_fusion
  75.0 4.1 %fusion.23 = (f32[512,512]{1,0:T(8,128)S(1)}, f32[512,512]{1,0:T(8,128)S(1)}, f32[512,512]{1,0:T(8,128)S(1)}) fusion(s32[512]{0:T(512)S(1)} %multiply_add_fusion.2), kind=kLoop, calls=%fused_computation.56 | loop fusion | flops 3932160 | bytes 3147776 | tf_op jit(solution)/shard_map/sin | solution.py:36
  79.1 1.7 fusion.16
  80.8 0.6 collective-permute-start.3
  81.4 15.0 %collective-permute-done.1.refs_0_ = f32[2048,128]{1,0:T(8,128)} collective-permute-done((f32[2048,128]{1,0:T(8,128)S(1)}, f32[2048,128]{1,0:T(8,128)}, u32[]{:S(2)}, u32[]{:S(2)}) %collective-permute-start.1) | collective-permute-done | bytes 1048608 | tf_op jit(solution)/shard_map/ppermute | solution.py:19
  96.4 6.0 %all-to-all-start.1 = ((f32[8,256,128]{2,1,0:T(8,128)}), f32[8,256,128]{2,1,0:T(8,128)}, u32[]{:S(2)}, u32[]{:S(2)}) async-start(f32[8,256,128]{2,1,0:T(8,128)} %get-tuple-element.20), calls=%async_computation.1 | async-start | bytes 2097152 | tf_op jit(solution)/shard_map/all_to_all | solution.py:23
  102.4 0.6 log_reduce_fusion
  103.0 3.7 %reduce-precision_convert_fusion = (bf16[1,512,1024]{2,1,0:T(8,128)(2,1)}, bf16[1,512,1024]{2,1,0:T(8,128)(2,1)}, bf16[1,512,1024]{2,1,0:T(8,128)(2,1)}, bf16[1,512,1024]{2,1,0:T(8,128)(2,1)}) fusion(f32[1,128,1024]{2,1,0:T(8,128)} %get-tuple-element.44, f32[1,128,1024]{2,1,0:T(8,128)} %get-tuple-element.35, f32[1,128,1024]{2,1,0:T(8,128)} %get-tuple-element.47, ...), kind=kLoop, calls=%fused_computation.1 | loop fusion | flops 7340032 | bytes 8388608 | tf_op jit(solution)/shard_map/convert_element_type | solution.py:48
  106.8 0.1 collective-permute-start.8
  106.9 0.5 collective-permute-start.7
  107.4 1.2 reduce-precision_convert_fusion.2
  108.5 0.1 collective-permute-start.5
  108.6 8.0 %collective-permute-done.3.refs_0_ = f32[2048,128]{1,0:T(8,128)} collective-permute-done((f32[2048,128]{1,0:T(8,128)S(1)}, f32[2048,128]{1,0:T(8,128)}, u32[]{:S(2)}, u32[]{:S(2)}) %collective-permute-start.3) | collective-permute-done | bytes 1048608 | tf_op jit(solution)/shard_map/ppermute | solution.py:19
  116.6 0.6 log_reduce_fusion.1
  117.2 0.5 collective-permute-start.6
  117.8 0.1 pad_maximum_fusion.11.coef_ref
  119.1 1.3 pad_maximum_fusion.5.refs_2_.refs_4_
  120.4 3.2 %pad_maximum_fusion.3.refs_2_ = bf16[2,512,1024]{2,1,0:T(8,128)(2,1)} fusion(bf16[1,512,1024]{2,1,0:T(8,128)(2,1)} %get-tuple-element.31, bf16[1,512,1024]{2,1,0:T(8,128)(2,1)} %get-tuple-element.30), kind=kLoop, calls=%fused_computation.21 | loop fusion | flops 1048576 | bytes 4194304 | tf_op jit(solution)/shard_map/stack | solution.py:48
  123.7 1.5 pad_maximum_fusion.1.refs_2_
  125.2 0.0 all-to-all-done.1
  125.2 0.1 collective-permute-start.2
  125.3 0.6 broadcast_in_dim.4.refs_3_.refs_5_
  125.9 6.8 %y_dft.7.refs_1_ = bf16[4,2048,128]{2,1,0:T(8,128)(2,1)S(1)} custom-call(f32[2,4]{1,0:T(2,128)S(1)} %pad_maximum_fusion.11.coef_ref, f32[2048,128]{1,0:T(8,128)} %collective-permute-done.1.refs_0_, f32[2048,128]{1,0:T(8,128)} %collective-permute-done.7.refs_1_, f32[2048,128]{1,0:T(8,128)S(1)} %get-tuple-element.19.refs_2_, ...), custom_call_target="tpu_custom_call" | custom-call | flops 1610612736 | bytes 7340032 | tf_op jit(solution)/shard_map/y_dft/pallas_call | solution.py:133
  132.7 6.8 %y_dft.5.refs_1_ = bf16[4,2048,128]{2,1,0:T(8,128)(2,1)S(1)} custom-call(f32[2,4]{1,0:T(2,128)S(1)} %pad_maximum_fusion.11.coef_ref, f32[2048,128]{1,0:T(8,128)} %collective-permute-done.3.refs_0_, f32[2048,128]{1,0:T(8,128)} %collective-permute-done.4.refs_1_, f32[2048,128]{1,0:T(8,128)S(1)} %get-tuple-element.21.refs_2_, ...), custom_call_target="tpu_custom_call" | custom-call | flops 1610612736 | bytes 7340032 | tf_op jit(solution)/shard_map/y_dft/pallas_call | solution.py:133
  139.5 6.0 %y_dft.6.refs_0_ = bf16[4,2048,128]{2,1,0:T(8,128)(2,1)S(1)} custom-call(f32[2,2]{1,0:T(2,128)S(1)} %reshape.420.coef_ref, f32[2048,128]{1,0:T(8,128)} %bitcast.12.refs_0_, f32[2048,128]{1,0:T(8,128)} %collective-permute-done.6.refs_1_, bf16[2,512,512]{2,1,0:T(8,128)(2,1)S(1)} %pad_maximum_fusion.5.refs_2_.refs_4_, ...), custom_call_target="tpu_custom_call" | custom-call | flops 1610612736 | bytes 5242880 | tf_op jit(solution)/shard_map/y_dft/pallas_call | solution.py:133
  145.5 9.3 %x_first.1.refs_3_ = f32[2048,1024]{1,0:T(8,128)} custom-call(bf16[4,2048,128]{2,1,0:T(8,128)(2,1)S(1)} %y_dft.6.refs_0_, bf16[4,2048,128]{2,1,0:T(8,128)(2,1)S(1)} %y_dft.7.refs_1_, bf16[2,512,1024]{2,1,0:T(8,128)(2,1)S(1)} %copy-done.1), custom_call_target="tpu_custom_call" | custom-call | flops 6442450944 | bytes 16777216 | tf_op jit(solution)/shard_map/x_first/pallas_call | solution.py:167
  154.8 5.5 %y_dft.4.refs_0_ = bf16[4,2048,128]{2,1,0:T(8,128)(2,1)S(1)} custom-call(f32[2,2]{1,0:T(2,128)S(1)} %reshape.420.coef_ref, f32[2048,128]{1,0:T(8,128)} %bitcast.5.refs_0_, f32[2048,128]{1,0:T(8,128)S(1)} %collective-permute-done.2.refs_1_, bf16[2,512,512]{2,1,0:T(8,128)(2,1)S(1)} %pad_maximum_fusion.5.refs_2_.refs_4_, ...), custom_call_target="tpu_custom_call" | custom-call | flops 1610612736 | bytes 5242880 | tf_op jit(solution)/shard_map/y_dft/pallas_call | solution.py:133
  160.3 0.0 copy-start
  160.3 0.6 broadcast_in_dim.5.refs_4_
  160.9 1.0 copy-done
  161.9 13.1 %x_last.1 = (f32[2,1,2048,512]{3,2,1,0:T(8,128)}, f32[8,128]{1,0:T(8,128)S(1)}) custom-call(bf16[4,2048,128]{2,1,0:T(8,128)(2,1)S(1)} %y_dft.4.refs_0_, bf16[4,2048,128]{2,1,0:T(8,128)(2,1)S(1)} %y_dft.5.refs_1_, bf16[2,512,1024]{2,1,0:T(8,128)(2,1)S(1)} %copy-done, f32[2048,1024]{1,0:T(8,128)} %x_first.1.refs_3_, ...), custom_call_target="tpu_custom_call" | custom-call | flops 6442450944 | bytes 25165824 | tf_op jit(solution)/shard_map/x_last/pallas_call | solution.py:214
  175.0 68.4 %all-gather.1 = f32[32,1,128]{2,1,0:T(1,128)S(1)} all-gather(f32[1,1,128]{2,1,0:T(1,128)S(1)} %bitcast.38), channel_id=2, replica_groups=mesh['gx'=4,'gy'=8] {'gx','gy'}, dimensions={0}, use_global_device_ids=true | all-gather | bytes 16896 | tf_op jit(solution)/shard_map/all_gather | solution.py:243
  243.4 0.6 reduce
  (37 shorter events, 0.1 us)
Async XLA Ops:
  4.4 7.3 %copy-start.2 = (f32[8,256,256]{2,1,0:T(8,128)}, f32[8,256,256]{2,1,0:T(8,128)S(1)}, u32[]{:S(2)}) copy-start(f32[8,256,256]{2,1,0:T(8,128)S(1)} %get-tuple-element.14) | copy-start | bytes 6291460
  4.4 55.6 %all-to-all-start = ((f32[8,256,256]{2,1,0:T(8,128)}), f32[8,256,256]{2,1,0:T(8,128)}, u32[]{:S(2)}, u32[]{:S(2)}) async-start(f32[8,256,256]{2,1,0:T(8,128)} %get-tuple-element.15), calls=%async_computation | async-start | bytes 4194304 | tf_op jit(solution)/shard_map/all_to_all | solution.py:23
  11.7 47.3 %collective-permute-start = (f32[8,256,256]{2,1,0:T(8,128)S(1)}, f32[8,256,256]{2,1,0:T(8,128)}, u32[]{:S(2)}, u32[]{:S(2)}) collective-permute-start(f32[8,256,256]{2,1,0:T(8,128)S(1)} %get-tuple-element.14), channel_id=1, source_target_pairs={{0,16},{8,24},{16,0},{24,8},{1,17},{9,25},{17,1},{25,9},{2,18},{10... | collective-permute-start | bytes 6291464 | tf_op jit(solution)/shard_map/ppermute | solution.py:19
  60.0 2.2 copy-start.3
  65.5 30.9 %all-to-all-start.2 = ((f32[8,256,128]{2,1,0:T(8,128)}), f32[8,256,128]{2,1,0:T(8,128)}, u32[]{:S(2)}, u32[]{:S(2)}) async-start(f32[8,256,128]{2,1,0:T(8,128)} %get-tuple-element.22), calls=%async_computation.2 | async-start | bytes 2097152 | tf_op jit(solution)/shard_map/all_to_all | solution.py:23
  70.1 26.3 %collective-permute-start.1 = (f32[2048,128]{1,0:T(8,128)S(1)}, f32[2048,128]{1,0:T(8,128)}, u32[]{:S(2)}, u32[]{:S(2)}) collective-permute-start(f32[2048,128]{1,0:T(8,128)S(1)} %get-tuple-element.19.refs_2_), channel_id=1, source_target_pairs={{0,16},{8,24},{16,0},{24,8},{1,17},{9,25},{17,1},{25,9},{2,18},{10... | collective-permute-start | bytes 3145736 | tf_op jit(solution)/shard_map/ppermute | solution.py:19
  80.8 21.6 %copy-start.8 = (f32[512]{0:T(512)S(1)}, f32[512]{0:T(512)}, u32[]{:S(2)}) copy-start(f32[512]{0:T(512)} %param.8) | copy-start | bytes 6148
  80.8 21.6 %copy-start.11 = (f32[512]{0:T(512)S(1)}, f32[512]{0:T(512)}, u32[]{:S(2)}) copy-start(f32[512]{0:T(512)} %param.11) | copy-start | bytes 6148
  80.8 21.6 %copy-start.12 = (f32[512]{0:T(512)S(1)}, f32[512]{0:T(512)}, u32[]{:S(2)}) copy-start(f32[512]{0:T(512)} %param.10) | copy-start | bytes 6148
  80.8 21.6 %copy-start.9 = (f32[2048]{0:T(1024)S(1)}, f32[2048]{0:T(1024)}, u32[]{:S(2)}) copy-start(f32[2048]{0:T(1024)} %param.7) | copy-start | bytes 24580
  80.8 35.8 %collective-permute-start.3 = (f32[2048,128]{1,0:T(8,128)S(1)}, f32[2048,128]{1,0:T(8,128)}, u32[]{:S(2)}, u32[]{:S(2)}) collective-permute-start(f32[2048,128]{1,0:T(8,128)S(1)} %get-tuple-element.21.refs_2_), channel_id=1, source_target_pairs={{0,16},{8,24},{16,0},{24,8},{1,17},{9,25},{17,1},{25,9},{2,18},{10... | collective-permute-start | bytes 3145736 | tf_op jit(solution)/shard_map/ppermute | solution.py:19
  96.4 28.8 %all-to-all-start.1 = ((f32[8,256,128]{2,1,0:T(8,128)}), f32[8,256,128]{2,1,0:T(8,128)}, u32[]{:S(2)}, u32[]{:S(2)}) async-start(f32[8,256,128]{2,1,0:T(8,128)} %get-tuple-element.20), calls=%async_computation.1 | async-start | bytes 2097152 | tf_op jit(solution)/shard_map/all_to_all | solution.py:23
  103.0 4.3 %copy-start.6 = (f32[1,256,512]{2,1,0:T(8,128)S(1)}, f32[1,256,512]{2,1,0:T(8,128)}, u32[]{:S(2)}) copy-start(f32[1,256,512]{2,1,0:T(8,128)} %get-tuple-element.50) | copy-start | bytes 1572868
  103.0 4.3 %copy-start.7 = (f32[1,256,512]{2,1,0:T(8,128)S(1)}, f32[1,256,512]{2,1,0:T(8,128)}, u32[]{:S(2)}) copy-start(f32[1,256,512]{2,1,0:T(8,128)} %get-tuple-element.51) | copy-start | bytes 1572868
  106.8 18.4 %collective-permute-start.8 = (f32[2048,128]{1,0:T(8,128)S(1)}, f32[2048,128]{1,0:T(8,128)}, u32[]{:S(2)}, u32[]{:S(2)}) collective-permute-start(f32[2048,128]{1,0:T(8,128)S(1)} %get-tuple-element.19.refs_2_), channel_id=1, source_target_pairs={{0,8},{8,0},{16,24},{24,16},{1,9},{9,1},{17,25},{25,17},{2,10},{10... | collective-permute-start | bytes 3145736 | tf_op jit(solution)/shard_map/ppermute | solution.py:19
  106.9 18.5 %collective-permute-start.7 = (f32[2048,128]{1,0:T(8,128)}, f32[2048,128]{1,0:T(8,128)}, u32[]{:S(2)}, u32[]{:S(2)}) collective-permute-start(f32[2048,128]{1,0:T(8,128)} %collective-permute-done.1.refs_0_), channel_id=1, source_target_pairs={{0,8},{8,0},{16,24},{24,16},{1,9},{9,1},{17,25},{25,17},{2,10},{10... | collective-permute-start | bytes 3145736 | tf_op jit(solution)/shard_map/ppermute | solution.py:19
  108.5 24.2 %collective-permute-start.5 = (f32[2048,128]{1,0:T(8,128)S(1)}, f32[2048,128]{1,0:T(8,128)}, u32[]{:S(2)}, u32[]{:S(2)}) collective-permute-start(f32[2048,128]{1,0:T(8,128)S(1)} %get-tuple-element.21.refs_2_), channel_id=1, source_target_pairs={{0,8},{8,0},{16,24},{24,16},{1,9},{9,1},{17,25},{25,17},{2,10},{10... | collective-permute-start | bytes 3145736 | tf_op jit(solution)/shard_map/ppermute | solution.py:19
  116.6 16.1 %collective-permute-start.4 = (f32[2048,128]{1,0:T(8,128)}, f32[2048,128]{1,0:T(8,128)}, u32[]{:S(2)}, u32[]{:S(2)}) collective-permute-start(f32[2048,128]{1,0:T(8,128)} %collective-permute-done.3.refs_0_), channel_id=1, source_target_pairs={{0,8},{8,0},{16,24},{24,16},{1,9},{9,1},{17,25},{25,17},{2,10},{10... | collective-permute-start | bytes 3145736 | tf_op jit(solution)/shard_map/ppermute | solution.py:19
  117.2 22.2 %collective-permute-start.6 = (f32[2048,128]{1,0:T(8,128)}, f32[2048,128]{1,0:T(8,128)}, u32[]{:S(2)}, u32[]{:S(2)}) collective-permute-start(f32[2048,128]{1,0:T(8,128)} %bitcast.12.refs_0_), channel_id=1, source_target_pairs={{0,8},{8,0},{16,24},{24,16},{1,9},{9,1},{17,25},{25,17},{2,10},{10... | collective-permute-start | bytes 3145736 | tf_op jit(solution)/shard_map/ppermute | solution.py:19
  120.4 3.2 %copy-start.4 = (bf16[1,512,1024]{2,1,0:T(8,128)(2,1)S(1)}, bf16[1,512,1024]{2,1,0:T(8,128)(2,1)}, u32[]{:S(2)}) copy-start(bf16[1,512,1024]{2,1,0:T(8,128)(2,1)} %get-tuple-element.61) | copy-start | bytes 3145732
  120.4 3.2 %copy-start.5 = (bf16[1,512,1024]{2,1,0:T(8,128)(2,1)S(1)}, bf16[1,512,1024]{2,1,0:T(8,128)(2,1)}, u32[]{:S(2)}) copy-start(bf16[1,512,1024]{2,1,0:T(8,128)(2,1)} %get-tuple-element.62) | copy-start | bytes 3145732
  123.7 1.5 copy-start.10
  125.2 29.6 %collective-permute-start.2 = (f32[2048,128]{1,0:T(8,128)}, f32[2048,128]{1,0:T(8,128)S(1)}, u32[]{:S(2)}, u32[]{:S(2)}) collective-permute-start(f32[2048,128]{1,0:T(8,128)} %bitcast.5.refs_0_), channel_id=1, source_target_pairs={{0,8},{8,0},{16,24},{24,16},{1,9},{9,1},{17,25},{25,17},{2,10},{10... | collective-permute-start | bytes 3145736 | tf_op jit(solution)/shard_map/ppermute | solution.py:19
  139.5 6.0 %copy-start.1 = (bf16[2,512,1024]{2,1,0:T(8,128)(2,1)S(1)}, bf16[2,512,1024]{2,1,0:T(8,128)(2,1)}, u32[]{:S(2)}) copy-start(bf16[2,512,1024]{2,1,0:T(8,128)(2,1)} %pad_maximum_fusion.3.refs_2_) | copy-start | bytes 6291460
  160.3 1.6 copy-start

commit v3 on v0

--- a/solution.py
+++ b/solution.py
@@ -10,7 +10,7 @@
 
 precision_top = lax.Precision.HIGHEST
 RADIX = 8
-VMEM_BYTES = 40 * 1024 * 1024
+Y_BYTES, X_BYTES = 20 * 1024 * 1024, 30 * 1024 * 1024
 
 
 def from_partner(value, axis, stride):
@@ -43,9 +43,10 @@
     return root_table(local_index, freqs, devices * width)
 
 
-def split_table(table):
+def split_table(table, axis, order):
     high = lax.reduce_precision(table, 8, 7)
-    return jnp.stack([high.astype(jnp.bfloat16), (table - high).astype(jnp.bfloat16)])
+    parts = [high.astype(jnp.bfloat16), (table - high).astype(jnp.bfloat16)]
+    return jnp.concatenate([parts[which] for which in order], axis)
 
 
 def split_value(value):
@@ -78,12 +79,8 @@
     return jnp.dot(left, right, preferred_element_type=jnp.float32)
 
 
-def dot_split(left_high, left_low, right_high, right_low):
-    return dot(left_high, right_high) + (dot(left_high, right_low) + dot(left_low, right_high))
-
-
 def y_kernel(count, coef_ref, *refs):
-    inputs, (table_ref, twist_ref, out_ref, high_ref, low_ref, step_ref) = refs[:count], refs[count:]
+    inputs, (table_ref, twist_ref, out_ref, split_ref, step_ref) = refs[:count], refs[count:]
     length, width = inputs[0].shape
     inner = length // RADIX
     for s in range(RADIX):
@@ -93,16 +90,10 @@
             for place in range(1, count):
                 mixed = mixed + parts[place] * coef_ref[which, place]
             high, low = split_value(mixed)
-            rows, cols = pl.ds(which * inner, inner), pl.ds(s * width, width)
-            high_ref[rows, cols] = high
-            low_ref[rows, cols] = low
-    piece = 2 * width
-
-    @pl.loop(0, RADIX * width // piece)
-    def _(block):
-        cols = pl.ds(pl.multiple_of(block * piece, piece), piece)
-        step_ref[:, cols] = dot_split(table_ref[0], table_ref[1], high_ref[:, cols], low_ref[:, cols])
-
+            cols = pl.ds(s * width, width)
+            for place, value in enumerate((high, high, low)):
+                split_ref[pl.ds((2 * place + which) * inner, inner), cols] = value
+    step_ref[...] = dot(table_ref[...], split_ref[...])
     rows_each = 16
 
     @pl.loop(0, inner // rows_each)
@@ -136,11 +127,10 @@
         in_specs=[pl.BlockSpec(memory_space=pltpu.SMEM)] + [whole] * (count + 2),
         out_specs=whole,
         scratch_shapes=[
-            pltpu.VMEM((2 * inner, RADIX * width), jnp.bfloat16),
-            pltpu.VMEM((2 * inner, RADIX * width), jnp.bfloat16),
+            pltpu.VMEM((6 * inner, RADIX * width), jnp.bfloat16),
             pltpu.VMEM((2 * inner, RADIX * width), jnp.float32),
         ],
-        compiler_params=pltpu.CompilerParams(vmem_limit_bytes=VMEM_BYTES),
+        compiler_params=pltpu.CompilerParams(vmem_limit_bytes=Y_BYTES),
         cost_estimate=pl.CostEstimate(
             flops=24 * inner * length * width, bytes_accessed=4 * length * width * (count + 3), transcendentals=0
         ),
@@ -149,9 +139,9 @@
 
 
 def x_product(parts, table_ref):
-    high = jnp.concatenate([ref[which] for ref in parts for which in (0, 2)], axis=1)
-    low = jnp.concatenate([ref[which] for ref in parts for which in (1, 3)], axis=1)
-    return dot_split(high, low, table_ref[0], table_ref[1])
+    high = [ref[which] for ref in parts for which in (0, 2)]
+    low = [ref[which] for ref in parts for which in (1, 3)]
+    return dot(jnp.concatenate(high + low + high, axis=1), table_ref[...])
 
 
 def x_first_kernel(count, *refs):
@@ -162,16 +152,16 @@
 def x_first(parts, table):
     count = len(parts)
     _, length, width = parts[0].shape
-    columns = table.shape[2]
-    rows = 256
+    columns = table.shape[1]
+    rows = length // 4
     return pl.pallas_call(
         functools.partial(x_first_kernel, count),
         out_shape=jax.ShapeDtypeStruct((length, columns), jnp.float32),
         grid=(length // rows,),
         in_specs=[pl.BlockSpec((4, rows, width), lambda i: (0, i, 0))] * count
-        + [pl.BlockSpec(table.shape, lambda i: (0, 0, 0))],
+        + [pl.BlockSpec(table.shape, lambda i: (0, 0))],
         out_specs=pl.BlockSpec((rows, columns), lambda i: (i, 0)),
-        compiler_params=pltpu.CompilerParams(vmem_limit_bytes=VMEM_BYTES),
+        compiler_params=pltpu.CompilerParams(vmem_limit_bytes=X_BYTES),
         cost_estimate=pl.CostEstimate(
             flops=12 * count * length * width * columns, bytes_accessed=8 * length * columns, transcendentals=0
         ),
@@ -209,8 +199,8 @@
 def x_last(parts, table, sums, row_pair, col_trio):
     count = len(parts)
     _, length, width = parts[0].shape
-    columns = table.shape[2]
-    rows = 256
+    columns = table.shape[1]
+    rows = length // 4
     return pl.pallas_call(
         functools.partial(x_last_kernel, count),
         out_shape=(
@@ -220,7 +210,7 @@
         grid=(length // rows,),
         in_specs=[pl.BlockSpec((4, rows, width), lambda i: (0, i, 0))] * count
         + [
-            pl.BlockSpec(table.shape, lambda i: (0, 0, 0)),
+            pl.BlockSpec(table.shape, lambda i: (0, 0)),
             pl.BlockSpec((rows, columns), lambda i: (i, 0)),
             pl.BlockSpec((2, rows, row_pair.shape[2]), lambda i: (0, i, 0)),
             pl.BlockSpec(col_trio.shape, lambda i: (0, 0)),
@@ -229,7 +219,7 @@
             pl.BlockSpec((2, 1, rows, columns // 2), lambda i: (0, 0, i, 0)),
             pl.BlockSpec((8, row_pair.shape[2]), lambda i: (0, 0)),
         ),
-        compiler_params=pltpu.CompilerParams(vmem_limit_bytes=VMEM_BYTES),
+        compiler_params=pltpu.CompilerParams(vmem_limit_bytes=X_BYTES),
         cost_estimate=pl.CostEstimate(
             flops=12 * count * length * width * columns,
             bytes_accessed=12 * length * columns,
@@ -240,17 +230,18 @@
 
 
 def sum_everywhere(tile):
-    axes = ("gx", "gy")
-    devices = lax.axis_size("gx") * lax.axis_size("gy")
-    copies = jnp.broadcast_to(tile[None], (devices,) + tile.shape)
-    return jnp.sum(lax.all_to_all(copies, axes, split_axis=0, concat_axis=0, tiled=True))
+    devices = lax.axis_size("gx")
+    others = [lax.ppermute(tile, "gx", [(s, s ^ m) for s in range(devices)]) for m in range(1, devices)]
+    tile = functools.reduce(jnp.add, others, tile)
+    copies = jnp.broadcast_to(tile[None], (lax.axis_size("gy"),) + tile.shape)
+    return jnp.sum(lax.all_to_all(copies, "gy", split_axis=0, concat_axis=0, tiled=True))
 
 
 def four_way(field, row_scale, col_scale, row_rate, col_shift, col_mix):
     position = lax.axis_index("gx")
     planes, rows, columns = field.shape
     length, width = planes * rows, columns // 4
-    cuts = lax.optimization_barrier(tuple(field[:, :, c * width : (c + 1) * width] for c in range(4)))
+    field_a, field_b = (field[:, :, : 2 * width], lax.optimization_barrier(field)[:, :, 2 * width :])
     sign = jnp.where(position < 2, 1.0, -1.0)
 
     own_real = jnp.where(position == 1, -1.0, jnp.where(position == 3, 0.0, 1.0))
@@ -263,7 +254,8 @@
     inner = length // RADIX
     index = jnp.arange(inner, dtype=jnp.int32)
     cos, sin = root_table(index, index, inner)
-    y_table = split_table(jnp.concatenate([jnp.concatenate([cos, -sin], 1), jnp.concatenate([sin, cos], 1)], 0))
+    y_table = jnp.concatenate([jnp.concatenate([cos, -sin], 1), jnp.concatenate([sin, cos], 1)], 0)
+    y_table = split_table(y_table, 1, (0, 1, 0))
     cos, sin = root_table(jnp.arange(RADIX, dtype=jnp.int32), index, length)
     twist = jnp.broadcast_to(jnp.stack([cos, sin])[:, :, :, None], (2, RADIX, inner, width))
     cos, sin = x_tables(columns, 4, position)
@@ -271,7 +263,7 @@
 
     def x_table(chunks):
         spans = [slice(c * width, (c + 1) * width) for c in chunks]
-        return split_table(jnp.concatenate([rows[s] for s in spans for rows in (real_rows, imag_rows)], 0))
+        return split_table(jnp.concatenate([rows[s] for s in spans for rows in (real_rows, imag_rows)], 0), 0, (0, 0, 1))
 
     norm = 1.0 / math.sqrt(length * columns * 4)
     row_pair = jnp.broadcast_to(jnp.stack([row_scale * norm, row_rate])[:, :, None], (2, length, 128))
@@ -279,19 +271,30 @@
     fixed = 2.0 * (columns * jnp.sum(jnp.log(row_scale)) + length * jnp.sum(jnp.log(col_scale)))
     fixed = fixed - length * columns * math.log(2.0 * math.pi)
 
-    first_a = [from_partner(cuts[c], "gx", 1) + sign * cuts[c] for c in (0, 1)]
-    first_b = [to_planes(cuts[c])[0] for c in (2, 3)]
-    second_a = [to_planes(value)[0] for value in first_a]
-    second_b = [from_partner(value, "gx", 1) for value in first_b]
-    parts = []
-    for step in range(2):
-        own, other = second_a[step], from_partner(second_a[step], "gx", 0)
-        parts.append(y_dft([own, other], coefs_a, y_table, twist))
-        late, early = second_b[step], first_b[step]
+    tables = (y_table, twist, x_table((0, 2)), x_table((1, 3)), row_pair, col_trio, coefs_a, coefs_b, fixed)
+    received, first_b, tables = lax.optimization_barrier((from_partner(field_a, "gx", 1), to_planes(field_b)[0], tables))
+    y_table, twist, table_one, table_two, row_pair, col_trio, coefs_a, coefs_b, fixed = tables
+    received_too, field_too = lax.optimization_barrier((received, field_a))
+    first_a = [
+        received[:, :, :width] + sign * field_a[:, :, :width],
+        received_too[:, :, width:] + sign * field_too[:, :, width:],
+    ]
+    first_b = [first_b[:, :width], lax.optimization_barrier(first_b)[:, width:]]
+
+    def y_part_a(own):
+        return y_dft([own, from_partner(own, "gx", 0)], coefs_a, y_table, twist)
+
+    def y_part_b(late, early):
         group = [late, from_partner(late, "gx", 0), early, from_partner(early, "gx", 0)]
-        parts.append(y_dft(group, coefs_b, y_table, twist))
-    sums = x_first(parts[:2], x_table((0, 2)))
-    latent, tile = x_last(parts[2:], x_table((1, 3)), sums, row_pair, col_trio)
+        return y_dft(group, coefs_b, y_table, twist)
+
+    second_a, second_b = to_planes(first_a[0])[0], from_partner(first_b[0], "gx", 1)
+    first_a[1], second_b = lax.optimization_barrier((first_a[1], second_b))
+    sums = x_first([y_part_a(second_a), y_part_b(second_b, first_b[0])], table_one)
+    second_a, second_b = to_planes(first_a[1])[0], from_partner(first_b[1], "gx", 1)
+    sums, second_a, second_b = lax.optimization_barrier((sums, second_a, second_b))
+    parts = [y_part_a(second_a), y_part_b(second_b, first_b[1])]
+    latent, tile = x_last(parts, table_two, sums, row_pair, col_trio)
     tile = tile + fixed / tile.size
     modes = length * columns * lax.axis_size("gx") * lax.axis_size("gy")
     return (latent, sum_everywhere(tile) / modes)

time: 220 us -> 178 us (0.81)
  blocking collectives: 46.1 us -> 12.3 us
  waiting for transfers between devices: 74.3 us -> 60.4 us
  local copies, waits for them, and re-layouts: 7.46 us -> 17 us
  Pallas kernels: 46.8 us -> 39.4 us
    all_to_all x2 -> x1, blocking collectives: 46.1 us -> 12.3 us  [sum_everywhere(): lax.all_to_all(copies, 'gy', split_axis=0, concat_axis=0, tiled=True)]
    ppermute x10 -> x9, waiting for transfers between devices: 63.4 us -> 49.3 us  [from_partner(): return lax.ppermute(value, axis, pairs)]
    concatenate x2 -> x4, other arithmetic: 0.54 us -> 5.28 us  [the longest x3 5.06 us: split_table(): return jnp.concatenate([parts[which] for which in order], axis)]
    slice x1 -> x4, local copies, waits for them, and re-layouts: 3.91 us -> 8.59 us  [the longest x2 3.72 us: four_way(): first_b = [first_b[:, :width], lax.optimization_barrier(first_b)[:, width:]]]
    unnamed x18 -> x32, local copies, waits for them, and re-layouts: 2.27 us -> 5.79 us
    pallas_call x4, Pallas kernels: 24.4 us -> 21.5 us  [y_dft(): pl.pallas_call(functools.partial(y_kernel, count), out_shape=jax.ShapeDty...]
    pallas_call x1, Pallas kernels: 13.1 us -> 10.5 us  [x_last(): pl.pallas_call(functools.partial(x_last_kernel, count), out_shape=(jax.Sh...]
    ppermute x10 -> x9, starting transfers between devices: 6.2 us -> 4.86 us  [from_partner(): return lax.ppermute(value, axis, pairs)]
  transfers between devices with their start and end apart: 13 -> 15, of which waited for: 5 -> 6; matrix products, arithmetic and copies ran while one was open for 9% -> 13% of each run, Pallas kernels for 13% -> 13%
where the time goes in v3:
time: 178 us; the launch traced here: 177 us
  waiting for transfers between devices  60.4 us (34%)
  Pallas kernels  39.4 us (22%)
  starting transfers between devices  22.9 us (13%)
  other arithmetic  21.2 us (12%)
  local copies, waits for them, and re-layouts  17 us (10%)
  blocking collectives  12.3 us (7%)
  between operations  4.01 us (2%)
    ppermute x9, waiting for transfers between devices, from_partner(): return lax.ppermute(value, axis, pairs)  49.3 us
    pallas_call x4, Pallas kernels, y_dft(): pl.pallas_call(functools.partial(y_kernel, count), out_shape=jax.ShapeDty...  21.5 us
    all_to_all x3, starting transfers between devices, to_planes(): return lax.all_to_all(values, 'gy', split_axis=0, concat_axis=1, tiled=True)  15.9 us
    all_to_all x1, blocking collectives, sum_everywhere(): lax.all_to_all(copies, 'gy', split_axis=0, concat_axis=0, tiled=True)  12.3 us
    pallas_call x1, Pallas kernels, x_last(): pl.pallas_call(functools.partial(x_last_kernel, count), out_shape=(jax.Sh...  10.5 us
    all_to_all x3, waiting for transfers between devices, to_planes(): return lax.all_to_all(values, 'gy', split_axis=0, concat_axis=1, tiled=True)  9.65 us
    pallas_call x1, Pallas kernels, x_first(): pl.pallas_call(functools.partial(x_first_kernel, count), out_shape=jax.Sh...  7.49 us
    unnamed x32, local copies, waits for them, and re-layouts  5.79 us
  transfers between devices with their start and end apart: 15, of which 6 were waited for; matrix products, arithmetic and copies ran while one was open for 13% of the time, Pallas kernels for 13%

profile of v3, /device:TPU:0, one launch (start us, length us, event | category | flops | bytes accessed | tf_op | source)
XLA Modules:
  0.0 177.3 jit_solution(15691971794040809417)
XLA Ops:
  0.6 3.3 %slice.49 = f32[8,256,256]{2,1,0:T(8,128)} slice(f32[8,256,512]{2,1,0:T(8,128)} %param.6), slice={[0:8], [0:256], [0:256]} | slice | bytes 4194304 | tf_op jit(solution)/shard_map/slice | solution.py:244
  3.9 3.0 %collective-permute-start = (f32[8,256,256]{2,1,0:T(8,128)}, f32[8,256,256]{2,1,0:T(8,128)}, u32[]{:S(2)}, u32[]{:S(2)}) collective-permute-start(f32[8,256,256]{2,1,0:T(8,128)} %slice.49), channel_id=1, source_target_pairs={{0,16},{8,24},{16,0},{24,8},{1,17},{9,25},{17,1},{25,9},{2,18},{10... | collective-permute-start | bytes 6291464 | tf_op jit(solution)/shard_map/ppermute | solution.py:19
  6.9 1.6 slice.65
  8.5 5.9 %all-to-all-start = ((f32[8,256,256]{2,1,0:T(8,128)}), f32[8,256,256]{2,1,0:T(8,128)}, u32[]{:S(2)}, u32[]{:S(2)}) async-start(f32[8,256,256]{2,1,0:T(8,128)} %slice.65), calls=%async_computation | async-start | bytes 4194304 | tf_op jit(solution)/shard_map/all_to_all | solution.py:23
  14.6 0.6 log_reduce_fusion.1
  15.4 1.0 fusion.30
  16.3 1.0 fusion.28
  17.4 1.1 fusion.6
  18.5 0.6 log_reduce_fusion
  19.1 4.1 %fusion.19 = (f32[512,512]{1,0:T(8,128)S(1)}, f32[512,512]{1,0:T(8,128)S(1)}, f32[512,512]{1,0:T(8,128)S(1)}) fusion(s32[512]{0:T(512)S(1)} %multiply_add_fusion.2), kind=kLoop, calls=%fused_computation.53 | loop fusion | flops 3932160 | bytes 3147776 | tf_op jit(solution)/shard_map/sin | solution.py:36
  24.9 0.4 copy-done.13
  25.3 0.3 copy-done.9
  25.8 1.3 pad_maximum_fusion.3.refs_2_.refs_4_
  27.1 0.9 reduce-precision_convert_fusion
  28.1 0.3 fusion.1
  28.4 1.9 %pad_maximum_fusion.1.refs_2_ = bf16[1536,1024]{1,0:T(8,128)(2,1)} fusion(bf16[512,1024]{1,0:T(8,128)(2,1)S(1)} %fusion.1, bf16[512,1024]{1,0:T(8,128)(2,1)S(1)} %get-tuple-element.42), kind=kLoop, calls=%fused_computation.11 | loop fusion | flops 9437184 | bytes 5242880 | tf_op jit(solution)/shard_map/concatenate | solution.py:49
  30.3 1.8 %pad_maximum_fusion.refs_2_ = bf16[1536,1024]{1,0:T(8,128)(2,1)} fusion(bf16[512,1024]{1,0:T(8,128)(2,1)S(1)} %get-tuple-element.66, bf16[512,1024]{1,0:T(8,128)(2,1)S(1)} %get-tuple-element.67), kind=kLoop, calls=%fused_computation.10 | loop fusion | flops 9437184 | bytes 5242880 | tf_op jit(solution)/shard_map/concatenate | solution.py:49
  32.1 20.7 %collective-permute-done = f32[8,256,256]{2,1,0:T(8,128)} collective-permute-done((f32[8,256,256]{2,1,0:T(8,128)}, f32[8,256,256]{2,1,0:T(8,128)}, u32[]{:S(2)}, u32[]{:S(2)}) %collective-permute-start) | collective-permute-done | bytes 2097184 | tf_op jit(solution)/shard_map/ppermute | solution.py:19
  52.8 9.6 %all-to-all-done = f32[8,256,256]{2,1,0:T(8,128)} async-done(((f32[8,256,256]{2,1,0:T(8,128)}), f32[8,256,256]{2,1,0:T(8,128)}, u32[]{:S(2)}, u32[]{:S(2)}) %all-to-all-start) | async-done | bytes 2097184 | tf_op jit(solution)/shard_map/all_to_all | solution.py:23
  62.5 0.6 broadcast_in_dim.6.refs_3_.refs_5_
  63.1 2.0 %broadcast_in_dim.7.refs_4_ = f32[2,2048,128]{2,1,0:T(8,128)} broadcast(f32[2,2048]{1,0:T(2,128)S(1)} %pad_maximum_fusion.5), dimensions={0,1} | broadcast | bytes 2113536 | tf_op jit(solution)/shard_map/broadcast_in_dim | solution.py:269
  65.0 2.7 %multiply_add_fusion.1 = f32[8,256,128]{2,1,0:T(8,128)} fusion(f32[8,256,512]{2,1,0:T(8,128)} %param.6, f32[8,256,256]{2,1,0:T(8,128)} %collective-permute-done, f32[]{:T(128)S(6)} %select_n.66), kind=kLoop, calls=%fused_computation.43 | loop fusion | flops 524288 | bytes 3145732 | tf_op jit(solution)/shard_map/add | solution.py:279
  67.7 4.2 %all-to-all-start.1 = ((f32[8,256,128]{2,1,0:T(8,128)}), f32[8,256,128]{2,1,0:T(8,128)}, u32[]{:S(2)}, u32[]{:S(2)}) async-start(f32[8,256,128]{2,1,0:T(8,128)} %multiply_add_fusion.1), calls=%async_computation.1 | async-start | bytes 2097152 | tf_op jit(solution)/shard_map/all_to_all | solution.py:23
  71.9 2.3 %slice.63.refs_2_ = f32[2048,128]{1,0:T(8,128)} slice(f32[2048,256]{1,0:T(8,128)} %bitcast), slice={[0:2048], [0:128]} | slice | bytes 2097152 | tf_op jit(solution)/shard_map/slice | solution.py:282
  74.2 0.5 collective-permute-start.2
  74.7 2.6 %multiply_add_fusion = f32[8,256,128]{2,1,0:T(8,128)} fusion(f32[8,256,256]{2,1,0:T(8,128)} %slice.49, f32[8,256,256]{2,1,0:T(8,128)} %collective-permute-done, f32[]{:T(128)S(6)} %select_n.66), kind=kLoop, calls=%fused_computation.42 | loop fusion | flops 524288 | bytes 3145732 | tf_op jit(solution)/shard_map/add | solution.py:280
  77.4 21.4 %collective-permute-done.2.refs_0_ = f32[2048,128]{1,0:T(8,128)} collective-permute-done((f32[2048,128]{1,0:T(8,128)}, f32[2048,128]{1,0:T(8,128)}, u32[]{:S(2)}, u32[]{:S(2)}) %collective-permute-start.2) | collective-permute-done | bytes 1048608 | tf_op jit(solution)/shard_map/ppermute | solution.py:19
  98.7 5.7 %all-to-all-start.2 = ((f32[8,256,128]{2,1,0:T(8,128)}), f32[8,256,128]{2,1,0:T(8,128)}, u32[]{:S(2)}, u32[]{:S(2)}) async-start(f32[8,256,128]{2,1,0:T(8,128)} %multiply_add_fusion), calls=%async_computation.2 | async-start | bytes 2097152 | tf_op jit(solution)/shard_map/all_to_all | solution.py:23
  104.5 0.3 collective-permute-start.1
  104.8 1.4 slice.78.refs_2_
  106.2 0.6 collective-permute-start.5
  106.8 6.0 %y_dft.5.refs_1_ = bf16[4,2048,128]{2,1,0:T(8,128)(2,1)S(1)} custom-call(f32[2,4]{1,0:T(2,128)S(1)} %pad_maximum_fusion.7.coef_ref, f32[2048,128]{1,0:T(8,128)} %collective-permute-done.2.refs_0_, f32[2048,128]{1,0:T(8,128)} %collective-permute-done.3.refs_1_, f32[2048,128]{1,0:T(8,128)} %slice.63.refs_2_, f32[2048,128]{1,0:T(8,128)} %collective-permute-done.4.refs_3_, ...), custom_call_target="tpu_custom_call" | custom-call | flops 1610612736 | bytes 7340032 | tf_op jit(solution)/shard_map/y_dft/pallas_call | solution.py:124
  112.8 4.7 %y_dft.4.refs_0_ = bf16[4,2048,128]{2,1,0:T(8,128)(2,1)S(1)} custom-call(f32[2,2]{1,0:T(2,128)S(1)} %reshape.95.coef_ref, f32[2048,128]{1,0:T(8,128)} %bitcast.10.refs_0_, f32[2048,128]{1,0:T(8,128)S(1)} %collective-permute-done.1.refs_1_, bf16[512,1536]{1,0:T(8,128)(2,1)S(1)} %copy-done, f32[2,8,256,128]{3,2,1,0:T(8,128)S(1)} %broadcast_in_dim.6.refs_3_.refs_5_), custom_call_target="tpu_custom_call" | custom-call | flops 1610612736 | bytes 5242880 | tf_op jit(solution)/shard_map/y_dft/pallas_call | solution.py:124
  117.5 7.5 %x_first.1.refs_3_ = f32[2048,1024]{1,0:T(8,128)S(1)} custom-call(bf16[4,2048,128]{2,1,0:T(8,128)(2,1)S(1)} %y_dft.4.refs_0_, bf16[4,2048,128]{2,1,0:T(8,128)(2,1)S(1)} %y_dft.5.refs_1_, bf16[1536,1024]{1,0:T(8,128)(2,1)S(1)} %copy-done.4), custom_call_target="tpu_custom_call" | custom-call | flops 6442450944 | bytes 16777216 | tf_op jit(solution)/shard_map/x_first/pallas_call | solution.py:157
  125.0 3.4 %copy-done.6 = f32[2048,1024]{1,0:T(8,128)} copy-done((f32[2048,1024]{1,0:T(8,128)}, f32[2048,1024]{1,0:T(8,128)S(1)}, u32[]{:S(2)}) %copy-start.6) | copy-done | bytes 8388632
  128.4 3.3 %collective-permute-done.5.refs_0_ = f32[2048,128]{1,0:T(8,128)} collective-permute-done((f32[2048,128]{1,0:T(8,128)S(1)}, f32[2048,128]{1,0:T(8,128)}, u32[]{:S(2)}, u32[]{:S(2)}) %collective-permute-start.5) | collective-permute-done | bytes 1048608 | tf_op jit(solution)/shard_map/ppermute | solution.py:19
  131.7 0.5 collective-permute-start.8
  132.2 3.9 %collective-permute-done.6.refs_1_ = f32[2048,128]{1,0:T(8,128)} collective-permute-done((f32[2048,128]{1,0:T(8,128)}, f32[2048,128]{1,0:T(8,128)}, u32[]{:S(2)}, u32[]{:S(2)}) %collective-permute-start.6) | collective-permute-done | bytes 1048608 | tf_op jit(solution)/shard_map/ppermute | solution.py:19
  136.2 1.4 copy-done.1
  137.6 5.0 %y_dft.6.refs_0_ = bf16[4,2048,128]{2,1,0:T(8,128)(2,1)S(1)} custom-call(f32[2,2]{1,0:T(2,128)S(1)} %reshape.95.coef_ref, f32[2048,128]{1,0:T(8,128)} %bitcast.11.refs_0_, f32[2048,128]{1,0:T(8,128)} %collective-permute-done.6.refs_1_, bf16[512,1536]{1,0:T(8,128)(2,1)S(1)} %copy-done.1, f32[2,8,256,128]{3,2,1,0:T(8,128)S(1)} %broadcast_in_dim.6.refs_3_.refs_5_), custom_call_target="tpu_custom_call" | custom-call | flops 1610612736 | bytes 5242880 | tf_op jit(solution)/shard_map/y_dft/pallas_call | solution.py:124
  142.6 5.8 %y_dft.7.refs_1_ = bf16[4,2048,128]{2,1,0:T(8,128)(2,1)S(1)} custom-call(f32[2,4]{1,0:T(2,128)S(1)} %pad_maximum_fusion.7.coef_ref, f32[2048,128]{1,0:T(8,128)} %collective-permute-done.5.refs_0_, f32[2048,128]{1,0:T(8,128)} %collective-permute-done.7.refs_1_, f32[2048,128]{1,0:T(8,128)S(1)} %slice.78.refs_2_, f32[2048,128]{1,0:T(8,128)} %collective-permute-done.8.refs_3_, ...), custom_call_target="tpu_custom_call" | custom-call | flops 1610612736 | bytes 7340032 | tf_op jit(solution)/shard_map/y_dft/pallas_call | solution.py:124
  148.5 10.5 %x_last.1 = (f32[2,1,2048,512]{3,2,1,0:T(8,128)}, f32[8,128]{1,0:T(8,128)S(1)}) custom-call(bf16[4,2048,128]{2,1,0:T(8,128)(2,1)S(1)} %y_dft.6.refs_0_, bf16[4,2048,128]{2,1,0:T(8,128)(2,1)S(1)} %y_dft.7.refs_1_, bf16[1536,1024]{1,0:T(8,128)(2,1)S(1)} %copy-done.3, f32[2048,1024]{1,0:T(8,128)S(1)} %copy-done.7, f32[2,2048,128]{2,1,0:T(8,128)S(1)} %copy-done.5, ...), custom_call_target="tpu_custom_call" | custom-call | flops 6442450944 | bytes 25165824 | tf_op jit(solution)/shard_map/x_last/pallas_call | solution.py:204
  158.9 0.5 collective-permute-start.10
  159.4 1.0 collective-permute-start.11
  160.4 0.7 collective-permute-start.9
  161.1 1.5 collective-permute-done.10
  162.6 12.3 %all_to_all.32 = f32[8,8,128]{2,1,0:T(8,128)S(1)} all-to-all(f32[8,8,128]{2,1,0:T(8,128)S(1)} %broadcast_in_dim.8), channel_id=1, replica_groups=mesh['gx'=4,'gy'=8] {'gy'}, dimensions={0} | all-to-all | bytes 65536 | tf_op jit(solution)/shard_map/all_to_all | solution.py:237
  174.9 0.6 reduce_sum.29
  (54 shorter events, 0.8 us)
Async XLA Ops:
  0.6 6.3 %copy-start.8 = (f32[8,256,512]{2,1,0:T(8,128)S(1)}, f32[8,256,512]{2,1,0:T(8,128)}, u32[]{:S(2)}) copy-start(f32[8,256,512]{2,1,0:T(8,128)} %param.6) | copy-start | bytes 12582916
  3.9 48.9 %collective-permute-start = (f32[8,256,256]{2,1,0:T(8,128)}, f32[8,256,256]{2,1,0:T(8,128)}, u32[]{:S(2)}, u32[]{:S(2)}) collective-permute-start(f32[8,256,256]{2,1,0:T(8,128)} %slice.49), channel_id=1, source_target_pairs={{0,16},{8,24},{16,0},{24,8},{1,17},{9,25},{17,1},{25,9},{2,18},{10... | collective-permute-start | bytes 6291464 | tf_op jit(solution)/shard_map/ppermute | solution.py:19
  8.5 6.1 %copy-start.11 = (f32[512]{0:T(512)S(1)}, f32[512]{0:T(512)}, u32[]{:S(2)}) copy-start(f32[512]{0:T(512)} %param.8) | copy-start | bytes 6148
  8.5 6.8 %copy-start.14 = (f32[512]{0:T(512)S(1)}, f32[512]{0:T(512)}, u32[]{:S(2)}) copy-start(f32[512]{0:T(512)} %param.11) | copy-start | bytes 6148
  8.5 6.8 %copy-start.15 = (f32[512]{0:T(512)S(1)}, f32[512]{0:T(512)}, u32[]{:S(2)}) copy-start(f32[512]{0:T(512)} %param.10) | copy-start | bytes 6148
  8.5 54.0 %all-to-all-start = ((f32[8,256,256]{2,1,0:T(8,128)}), f32[8,256,256]{2,1,0:T(8,128)}, u32[]{:S(2)}, u32[]{:S(2)}) async-start(f32[8,256,256]{2,1,0:T(8,128)} %slice.65), calls=%async_computation | async-start | bytes 4194304 | tf_op jit(solution)/shard_map/all_to_all | solution.py:23
  14.4 4.1 %copy-start.12 = (f32[2048]{0:T(1024)S(1)}, f32[2048]{0:T(1024)}, u32[]{:S(2)}) copy-start(f32[2048]{0:T(1024)} %param.7) | copy-start | bytes 24580
  24.6 0.7 copy-start.13
  24.6 1.0 copy-start.9
  24.6 1.2 copy-start.10
  67.7 31.0 %all-to-all-start.1 = ((f32[8,256,128]{2,1,0:T(8,128)}), f32[8,256,128]{2,1,0:T(8,128)}, u32[]{:S(2)}, u32[]{:S(2)}) async-start(f32[8,256,128]{2,1,0:T(8,128)} %multiply_add_fusion.1), calls=%async_computation.1 | async-start | bytes 2097152 | tf_op jit(solution)/shard_map/all_to_all | solution.py:23
  74.2 24.5 %collective-permute-start.2 = (f32[2048,128]{1,0:T(8,128)}, f32[2048,128]{1,0:T(8,128)}, u32[]{:S(2)}, u32[]{:S(2)}) collective-permute-start(f32[2048,128]{1,0:T(8,128)} %slice.63.refs_2_), channel_id=1, source_target_pairs={{0,16},{8,24},{16,0},{24,8},{1,17},{9,25},{17,1},{25,9},{2,18},{10... | collective-permute-start | bytes 3145736 | tf_op jit(solution)/shard_map/ppermute | solution.py:19
  74.7 32.0 %collective-permute-start.4 = (f32[2048,128]{1,0:T(8,128)}, f32[2048,128]{1,0:T(8,128)}, u32[]{:S(2)}, u32[]{:S(2)}) collective-permute-start(f32[2048,128]{1,0:T(8,128)} %slice.63.refs_2_), channel_id=1, source_target_pairs={{0,8},{8,0},{16,24},{24,16},{1,9},{9,1},{17,25},{25,17},{2,10},{10... | collective-permute-start | bytes 3145736 | tf_op jit(solution)/shard_map/ppermute | solution.py:19
  98.7 8.0 %collective-permute-start.3 = (f32[2048,128]{1,0:T(8,128)}, f32[2048,128]{1,0:T(8,128)}, u32[]{:S(2)}, u32[]{:S(2)}) collective-permute-start(f32[2048,128]{1,0:T(8,128)} %collective-permute-done.2.refs_0_), channel_id=1, source_target_pairs={{0,8},{8,0},{16,24},{24,16},{1,9},{9,1},{17,25},{25,17},{2,10},{10... | collective-permute-start | bytes 3145736 | tf_op jit(solution)/shard_map/ppermute | solution.py:19
  98.7 33.0 %all-to-all-start.2 = ((f32[8,256,128]{2,1,0:T(8,128)}), f32[8,256,128]{2,1,0:T(8,128)}, u32[]{:S(2)}, u32[]{:S(2)}) async-start(f32[8,256,128]{2,1,0:T(8,128)} %multiply_add_fusion), calls=%async_computation.2 | async-start | bytes 2097152 | tf_op jit(solution)/shard_map/all_to_all | solution.py:23
  104.5 2.3 %copy-start = (bf16[512,1536]{1,0:T(8,128)(2,1)S(1)}, bf16[512,1536]{1,0:T(8,128)(2,1)}, u32[]{:S(2)}) copy-start(bf16[512,1536]{1,0:T(8,128)(2,1)} %pad_maximum_fusion.3.refs_2_.refs_4_) | copy-start | bytes 4718596
  104.5 8.3 %collective-permute-start.1 = (f32[2048,128]{1,0:T(8,128)}, f32[2048,128]{1,0:T(8,128)S(1)}, u32[]{:S(2)}, u32[]{:S(2)}) collective-permute-start(f32[2048,128]{1,0:T(8,128)} %bitcast.10.refs_0_), channel_id=1, source_target_pairs={{0,8},{8,0},{16,24},{24,16},{1,9},{9,1},{17,25},{25,17},{2,10},{10... | collective-permute-start | bytes 3145736 | tf_op jit(solution)/shard_map/ppermute | solution.py:19
  106.2 25.5 %collective-permute-start.5 = (f32[2048,128]{1,0:T(8,128)S(1)}, f32[2048,128]{1,0:T(8,128)}, u32[]{:S(2)}, u32[]{:S(2)}) collective-permute-start(f32[2048,128]{1,0:T(8,128)S(1)} %slice.78.refs_2_), channel_id=1, source_target_pairs={{0,16},{8,24},{16,0},{24,8},{1,17},{9,25},{17,1},{25,9},{2,18},{10... | collective-permute-start | bytes 3145736 | tf_op jit(solution)/shard_map/ppermute | solution.py:19
  112.8 4.7 %copy-start.4 = (bf16[1536,1024]{1,0:T(8,128)(2,1)S(1)}, bf16[1536,1024]{1,0:T(8,128)(2,1)}, u32[]{:S(2)}) copy-start(bf16[1536,1024]{1,0:T(8,128)(2,1)} %pad_maximum_fusion.refs_2_) | copy-start | bytes 9437188
  125.0 3.4 %copy-start.6 = (f32[2048,1024]{1,0:T(8,128)}, f32[2048,1024]{1,0:T(8,128)S(1)}, u32[]{:S(2)}) copy-start(f32[2048,1024]{1,0:T(8,128)S(1)} %x_first.1.refs_3_) | copy-start | bytes 25165828
  131.7 4.5 %collective-permute-start.6 = (f32[2048,128]{1,0:T(8,128)}, f32[2048,128]{1,0:T(8,128)}, u32[]{:S(2)}, u32[]{:S(2)}) collective-permute-start(f32[2048,128]{1,0:T(8,128)} %bitcast.11.refs_0_), channel_id=1, source_target_pairs={{0,8},{8,0},{16,24},{24,16},{1,9},{9,1},{17,25},{25,17},{2,10},{10... | collective-permute-start | bytes 3145736 | tf_op jit(solution)/shard_map/ppermute | solution.py:19
  131.7 10.9 %collective-permute-start.8 = (f32[2048,128]{1,0:T(8,128)S(1)}, f32[2048,128]{1,0:T(8,128)}, u32[]{:S(2)}, u32[]{:S(2)}) collective-permute-start(f32[2048,128]{1,0:T(8,128)S(1)} %slice.78.refs_2_), channel_id=1, source_target_pairs={{0,8},{8,0},{16,24},{24,16},{1,9},{9,1},{17,25},{25,17},{2,10},{10... | collective-permute-start | bytes 3145736 | tf_op jit(solution)/shard_map/ppermute | solution.py:19
  132.2 10.4 %collective-permute-start.7 = (f32[2048,128]{1,0:T(8,128)}, f32[2048,128]{1,0:T(8,128)}, u32[]{:S(2)}, u32[]{:S(2)}) collective-permute-start(f32[2048,128]{1,0:T(8,128)} %collective-permute-done.5.refs_0_), channel_id=1, source_target_pairs={{0,8},{8,0},{16,24},{24,16},{1,9},{9,1},{17,25},{25,17},{2,10},{10... | collective-permute-start | bytes 3145736 | tf_op jit(solution)/shard_map/ppermute | solution.py:19
  136.2 1.4 copy-start.1
  137.6 5.0 %copy-start.2 = (bf16[512,1536]{1,0:T(8,128)(2,1)S(1)}, bf16[512,1536]{1,0:T(8,128)(2,1)}, u32[]{:S(2)}) copy-start(bf16[512,1536]{1,0:T(8,128)(2,1)} %pad_maximum_fusion.3.refs_2_.refs_4_) | copy-start | bytes 4718596
  137.6 10.9 %copy-start.7 = (f32[2048,1024]{1,0:T(8,128)S(1)}, f32[2048,1024]{1,0:T(8,128)}, u32[]{:S(2)}) copy-start(f32[2048,1024]{1,0:T(8,128)} %copy-done.6) | copy-start | bytes 25165828
  142.6 5.9 %copy-start.3 = (bf16[1536,1024]{1,0:T(8,128)(2,1)S(1)}, bf16[1536,1024]{1,0:T(8,128)(2,1)}, u32[]{:S(2)}) copy-start(bf16[1536,1024]{1,0:T(8,128)(2,1)} %pad_maximum_fusion.1.refs_2_) | copy-start | bytes 9437188
  142.6 5.9 %copy-start.5 = (f32[2,2048,128]{2,1,0:T(8,128)S(1)}, f32[2,2048,128]{2,1,0:T(8,128)}, u32[]{:S(2)}) copy-start(f32[2,2048,128]{2,1,0:T(8,128)} %broadcast_in_dim.7.refs_4_) | copy-start | bytes 6291460
  158.9 3.6 %collective-permute-start.10 = (f32[8,128]{1,0:T(8,128)S(1)}, f32[8,128]{1,0:T(8,128)S(1)}, u32[]{:S(2)}, u32[]{:S(2)}) collective-permute-start(f32[8,128]{1,0:T(8,128)S(1)} %broadcast_add_fusion), channel_id=1, source_target_pairs={{0,16},{8,24},{16,0},{24,8},{1,17},{9,25},{17,1},{25,9},{2,18},{10... | collective-permute-start | bytes 12296 | tf_op jit(solution)/shard_map/ppermute | solution.py:234
  159.4 3.1 %collective-permute-start.11 = (f32[8,128]{1,0:T(8,128)S(1)}, f32[8,128]{1,0:T(8,128)S(1)}, u32[]{:S(2)}, u32[]{:S(2)}) collective-permute-start(f32[8,128]{1,0:T(8,128)S(1)} %broadcast_add_fusion), channel_id=1, source_target_pairs={{0,24},{8,16},{16,8},{24,0},{1,25},{9,17},{17,9},{25,1},{2,26},{10... | collective-permute-start | bytes 12296 | tf_op jit(solution)/shard_map/ppermute | solution.py:234
  160.4 2.1 %collective-permute-start.9 = (f32[8,128]{1,0:T(8,128)S(1)}, f32[8,128]{1,0:T(8,128)S(1)}, u32[]{:S(2)}, u32[]{:S(2)}) collective-permute-start(f32[8,128]{1,0:T(8,128)S(1)} %broadcast_add_fusion), channel_id=1, source_target_pairs={{0,8},{8,0},{16,24},{24,16},{1,9},{9,1},{17,25},{25,17},{2,10},{10... | collective-permute-start | bytes 12296 | tf_op jit(solution)/shard_map/ppermute | solution.py:234

commit v4 on v3

--- a/solution.py
+++ b/solution.py
@@ -10,7 +10,8 @@
 
 precision_top = lax.Precision.HIGHEST
 RADIX = 8
-Y_BYTES, X_BYTES = 20 * 1024 * 1024, 30 * 1024 * 1024
+LANES = 128
+Y_BYTES, X_BYTES = 28 * 1024 * 1024, 30 * 1024 * 1024
 
 
 def from_partner(value, axis, stride):
@@ -80,28 +81,28 @@
 
 
 def y_kernel(count, coef_ref, *refs):
-    inputs, (table_ref, twist_ref, out_ref, split_ref, step_ref) = refs[:count], refs[count:]
+    inputs, (table_ref, twist_ref, out_ref, mix_ref, split_ref, step_ref) = refs[:count], refs[count:]
     length, width = inputs[0].shape
     inner = length // RADIX
-    for s in range(RADIX):
-        parts = [ref[pl.ds(s, inner, stride=RADIX), :] for ref in inputs]
+    for lane in range(0, width, LANES):
+        parts = [ref[:, pl.ds(lane, LANES)] for ref in inputs]
         for which in range(2):
             mixed = parts[0] * coef_ref[which, 0]
             for place in range(1, count):
                 mixed = mixed + parts[place] * coef_ref[which, place]
-            high, low = split_value(mixed)
-            cols = pl.ds(s * width, width)
-            for place, value in enumerate((high, high, low)):
-                split_ref[pl.ds((2 * place + which) * inner, inner), cols] = value
+            mix_ref[...] = mixed
+            for s in range(RADIX):
+                high, low = split_value(mix_ref[pl.ds(s, inner, stride=RADIX), :])
+                cols = pl.ds(s * width + lane, LANES)
+                for place, value in enumerate((high, high, low)):
+                    split_ref[pl.ds((2 * place + which) * inner, inner), cols] = value
     step_ref[...] = dot(table_ref[...], split_ref[...])
     rows_each = 16
 
-    @pl.loop(0, inner // rows_each)
-    def _(block):
-        start = pl.multiple_of(block * rows_each, rows_each)
+    def finish(start, lane):
         values = []
         for s in range(RADIX):
-            cols = pl.ds(s * width, width)
+            cols = pl.ds(s * width + lane, LANES)
             re = step_ref[pl.ds(start, rows_each), cols]
             im = step_ref[pl.ds(pl.multiple_of(start + inner, rows_each), rows_each), cols]
             if s:
@@ -112,8 +113,14 @@
             rows = pl.ds(pl.multiple_of(kb * inner + start, rows_each), rows_each)
             for which in range(2):
                 high, low = split_value(pair[which])
-                out_ref[2 * which, rows, :] = high
-                out_ref[2 * which + 1, rows, :] = low
+                out_ref[2 * which, rows, pl.ds(lane, LANES)] = high
+                out_ref[2 * which + 1, rows, pl.ds(lane, LANES)] = low
+
+    @pl.loop(0, inner // rows_each)
+    def _(block):
+        start = pl.multiple_of(block * rows_each, rows_each)
+        for lane in range(0, width, LANES):
+            finish(start, lane)
 
 
 def y_dft(inputs, coefs, table, twist):
@@ -127,6 +134,7 @@
         in_specs=[pl.BlockSpec(memory_space=pltpu.SMEM)] + [whole] * (count + 2),
         out_specs=whole,
         scratch_shapes=[
+            pltpu.VMEM((length, LANES), jnp.float32),
             pltpu.VMEM((6 * inner, RADIX * width), jnp.bfloat16),
             pltpu.VMEM((2 * inner, RADIX * width), jnp.float32),
         ],
@@ -150,20 +158,19 @@
 
 
 def x_first(parts, table):
-    count = len(parts)
-    _, length, width = parts[0].shape
+    count, length = len(parts), parts[0].shape[1]
     columns = table.shape[1]
     rows = length // 4
     return pl.pallas_call(
         functools.partial(x_first_kernel, count),
         out_shape=jax.ShapeDtypeStruct((length, columns), jnp.float32),
         grid=(length // rows,),
-        in_specs=[pl.BlockSpec((4, rows, width), lambda i: (0, i, 0))] * count
+        in_specs=[pl.BlockSpec((4, rows, part.shape[2]), lambda i: (0, i, 0)) for part in parts]
         + [pl.BlockSpec(table.shape, lambda i: (0, 0))],
         out_specs=pl.BlockSpec((rows, columns), lambda i: (i, 0)),
         compiler_params=pltpu.CompilerParams(vmem_limit_bytes=X_BYTES),
         cost_estimate=pl.CostEstimate(
-            flops=12 * count * length * width * columns, bytes_accessed=8 * length * columns, transcendentals=0
+            flops=2 * length * table.size, bytes_accessed=8 * length * columns, transcendentals=0
         ),
         name="x_first",
     )(*parts, table)
@@ -173,15 +180,21 @@
     parts, (table_ref, sum_ref, row_ref, col_ref, out_ref, total_ref) = refs[:count], refs[count:]
     spec = sum_ref[...] + x_product(parts, table_ref)
     columns = spec.shape[1] // 2
-    lanes = row_ref.shape[2]
+    lanes = LANES
+    row_scale, row_rate = [
+        jnp.concatenate(
+            [jnp.broadcast_to(row_ref[which, 0, c : c + 1, :], (lanes, lanes)).T for c in range(row_ref.shape[2])], 0
+        )
+        for which in range(2)
+    ]
     total = None
     for tile in range(columns // lanes):
         cols = pl.ds(tile * lanes, lanes)
         col_scale, col_shift, col_mix = col_ref[0:1, cols], col_ref[1:2, cols], col_ref[2:3, cols]
-        scale = row_ref[0] * col_scale
+        scale = row_scale * col_scale
         latent_u = spec[:, tile * lanes : (tile + 1) * lanes] * scale
         latent_v = spec[:, columns + tile * lanes : columns + (tile + 1) * lanes] * scale
-        log_scale = row_ref[1] * jnp.tanh(latent_u + col_shift)
+        log_scale = row_rate * jnp.tanh(latent_u + col_shift)
         latent_w = latent_v * jnp.exp(log_scale) + col_mix * latent_u
         out_ref[0, 0, :, cols] = latent_u
         out_ref[1, 0, :, cols] = latent_w
@@ -197,31 +210,30 @@
 
 
 def x_last(parts, table, sums, row_pair, col_trio):
-    count = len(parts)
-    _, length, width = parts[0].shape
+    count, length = len(parts), parts[0].shape[1]
     columns = table.shape[1]
     rows = length // 4
     return pl.pallas_call(
         functools.partial(x_last_kernel, count),
         out_shape=(
             jax.ShapeDtypeStruct((2, 1, length, columns // 2), jnp.float32),
-            jax.ShapeDtypeStruct((8, row_pair.shape[2]), jnp.float32),
+            jax.ShapeDtypeStruct((8, LANES), jnp.float32),
         ),
         grid=(length // rows,),
-        in_specs=[pl.BlockSpec((4, rows, width), lambda i: (0, i, 0))] * count
+        in_specs=[pl.BlockSpec((4, rows, part.shape[2]), lambda i: (0, i, 0)) for part in parts]
         + [
             pl.BlockSpec(table.shape, lambda i: (0, 0)),
             pl.BlockSpec((rows, columns), lambda i: (i, 0)),
-            pl.BlockSpec((2, rows, row_pair.shape[2]), lambda i: (0, i, 0)),
+            pl.BlockSpec((2, 1, rows // LANES, LANES), lambda i: (0, i, 0, 0)),
             pl.BlockSpec(col_trio.shape, lambda i: (0, 0)),
         ],
         out_specs=(
             pl.BlockSpec((2, 1, rows, columns // 2), lambda i: (0, 0, i, 0)),
-            pl.BlockSpec((8, row_pair.shape[2]), lambda i: (0, 0)),
+            pl.BlockSpec((8, LANES), lambda i: (0, 0)),
         ),
         compiler_params=pltpu.CompilerParams(vmem_limit_bytes=X_BYTES),
         cost_estimate=pl.CostEstimate(
-            flops=12 * count * length * width * columns,
+            flops=2 * length * table.size,
             bytes_accessed=12 * length * columns,
             transcendentals=length * columns,
         ),
@@ -230,18 +242,19 @@
 
 
 def sum_everywhere(tile):
-    devices = lax.axis_size("gx")
-    others = [lax.ppermute(tile, "gx", [(s, s ^ m) for s in range(devices)]) for m in range(1, devices)]
-    tile = functools.reduce(jnp.add, others, tile)
-    copies = jnp.broadcast_to(tile[None], (lax.axis_size("gy"),) + tile.shape)
-    return jnp.sum(lax.all_to_all(copies, "gy", split_axis=0, concat_axis=0, tiled=True))
+    axes = ("gx", "gy")
+    devices = lax.axis_size("gx") * lax.axis_size("gy")
+    copies = jnp.broadcast_to(tile[None], (devices,) + tile.shape)
+    return jnp.sum(lax.all_to_all(copies, axes, split_axis=0, concat_axis=0, tiled=True))
 
 
 def four_way(field, row_scale, col_scale, row_rate, col_shift, col_mix):
     position = lax.axis_index("gx")
     planes, rows, columns = field.shape
     length, width = planes * rows, columns // 4
-    field_a, field_b = (field[:, :, : 2 * width], lax.optimization_barrier(field)[:, :, 2 * width :])
+    quarters = [slice(0, width), slice(width, 2 * width)]
+    field_b, field_rest = lax.optimization_barrier((field[:, :, 2 * width :], field))
+    field_a = field_rest[:, :, : 2 * width]
     sign = jnp.where(position < 2, 1.0, -1.0)
 
     own_real = jnp.where(position == 1, -1.0, jnp.where(position == 3, 0.0, 1.0))
@@ -256,45 +269,39 @@
     cos, sin = root_table(index, index, inner)
     y_table = jnp.concatenate([jnp.concatenate([cos, -sin], 1), jnp.concatenate([sin, cos], 1)], 0)
     y_table = split_table(y_table, 1, (0, 1, 0))
-    cos, sin = root_table(jnp.arange(RADIX, dtype=jnp.int32), index, length)
-    twist = jnp.broadcast_to(jnp.stack([cos, sin])[:, :, :, None], (2, RADIX, inner, width))
+    grid = [lax.broadcasted_iota(jnp.int32, (RADIX, inner, LANES), axis) for axis in range(2)]
+    angle = (grid[0] * grid[1]).astype(jnp.float32) * (-2.0 * math.pi / length)
+    twist = jnp.stack([jnp.cos(angle), jnp.sin(angle)])
     cos, sin = x_tables(columns, 4, position)
     real_rows, imag_rows = jnp.concatenate([cos, sin], 1), jnp.concatenate([-sin, cos], 1)
 
-    def x_table(chunks):
-        spans = [slice(c * width, (c + 1) * width) for c in chunks]
+    def x_table(*spans):
         return split_table(jnp.concatenate([rows[s] for s in spans for rows in (real_rows, imag_rows)], 0), 0, (0, 0, 1))
 
     norm = 1.0 / math.sqrt(length * columns * 4)
-    row_pair = jnp.broadcast_to(jnp.stack([row_scale * norm, row_rate])[:, :, None], (2, length, 128))
+    row_pair = jnp.stack([row_scale * norm, row_rate]).reshape(2, 4, length // 4 // LANES, LANES)
     col_trio = jnp.stack([col_scale, col_shift, col_mix])
     fixed = 2.0 * (columns * jnp.sum(jnp.log(row_scale)) + length * jnp.sum(jnp.log(col_scale)))
     fixed = fixed - length * columns * math.log(2.0 * math.pi)
 
-    tables = (y_table, twist, x_table((0, 2)), x_table((1, 3)), row_pair, col_trio, coefs_a, coefs_b, fixed)
-    received, first_b, tables = lax.optimization_barrier((from_partner(field_a, "gx", 1), to_planes(field_b)[0], tables))
-    y_table, twist, table_one, table_two, row_pair, col_trio, coefs_a, coefs_b, fixed = tables
-    received_too, field_too = lax.optimization_barrier((received, field_a))
-    first_a = [
-        received[:, :, :width] + sign * field_a[:, :, :width],
-        received_too[:, :, width:] + sign * field_too[:, :, width:],
-    ]
-    first_b = [first_b[:, :width], lax.optimization_barrier(first_b)[:, width:]]
+    received = from_partner(field_a, "gx", 1)
+    first_a = [received[:, :, span] + sign * field_a[:, :, span] for span in quarters]
+    tables = (y_table, twist, x_table(quarters[0]), x_table(slice(2 * width, None), quarters[1]), row_pair, col_trio)
+    state = lax.optimization_barrier((first_a, to_planes(field_b)[0], tables, coefs_a, coefs_b, fixed))
+    first_a, first_b, (y_table, twist, table_one, table_two, row_pair, col_trio), coefs_a, coefs_b, fixed = state
 
     def y_part_a(own):
         return y_dft([own, from_partner(own, "gx", 0)], coefs_a, y_table, twist)
 
-    def y_part_b(late, early):
-        group = [late, from_partner(late, "gx", 0), early, from_partner(early, "gx", 0)]
-        return y_dft(group, coefs_b, y_table, twist)
-
-    second_a, second_b = to_planes(first_a[0])[0], from_partner(first_b[0], "gx", 1)
-    first_a[1], second_b = lax.optimization_barrier((first_a[1], second_b))
-    sums = x_first([y_part_a(second_a), y_part_b(second_b, first_b[0])], table_one)
-    second_a, second_b = to_planes(first_a[1])[0], from_partner(first_b[1], "gx", 1)
-    sums, second_a, second_b = lax.optimization_barrier((sums, second_a, second_b))
-    parts = [y_part_a(second_a), y_part_b(second_b, first_b[1])]
-    latent, tile = x_last(parts, table_two, sums, row_pair, col_trio)
+    second_b = from_partner(first_b, "gx", 1)
+    second_a = to_planes(first_a[0])[0]
+    second_a, first_a[1] = lax.optimization_barrier((second_a, first_a[1]))
+    last_a = to_planes(first_a[1])[0]
+    sums = x_first([y_part_a(second_a)], table_one)
+    group = [second_b, from_partner(second_b, "gx", 0), first_b, from_partner(first_b, "gx", 0)]
+    part_b = y_dft(group, coefs_b, y_table, twist)
+    sums, part_b, last_a = lax.optimization_barrier((sums, part_b, last_a))
+    latent, tile = x_last([part_b, y_part_a(last_a)], table_two, sums, row_pair, col_trio)
     tile = tile + fixed / tile.size
     modes = length * columns * lax.axis_size("gx") * lax.axis_size("gy")
     return (latent, sum_everywhere(tile) / modes)

time: 178 us -> 193 us (1.084)
  other arithmetic: 21.2 us -> 29.1 us
  local copies, waits for them, and re-layouts: 17 us -> 23.7 us
    ppermute x9 -> x6, waiting for transfers between devices: 49.3 us -> 62.1 us  [from_partner(): return lax.ppermute(value, axis, pairs)]
    unnamed x32 -> x50, local copies, waits for them, and re-layouts: 5.79 us -> 17.5 us
    all_to_all x3, waiting for transfers between devices: 9.65 us -> 0.01 us  [to_planes(): return lax.all_to_all(values, 'gy', split_axis=0, concat_axis=1, tiled=True)]
    convert_element_type x3 -> x4, other arithmetic: 2.36 us -> 7.67 us  [split_table(): parts = [high.astype(jnp.bfloat16), (table - high).astype(jnp.bfloat16)]]
    pallas_call x1, Pallas kernels: 10.5 us -> 14.1 us  [x_last(): pl.pallas_call(functools.partial(x_last_kernel, count), out_shape=(jax.Sh...]
    pallas_call x1, Pallas kernels: 7.49 us -> 4.11 us  [x_first(): pl.pallas_call(functools.partial(x_first_kernel, count), out_shape=jax.Sh...]
    sin x0 -> x1, other arithmetic: none -> 3.23 us  [four_way(): twist = jnp.stack([jnp.cos(angle), jnp.sin(angle)])]
    broadcast_in_dim x3 -> x1, local copies, waits for them, and re-layouts: 2.56 us -> 0.01 us  [sum_everywhere(): copies = jnp.broadcast_to(tile[None], (devices,) + tile.shape)]
  transfers between devices with their start and end apart: 15 -> 9, of which waited for: 6 -> 4; matrix products, arithmetic and copies ran while one was open for 13% -> 16% of each run, Pallas kernels for 13% -> 10%
where the time goes in v4:
time: 193 us
  waiting for transfers between devices  62.1 us (32%)
  Pallas kernels  38.2 us (20%)
  other arithmetic  29.1 us (15%)
  local copies, waits for them, and re-layouts  23.7 us (12%)
  starting transfers between devices  21.9 us (11%)
  blocking collectives  13.6 us (7%)
  between operations  4.04 us (2%)
    ppermute x6, waiting for transfers between devices, from_partner(): return lax.ppermute(value, axis, pairs)  62.1 us
    pallas_call x3, Pallas kernels, y_dft(): pl.pallas_call(functools.partial(y_kernel, count), out_shape=jax.ShapeDty...  20 us
    all_to_all x3, starting transfers between devices, to_planes(): return lax.all_to_all(values, 'gy', split_axis=0, concat_axis=1, tiled=True)  18.4 us
    unnamed x50, local copies, waits for them, and re-layouts  17.5 us
    pallas_call x1, Pallas kernels, x_last(): pl.pallas_call(functools.partial(x_last_kernel, count), out_shape=(jax.Sh...  14.1 us
    all_to_all x1, blocking collectives, sum_everywhere(): lax.all_to_all(copies, axes, split_axis=0, concat_axis=0, tiled=True)  13.6 us
    convert_element_type x4, other arithmetic, split_table(): parts = [high.astype(jnp.bfloat16), (table - high).astype(jnp.bfloat16)]  7.67 us
    concatenate x3, other arithmetic, split_table(): return jnp.concatenate([parts[which] for which in order], axis)  6.61 us
  transfers between devices with their start and end apart: 9, of which 4 were waited for; matrix products, arithmetic and copies ran while one was open for 16% of the time, Pallas kernels for 10%

profile of v4, /device:TPU:0, one launch (start us, length us, event | category | flops | bytes accessed | tf_op | source)
XLA Modules:
  0.0 192.7 jit_solution(2901762611957623632)
XLA Ops:
  0.6 3.0 %slice.38 = f32[8,256,256]{2,1,0:T(8,128)} slice(f32[8,256,512]{2,1,0:T(8,128)} %param.6), slice={[0:8], [0:256], [256:512]} | slice | bytes 4194304 | tf_op jit(solution)/shard_map/slice | solution.py:256
  3.7 7.3 %all-to-all-start = ((f32[8,256,256]{2,1,0:T(8,128)}), f32[8,256,256]{2,1,0:T(8,128)}, u32[]{:S(2)}, u32[]{:S(2)}) async-start(f32[8,256,256]{2,1,0:T(8,128)} %slice.38), calls=%async_computation | async-start | bytes 4194304 | tf_op jit(solution)/shard_map/all_to_all | solution.py:24
  11.0 3.1 %slice.39 = f32[8,256,256]{2,1,0:T(8,128)} slice(f32[8,256,512]{2,1,0:T(8,128)} %param.6), slice={[0:8], [0:256], [0:256]} | slice | bytes 4194304 | tf_op jit(solution)/shard_map/slice | solution.py:257
  14.0 1.5 collective-permute-start
  15.6 0.7 log_reduce_fusion.1
  16.3 0.1 reshape.55.coef_ref
  16.4 0.6 log_reduce_fusion
  17.1 1.0 fusion.28
  18.1 1.0 fusion.26
  19.1 1.1 fusion.4
  20.2 4.1 %fusion.17 = (f32[512,512]{1,0:T(8,128)S(1)}, f32[512,512]{1,0:T(8,128)S(1)}, f32[512,512]{1,0:T(8,128)S(1)}) fusion(s32[512]{0:T(512)S(1)} %multiply_add_fusion), kind=kLoop, calls=%fused_computation.46 | loop fusion | flops 3932160 | bytes 3147776 | tf_op jit(solution)/shard_map/sin | solution.py:37
  24.4 2.2 %reduce-precision_convert_fusion.1 = (bf16[256,1024]{1,0:T(8,128)(2,1)}, bf16[256,1024]{1,0:T(8,128)(2,1)}, f32[256,1024]{1,0:T(8,128)}, f32[256,1024]{1,0:T(8,128)}) fusion(f32[512,512]{1,0:T(8,128)S(1)} %get-tuple-element.58, f32[512,512]{1,0:T(8,128)S(1)} %get-tuple-element.57, f32[512,512]{1,0:T(8,128)S(1)} %get-tuple-element.56), kind=kLoop, calls=%fused_computation.23 | loop fusion | flops 3145728 | bytes 6291456 | tf_op jit(solution)/shard_map/convert_element_type | solution.py:49
  26.6 0.1 copy-done.14
  28.1 2.7 %pad_maximum_fusion.3.refs_1_ = bf16[768,1024]{1,0:T(8,128)(2,1)} fusion(bf16[256,1024]{1,0:T(8,128)(2,1)} %get-tuple-element.49, bf16[256,1024]{1,0:T(8,128)(2,1)} %get-tuple-element.48), kind=kLoop, calls=%fused_computation.18 | loop fusion | flops 4718592 | bytes 2621440 | tf_op jit(solution)/shard_map/concatenate | solution.py:50
  30.8 3.2 %fusion.14 = (f32[1,8,256,128]{3,2,1,0:T(8,128)S(1)}, f32[1,8,256,128]{3,2,1,0:T(8,128)S(1)}) fusion(), kind=kLoop, calls=%fused_computation.43 | loop fusion | flops 786432 | bytes 2097152 | tf_op jit(solution)/shard_map/sin | solution.py:274
  34.1 0.2 pad_maximum_fusion.1.refs_3_.refs_5_
  34.3 1.3 pad_maximum_fusion.2.refs_2_.refs_4_
  35.5 0.6 copy-done.15
  36.1 0.3 copy-done.16
  36.5 0.3 copy-done.17
  36.8 3.8 %reduce-precision_convert_fusion = (bf16[768,1024]{1,0:T(8,128)(2,1)S(1)}, f32[768,1024]{1,0:T(8,128)S(1)}) fusion(f32[512,512]{1,0:T(8,128)S(1)} %copy-done.15, f32[512,512]{1,0:T(8,128)S(1)} %copy-done.13, f32[512,512]{1,0:T(8,128)S(1)} %get-tuple-element.56, f32[256,1024]{1,0:T(8,128)S(1)} %copy-done.17, f32[256,1024]{1,0:T(8,128)S(1)} %copy-done.16), kind=kLoop, calls=%fused_computation.4 | loop fusion | flops 11796480 | bytes 9961472 | tf_op jit(solution)/shard_map/convert_element_type | solution.py:49
  40.6 0.5 fusion
  41.1 2.7 %pad_maximum_fusion.refs_2_ = bf16[2304,1024]{1,0:T(8,128)(2,1)} fusion(bf16[768,1024]{1,0:T(8,128)(2,1)S(1)} %fusion, bf16[768,1024]{1,0:T(8,128)(2,1)S(1)} %get-tuple-element.44), kind=kLoop, calls=%fused_computation.2 | loop fusion | flops 14155776 | bytes 7864320 | tf_op jit(solution)/shard_map/concatenate | solution.py:50
  43.8 17.6 %collective-permute-done = f32[8,256,256]{2,1,0:T(8,128)} collective-permute-done((f32[8,256,256]{2,1,0:T(8,128)}, f32[8,256,256]{2,1,0:T(8,128)}, u32[]{:S(2)}, u32[]{:S(2)}) %collective-permute-start) | collective-permute-done | bytes 2097184 | tf_op jit(solution)/shard_map/ppermute | solution.py:20
  61.4 3.2 %slice_add_fusion = (f32[8,256,128]{2,1,0:T(8,128)}, f32[8,256,128]{2,1,0:T(8,128)}) fusion(f32[8,256,256]{2,1,0:T(8,128)} %collective-permute-done, f32[8,256,512]{2,1,0:T(8,128)S(1)} %copy-done.11, f32[]{:T(128)S(6)} %select_n.39), kind=kLoop, calls=%fused_computation.37 | loop fusion | flops 1048576 | bytes 6291460 | tf_op jit(solution)/shard_map/add | solution.py:288
  64.7 1.5 collective-permute-start.2
  66.2 5.7 %all-to-all-start.1 = ((f32[8,256,128]{2,1,0:T(8,128)}), f32[8,256,128]{2,1,0:T(8,128)S(1)}, u32[]{:S(2)}, u32[]{:S(2)}) async-start(f32[8,256,128]{2,1,0:T(8,128)} %get-tuple-element.26), calls=%async_computation.1 | async-start | bytes 2097152 | tf_op jit(solution)/shard_map/all_to_all | solution.py:24
  71.9 39.2 %collective-permute-done.2.refs_0_ = f32[2048,256]{1,0:T(8,128)} collective-permute-done((f32[2048,256]{1,0:T(8,128)}, f32[2048,256]{1,0:T(8,128)}, u32[]{:S(2)}, u32[]{:S(2)}) %collective-permute-start.2) | collective-permute-done | bytes 2097184 | tf_op jit(solution)/shard_map/ppermute | solution.py:20
  111.2 1.0 copy-done.7
  112.1 5.4 %all-to-all-start.2 = ((f32[8,256,128]{2,1,0:T(8,128)}), f32[8,256,128]{2,1,0:T(8,128)S(1)}, u32[]{:S(2)}, u32[]{:S(2)}) async-start(f32[8,256,128]{2,1,0:T(8,128)} %get-tuple-element.34), calls=%async_computation.2 | async-start | bytes 2097152 | tf_op jit(solution)/shard_map/all_to_all | solution.py:24
  117.6 0.2 collective-permute-start.1
  117.8 2.6 %collective-permute-done.1.refs_1_ = f32[2048,128]{1,0:T(8,128)S(1)} collective-permute-done((f32[2048,128]{1,0:T(8,128)}, f32[2048,128]{1,0:T(8,128)S(1)}, u32[]{:S(2)}, u32[]{:S(2)}) %collective-permute-start.1) | collective-permute-done | bytes 1048608 | tf_op jit(solution)/shard_map/ppermute | solution.py:20
  120.4 1.4 copy-done
  121.8 1.2 copy-done.8
  123.1 4.0 %y_dft.3.refs_0_ = bf16[4,2048,128]{2,1,0:T(8,128)(2,1)S(1)} custom-call(f32[2,2]{1,0:T(2,128)S(1)} %reshape.55.coef_ref, f32[2048,128]{1,0:T(8,128)S(1)} %bitcast.15, f32[2048,128]{1,0:T(8,128)S(1)} %collective-permute-done.1.refs_1_, bf16[512,1536]{1,0:T(8,128)(2,1)S(1)} %copy-done, f32[2,8,256,128]{3,2,1,0:T(8,128)S(1)} %pad_maximum_fusion.1.refs_3_.refs_5_), custom_call_target="tpu_custom_call" | custom-call | flops 1610612736 | bytes 5242880 | tf_op jit(solution)/shard_map/y_dft/pallas_call | solution.py:131
  127.1 4.1 %x_first.1.refs_3_ = f32[2048,1024]{1,0:T(8,128)S(1)} custom-call(bf16[4,2048,128]{2,1,0:T(8,128)(2,1)S(1)} %y_dft.3.refs_0_, bf16[768,1024]{1,0:T(8,128)(2,1)S(1)} %copy-done.5), custom_call_target="tpu_custom_call" | custom-call | flops 3221225472 | bytes 16777216 | tf_op jit(solution)/shard_map/x_first/pallas_call | solution.py:164
  131.2 3.4 %copy-done.3 = f32[2048,1024]{1,0:T(8,128)} copy-done((f32[2048,1024]{1,0:T(8,128)}, f32[2048,1024]{1,0:T(8,128)S(1)}, u32[]{:S(2)}) %copy-start.3) | copy-done | bytes 8388632
  134.6 11.2 %y_dft.4.refs_0_ = bf16[4,2048,256]{2,1,0:T(8,128)(2,1)S(1)} custom-call(f32[2,4]{1,0:T(2,128)S(1)} %pad_maximum_fusion.7.coef_ref, f32[2048,256]{1,0:T(8,128)} %collective-permute-done.2.refs_0_, f32[2048,256]{1,0:T(8,128)} %collective-permute-done.3.refs_1_, f32[2048,256]{1,0:T(8,128)} %bitcast.refs_2_, f32[2048,256]{1,0:T(8,128)} %collective-permute-done.4.refs_3_, ...), custom_call_target="tpu_custom_call" | custom-call | flops 3221225472 | bytes 14680064 | tf_op jit(solution)/shard_map/y_dft/pallas_call | solution.py:131
  145.8 2.0 %copy-done.9 = bf16[4,2048,256]{2,1,0:T(8,128)(2,1)} copy-done((bf16[4,2048,256]{2,1,0:T(8,128)(2,1)}, bf16[4,2048,256]{2,1,0:T(8,128)(2,1)S(1)}, u32[]{:S(2)}) %copy-start.9) | copy-done | bytes 4194328
  147.8 0.2 collective-permute-start.5
  148.0 2.6 %collective-permute-done.5.refs_1_ = f32[2048,128]{1,0:T(8,128)} collective-permute-done((f32[2048,128]{1,0:T(8,128)S(1)}, f32[2048,128]{1,0:T(8,128)}, u32[]{:S(2)}, u32[]{:S(2)}) %collective-permute-start.5) | collective-permute-done | bytes 1048608 | tf_op jit(solution)/shard_map/ppermute | solution.py:20
  150.6 1.4 copy-done.2
  152.0 4.8 %y_dft.5.refs_1_ = bf16[4,2048,128]{2,1,0:T(8,128)(2,1)S(1)} custom-call(f32[2,2]{1,0:T(2,128)S(1)} %reshape.55.coef_ref, f32[2048,128]{1,0:T(8,128)S(1)} %bitcast.13, f32[2048,128]{1,0:T(8,128)} %collective-permute-done.5.refs_1_, bf16[512,1536]{1,0:T(8,128)(2,1)S(1)} %copy-done.2, f32[2,8,256,128]{3,2,1,0:T(8,128)S(1)} %pad_maximum_fusion.1.refs_3_.refs_5_), custom_call_target="tpu_custom_call" | custom-call | flops 1610612736 | bytes 5242880 | tf_op jit(solution)/shard_map/y_dft/pallas_call | solution.py:131
  156.9 3.4 %copy-done.4 = f32[2048,1024]{1,0:T(8,128)S(1)} copy-done((f32[2048,1024]{1,0:T(8,128)S(1)}, f32[2048,1024]{1,0:T(8,128)}, u32[]{:S(2)}) %copy-start.4) | copy-done | bytes 8388632
  160.2 2.3 %copy-done.6 = bf16[2304,1024]{1,0:T(8,128)(2,1)S(1)} copy-done((bf16[2304,1024]{1,0:T(8,128)(2,1)S(1)}, bf16[2304,1024]{1,0:T(8,128)(2,1)}, u32[]{:S(2)}) %copy-start.6) | copy-done | bytes 4718616
  162.6 14.1 %x_last.1 = (f32[2,1,2048,512]{3,2,1,0:T(8,128)}, f32[8,128]{1,0:T(8,128)S(1)}) custom-call(bf16[4,2048,256]{2,1,0:T(8,128)(2,1)S(1)} %copy-done.10, bf16[4,2048,128]{2,1,0:T(8,128)(2,1)S(1)} %y_dft.5.refs_1_, bf16[2304,1024]{1,0:T(8,128)(2,1)S(1)} %copy-done.6, f32[2048,1024]{1,0:T(8,128)S(1)} %copy-done.4, f32[2,4,4,128]{3,2,1,0:T(4,128)S(1)} %pad_maximum_fusion.5.refs_4_, ...), custom_call_target="tpu_custom_call" | custom-call | flops 9663676416 | bytes 25165824 | tf_op jit(solution)/shard_map/x_last/pallas_call | solution.py:216
  176.6 13.6 %all_to_all.32 = f32[32,8,128]{2,1,0:T(8,128)S(1)} all-to-all(f32[32,8,128]{2,1,0:T(8,128)S(1)} %broadcast_in_dim.2), channel_id=1, replica_groups=mesh['gx'=4,'gy'=8] {'gx','gy'}, dimensions={0} | all-to-all | bytes 262144 | tf_op jit(solution)/shard_map/all_to_all | solution.py:248
  190.3 0.6 reduce_sum.29
  (53 shorter events, 0.3 us)
Async XLA Ops:
  3.7 61.0 %all-to-all-start = ((f32[8,256,256]{2,1,0:T(8,128)}), f32[8,256,256]{2,1,0:T(8,128)}, u32[]{:S(2)}, u32[]{:S(2)}) async-start(f32[8,256,256]{2,1,0:T(8,128)} %slice.38), calls=%async_computation | async-start | bytes 4194304 | tf_op jit(solution)/shard_map/all_to_all | solution.py:24
  10.9 4.6 %copy-start.20 = (f32[512]{0:T(512)S(1)}, f32[512]{0:T(512)}, u32[]{:S(2)}) copy-start(f32[512]{0:T(512)} %param.8) | copy-start | bytes 6148
  10.9 5.5 %copy-start.21 = (f32[2048]{0:T(1024)S(1)}, f32[2048]{0:T(1024)}, u32[]{:S(2)}) copy-start(f32[2048]{0:T(1024)} %param.7) | copy-start | bytes 24580
  10.9 6.1 %copy-start.22 = (f32[2048]{0:T(1024)S(1)}, f32[2048]{0:T(1024)}, u32[]{:S(2)}) copy-start(f32[2048]{0:T(1024)} %param.9) | copy-start | bytes 24580
  11.0 6.1 %copy-start.23 = (f32[512]{0:T(512)S(1)}, f32[512]{0:T(512)}, u32[]{:S(2)}) copy-start(f32[512]{0:T(512)} %param.11) | copy-start | bytes 6148
  11.0 6.1 %copy-start.24 = (f32[512]{0:T(512)S(1)}, f32[512]{0:T(512)}, u32[]{:S(2)}) copy-start(f32[512]{0:T(512)} %param.10) | copy-start | bytes 6148
  14.0 47.4 %collective-permute-start = (f32[8,256,256]{2,1,0:T(8,128)}, f32[8,256,256]{2,1,0:T(8,128)}, u32[]{:S(2)}, u32[]{:S(2)}) collective-permute-start(f32[8,256,256]{2,1,0:T(8,128)} %slice.39), channel_id=1, source_target_pairs={{0,16},{8,24},{16,0},{24,8},{1,17},{9,25},{17,1},{25,9},{2,18},{10... | collective-permute-start | bytes 6291464 | tf_op jit(solution)/shard_map/ppermute | solution.py:20
  24.4 2.2 %copy-start.12 = (f32[512,512]{1,0:T(8,128)}, f32[512,512]{1,0:T(8,128)S(1)}, u32[]{:S(2)}) copy-start(f32[512,512]{1,0:T(8,128)S(1)} %get-tuple-element.57) | copy-start | bytes 3145732
  24.4 2.4 %copy-start.14 = (f32[512,512]{1,0:T(8,128)}, f32[512,512]{1,0:T(8,128)S(1)}, u32[]{:S(2)}) copy-start(f32[512,512]{1,0:T(8,128)S(1)} %get-tuple-element.58) | copy-start | bytes 3145732
  30.8 3.5 %copy-start.18 = (bf16[512,512]{1,0:T(8,128)(2,1)S(1)}, bf16[512,512]{1,0:T(8,128)(2,1)}, u32[]{:S(2)}) copy-start(bf16[512,512]{1,0:T(8,128)(2,1)} %get-tuple-element.52) | copy-start | bytes 1572868
  30.8 3.5 %copy-start.19 = (bf16[512,512]{1,0:T(8,128)(2,1)S(1)}, bf16[512,512]{1,0:T(8,128)(2,1)}, u32[]{:S(2)}) copy-start(bf16[512,512]{1,0:T(8,128)(2,1)} %get-tuple-element.53) | copy-start | bytes 1572868
  34.0 1.5 copy-start.13
  34.0 2.1 %copy-start.15 = (f32[512,512]{1,0:T(8,128)S(1)}, f32[512,512]{1,0:T(8,128)}, u32[]{:S(2)}) copy-start(f32[512,512]{1,0:T(8,128)} %copy-done.14) | copy-start | bytes 3145732
  34.0 2.4 %copy-start.16 = (f32[256,1024]{1,0:T(8,128)S(1)}, f32[256,1024]{1,0:T(8,128)}, u32[]{:S(2)}) copy-start(f32[256,1024]{1,0:T(8,128)} %get-tuple-element.50) | copy-start | bytes 3145732
  34.1 2.7 %copy-start.17 = (f32[256,1024]{1,0:T(8,128)S(1)}, f32[256,1024]{1,0:T(8,128)}, u32[]{:S(2)}) copy-start(f32[256,1024]{1,0:T(8,128)} %get-tuple-element.51) | copy-start | bytes 3145732
  41.1 20.3 %copy-start.11 = (f32[8,256,512]{2,1,0:T(8,128)S(1)}, f32[8,256,512]{2,1,0:T(8,128)}, u32[]{:S(2)}) copy-start(f32[8,256,512]{2,1,0:T(8,128)} %param.6) | copy-start | bytes 12582916
  64.7 46.5 %collective-permute-start.2 = (f32[2048,256]{1,0:T(8,128)}, f32[2048,256]{1,0:T(8,128)}, u32[]{:S(2)}, u32[]{:S(2)}) collective-permute-start(f32[2048,256]{1,0:T(8,128)} %bitcast.refs_2_), channel_id=1, source_target_pairs={{0,16},{8,24},{16,0},{24,8},{1,17},{9,25},{17,1},{25,9},{2,18},{10... | collective-permute-start | bytes 6291464 | tf_op jit(solution)/shard_map/ppermute | solution.py:20
  66.2 45.0 %all-to-all-start.1 = ((f32[8,256,128]{2,1,0:T(8,128)}), f32[8,256,128]{2,1,0:T(8,128)S(1)}, u32[]{:S(2)}, u32[]{:S(2)}) async-start(f32[8,256,128]{2,1,0:T(8,128)} %get-tuple-element.26), calls=%async_computation.1 | async-start | bytes 2097152 | tf_op jit(solution)/shard_map/all_to_all | solution.py:24
  71.9 62.7 %collective-permute-start.4 = (f32[2048,256]{1,0:T(8,128)}, f32[2048,256]{1,0:T(8,128)}, u32[]{:S(2)}, u32[]{:S(2)}) collective-permute-start(f32[2048,256]{1,0:T(8,128)} %bitcast.refs_2_), channel_id=1, source_target_pairs={{0,8},{8,0},{16,24},{24,16},{1,9},{9,1},{17,25},{25,17},{2,10},{10... | collective-permute-start | bytes 6291464 | tf_op jit(solution)/shard_map/ppermute | solution.py:20
  111.2 23.5 %collective-permute-start.3 = (f32[2048,256]{1,0:T(8,128)}, f32[2048,256]{1,0:T(8,128)}, u32[]{:S(2)}, u32[]{:S(2)}) collective-permute-start(f32[2048,256]{1,0:T(8,128)} %collective-permute-done.2.refs_0_), channel_id=1, source_target_pairs={{0,8},{8,0},{16,24},{24,16},{1,9},{9,1},{17,25},{25,17},{2,10},{10... | collective-permute-start | bytes 6291464 | tf_op jit(solution)/shard_map/ppermute | solution.py:20
  111.2 1.0 copy-start.7
  112.1 35.7 %all-to-all-start.2 = ((f32[8,256,128]{2,1,0:T(8,128)}), f32[8,256,128]{2,1,0:T(8,128)S(1)}, u32[]{:S(2)}, u32[]{:S(2)}) async-start(f32[8,256,128]{2,1,0:T(8,128)} %get-tuple-element.34), calls=%async_computation.2 | async-start | bytes 2097152 | tf_op jit(solution)/shard_map/all_to_all | solution.py:24
  117.6 2.9 %collective-permute-start.1 = (f32[2048,128]{1,0:T(8,128)}, f32[2048,128]{1,0:T(8,128)S(1)}, u32[]{:S(2)}, u32[]{:S(2)}) collective-permute-start(f32[2048,128]{1,0:T(8,128)} %bitcast.14), channel_id=1, source_target_pairs={{0,8},{8,0},{16,24},{24,16},{1,9},{9,1},{17,25},{25,17},{2,10},{10... | collective-permute-start | bytes 3145736 | tf_op jit(solution)/shard_map/ppermute | solution.py:20
  120.4 1.4 copy-start
  121.8 1.2 copy-start.8
  123.1 4.0 %copy-start.5 = (bf16[768,1024]{1,0:T(8,128)(2,1)S(1)}, bf16[768,1024]{1,0:T(8,128)(2,1)}, u32[]{:S(2)}) copy-start(bf16[768,1024]{1,0:T(8,128)(2,1)} %pad_maximum_fusion.3.refs_1_) | copy-start | bytes 4718596
  127.1 7.5 %copy-start.1 = (bf16[512,1536]{1,0:T(8,128)(2,1)S(1)}, bf16[512,1536]{1,0:T(8,128)(2,1)}, u32[]{:S(2)}) copy-start(bf16[512,1536]{1,0:T(8,128)(2,1)} %pad_maximum_fusion.2.refs_2_.refs_4_) | copy-start | bytes 4718596
  131.2 3.4 %copy-start.3 = (f32[2048,1024]{1,0:T(8,128)}, f32[2048,1024]{1,0:T(8,128)S(1)}, u32[]{:S(2)}) copy-start(f32[2048,1024]{1,0:T(8,128)S(1)} %x_first.1.refs_3_) | copy-start | bytes 25165828
  145.8 2.0 %copy-start.9 = (bf16[4,2048,256]{2,1,0:T(8,128)(2,1)}, bf16[4,2048,256]{2,1,0:T(8,128)(2,1)S(1)}, u32[]{:S(2)}) copy-start(bf16[4,2048,256]{2,1,0:T(8,128)(2,1)S(1)} %y_dft.4.refs_0_) | copy-start | bytes 12582916
  147.8 2.8 %collective-permute-start.5 = (f32[2048,128]{1,0:T(8,128)S(1)}, f32[2048,128]{1,0:T(8,128)}, u32[]{:S(2)}, u32[]{:S(2)}) collective-permute-start(f32[2048,128]{1,0:T(8,128)S(1)} %bitcast.12), channel_id=1, source_target_pairs={{0,8},{8,0},{16,24},{24,16},{1,9},{9,1},{17,25},{25,17},{2,10},{10... | collective-permute-start | bytes 3145736 | tf_op jit(solution)/shard_map/ppermute | solution.py:20
  150.6 1.4 copy-start.2
  152.0 4.8 %copy-start.10 = (bf16[4,2048,256]{2,1,0:T(8,128)(2,1)S(1)}, bf16[4,2048,256]{2,1,0:T(8,128)(2,1)}, u32[]{:S(2)}) copy-start(bf16[4,2048,256]{2,1,0:T(8,128)(2,1)} %copy-done.9) | copy-start | bytes 12582916
  156.9 3.4 %copy-start.4 = (f32[2048,1024]{1,0:T(8,128)S(1)}, f32[2048,1024]{1,0:T(8,128)}, u32[]{:S(2)}) copy-start(f32[2048,1024]{1,0:T(8,128)} %copy-done.3) | copy-start | bytes 25165828
  160.2 2.3 %copy-start.6 = (bf16[2304,1024]{1,0:T(8,128)(2,1)S(1)}, bf16[2304,1024]{1,0:T(8,128)(2,1)}, u32[]{:S(2)}) copy-start(bf16[2304,1024]{1,0:T(8,128)(2,1)} %pad_maximum_fusion.refs_2_) | copy-start | bytes 14155780

commit v5 on v4

--- a/solution.py
+++ b/solution.py
@@ -11,7 +11,7 @@
 precision_top = lax.Precision.HIGHEST
 RADIX = 8
 LANES = 128
-Y_BYTES, X_BYTES = 28 * 1024 * 1024, 30 * 1024 * 1024
+X_BYTES = 30 * 1024 * 1024
 
 
 def from_partner(value, axis, stride):
@@ -22,6 +22,32 @@
 
 def to_planes(values):
     return lax.all_to_all(values, "gy", split_axis=0, concat_axis=1, tiled=True)
+
+
+def cut_kernel(field_ref, left_ref, right_ref, sems):
+    half = left_ref.shape[2]
+    copies = [
+        pltpu.make_async_copy(field_ref.at[:, :, pl.ds(place * half, half)], out_ref, sems.at[place])
+        for place, out_ref in enumerate((left_ref, right_ref))
+    ]
+    for copy in copies:
+        copy.start()
+    for copy in copies:
+        copy.wait()
+
+
+def cut_in_half(field):
+    planes, rows, columns = field.shape
+    return pl.pallas_call(
+        cut_kernel,
+        out_shape=[jax.ShapeDtypeStruct((planes, rows, columns // 2), jnp.float32)] * 2,
+        in_specs=[pl.BlockSpec(memory_space=pl.ANY)],
+        out_specs=[pl.BlockSpec(memory_space=pltpu.VMEM)] * 2,
+        scratch_shapes=[pltpu.SemaphoreType.DMA((2,))],
+        compiler_params=pltpu.CompilerParams(vmem_limit_bytes=56 * 1024 * 1024),
+        cost_estimate=pl.CostEstimate(flops=0, bytes_accessed=8 * field.size, transcendentals=0),
+        name="cut_in_half",
+    )(field)
 
 
 def reverse_bits(value, count):
@@ -138,7 +164,7 @@
             pltpu.VMEM((6 * inner, RADIX * width), jnp.bfloat16),
             pltpu.VMEM((2 * inner, RADIX * width), jnp.float32),
         ],
-        compiler_params=pltpu.CompilerParams(vmem_limit_bytes=Y_BYTES),
+        compiler_params=pltpu.CompilerParams(vmem_limit_bytes=(8 + 20 * width // 256) * 1024 * 1024),
         cost_estimate=pl.CostEstimate(
             flops=24 * inner * length * width, bytes_accessed=4 * length * width * (count + 3), transcendentals=0
         ),
@@ -166,7 +192,7 @@
         out_shape=jax.ShapeDtypeStruct((length, columns), jnp.float32),
         grid=(length // rows,),
         in_specs=[pl.BlockSpec((4, rows, part.shape[2]), lambda i: (0, i, 0)) for part in parts]
-        + [pl.BlockSpec(table.shape, lambda i: (0, 0))],
+        + [pl.BlockSpec(table.shape, lambda i: (0, 0), pipeline_mode=pl.Buffered(1))],
         out_specs=pl.BlockSpec((rows, columns), lambda i: (i, 0)),
         compiler_params=pltpu.CompilerParams(vmem_limit_bytes=X_BYTES),
         cost_estimate=pl.CostEstimate(
@@ -222,7 +248,7 @@
         grid=(length // rows,),
         in_specs=[pl.BlockSpec((4, rows, part.shape[2]), lambda i: (0, i, 0)) for part in parts]
         + [
-            pl.BlockSpec(table.shape, lambda i: (0, 0)),
+            pl.BlockSpec(table.shape, lambda i: (0, 0), pipeline_mode=pl.Buffered(1)),
             pl.BlockSpec((rows, columns), lambda i: (i, 0)),
             pl.BlockSpec((2, 1, rows // LANES, LANES), lambda i: (0, i, 0, 0)),
             pl.BlockSpec(col_trio.shape, lambda i: (0, 0)),
@@ -252,9 +278,7 @@
     position = lax.axis_index("gx")
     planes, rows, columns = field.shape
     length, width = planes * rows, columns // 4
-    quarters = [slice(0, width), slice(width, 2 * width)]
-    field_b, field_rest = lax.optimization_barrier((field[:, :, 2 * width :], field))
-    field_a = field_rest[:, :, : 2 * width]
+    field_a, field_b = cut_in_half(field)
     sign = jnp.where(position < 2, 1.0, -1.0)
 
     own_real = jnp.where(position == 1, -1.0, jnp.where(position == 3, 0.0, 1.0))
@@ -284,24 +308,23 @@
     fixed = 2.0 * (columns * jnp.sum(jnp.log(row_scale)) + length * jnp.sum(jnp.log(col_scale)))
     fixed = fixed - length * columns * math.log(2.0 * math.pi)
 
-    received = from_partner(field_a, "gx", 1)
-    first_a = [received[:, :, span] + sign * field_a[:, :, span] for span in quarters]
-    tables = (y_table, twist, x_table(quarters[0]), x_table(slice(2 * width, None), quarters[1]), row_pair, col_trio)
+    first_a = from_partner(field_a, "gx", 1) + sign * field_a
+    spans = [slice(2 * width, 3 * width), slice(3 * width, None), slice(0, 2 * width)]
+    tables = (y_table, twist, x_table(spans[0]), x_table(*spans[1:]), row_pair, col_trio)
     state = lax.optimization_barrier((first_a, to_planes(field_b)[0], tables, coefs_a, coefs_b, fixed))
     first_a, first_b, (y_table, twist, table_one, table_two, row_pair, col_trio), coefs_a, coefs_b, fixed = state
-
-    def y_part_a(own):
-        return y_dft([own, from_partner(own, "gx", 0)], coefs_a, y_table, twist)
-
-    second_b = from_partner(first_b, "gx", 1)
-    second_a = to_planes(first_a[0])[0]
-    second_a, first_a[1] = lax.optimization_barrier((second_a, first_a[1]))
-    last_a = to_planes(first_a[1])[0]
-    sums = x_first([y_part_a(second_a)], table_one)
-    group = [second_b, from_partner(second_b, "gx", 0), first_b, from_partner(first_b, "gx", 0)]
-    part_b = y_dft(group, coefs_b, y_table, twist)
-    sums, part_b, last_a = lax.optimization_barrier((sums, part_b, last_a))
-    latent, tile = x_last([part_b, y_part_a(last_a)], table_two, sums, row_pair, col_trio)
+    second_a = to_planes(first_a)[0]
+
+    def y_part_b(early):
+        late = from_partner(early, "gx", 1)
+        group = [late, from_partner(late, "gx", 0), early, from_partner(early, "gx", 0)]
+        return y_dft(group, coefs_b, y_table, twist)
+
+    parts = [y_part_b(first_b[:, :width]), y_part_b(first_b[:, width:])]
+    sums = x_first(parts[:1], table_one)
+    sums, parts[1], second_a = lax.optimization_barrier((sums, parts[1], second_a))
+    parts.append(y_dft([second_a, from_partner(second_a, "gx", 0)], coefs_a, y_table, twist))
+    latent, tile = x_last(parts[1:], table_two, sums, row_pair, col_trio)
     tile = tile + fixed / tile.size
     modes = length * columns * lax.axis_size("gx") * lax.axis_size("gy")
     return (latent, sum_everywhere(tile) / modes)

time: 193 us -> 183 us (0.948)
  local copies, waits for them, and re-layouts: 23.7 us -> 10.4 us
  waiting for transfers between devices: 62.1 us -> 74 us
  other arithmetic: 29.1 us -> 22.2 us
  starting transfers between devices: 21.9 us -> 17.7 us
  Pallas kernels: 38.2 us -> 40.9 us
    ppermute x6 -> x8, waiting for transfers between devices: 62.1 us -> 74 us  [from_partner(): return lax.ppermute(value, axis, pairs)]
    unnamed x50 -> x26, local copies, waits for them, and re-layouts: 17.5 us -> 8.52 us
    convert_element_type x4, other arithmetic: 7.67 us -> 1.66 us  [split_table(): parts = [high.astype(jnp.bfloat16), (table - high).astype(jnp.bfloat16)]]
    all_to_all x3 -> x2, starting transfers between devices: 18.4 us -> 13.1 us  [to_planes(): return lax.all_to_all(values, 'gy', split_axis=0, concat_axis=1, tiled=True)]
    slice x2 -> x1, local copies, waits for them, and re-layouts: 6.1 us -> 1.8 us  [four_way(): parts = [y_part_b(first_b[:, :width]), y_part_b(first_b[:, width:])]]
    pallas_call x0 -> x1, Pallas kernels: none -> 4.3 us  [cut_in_half(): pl.pallas_call(cut_kernel, out_shape=[jax.ShapeDtypeStruct((planes, rows,...]
    ppermute x6 -> x8, starting transfers between devices: 3.5 us -> 4.63 us  [from_partner(): return lax.ppermute(value, axis, pairs)]
  transfers between devices with their start and end apart: 9 -> 10, of which waited for: 4 -> 4; matrix products, arithmetic and copies ran while one was open for 16% -> 13% of each run, Pallas kernels for 10% -> 7%
where the time goes in v5:
time: 183 us; the launch traced here: 182 us
  waiting for transfers between devices  74 us (40%)
  Pallas kernels  40.9 us (22%)
  other arithmetic  22.2 us (12%)
  starting transfers between devices  17.7 us (10%)
  blocking collectives  13.3 us (7%)
  local copies, waits for them, and re-layouts  10.4 us (6%)
  between operations  3.88 us (2%)
    ppermute x8, waiting for transfers between devices, from_partner(): return lax.ppermute(value, axis, pairs)  74 us
    pallas_call x3, Pallas kernels, y_dft(): pl.pallas_call(functools.partial(y_kernel, count), out_shape=jax.ShapeDty...  18.4 us
    pallas_call x1, Pallas kernels, x_last(): pl.pallas_call(functools.partial(x_last_kernel, count), out_shape=(jax.Sh...  14.1 us
    all_to_all x1, blocking collectives, sum_everywhere(): lax.all_to_all(copies, axes, split_axis=0, concat_axis=0, tiled=True)  13.3 us
    all_to_all x2, starting transfers between devices, to_planes(): return lax.all_to_all(values, 'gy', split_axis=0, concat_axis=1, tiled=True)  13.1 us
    unnamed x26, local copies, waits for them, and re-layouts  8.52 us
    sin x2, other arithmetic, root_table(): return (jnp.cos(angle), jnp.sin(angle))  5.16 us
    concatenate x3, other arithmetic, split_table(): return jnp.concatenate([parts[which] for which in order], axis)  5.13 us
  transfers between devices with their start and end apart: 10, of which 4 were waited for; matrix products, arithmetic and copies ran while one was open for 13% of the time, Pallas kernels for 7%

profile of v5, /device:TPU:0, one launch (start us, length us, event | category | flops | bytes accessed | tf_op | source)
XLA Modules:
  0.0 182.4 jit_solution(4887121820548955726)
XLA Ops:
  0.6 4.3 %cut_in_half.1 = (f32[8,256,256]{2,1,0:T(8,128)}, f32[8,256,256]{2,1,0:T(8,128)}) custom-call(f32[8,256,512]{2,1,0:T(8,128)} %field_ref.1), custom_call_target="tpu_custom_call" | custom-call | bytes 8388608 | tf_op jit(solution)/shard_map/cut_in_half/pallas_call | solution.py:41
  4.9 0.0 copy-start.8
  4.9 0.0 copy-start.9
  5.0 0.0 copy-start.11
  5.0 0.0 copy-start.12
  5.0 0.0 copy-start.10
  5.0 7.4 %all-to-all-start = ((f32[8,256,256]{2,1,0:T(8,128)}), f32[8,256,256]{2,1,0:T(8,128)}, u32[]{:S(2)}, u32[]{:S(2)}) async-start(f32[8,256,256]{2,1,0:T(8,128)} %get-tuple-element.21), calls=%async_computation | async-start | bytes 4194304 | tf_op jit(solution)/shard_map/all_to_all | solution.py:24
  12.4 1.5 collective-permute-start
  13.9 0.6 log_reduce_fusion.1
  14.5 0.1 pad_maximum_fusion.9
  14.6 0.1 reshape.51.coef_ref
  14.7 0.6 log_reduce_fusion
  16.5 0.1 pad_maximum_fusion.8.coef_ref
  16.7 1.0 fusion.28
  17.6 1.0 fusion.26
  18.7 0.2 fusion.6
  18.8 4.1 %fusion.17 = (f32[512,512]{1,0:T(8,128)S(1)}, f32[512,512]{1,0:T(8,128)S(1)}, f32[512,512]{1,0:T(8,128)S(1)}) fusion(s32[512]{0:T(512)S(1)} %multiply_add_fusion.1), kind=kLoop, calls=%fused_computation.45 | loop fusion | flops 3932160 | bytes 3147776 | tf_op jit(solution)/shard_map/sin | solution.py:63
  23.0 0.1 reduce-precision_convert_fusion.1
  23.1 0.1 fusion.7
  23.3 1.4 pad_maximum_fusion.5.refs_1_
  24.7 3.2 %fusion.14 = (f32[1,8,256,128]{3,2,1,0:T(8,128)S(1)}, f32[1,8,256,128]{3,2,1,0:T(8,128)S(1)}) fusion(), kind=kLoop, calls=%fused_computation.42 | loop fusion | flops 786432 | bytes 2097152 | tf_op jit(solution)/shard_map/sin | solution.py:298
  27.9 0.1 pad_maximum_fusion.3.refs_5_.refs_3_
  28.0 1.2 pad_maximum_fusion.4.refs_4_.refs_2_
  29.3 1.2 reduce-precision_convert_fusion
  30.5 2.5 %pad_maximum_fusion.refs_2_ = bf16[2304,1024]{1,0:T(8,128)(2,1)} fusion(bf16[768,1024]{1,0:T(8,128)(2,1)S(1)} %get-tuple-element.41, bf16[768,1024]{1,0:T(8,128)(2,1)S(1)} %get-tuple-element.40), kind=kLoop, calls=%fused_computation.4 | loop fusion | flops 14155776 | bytes 7864320 | tf_op jit(solution)/shard_map/concatenate | solution.py:76
  33.0 26.8 %collective-permute-done = f32[8,256,256]{2,1,0:T(8,128)} collective-permute-done((f32[8,256,256]{2,1,0:T(8,128)}, f32[8,256,256]{2,1,0:T(8,128)}, u32[]{:S(2)}, u32[]{:S(2)}) %collective-permute-start) | collective-permute-done | bytes 2097184 | tf_op jit(solution)/shard_map/ppermute | solution.py:20
  59.8 3.9 %multiply_add_fusion = f32[8,256,256]{2,1,0:T(8,128)} fusion(f32[8,256,256]{2,1,0:T(8,128)} %collective-permute-done, f32[8,256,256]{2,1,0:T(8,128)} %get-tuple-element.20, f32[]{:T(128)S(6)} %select_n.39), kind=kLoop, calls=%fused_computation.18 | loop fusion | flops 1048576 | bytes 6291460 | tf_op jit(solution)/shard_map/add | solution.py:311
  63.7 5.7 %all-to-all-start.1 = ((f32[8,256,256]{2,1,0:T(8,128)}), f32[8,256,256]{2,1,0:T(8,128)}, u32[]{:S(2)}, u32[]{:S(2)}) async-start(f32[8,256,256]{2,1,0:T(8,128)} %multiply_add_fusion), calls=%async_computation.1 | async-start | bytes 4194304 | tf_op jit(solution)/shard_map/all_to_all | solution.py:24
  69.4 1.8 fusion.30
  71.2 1.6 collective-permute-start.4
  72.8 0.5 collective-permute-start.1
  73.3 24.1 %collective-permute-done.4.refs_0_ = f32[2048,128]{1,0:T(8,128)S(1)} collective-permute-done((f32[2048,128]{1,0:T(8,128)S(1)}, f32[2048,128]{1,0:T(8,128)S(1)}, u32[]{:S(2)}, u32[]{:S(2)}) %collective-permute-start.4) | collective-permute-done | bytes 1048608 | tf_op jit(solution)/shard_map/ppermute | solution.py:20
  97.4 0.5 collective-permute-start.3
  97.9 19.0 %collective-permute-done.1.refs_0_ = f32[2048,128]{1,0:T(8,128)S(1)} collective-permute-done((f32[2048,128]{1,0:T(8,128)S(1)}, f32[2048,128]{1,0:T(8,128)S(1)}, u32[]{:S(2)}, u32[]{:S(2)}) %collective-permute-start.1) | collective-permute-done | bytes 1048608 | tf_op jit(solution)/shard_map/ppermute | solution.py:20
  116.9 4.4 %y_dft.4.refs_0_ = bf16[4,2048,128]{2,1,0:T(8,128)(2,1)S(1)} custom-call(f32[2,4]{1,0:T(2,128)S(1)} %pad_maximum_fusion.8.coef_ref, f32[2048,128]{1,0:T(8,128)S(1)} %collective-permute-done.4.refs_0_, f32[2048,128]{1,0:T(8,128)S(1)} %collective-permute-done.5.refs_1_, f32[2048,128]{1,0:T(8,128)S(1)} %get-tuple-element.42.refs_2_, ...), custom_call_target="tpu_custom_call" | custom-call | flops 1610612736 | bytes 7340032 | tf_op jit(solution)/shard_map/y_dft/pallas_call | solution.py:157
  121.3 1.3 copy-done.6
  122.7 4.4 %y_dft.3.refs_0_ = bf16[4,2048,128]{2,1,0:T(8,128)(2,1)S(1)} custom-call(f32[2,4]{1,0:T(2,128)S(1)} %pad_maximum_fusion.8.coef_ref, f32[2048,128]{1,0:T(8,128)S(1)} %collective-permute-done.1.refs_0_, f32[2048,128]{1,0:T(8,128)S(1)} %collective-permute-done.2.refs_1_, f32[2048,128]{1,0:T(8,128)S(1)} %get-tuple-element.43.refs_2_, ...), custom_call_target="tpu_custom_call" | custom-call | flops 1610612736 | bytes 7340032 | tf_op jit(solution)/shard_map/y_dft/pallas_call | solution.py:157
  127.1 4.1 %x_first.1.refs_3_ = f32[2048,1024]{1,0:T(8,128)S(1)} custom-call(bf16[4,2048,128]{2,1,0:T(8,128)(2,1)S(1)} %y_dft.3.refs_0_, bf16[768,1024]{1,0:T(8,128)(2,1)S(1)} %copy-done.4), custom_call_target="tpu_custom_call" | custom-call | flops 3221225472 | bytes 16777216 | tf_op jit(solution)/shard_map/x_first/pallas_call | solution.py:190
  131.2 0.0 copy-start.2
  131.2 3.4 %copy-done.2 = f32[2048,1024]{1,0:T(8,128)} copy-done((f32[2048,1024]{1,0:T(8,128)}, f32[2048,1024]{1,0:T(8,128)S(1)}, u32[]{:S(2)}) %copy-start.2) | copy-done | bytes 8388632
  134.6 0.5 collective-permute-start.7
  135.1 4.1 %collective-permute-done.7.refs_1_ = f32[2048,256]{1,0:T(8,128)} collective-permute-done((f32[2048,256]{1,0:T(8,128)}, f32[2048,256]{1,0:T(8,128)}, u32[]{:S(2)}, u32[]{:S(2)}) %collective-permute-start.7) | collective-permute-done | bytes 2097184 | tf_op jit(solution)/shard_map/ppermute | solution.py:20
  139.3 1.4 copy-done.1
  140.7 9.6 %y_dft.5.refs_1_ = bf16[4,2048,256]{2,1,0:T(8,128)(2,1)S(1)} custom-call(f32[2,2]{1,0:T(2,128)S(1)} %reshape.51.coef_ref, f32[2048,256]{1,0:T(8,128)} %bitcast.10.refs_0_, f32[2048,256]{1,0:T(8,128)} %collective-permute-done.7.refs_1_, bf16[512,1536]{1,0:T(8,128)(2,1)S(1)} %copy-done.1, f32[2,8,256,128]{3,2,1,0:T(8,128)S(1)} %pad_maximum_fusion.3.refs_5_.refs_3_), custom_call_target="tpu_custom_call" | custom-call | flops 3221225472 | bytes 10485760 | tf_op jit(solution)/shard_map/y_dft/pallas_call | solution.py:157
  150.3 2.3 %copy-done.5 = bf16[2304,1024]{1,0:T(8,128)(2,1)S(1)} copy-done((bf16[2304,1024]{1,0:T(8,128)(2,1)S(1)}, bf16[2304,1024]{1,0:T(8,128)(2,1)}, u32[]{:S(2)}) %copy-start.5) | copy-done | bytes 4718616
  152.6 14.1 %x_last.1 = (f32[2,1,2048,512]{3,2,1,0:T(8,128)}, f32[8,128]{1,0:T(8,128)S(1)}) custom-call(bf16[4,2048,128]{2,1,0:T(8,128)(2,1)S(1)} %copy-done.7, bf16[4,2048,256]{2,1,0:T(8,128)(2,1)S(1)} %y_dft.5.refs_1_, bf16[2304,1024]{1,0:T(8,128)(2,1)S(1)} %copy-done.5, f32[2048,1024]{1,0:T(8,128)S(1)} %copy-done.3, f32[2,4,4,128]{3,2,1,0:T(4,128)S(1)} %pad_maximum_fusion.6.refs_4_, ...), custom_call_target="tpu_custom_call" | custom-call | flops 9663676416 | bytes 25165824 | tf_op jit(solution)/shard_map/x_last/pallas_call | solution.py:242
  166.7 13.3 %all_to_all.23 = f32[32,8,128]{2,1,0:T(8,128)S(1)} all-to-all(f32[32,8,128]{2,1,0:T(8,128)S(1)} %broadcast_in_dim.2), channel_id=1, replica_groups=mesh['gx'=4,'gy'=8] {'gx','gy'}, dimensions={0} | all-to-all | bytes 262144 | tf_op jit(solution)/shard_map/all_to_all | solution.py:274
  180.0 0.6 reduce_sum.29
  (31 shorter events, 0.1 us)
Async XLA Ops:
  4.9 9.0 %copy-start.8 = (f32[512]{0:T(512)S(1)}, f32[512]{0:T(512)}, u32[]{:S(2)}) copy-start(f32[512]{0:T(512)} %param.8) | copy-start | bytes 6148
  4.9 9.7 %copy-start.9 = (f32[2048]{0:T(1024)S(1)}, f32[2048]{0:T(1024)}, u32[]{:S(2)}) copy-start(f32[2048]{0:T(1024)} %param.7) | copy-start | bytes 24580
  5.0 11.7 %copy-start.11 = (f32[512]{0:T(512)S(1)}, f32[512]{0:T(512)}, u32[]{:S(2)}) copy-start(f32[512]{0:T(512)} %param.11) | copy-start | bytes 6148
  5.0 11.7 %copy-start.12 = (f32[512]{0:T(512)S(1)}, f32[512]{0:T(512)}, u32[]{:S(2)}) copy-start(f32[512]{0:T(512)} %param.10) | copy-start | bytes 6148
  5.0 11.7 %copy-start.10 = (f32[2048]{0:T(1024)S(1)}, f32[2048]{0:T(1024)}, u32[]{:S(2)}) copy-start(f32[2048]{0:T(1024)} %param.9) | copy-start | bytes 24580
  5.0 58.7 %all-to-all-start = ((f32[8,256,256]{2,1,0:T(8,128)}), f32[8,256,256]{2,1,0:T(8,128)}, u32[]{:S(2)}, u32[]{:S(2)}) async-start(f32[8,256,256]{2,1,0:T(8,128)} %get-tuple-element.21), calls=%async_computation | async-start | bytes 4194304 | tf_op jit(solution)/shard_map/all_to_all | solution.py:24
  12.4 47.4 %collective-permute-start = (f32[8,256,256]{2,1,0:T(8,128)}, f32[8,256,256]{2,1,0:T(8,128)}, u32[]{:S(2)}, u32[]{:S(2)}) collective-permute-start(f32[8,256,256]{2,1,0:T(8,128)} %get-tuple-element.20), channel_id=1, source_target_pairs={{0,16},{8,24},{16,0},{24,8},{1,17},{9,25},{17,1},{25,9},{2,18},{10... | collective-permute-start | bytes 6291464 | tf_op jit(solution)/shard_map/ppermute | solution.py:20
  63.7 70.9 %all-to-all-start.1 = ((f32[8,256,256]{2,1,0:T(8,128)}), f32[8,256,256]{2,1,0:T(8,128)}, u32[]{:S(2)}, u32[]{:S(2)}) async-start(f32[8,256,256]{2,1,0:T(8,128)} %multiply_add_fusion), calls=%async_computation.1 | async-start | bytes 4194304 | tf_op jit(solution)/shard_map/all_to_all | solution.py:24
  69.4 47.5 %copy-start = (bf16[512,1536]{1,0:T(8,128)(2,1)S(1)}, bf16[512,1536]{1,0:T(8,128)(2,1)}, u32[]{:S(2)}) copy-start(bf16[512,1536]{1,0:T(8,128)(2,1)} %pad_maximum_fusion.4.refs_4_.refs_2_) | copy-start | bytes 4718596
  71.2 26.2 %collective-permute-start.4 = (f32[2048,128]{1,0:T(8,128)S(1)}, f32[2048,128]{1,0:T(8,128)S(1)}, u32[]{:S(2)}, u32[]{:S(2)}) collective-permute-start(f32[2048,128]{1,0:T(8,128)S(1)} %get-tuple-element.42.refs_2_), channel_id=1, source_target_pairs={{0,16},{8,24},{16,0},{24,8},{1,17},{9,25},{17,1},{25,9},{2,18},{10... | collective-permute-start | bytes 3145736 | tf_op jit(solution)/shard_map/ppermute | solution.py:20
  72.8 44.1 %collective-permute-start.1 = (f32[2048,128]{1,0:T(8,128)S(1)}, f32[2048,128]{1,0:T(8,128)S(1)}, u32[]{:S(2)}, u32[]{:S(2)}) collective-permute-start(f32[2048,128]{1,0:T(8,128)S(1)} %get-tuple-element.43.refs_2_), channel_id=1, source_target_pairs={{0,16},{8,24},{16,0},{24,8},{1,17},{9,25},{17,1},{25,9},{2,18},{10... | collective-permute-start | bytes 3145736 | tf_op jit(solution)/shard_map/ppermute | solution.py:20
  73.3 43.6 %collective-permute-start.6 = (f32[2048,128]{1,0:T(8,128)S(1)}, f32[2048,128]{1,0:T(8,128)S(1)}, u32[]{:S(2)}, u32[]{:S(2)}) collective-permute-start(f32[2048,128]{1,0:T(8,128)S(1)} %get-tuple-element.42.refs_2_), channel_id=1, source_target_pairs={{0,8},{8,0},{16,24},{24,16},{1,9},{9,1},{17,25},{25,17},{2,10},{10... | collective-permute-start | bytes 3145736 | tf_op jit(solution)/shard_map/ppermute | solution.py:20
  97.4 19.5 %collective-permute-start.5 = (f32[2048,128]{1,0:T(8,128)S(1)}, f32[2048,128]{1,0:T(8,128)S(1)}, u32[]{:S(2)}, u32[]{:S(2)}) collective-permute-start(f32[2048,128]{1,0:T(8,128)S(1)} %collective-permute-done.4.refs_0_), channel_id=1, source_target_pairs={{0,8},{8,0},{16,24},{24,16},{1,9},{9,1},{17,25},{25,17},{2,10},{10... | collective-permute-start | bytes 3145736 | tf_op jit(solution)/shard_map/ppermute | solution.py:20
  97.4 25.3 %collective-permute-start.3 = (f32[2048,128]{1,0:T(8,128)S(1)}, f32[2048,128]{1,0:T(8,128)S(1)}, u32[]{:S(2)}, u32[]{:S(2)}) collective-permute-start(f32[2048,128]{1,0:T(8,128)S(1)} %get-tuple-element.43.refs_2_), channel_id=1, source_target_pairs={{0,8},{8,0},{16,24},{24,16},{1,9},{9,1},{17,25},{25,17},{2,10},{10... | collective-permute-start | bytes 3145736 | tf_op jit(solution)/shard_map/ppermute | solution.py:20
  116.9 5.8 %collective-permute-start.2 = (f32[2048,128]{1,0:T(8,128)S(1)}, f32[2048,128]{1,0:T(8,128)S(1)}, u32[]{:S(2)}, u32[]{:S(2)}) collective-permute-start(f32[2048,128]{1,0:T(8,128)S(1)} %collective-permute-done.1.refs_0_), channel_id=1, source_target_pairs={{0,8},{8,0},{16,24},{24,16},{1,9},{9,1},{17,25},{25,17},{2,10},{10... | collective-permute-start | bytes 3145736 | tf_op jit(solution)/shard_map/ppermute | solution.py:20
  121.3 1.4 copy-start.6
  122.7 4.4 %copy-start.4 = (bf16[768,1024]{1,0:T(8,128)(2,1)S(1)}, bf16[768,1024]{1,0:T(8,128)(2,1)}, u32[]{:S(2)}) copy-start(bf16[768,1024]{1,0:T(8,128)(2,1)} %pad_maximum_fusion.5.refs_1_) | copy-start | bytes 4718596
  131.2 3.4 %copy-start.2 = (f32[2048,1024]{1,0:T(8,128)}, f32[2048,1024]{1,0:T(8,128)S(1)}, u32[]{:S(2)}) copy-start(f32[2048,1024]{1,0:T(8,128)S(1)} %x_first.1.refs_3_) | copy-start | bytes 25165828
  134.6 4.6 %collective-permute-start.7 = (f32[2048,256]{1,0:T(8,128)}, f32[2048,256]{1,0:T(8,128)}, u32[]{:S(2)}, u32[]{:S(2)}) collective-permute-start(f32[2048,256]{1,0:T(8,128)} %bitcast.10.refs_0_), channel_id=1, source_target_pairs={{0,8},{8,0},{16,24},{24,16},{1,9},{9,1},{17,25},{25,17},{2,10},{10... | collective-permute-start | bytes 6291464 | tf_op jit(solution)/shard_map/ppermute | solution.py:20
  139.3 1.4 copy-start.1
  140.7 9.6 %copy-start.3 = (f32[2048,1024]{1,0:T(8,128)S(1)}, f32[2048,1024]{1,0:T(8,128)}, u32[]{:S(2)}) copy-start(f32[2048,1024]{1,0:T(8,128)} %copy-done.2) | copy-start | bytes 25165828
  140.7 9.6 %copy-start.7 = (bf16[4,2048,128]{2,1,0:T(8,128)(2,1)S(1)}, bf16[4,2048,128]{2,1,0:T(8,128)(2,1)}, u32[]{:S(2)}) copy-start(bf16[4,2048,128]{2,1,0:T(8,128)(2,1)} %copy-done.6) | copy-start | bytes 6291460
  150.3 2.3 %copy-start.5 = (bf16[2304,1024]{1,0:T(8,128)(2,1)S(1)}, bf16[2304,1024]{1,0:T(8,128)(2,1)}, u32[]{:S(2)}) copy-start(bf16[2304,1024]{1,0:T(8,128)(2,1)} %pad_maximum_fusion.refs_2_) | copy-start | bytes 14155780

commit v6 on v4

v6 whole, which is shorter than its diff:
```python
import functools
import math

import jax
import jax.numpy as jnp
from jax import lax
from jax.experimental import pallas as pl
from jax.experimental.pallas import tpu as pltpu
from jax.sharding import PartitionSpec as P

precision_top = lax.Precision.HIGHEST
RADIX = 8
LANES = 128
CUT_BYTES, SMALL_BYTES, Y_BYTES, X_BYTES = [size * 1024 * 1024 for size in (56, 8, 20, 24)]


def from_partner(value, axis, stride):
    mask = 2**stride
    pairs = [(source, source ^ mask) for source in range(lax.axis_size(axis))]
    return lax.ppermute(value, axis, pairs)


def to_planes(values):
    return lax.all_to_all(values, "gy", split_axis=0, concat_axis=1, tiled=True)


def cut_kernel(place, field_ref, *refs):
    out_ref, sem = refs[-2:]
    half = out_ref.shape[2]
    copy = pltpu.make_async_copy(field_ref.at[:, :, pl.ds(place * half, half)], out_ref, sem)
    copy.start()
    copy.wait()


def cut_half(field, place, *earlier):
    planes, rows, columns = field.shape
    anywhere = pl.BlockSpec(memory_space=pl.ANY)
    return pl.pallas_call(
        functools.partial(cut_kernel, place),
        out_shape=jax.ShapeDtypeStruct((planes, rows, columns // 2), jnp.float32),
        in_specs=[anywhere] * (1 + len(earlier)),
        out_specs=anywhere,
        scratch_shapes=[pltpu.SemaphoreType.DMA],
        compiler_params=pltpu.CompilerParams(vmem_limit_bytes=CUT_BYTES),
        cost_estimate=pl.CostEstimate(flops=0, bytes_accessed=4 * field.size, transcendentals=0),
        name="cut_half",
    )(field, *earlier)


def pick_columns(left, right, odd):
    lane = lax.broadcasted_iota(jnp.int32, left.shape, 1)
    index = (2 * lane + odd) % LANES
    chosen = [jnp.take_along_axis(tile, index, axis=1, mode="promise_in_bounds") for tile in (left, right)]
    return jnp.where(lane < LANES // 2, *chosen)


def combine_kernel(sign_ref, late_ref, early_ref, out_ref):
    sign = sign_ref[0]
    left, right = [
        late_ref[0, :, pl.ds(lane, LANES)] + sign * early_ref[0, :, pl.ds(lane, LANES)] for lane in (0, LANES)
    ]
    for odd in range(2):
        out_ref[0, :, pl.ds(odd * LANES, LANES)] = pick_columns(left, right, odd)


def combine(sign, late, early):
    planes, rows, columns = late.shape
    block = pl.BlockSpec((1, rows, columns), lambda i: (i, 0, 0))
    return pl.pallas_call(
        combine_kernel,
        out_shape=jax.ShapeDtypeStruct(late.shape, jnp.float32),
        grid=(planes,),
        in_specs=[pl.BlockSpec(memory_space=pltpu.SMEM), block, block],
        out_specs=block,
        cost_estimate=pl.CostEstimate(flops=2 * late.size, bytes_accessed=12 * late.size, transcendentals=0),
        compiler_params=pltpu.CompilerParams(vmem_limit_bytes=SMALL_BYTES),
        name="combine",
    )(sign, late, early)


def part_kernel(value_ref, *out_refs):
    left, right = [value_ref[:, pl.ds(lane, LANES)] for lane in (0, LANES)]
    for odd, out_ref in enumerate(out_refs):
        out_ref[...] = pick_columns(left, right, odd)


def part_columns(value):
    length, columns = value.shape
    rows = length // 8
    return pl.pallas_call(
        part_kernel,
        out_shape=[jax.ShapeDtypeStruct((length, columns // 2), jnp.float32)] * 2,
        grid=(length // rows,),
        in_specs=[pl.BlockSpec((rows, columns), lambda i: (i, 0))],
        out_specs=[pl.BlockSpec((rows, columns // 2), lambda i: (i, 0))] * 2,
        cost_estimate=pl.CostEstimate(flops=value.size, bytes_accessed=8 * value.size, transcendentals=0),
        compiler_params=pltpu.CompilerParams(vmem_limit_bytes=SMALL_BYTES),
        name="part_columns",
    )(value)


def reverse_bits(value, count):
    result = value * 0
    for place in range(count):
        result = result + (value >> place & 1) * (1 << count - 1 - place)
    return result


def root_table(row_index, freqs, length):
    phase = row_index[:, None] * freqs[None, :] % length
    angle = phase.astype(jnp.float32) * (-2.0 * math.pi / length)
    return (jnp.cos(angle), jnp.sin(angle))


def x_tables(rows, width, devices, position):
    levels = devices.bit_length() - 1
    local_index = jnp.arange(width, dtype=jnp.int32)
    freqs = reverse_bits(position, levels) + devices * local_index
    return root_table(rows, freqs, devices * width)


def split_table(table, axis, order):
    high = lax.reduce_precision(table, 8, 7)
    parts = [high.astype(jnp.bfloat16), (table - high).astype(jnp.bfloat16)]
    return jnp.concatenate([parts[which] for which in order], axis)


def split_value(value):
    high = value.astype(jnp.bfloat16)
    return high, (value - high.astype(jnp.float32)).astype(jnp.bfloat16)


def small_fft(values):
    count = len(values)
    if count == 1:
        return values
    even, odd = small_fft(values[0::2]), small_fft(values[1::2])
    first, second = [], []
    root_half = math.sqrt(0.5)
    for place in range(count // 2):
        (er, ei), (re, im) = even[place], odd[place]
        turn = place * 8 // count
        if turn == 1:
            re, im = (re + im) * root_half, (im - re) * root_half
        elif turn == 2:
            re, im = im, -re
        elif turn == 3:
            re, im = (im - re) * root_half, (re + im) * -root_half
        first.append((er + re, ei + im))
        second.append((er - re, ei - im))
    return first + second


def dot(left, right):
    return jnp.dot(left, right, preferred_element_type=jnp.float32)


def y_kernel(lanes, coef_ref, *refs):
    count = len(lanes)
    inputs, (table_ref, twist_ref, out_ref, mix_ref, split_ref, step_ref) = refs[:count], refs[count:]
    inner = mix_ref.shape[0] // RADIX
    parts = [ref[:, pl.ds(lane, LANES)] for ref, lane in zip(inputs, lanes)]
    for which in range(2):
        mixed = parts[0] * coef_ref[which, 0]
        for place in range(1, count):
            mixed = mixed + parts[place] * coef_ref[which, place]
        mix_ref[...] = mixed
        for s in range(RADIX):
            high, low = split_value(mix_ref[pl.ds(s, inner, stride=RADIX), :])
            for place, value in enumerate((high, high, low)):
                split_ref[pl.ds((2 * place + which) * inner, inner), pl.ds(s * LANES, LANES)] = value
    step_ref[...] = dot(table_ref[...], split_ref[...])
    rows_each = 16

    @pl.loop(0, inner // rows_each, unroll=2)
    def _(block):
        start = pl.multiple_of(block * rows_each, rows_each)
        values = []
        for s in range(RADIX):
            cols = pl.ds(s * LANES, LANES)
            re = step_ref[pl.ds(start, rows_each), cols]
            im = step_ref[pl.ds(pl.multiple_of(start + inner, rows_each), rows_each), cols]
            if s:
                cos, sin = twist_ref[0, s, pl.ds(start, rows_each), :], twist_ref[1, s, pl.ds(start, rows_each), :]
                re, im = re * cos - im * sin, re * sin + im * cos
            values.append((re, im))
        for kb, pair in enumerate(small_fft(values)):
            rows = pl.ds(pl.multiple_of(kb * inner + start, rows_each), rows_each)
            for which in range(2):
                high, low = split_value(pair[which])
                out_ref[2 * which, rows, :] = high
                out_ref[2 * which + 1, rows, :] = low


def y_dft(inputs, coefs, table, twist):
    arrays, lanes = zip(*inputs)
    length = arrays[0].shape[0]
    inner = length // RADIX
    whole = pl.BlockSpec(memory_space=pltpu.VMEM)
    return pl.pallas_call(
        functools.partial(y_kernel, lanes),
        out_shape=jax.ShapeDtypeStruct((4, length, LANES), jnp.bfloat16),
        in_specs=[pl.BlockSpec(memory_space=pltpu.SMEM)] + [whole] * (len(arrays) + 2),
        out_specs=whole,
        scratch_shapes=[
            pltpu.VMEM((length, LANES), jnp.float32),
            pltpu.VMEM((6 * inner, RADIX * LANES), jnp.bfloat16),
            pltpu.VMEM((2 * inner, RADIX * LANES), jnp.float32),
        ],
        compiler_params=pltpu.CompilerParams(vmem_limit_bytes=Y_BYTES),
        cost_estimate=pl.CostEstimate(
            flops=24 * inner * length * LANES, bytes_accessed=4 * length * LANES * (len(arrays) + 3), transcendentals=0
        ),
        name="y_dft",
    )(coefs, *arrays, table, twist)


def x_product(parts, table_ref):
    high = [ref[which] for ref in parts for which in (0, 2)]
    low = [ref[which] for ref in parts for which in (1, 3)]
    return dot(jnp.concatenate(high + low + high, axis=1), table_ref[...])


def x_kernel(count, *refs):
    parts, (even_ref, odd_ref, row_ref, col_ref, out_ref, total_ref) = refs[: 2 * count], refs[2 * count :]
    even, odd = x_product(parts[:count], even_ref), x_product(parts[count:], odd_ref)
    half = even.shape[1] // 2
    lanes = LANES
    row_scale, row_rate = [
        jnp.concatenate(
            [jnp.broadcast_to(row_ref[which, 0, c : c + 1, :], (lanes, lanes)).T for c in range(row_ref.shape[2])], 0
        )
        for which in range(2)
    ]
    total = None
    for tile in range(half // lanes):
        real, imag = [slice(start, start + lanes) for start in (tile * lanes, half + tile * lanes)]
        for upper in range(2):
            cols = pl.ds(upper * half + tile * lanes, lanes)
            spec_real = even[:, real] - odd[:, real] if upper else even[:, real] + odd[:, real]
            spec_imag = even[:, imag] - odd[:, imag] if upper else even[:, imag] + odd[:, imag]
            col_scale, col_shift, col_mix = col_ref[0:1, cols], col_ref[1:2, cols], col_ref[2:3, cols]
            scale = row_scale * col_scale
            latent_u = spec_real * scale
            latent_v = spec_imag * scale
            log_scale = row_rate * jnp.tanh(latent_u + col_shift)
            latent_w = latent_v * jnp.exp(log_scale) + col_mix * latent_u
            out_ref[0, 0, :, cols] = latent_u
            out_ref[1, 0, :, cols] = latent_w
            terms = log_scale - 0.5 * (latent_u * latent_u + latent_w * latent_w)
            terms = jnp.sum(terms.reshape(-1, 8, lanes), axis=0)
            total = terms if total is None else total + terms

    @pl.when(pl.program_id(0) == 0)
    def _():
        total_ref[...] = jnp.zeros_like(total_ref)

    total_ref[...] += total


def x_dft(even_parts, odd_parts, even_table, odd_table, row_pair, col_trio):
    parts, count, length = even_parts + odd_parts, len(even_parts), even_parts[0].shape[1]
    columns = even_table.shape[1]
    rows = length // row_pair.shape[1]
    fixed = [pl.BlockSpec(table.shape, lambda i: (0, 0), pipeline_mode=pl.Buffered(1)) for table in (even_table, odd_table)]
    return pl.pallas_call(
        functools.partial(x_kernel, count),
        out_shape=(
            jax.ShapeDtypeStruct((2, 1, length, columns), jnp.float32),
            jax.ShapeDtypeStruct((8, LANES), jnp.float32),
        ),
        grid=(length // rows,),
        in_specs=[pl.BlockSpec((4, rows, part.shape[2]), lambda i: (0, i, 0)) for part in parts]
        + fixed
        + [
            pl.BlockSpec((2, 1, rows // LANES, LANES), lambda i: (0, i, 0, 0)),
            pl.BlockSpec(col_trio.shape, lambda i: (0, 0)),
        ],
        out_specs=(
            pl.BlockSpec((2, 1, rows, columns), lambda i: (0, 0, i, 0)),
            pl.BlockSpec((8, LANES), lambda i: (0, 0)),
        ),
        compiler_params=pltpu.CompilerParams(vmem_limit_bytes=X_BYTES),
        cost_estimate=pl.CostEstimate(
            flops=4 * length * even_table.size,
            bytes_accessed=16 * length * columns,
            transcendentals=2 * length * columns,
        ),
        name="x_dft",
    )(*parts, even_table, odd_table, row_pair, col_trio)


def sum_everywhere(tile):
    axes = ("gx", "gy")
    devices = lax.axis_size("gx") * lax.axis_size("gy")
    copies = jnp.broadcast_to(tile[None], (devices,) + tile.shape)
    return jnp.sum(lax.all_to_all(copies, axes, split_axis=0, concat_axis=0, tiled=True))


def four_way(field, row_scale, col_scale, row_rate, col_shift, col_mix):
    position = lax.axis_index("gx")
    planes, rows, columns = field.shape
    length, width = planes * rows, columns // 4
    field_a = cut_half(field, 0)
    field_b = cut_half(field, 1, field_a)
    sign = jnp.where(position < 2, 1.0, -1.0)

    own_real = jnp.where(position == 1, -1.0, jnp.where(position == 3, 0.0, 1.0))
    other_real = jnp.where(position == 2, 0.0, 1.0)
    own_imag = jnp.where(position == 3, 1.0, 0.0)
    other_imag = jnp.where(position == 2, -1.0, 0.0)
    coefs_a = jnp.stack([own_real, other_real, own_imag, other_imag]).reshape(2, 2)
    coefs_b = jnp.concatenate([coefs_a, coefs_a * sign], axis=1)

    inner = length // RADIX
    index = jnp.arange(inner, dtype=jnp.int32)
    cos, sin = root_table(index, index, inner)
    y_table = jnp.concatenate([jnp.concatenate([cos, -sin], 1), jnp.concatenate([sin, cos], 1)], 0)
    y_table = split_table(y_table, 1, (0, 1, 0))
    grid = [lax.broadcasted_iota(jnp.int32, (RADIX, inner, LANES), axis) for axis in range(2)]
    angle = (grid[0] * grid[1]).astype(jnp.float32) * (-2.0 * math.pi / length)
    twist = jnp.stack([jnp.cos(angle), jnp.sin(angle)])
    order = jnp.arange(width, dtype=jnp.int32) * 2

    def x_table(odd):
        rows = jnp.concatenate([order + (2 * width + odd), order + odd])
        cos, sin = [part[:, : 2 * width].reshape(2, width, 2 * width) for part in x_tables(rows, columns, 4, position)]
        table = jnp.stack([jnp.concatenate([cos, sin], 2), jnp.concatenate([-sin, cos], 2)], 1)
        return split_table(table.reshape(columns, columns), 0, (0, 0, 1))

    norm = 1.0 / math.sqrt(length * columns * 4)
    row_pair = jnp.stack([row_scale * norm, row_rate]).reshape(2, 4, length // 4 // LANES, LANES)
    col_trio = jnp.stack([col_scale, col_shift, col_mix])
    fixed = 2.0 * (columns * jnp.sum(jnp.log(row_scale)) + length * jnp.sum(jnp.log(col_scale)))
    fixed = fixed - length * columns * math.log(2.0 * math.pi)

    first_a = combine(sign.reshape(1), from_partner(field_a, "gx", 1), field_a)
    tables = (y_table, twist, x_table(0), x_table(1), row_pair, col_trio)
    state = lax.optimization_barrier((first_a, to_planes(field_b)[0], tables, coefs_a, coefs_b, fixed))
    first_a, first_b, (y_table, twist, even_table, odd_table, row_pair, col_trio), coefs_a, coefs_b, fixed = state
    second_a = to_planes(first_a)[0]

    def y_part_b(early, late):
        group = [late, from_partner(late, "gx", 0), early, from_partner(early, "gx", 0)]
        return y_dft([(value, 0) for value in group], coefs_b, y_table, twist)

    early_b = part_columns(first_b)
    late_b = [from_partner(value, "gx", 1) for value in early_b]
    even_b = y_part_b(early_b[0], late_b[0])
    even_b, late_b[1] = lax.optimization_barrier((even_b, late_b[1]))
    odd_b = y_part_b(early_b[1], late_b[1])
    group = [second_a, from_partner(second_a, "gx", 0)]
    even_a, odd_a = [y_dft([(value, lane) for value in group], coefs_a, y_table, twist) for lane in (0, width)]
    latent, tile = x_dft([even_b, even_a], [odd_b, odd_a], even_table, odd_table, row_pair, col_trio)
    tile = tile + fixed / tile.size
    modes = length * columns * lax.axis_size("gx") * lax.axis_size("gy")
    return (latent, sum_everywhere(tile) / modes)


def complex_einsum(form, real_part, imag_part, cos_part, sin_part):
    first = jnp.einsum(form, real_part, cos_part, precision=precision_top)
    second = jnp.einsum(form, real_part, sin_part, precision=precision_top)
    first = first - jnp.einsum(form, imag_part, sin_part, precision=precision_top)
    second = second + jnp.einsum(form, imag_part, cos_part, precision=precision_top)
    return (first, second)


def x_butterfly(field):
    devices = lax.axis_size("gx")
    levels = devices.bit_length() - 1
    position = lax.axis_index("gx")
    real_part, imag_part = field, jnp.zeros_like(field)
    for level in range(levels - 1, -1, -1):
        half = 1 << level
        lower = position // half % 2 == 0
        offset = position % half
        angle = offset.astype(jnp.float32) * (-math.pi / half)
        cos_twist = jnp.where(lower, 1.0, jnp.cos(angle))
        sin_twist = jnp.where(lower, 0.0, jnp.sin(angle))
        other = from_partner(jnp.stack([real_part, imag_part]), "gx", level)
        diff_real = jnp.where(lower, real_part + other[0], other[0] - real_part)
        diff_imag = jnp.where(lower, imag_part + other[1], other[1] - imag_part)
        real_part = diff_real * cos_twist - diff_imag * sin_twist
        imag_part = diff_real * sin_twist + diff_imag * cos_twist
    width = field.shape[2]
    cos_part, sin_part = x_tables(jnp.arange(width, dtype=jnp.int32), width, devices, position)
    real_part, imag_part = complex_einsum("zyn,nk->zyk", real_part, imag_part, cos_part, sin_part)
    return (to_planes(real_part), to_planes(imag_part))


def y_transform(real_part, imag_part):
    planes, length, width = real_part.shape
    outer = 1 << (length.bit_length() - 1) // 2
    inner = length // outer
    outer_index = jnp.arange(outer, dtype=jnp.int32)
    inner_index = jnp.arange(inner, dtype=jnp.int32)
    cos_one, sin_one = root_table(outer_index, outer_index, outer)
    cos_two, sin_two = root_table(inner_index, inner_index, inner)
    cos_mid, sin_mid = root_table(outer_index, inner_index, length)
    shaped_real = real_part.reshape(planes, outer, inner, width)
    shaped_imag = imag_part.reshape(planes, outer, inner, width)
    step_real, step_imag = complex_einsum("zabc,ak->zkbc", shaped_real, shaped_imag, cos_one, sin_one)
    twist_cos = cos_mid[None, :, :, None]
    twist_sin = sin_mid[None, :, :, None]
    turned_real = step_real * twist_cos - step_imag * twist_sin
    turned_imag = step_real * twist_sin + step_imag * twist_cos
    final_real, final_imag = complex_einsum("zkbc,bj->zjkc", turned_real, turned_imag, cos_two, sin_two)
    return (final_real.reshape(planes, length, width), final_imag.reshape(planes, length, width))


def any_way(field, row_scale, col_scale, row_rate, col_shift, col_mix):
    spec_real, spec_imag = y_transform(*x_butterfly(field))
    length = spec_real.shape[1]
    total_cols = spec_real.shape[2] * lax.axis_size("gx")
    norm_factor = 1.0 / math.sqrt(length * total_cols)
    scale = row_scale[None, :, None] * col_scale[None, None, :]
    latent_u = spec_real * norm_factor * scale
    latent_v = spec_imag * norm_factor * scale
    log_scale = row_rate[None, :, None] * jnp.tanh(latent_u + col_shift[None, None, :])
    latent_w = latent_v * jnp.exp(log_scale) + col_mix[None, None, :] * latent_u
    terms = (
        -0.5 * (latent_u * latent_u + latent_w * latent_w)
        - math.log(2.0 * math.pi)
        + log_scale
        + 2.0 * jnp.log(scale)
    )
    mode_count = spec_real.size * lax.axis_size("gx") * lax.axis_size("gy")
    loglik = lax.psum(jnp.sum(terms), ("gx", "gy")) / mode_count
    return (jnp.stack([latent_u, latent_w]), loglik)


def per_device(field, *scales):
    return (four_way if lax.axis_size("gx") == 4 else any_way)(field, *scales)


def solution(mesh):
    return jax.shard_map(
        per_device,
        mesh=mesh,
        in_specs=(P(None, "gy", "gx"), P(), P("gx"), P(), P("gx"), P("gx")),
        out_specs=(P(None, "gy", None, "gx"), P()),
        check_vma=False,
    )
```

time: 193 us -> 295 us (1.53)
  Pallas kernels: 38.2 us -> 174 us
  other arithmetic: 29.1 us -> 12.7 us
  local copies, waits for them, and re-layouts: 23.7 us -> 7.52 us
  waiting for transfers between devices: 62.1 us -> 69.9 us
  starting transfers between devices: 21.9 us -> 14.9 us
    pallas_call x5 -> x9, Pallas kernels: 38.2 us -> 174 us  [the longest x2 129 us: cut_half(): pl.pallas_call(functools.partial(cut_kernel, place), out_shape=jax.ShapeD...]
    all_to_all x3 -> x2, waiting for transfers between devices: 0.01 us -> 43.2 us  [to_planes(): return lax.all_to_all(values, 'gy', split_axis=0, concat_axis=1, tiled=True)]
    ppermute x6 -> x8, waiting for transfers between devices: 62.1 us -> 26.7 us  [from_partner(): return lax.ppermute(value, axis, pairs)]
    unnamed x50 -> x26, local copies, waits for them, and re-layouts: 17.5 us -> 5.49 us
    all_to_all x3 -> x2, starting transfers between devices: 18.4 us -> 10.3 us  [to_planes(): return lax.all_to_all(values, 'gy', split_axis=0, concat_axis=1, tiled=True)]
    convert_element_type x4 -> x3, other arithmetic: 7.67 us -> 0.43 us  [split_table(): parts = [high.astype(jnp.bfloat16), (table - high).astype(jnp.bfloat16)]]
    slice x2 -> x0, local copies, waits for them, and re-layouts: 6.1 us -> none  [the longest x1 3.05 us: four_way(): field_a = field_rest[:, :, :2 * width]]
    sin x2 -> x1, other arithmetic: 5.16 us -> 1.03 us  [root_table(): return (jnp.cos(angle), jnp.sin(angle))]
  transfers between devices with their start and end apart: 9 -> 10, of which waited for: 4 -> 4; matrix products, arithmetic and copies ran while one was open for 16% -> 5% of each run, Pallas kernels for 10% -> 30%
where the time goes in v6:
time: 295 us
  Pallas kernels  174 us (59%)
  waiting for transfers between devices  69.9 us (24%)
  starting transfers between devices  14.9 us (5%)
  other arithmetic  12.7 us (4%)
  blocking collectives  11.3 us (4%)
  local copies, waits for them, and re-layouts  7.52 us (3%)
  between operations  4.14 us (1%)
    pallas_call x2, Pallas kernels, cut_half(): pl.pallas_call(functools.partial(cut_kernel, place), out_shape=jax.ShapeD...  129 us
    all_to_all x2, waiting for transfers between devices, to_planes(): return lax.all_to_all(values, 'gy', split_axis=0, concat_axis=1, tiled=True)  43.2 us
    ppermute x8, waiting for transfers between devices, from_partner(): return lax.ppermute(value, axis, pairs)  26.7 us
    pallas_call x4, Pallas kernels, y_dft(): pl.pallas_call(functools.partial(y_kernel, lanes), out_shape=jax.ShapeDty...  22.9 us
    pallas_call x1, Pallas kernels, x_dft(): pl.pallas_call(functools.partial(x_kernel, count), out_shape=(jax.ShapeDt...  11.4 us
    all_to_all x1, blocking collectives, sum_everywhere(): lax.all_to_all(copies, axes, split_axis=0, concat_axis=0, tiled=True)  11.3 us
    all_to_all x2, starting transfers between devices, to_planes(): return lax.all_to_all(values, 'gy', split_axis=0, concat_axis=1, tiled=True)  10.3 us
    pallas_call x1, Pallas kernels, part_columns(): pl.pallas_call(part_kernel, out_shape=[jax.ShapeDtypeStruct((length, colu...  5.91 us
  transfers between devices with their start and end apart: 10, of which 4 were waited for; matrix products, arithmetic and copies ran while one was open for 5% of the time, Pallas kernels for 30%

profile of v6, /device:TPU:0, one launch (start us, length us, event | category | flops | bytes accessed | tf_op | source)
XLA Modules:
  0.0 294.8 jit_solution(34756493868271333)
XLA Ops:
  0.6 64.6 %cut_half.2.early_ref.refs_0_ = f32[8,256,256]{2,1,0:T(8,128)} custom-call(f32[8,256,512]{2,1,0:T(8,128)} %field_ref.3), custom_call_target="tpu_custom_call" | custom-call | bytes 4194304 | tf_op jit(solution)/shard_map/cut_half/pallas_call | solution.py:38
  65.3 3.0 %collective-permute-start = (f32[8,256,256]{2,1,0:T(8,128)}, f32[8,256,256]{2,1,0:T(8,128)}, u32[]{:S(2)}, u32[]{:S(2)}) collective-permute-start(f32[8,256,256]{2,1,0:T(8,128)} %cut_half.2.early_ref.refs_0_), channel_id=1, source_target_pairs={{0,16},{8,24},{16,0},{24,8},{1,17},{9,25},{17,1},{25,9},{2,18},{10... | collective-permute-start | bytes 6291464 | tf_op jit(solution)/shard_map/ppermute | solution.py:20
  68.3 64.6 %cut_half.3 = f32[8,256,256]{2,1,0:T(8,128)} custom-call(f32[8,256,512]{2,1,0:T(8,128)} %field_ref.3, f32[8,256,256]{2,1,0:T(8,128)} %cut_half.2.early_ref.refs_0_), custom_call_target="tpu_custom_call" | custom-call | bytes 4194304 | tf_op jit(solution)/shard_map/cut_half/pallas_call | solution.py:38
  133.0 5.8 %all-to-all-start = ((f32[8,256,256]{2,1,0:T(8,128)}), f32[8,256,256]{2,1,0:T(8,128)}, u32[]{:S(2)}, u32[]{:S(2)}) async-start(f32[8,256,256]{2,1,0:T(8,128)} %cut_half.3), calls=%async_computation | async-start | bytes 4194304 | tf_op jit(solution)/shard_map/all_to_all | solution.py:24
  138.8 0.0 copy-start.9
  138.9 0.5 fusion.8
  139.4 1.0 slice_sine_fusion
  140.4 1.0 slice_sine_fusion.1
  141.4 0.1 pad_maximum_fusion.9
  141.5 0.1 reshape.81.coef_ref
  141.6 0.6 log_reduce_fusion.1
  142.9 0.6 log_reduce_fusion
  144.2 1.0 fusion.19
  145.2 1.0 fusion.17
  146.3 0.1 maximum_bitcast_fusion.2
  146.4 0.1 pad_maximum_fusion.5
  146.5 0.1 maximum_bitcast_fusion
  146.6 0.1 pad_maximum_fusion.8.coef_ref
  146.6 0.1 pad_maximum_fusion.4
  146.7 0.2 fusion
  146.9 3.2 %fusion.3 = (f32[1,8,256,128]{3,2,1,0:T(8,128)S(1)}, f32[1,8,256,128]{3,2,1,0:T(8,128)S(1)}) fusion(), kind=kLoop, calls=%fused_computation.17 | loop fusion | flops 786432 | bytes 2097152 | tf_op jit(solution)/shard_map/sin | solution.py:322
  150.1 0.1 pad_maximum_fusion.refs_5_.refs_3_
  150.3 0.1 reduce-precision_convert_fusion
  150.4 0.1 reduce-precision_convert_fusion.1
  150.5 1.3 pad_maximum_fusion.1.refs_4_.refs_2_
  151.8 1.4 pad_maximum_fusion.3.refs_5_
  153.2 1.3 pad_maximum_fusion.2.refs_4_
  154.4 5.0 %combine.1 = f32[8,256,256]{2,1,0:T(8,128)S(1)} custom-call(f32[1]{0:T(128)} %bitcast.sign_ref, f32[8,256,256]{2,1,0:T(8,128)} %collective-permute-done.late_ref, f32[8,256,256]{2,1,0:T(8,128)S(1)} %copy-done.2), custom_call_target="tpu_custom_call" | custom-call | flops 1048576 | bytes 6291456 | tf_op jit(solution)/shard_map/combine/pallas_call | solution.py:69
  159.4 1.3 copy-done.3
  160.8 26.1 %all-to-all-done = f32[8,256,256]{2,1,0:T(8,128)} async-done(((f32[8,256,256]{2,1,0:T(8,128)}), f32[8,256,256]{2,1,0:T(8,128)}, u32[]{:S(2)}, u32[]{:S(2)}) %all-to-all-start) | async-done | bytes 2097184 | tf_op jit(solution)/shard_map/all_to_all | solution.py:24
  186.8 4.5 %all-to-all-start.1 = ((f32[8,256,256]{2,1,0:T(8,128)}), f32[8,256,256]{2,1,0:T(8,128)}, u32[]{:S(2)}, u32[]{:S(2)}) async-start(f32[8,256,256]{2,1,0:T(8,128)} %copy-done.3), calls=%async_computation.1 | async-start | bytes 4194304 | tf_op jit(solution)/shard_map/all_to_all | solution.py:24
  191.4 5.9 %part_columns.1 = (f32[2048,128]{1,0:T(8,128)}, f32[2048,128]{1,0:T(8,128)S(1)}) custom-call(f32[2048,256]{1,0:T(8,128)} %bitcast.1.value_ref), custom_call_target="tpu_custom_call" | custom-call | flops 524288 | bytes 4194304 | tf_op jit(solution)/shard_map/part_columns/pallas_call | solution.py:90
  197.3 0.5 collective-permute-start.1
  197.8 23.7 %collective-permute-done.1.refs_0_ = f32[2048,128]{1,0:T(8,128)} collective-permute-done((f32[2048,128]{1,0:T(8,128)}, f32[2048,128]{1,0:T(8,128)}, u32[]{:S(2)}, u32[]{:S(2)}) %collective-permute-start.1) | collective-permute-done | bytes 1048608 | tf_op jit(solution)/shard_map/ppermute | solution.py:20
  221.5 0.5 collective-permute-start.4
  222.0 17.1 %all-to-all-done.1 = f32[8,256,256]{2,1,0:T(8,128)} async-done(((f32[8,256,256]{2,1,0:T(8,128)}), f32[8,256,256]{2,1,0:T(8,128)}, u32[]{:S(2)}, u32[]{:S(2)}) %all-to-all-start.1) | async-done | bytes 2097184 | tf_op jit(solution)/shard_map/all_to_all | solution.py:24
  239.1 0.5 collective-permute-start.7
  239.6 1.4 copy-done
  241.0 5.9 %y_dft.4.refs_0_ = bf16[4,2048,128]{2,1,0:T(8,128)(2,1)S(1)} custom-call(f32[2,4]{1,0:T(2,128)S(1)} %pad_maximum_fusion.8.coef_ref, f32[2048,128]{1,0:T(8,128)} %collective-permute-done.1.refs_0_, f32[2048,128]{1,0:T(8,128)} %collective-permute-done.2.refs_1_, f32[2048,128]{1,0:T(8,128)} %get-tuple-element.21.refs_2_, ...), custom_call_target="tpu_custom_call" | custom-call | flops 1610612736 | bytes 7340032 | tf_op jit(solution)/shard_map/y_dft/pallas_call | solution.py:200
  246.9 1.3 copy-done.4
  248.3 3.0 %collective-permute-done.6.refs_1_ = f32[2048,128]{1,0:T(8,128)} collective-permute-done((f32[2048,128]{1,0:T(8,128)}, f32[2048,128]{1,0:T(8,128)}, u32[]{:S(2)}, u32[]{:S(2)}) %collective-permute-start.6) | collective-permute-done | bytes 1048608 | tf_op jit(solution)/shard_map/ppermute | solution.py:20
  251.2 1.4 copy-done.1
  252.7 5.6 %y_dft.6.refs_2_ = bf16[4,2048,128]{2,1,0:T(8,128)(2,1)S(1)} custom-call(f32[2,4]{1,0:T(2,128)S(1)} %pad_maximum_fusion.8.coef_ref, f32[2048,128]{1,0:T(8,128)} %collective-permute-done.4.refs_0_, f32[2048,128]{1,0:T(8,128)} %collective-permute-done.6.refs_1_, f32[2048,128]{1,0:T(8,128)S(1)} %get-tuple-element.24.refs_2_, ...), custom_call_target="tpu_custom_call" | custom-call | flops 1610612736 | bytes 7340032 | tf_op jit(solution)/shard_map/y_dft/pallas_call | solution.py:200
  258.3 5.6 %y_dft.7.refs_3_ = bf16[4,2048,128]{2,1,0:T(8,128)(2,1)S(1)} custom-call(f32[2,2]{1,0:T(2,128)S(1)} %reshape.81.coef_ref, f32[2048,256]{1,0:T(8,128)} %bitcast.23.refs_0_, f32[2048,256]{1,0:T(8,128)} %collective-permute-done.5.refs_1_, bf16[512,1536]{1,0:T(8,128)(2,1)S(1)} %copy-done.1, f32[2,8,256,128]{3,2,1,0:T(8,128)S(1)} %pad_maximum_fusion.refs_5_.refs_3_), custom_call_target="tpu_custom_call" | custom-call | flops 1610612736 | bytes 5242880 | tf_op jit(solution)/shard_map/y_dft/pallas_call | solution.py:200
  263.9 5.8 %y_dft.5.refs_1_ = bf16[4,2048,128]{2,1,0:T(8,128)(2,1)S(1)} custom-call(f32[2,2]{1,0:T(2,128)S(1)} %reshape.81.coef_ref, f32[2048,256]{1,0:T(8,128)} %bitcast.23.refs_0_, f32[2048,256]{1,0:T(8,128)} %collective-permute-done.5.refs_1_, bf16[512,1536]{1,0:T(8,128)(2,1)S(1)} %copy-done.1, f32[2,8,256,128]{3,2,1,0:T(8,128)S(1)} %pad_maximum_fusion.refs_5_.refs_3_), custom_call_target="tpu_custom_call" | custom-call | flops 1610612736 | bytes 5242880 | tf_op jit(solution)/shard_map/y_dft/pallas_call | solution.py:200
  269.7 11.4 %x_dft.1 = (f32[2,1,2048,512]{3,2,1,0:T(8,128)}, f32[8,128]{1,0:T(8,128)S(1)}) custom-call(bf16[4,2048,128]{2,1,0:T(8,128)(2,1)S(1)} %copy-done.5, bf16[4,2048,128]{2,1,0:T(8,128)(2,1)S(1)} %y_dft.5.refs_1_, bf16[4,2048,128]{2,1,0:T(8,128)(2,1)S(1)} %y_dft.6.refs_2_, bf16[4,2048,128]{2,1,0:T(8,128)(2,1)S(1)} %y_dft.7.refs_3_, ...), custom_call_target="tpu_custom_call" | custom-call | flops 6442450944 | bytes 16777216 | tf_op jit(solution)/shard_map/x_dft/pallas_call | solution.py:266
  281.1 11.3 %all_to_all.23 = f32[32,8,128]{2,1,0:T(8,128)S(1)} all-to-all(f32[32,8,128]{2,1,0:T(8,128)S(1)} %broadcast_in_dim.2), channel_id=1, replica_groups=mesh['gx'=4,'gy'=8] {'gx','gy'}, dimensions={0} | all-to-all | bytes 262144 | tf_op jit(solution)/shard_map/all_to_all | solution.py:297
  292.4 0.6 reduce_sum.29
  (43 shorter events, 0.2 us)
Async XLA Ops:
  65.3 89.2 %collective-permute-start = (f32[8,256,256]{2,1,0:T(8,128)}, f32[8,256,256]{2,1,0:T(8,128)}, u32[]{:S(2)}, u32[]{:S(2)}) collective-permute-start(f32[8,256,256]{2,1,0:T(8,128)} %cut_half.2.early_ref.refs_0_), channel_id=1, source_target_pairs={{0,16},{8,24},{16,0},{24,8},{1,17},{9,25},{17,1},{25,9},{2,18},{10... | collective-permute-start | bytes 6291464 | tf_op jit(solution)/shard_map/ppermute | solution.py:20
  133.0 53.9 %all-to-all-start = ((f32[8,256,256]{2,1,0:T(8,128)}), f32[8,256,256]{2,1,0:T(8,128)}, u32[]{:S(2)}, u32[]{:S(2)}) async-start(f32[8,256,256]{2,1,0:T(8,128)} %cut_half.3), calls=%async_computation | async-start | bytes 4194304 | tf_op jit(solution)/shard_map/all_to_all | solution.py:24
  138.8 2.9 copy-start.8
  138.8 4.1 %copy-start.9 = (f32[2048]{0:T(1024)S(1)}, f32[2048]{0:T(1024)}, u32[]{:S(2)}) copy-start(f32[2048]{0:T(1024)} %param.7) | copy-start | bytes 24580
  138.8 5.4 %copy-start.11 = (f32[512]{0:T(512)S(1)}, f32[512]{0:T(512)}, u32[]{:S(2)}) copy-start(f32[512]{0:T(512)} %param.11) | copy-start | bytes 6148
  138.8 5.4 %copy-start.12 = (f32[512]{0:T(512)S(1)}, f32[512]{0:T(512)}, u32[]{:S(2)}) copy-start(f32[512]{0:T(512)} %param.10) | copy-start | bytes 6148
  138.8 5.4 %copy-start.10 = (f32[2048]{0:T(1024)S(1)}, f32[2048]{0:T(1024)}, u32[]{:S(2)}) copy-start(f32[2048]{0:T(1024)} %param.9) | copy-start | bytes 24580
  151.8 2.6 copy-start.2
  159.4 1.3 copy-start.3
  186.8 52.3 %all-to-all-start.1 = ((f32[8,256,256]{2,1,0:T(8,128)}), f32[8,256,256]{2,1,0:T(8,128)}, u32[]{:S(2)}, u32[]{:S(2)}) async-start(f32[8,256,256]{2,1,0:T(8,128)} %copy-done.3), calls=%async_computation.1 | async-start | bytes 4194304 | tf_op jit(solution)/shard_map/all_to_all | solution.py:24
  197.3 24.2 %collective-permute-start.1 = (f32[2048,128]{1,0:T(8,128)}, f32[2048,128]{1,0:T(8,128)}, u32[]{:S(2)}, u32[]{:S(2)}) collective-permute-start(f32[2048,128]{1,0:T(8,128)} %get-tuple-element.21.refs_2_), channel_id=1, source_target_pairs={{0,16},{8,24},{16,0},{24,8},{1,17},{9,25},{17,1},{25,9},{2,18},{10... | collective-permute-start | bytes 3145736 | tf_op jit(solution)/shard_map/ppermute | solution.py:20
  197.8 41.8 %collective-permute-start.3 = (f32[2048,128]{1,0:T(8,128)}, f32[2048,128]{1,0:T(8,128)}, u32[]{:S(2)}, u32[]{:S(2)}) collective-permute-start(f32[2048,128]{1,0:T(8,128)} %get-tuple-element.21.refs_2_), channel_id=1, source_target_pairs={{0,8},{8,0},{16,24},{24,16},{1,9},{9,1},{17,25},{25,17},{2,10},{10... | collective-permute-start | bytes 3145736 | tf_op jit(solution)/shard_map/ppermute | solution.py:20
  221.5 18.1 %collective-permute-start.2 = (f32[2048,128]{1,0:T(8,128)}, f32[2048,128]{1,0:T(8,128)}, u32[]{:S(2)}, u32[]{:S(2)}) collective-permute-start(f32[2048,128]{1,0:T(8,128)} %collective-permute-done.1.refs_0_), channel_id=1, source_target_pairs={{0,8},{8,0},{16,24},{24,16},{1,9},{9,1},{17,25},{25,17},{2,10},{10... | collective-permute-start | bytes 3145736 | tf_op jit(solution)/shard_map/ppermute | solution.py:20
  221.5 26.7 %collective-permute-start.4 = (f32[2048,128]{1,0:T(8,128)S(1)}, f32[2048,128]{1,0:T(8,128)}, u32[]{:S(2)}, u32[]{:S(2)}) collective-permute-start(f32[2048,128]{1,0:T(8,128)S(1)} %get-tuple-element.24.refs_2_), channel_id=1, source_target_pairs={{0,16},{8,24},{16,0},{24,8},{1,17},{9,25},{17,1},{25,9},{2,18},{10... | collective-permute-start | bytes 3145736 | tf_op jit(solution)/shard_map/ppermute | solution.py:20
  239.1 19.2 %collective-permute-start.5 = (f32[2048,256]{1,0:T(8,128)}, f32[2048,256]{1,0:T(8,128)}, u32[]{:S(2)}, u32[]{:S(2)}) collective-permute-start(f32[2048,256]{1,0:T(8,128)} %bitcast.23.refs_0_), channel_id=1, source_target_pairs={{0,8},{8,0},{16,24},{24,16},{1,9},{9,1},{17,25},{25,17},{2,10},{10... | collective-permute-start | bytes 6291464 | tf_op jit(solution)/shard_map/ppermute | solution.py:20
  239.1 9.1 %collective-permute-start.7 = (f32[2048,128]{1,0:T(8,128)S(1)}, f32[2048,128]{1,0:T(8,128)}, u32[]{:S(2)}, u32[]{:S(2)}) collective-permute-start(f32[2048,128]{1,0:T(8,128)S(1)} %get-tuple-element.24.refs_2_), channel_id=1, source_target_pairs={{0,8},{8,0},{16,24},{24,16},{1,9},{9,1},{17,25},{25,17},{2,10},{10... | collective-permute-start | bytes 3145736 | tf_op jit(solution)/shard_map/ppermute | solution.py:20
  239.6 1.4 copy-start
  246.9 1.3 copy-start.4
  248.2 3.0 %collective-permute-start.6 = (f32[2048,128]{1,0:T(8,128)}, f32[2048,128]{1,0:T(8,128)}, u32[]{:S(2)}, u32[]{:S(2)}) collective-permute-start(f32[2048,128]{1,0:T(8,128)} %collective-permute-done.4.refs_0_), channel_id=1, source_target_pairs={{0,8},{8,0},{16,24},{24,16},{1,9},{9,1},{17,25},{25,17},{2,10},{10... | collective-permute-start | bytes 3145736 | tf_op jit(solution)/shard_map/ppermute | solution.py:20
  251.2 1.4 copy-start.1
  263.9 5.8 %copy-start.5 = (bf16[4,2048,128]{2,1,0:T(8,128)(2,1)S(1)}, bf16[4,2048,128]{2,1,0:T(8,128)(2,1)}, u32[]{:S(2)}) copy-start(bf16[4,2048,128]{2,1,0:T(8,128)(2,1)} %copy-done.4) | copy-start | bytes 6291460
  263.9 5.8 %copy-start.6 = (bf16[1536,512]{1,0:T(8,128)(2,1)S(1)}, bf16[1536,512]{1,0:T(8,128)(2,1)}, u32[]{:S(2)}) copy-start(bf16[1536,512]{1,0:T(8,128)(2,1)} %pad_maximum_fusion.3.refs_5_) | copy-start | bytes 4718596
  263.9 5.8 %copy-start.7 = (bf16[1536,512]{1,0:T(8,128)(2,1)S(1)}, bf16[1536,512]{1,0:T(8,128)(2,1)}, u32[]{:S(2)}) copy-start(bf16[1536,512]{1,0:T(8,128)(2,1)} %pad_maximum_fusion.2.refs_4_) | copy-start | bytes 4718596

commit v7 on v6

--- a/solution.py
+++ b/solution.py
@@ -11,7 +11,7 @@
 precision_top = lax.Precision.HIGHEST
 RADIX = 8
 LANES = 128
-CUT_BYTES, SMALL_BYTES, Y_BYTES, X_BYTES = [size * 1024 * 1024 for size in (56, 8, 20, 24)]
+SMALL_BYTES, Y_BYTES, X_BYTES = [size * 1024 * 1024 for size in (8, 32, 24)]
 
 
 def from_partner(value, axis, stride):
@@ -24,32 +24,9 @@
     return lax.all_to_all(values, "gy", split_axis=0, concat_axis=1, tiled=True)
 
 
-def cut_kernel(place, field_ref, *refs):
-    out_ref, sem = refs[-2:]
-    half = out_ref.shape[2]
-    copy = pltpu.make_async_copy(field_ref.at[:, :, pl.ds(place * half, half)], out_ref, sem)
-    copy.start()
-    copy.wait()
-
-
-def cut_half(field, place, *earlier):
-    planes, rows, columns = field.shape
-    anywhere = pl.BlockSpec(memory_space=pl.ANY)
-    return pl.pallas_call(
-        functools.partial(cut_kernel, place),
-        out_shape=jax.ShapeDtypeStruct((planes, rows, columns // 2), jnp.float32),
-        in_specs=[anywhere] * (1 + len(earlier)),
-        out_specs=anywhere,
-        scratch_shapes=[pltpu.SemaphoreType.DMA],
-        compiler_params=pltpu.CompilerParams(vmem_limit_bytes=CUT_BYTES),
-        cost_estimate=pl.CostEstimate(flops=0, bytes_accessed=4 * field.size, transcendentals=0),
-        name="cut_half",
-    )(field, *earlier)
-
-
 def pick_columns(left, right, odd):
     lane = lax.broadcasted_iota(jnp.int32, left.shape, 1)
-    index = (2 * lane + odd) % LANES
+    index = (2 * lane + odd) & (LANES - 1)
     chosen = [jnp.take_along_axis(tile, index, axis=1, mode="promise_in_bounds") for tile in (left, right)]
     return jnp.where(lane < LANES // 2, *chosen)
 
@@ -76,27 +53,6 @@
         compiler_params=pltpu.CompilerParams(vmem_limit_bytes=SMALL_BYTES),
         name="combine",
     )(sign, late, early)
-
-
-def part_kernel(value_ref, *out_refs):
-    left, right = [value_ref[:, pl.ds(lane, LANES)] for lane in (0, LANES)]
-    for odd, out_ref in enumerate(out_refs):
-        out_ref[...] = pick_columns(left, right, odd)
-
-
-def part_columns(value):
-    length, columns = value.shape
-    rows = length // 8
-    return pl.pallas_call(
-        part_kernel,
-        out_shape=[jax.ShapeDtypeStruct((length, columns // 2), jnp.float32)] * 2,
-        grid=(length // rows,),
-        in_specs=[pl.BlockSpec((rows, columns), lambda i: (i, 0))],
-        out_specs=[pl.BlockSpec((rows, columns // 2), lambda i: (i, 0))] * 2,
-        cost_estimate=pl.CostEstimate(flops=value.size, bytes_accessed=8 * value.size, transcendentals=0),
-        compiler_params=pltpu.CompilerParams(vmem_limit_bytes=SMALL_BYTES),
-        name="part_columns",
-    )(value)
 
 
 def reverse_bits(value, count):
@@ -155,101 +111,112 @@
     return jnp.dot(left, right, preferred_element_type=jnp.float32)
 
 
-def y_kernel(lanes, coef_ref, *refs):
-    count = len(lanes)
-    inputs, (table_ref, twist_ref, out_ref, mix_ref, split_ref, step_ref) = refs[:count], refs[count:]
-    inner = mix_ref.shape[0] // RADIX
-    parts = [ref[:, pl.ds(lane, LANES)] for ref, lane in zip(inputs, lanes)]
-    for which in range(2):
-        mixed = parts[0] * coef_ref[which, 0]
-        for place in range(1, count):
-            mixed = mixed + parts[place] * coef_ref[which, place]
-        mix_ref[...] = mixed
-        for s in range(RADIX):
-            high, low = split_value(mix_ref[pl.ds(s, inner, stride=RADIX), :])
-            for place, value in enumerate((high, high, low)):
-                split_ref[pl.ds((2 * place + which) * inner, inner), pl.ds(s * LANES, LANES)] = value
-    step_ref[...] = dot(table_ref[...], split_ref[...])
-    rows_each = 16
-
-    @pl.loop(0, inner // rows_each, unroll=2)
-    def _(block):
-        start = pl.multiple_of(block * rows_each, rows_each)
-        values = []
-        for s in range(RADIX):
-            cols = pl.ds(s * LANES, LANES)
-            re = step_ref[pl.ds(start, rows_each), cols]
-            im = step_ref[pl.ds(pl.multiple_of(start + inner, rows_each), rows_each), cols]
-            if s:
-                cos, sin = twist_ref[0, s, pl.ds(start, rows_each), :], twist_ref[1, s, pl.ds(start, rows_each), :]
-                re, im = re * cos - im * sin, re * sin + im * cos
-            values.append((re, im))
-        for kb, pair in enumerate(small_fft(values)):
-            rows = pl.ds(pl.multiple_of(kb * inner + start, rows_each), rows_each)
-            for which in range(2):
-                high, low = split_value(pair[which])
-                out_ref[2 * which, rows, :] = high
-                out_ref[2 * which + 1, rows, :] = low
-
-
-def y_dft(inputs, coefs, table, twist):
-    arrays, lanes = zip(*inputs)
-    length = arrays[0].shape[0]
+def y_kernel(count, pick, coef_ref, *refs):
+    inputs, (table_ref, twist_ref, *out_refs, mix_ref, split_ref, step_ref) = refs[:count], refs[count:]
+    length = mix_ref.shape[1]
+    inner = length // RADIX
+    rows_each = 128
+    for start in range(0, length, rows_each):
+        rows = pl.ds(start, rows_each)
+        for which in range(2):
+            tiles = []
+            for lane in (0, LANES):
+                mixed = inputs[0][rows, pl.ds(lane, LANES)] * coef_ref[which, 0]
+                for place in range(1, count):
+                    mixed = mixed + inputs[place][rows, pl.ds(lane, LANES)] * coef_ref[which, place]
+                tiles.append(mixed)
+            for tile in range(2):
+                mix_ref[2 * tile + which, rows, :] = pick_columns(*tiles, tile) if pick else tiles[tile]
+    for tile, out_ref in enumerate(out_refs):
+        for which in range(2):
+            for s in range(RADIX):
+                high, low = split_value(mix_ref[2 * tile + which, pl.ds(s, inner, stride=RADIX), :])
+                for place, value in enumerate((high, high, low)):
+                    split_ref[tile, pl.ds((2 * place + which) * inner, inner), pl.ds(s * LANES, LANES)] = value
+        half = inner // 2
+        for part in range(2):
+            step_ref[tile, part] = dot(table_ref[pl.ds(part * inner, inner), :], split_ref[tile])
+            for start in range(0, half, 16):
+                values = []
+                for s in range(RADIX):
+                    cols = pl.ds(s * LANES, LANES)
+                    re = step_ref[tile, part, pl.ds(start, 16), cols]
+                    im = step_ref[tile, part, pl.ds(half + start, 16), cols]
+                    if s:
+                        cos, sin = [twist_ref[k, s, pl.ds(part * half + start, 16), :] for k in range(2)]
+                        re, im = re * cos - im * sin, re * sin + im * cos
+                    values.append((re, im))
+                for kb, pair in enumerate(small_fft(values)):
+                    rows = pl.ds(kb * inner + part * half + start, 16)
+                    for which in range(2):
+                        high, low = split_value(pair[which])
+                        out_ref[2 * which, rows, :] = high
+                        out_ref[2 * which + 1, rows, :] = low
+
+
+def y_dft(inputs, pick, coefs, table, twist):
+    length = inputs[0].shape[0]
     inner = length // RADIX
     whole = pl.BlockSpec(memory_space=pltpu.VMEM)
     return pl.pallas_call(
-        functools.partial(y_kernel, lanes),
-        out_shape=jax.ShapeDtypeStruct((4, length, LANES), jnp.bfloat16),
-        in_specs=[pl.BlockSpec(memory_space=pltpu.SMEM)] + [whole] * (len(arrays) + 2),
-        out_specs=whole,
+        functools.partial(y_kernel, len(inputs), pick),
+        out_shape=[jax.ShapeDtypeStruct((4, length, LANES), jnp.bfloat16)] * 2,
+        in_specs=[pl.BlockSpec(memory_space=pltpu.SMEM)] + [whole] * (len(inputs) + 2),
+        out_specs=[whole] * 2,
         scratch_shapes=[
-            pltpu.VMEM((length, LANES), jnp.float32),
-            pltpu.VMEM((6 * inner, RADIX * LANES), jnp.bfloat16),
-            pltpu.VMEM((2 * inner, RADIX * LANES), jnp.float32),
+            pltpu.VMEM((4, length, LANES), jnp.float32),
+            pltpu.VMEM((2, 6 * inner, RADIX * LANES), jnp.bfloat16),
+            pltpu.VMEM((2, 2, inner, RADIX * LANES), jnp.float32),
         ],
         compiler_params=pltpu.CompilerParams(vmem_limit_bytes=Y_BYTES),
         cost_estimate=pl.CostEstimate(
-            flops=24 * inner * length * LANES, bytes_accessed=4 * length * LANES * (len(arrays) + 3), transcendentals=0
+            flops=48 * inner * length * LANES, bytes_accessed=8 * length * LANES * (len(inputs) + 3), transcendentals=0
         ),
         name="y_dft",
-    )(coefs, *arrays, table, twist)
-
-
-def x_product(parts, table_ref):
-    high = [ref[which] for ref in parts for which in (0, 2)]
-    low = [ref[which] for ref in parts for which in (1, 3)]
+    )(coefs, *inputs, table, twist)
+
+
+def x_product(parts, table_ref, rows):
+    high = [ref[which, rows, :] for ref in parts for which in (0, 2)]
+    low = [ref[which, rows, :] for ref in parts for which in (1, 3)]
     return dot(jnp.concatenate(high + low + high, axis=1), table_ref[...])
 
 
 def x_kernel(count, *refs):
     parts, (even_ref, odd_ref, row_ref, col_ref, out_ref, total_ref) = refs[: 2 * count], refs[2 * count :]
-    even, odd = x_product(parts[:count], even_ref), x_product(parts[count:], odd_ref)
-    half = even.shape[1] // 2
+    half = even_ref.shape[1] // 2
     lanes = LANES
-    row_scale, row_rate = [
-        jnp.concatenate(
-            [jnp.broadcast_to(row_ref[which, 0, c : c + 1, :], (lanes, lanes)).T for c in range(row_ref.shape[2])], 0
-        )
-        for which in range(2)
-    ]
     total = None
-    for tile in range(half // lanes):
-        real, imag = [slice(start, start + lanes) for start in (tile * lanes, half + tile * lanes)]
-        for upper in range(2):
-            cols = pl.ds(upper * half + tile * lanes, lanes)
-            spec_real = even[:, real] - odd[:, real] if upper else even[:, real] + odd[:, real]
-            spec_imag = even[:, imag] - odd[:, imag] if upper else even[:, imag] + odd[:, imag]
-            col_scale, col_shift, col_mix = col_ref[0:1, cols], col_ref[1:2, cols], col_ref[2:3, cols]
-            scale = row_scale * col_scale
-            latent_u = spec_real * scale
-            latent_v = spec_imag * scale
-            log_scale = row_rate * jnp.tanh(latent_u + col_shift)
-            latent_w = latent_v * jnp.exp(log_scale) + col_mix * latent_u
-            out_ref[0, 0, :, cols] = latent_u
-            out_ref[1, 0, :, cols] = latent_w
-            terms = log_scale - 0.5 * (latent_u * latent_u + latent_w * latent_w)
-            terms = jnp.sum(terms.reshape(-1, 8, lanes), axis=0)
-            total = terms if total is None else total + terms
+    spans = [pl.ds(start, 2 * lanes) for start in range(0, out_ref.shape[2], 2 * lanes)]
+    products = [(x_product(parts[:count], even_ref, rows), x_product(parts[count:], odd_ref, rows)) for rows in spans]
+    for rows, (even, odd) in zip(spans, products):
+        row_scale, row_rate = [
+            jnp.concatenate(
+                [
+                    jnp.broadcast_to(row_ref[which, 0, c : c + 1, :], (lanes, lanes)).T
+                    for c in range(rows.start // lanes, rows.start // lanes + 2)
+                ],
+                0,
+            )
+            for which in range(2)
+        ]
+        for tile in range(half // lanes):
+            real, imag = [slice(start, start + lanes) for start in (tile * lanes, half + tile * lanes)]
+            for upper in range(2):
+                cols = pl.ds(upper * half + tile * lanes, lanes)
+                spec_real = even[:, real] - odd[:, real] if upper else even[:, real] + odd[:, real]
+                spec_imag = even[:, imag] - odd[:, imag] if upper else even[:, imag] + odd[:, imag]
+                col_scale, col_shift, col_mix = col_ref[0:1, cols], col_ref[1:2, cols], col_ref[2:3, cols]
+                scale = row_scale * col_scale
+                latent_u = spec_real * scale
+                latent_v = spec_imag * scale
+                log_scale = row_rate * jnp.tanh(latent_u + col_shift)
+                latent_w = latent_v * jnp.exp(log_scale) + col_mix * latent_u
+                out_ref[0, 0, rows, cols] = latent_u
+                out_ref[1, 0, rows, cols] = latent_w
+                terms = log_scale - 0.5 * (latent_u * latent_u + latent_w * latent_w)
+                terms = jnp.sum(terms.reshape(-1, 8, lanes), axis=0)
+                total = terms if total is None else total + terms
 
     @pl.when(pl.program_id(0) == 0)
     def _():
@@ -301,8 +268,8 @@
     position = lax.axis_index("gx")
     planes, rows, columns = field.shape
     length, width = planes * rows, columns // 4
-    field_a = cut_half(field, 0)
-    field_b = cut_half(field, 1, field_a)
+    field_a, field_rest = lax.optimization_barrier((field[:, :, : 2 * width], field))
+    field_b = field_rest[:, :, 2 * width :]
     sign = jnp.where(position < 2, 1.0, -1.0)
 
     own_real = jnp.where(position == 1, -1.0, jnp.where(position == 3, 0.0, 1.0))
@@ -315,7 +282,8 @@
     inner = length // RADIX
     index = jnp.arange(inner, dtype=jnp.int32)
     cos, sin = root_table(index, index, inner)
-    y_table = jnp.concatenate([jnp.concatenate([cos, -sin], 1), jnp.concatenate([sin, cos], 1)], 0)
+    y_table = [jnp.concatenate(pair, 1).reshape(2, 1, inner // 2, 2 * inner) for pair in ((cos, -sin), (sin, cos))]
+    y_table = jnp.concatenate(y_table, 1).reshape(2 * inner, 2 * inner)
     y_table = split_table(y_table, 1, (0, 1, 0))
     grid = [lax.broadcasted_iota(jnp.int32, (RADIX, inner, LANES), axis) for axis in range(2)]
     angle = (grid[0] * grid[1]).astype(jnp.float32) * (-2.0 * math.pi / length)
@@ -340,17 +308,10 @@
     first_a, first_b, (y_table, twist, even_table, odd_table, row_pair, col_trio), coefs_a, coefs_b, fixed = state
     second_a = to_planes(first_a)[0]
 
-    def y_part_b(early, late):
-        group = [late, from_partner(late, "gx", 0), early, from_partner(early, "gx", 0)]
-        return y_dft([(value, 0) for value in group], coefs_b, y_table, twist)
-
-    early_b = part_columns(first_b)
-    late_b = [from_partner(value, "gx", 1) for value in early_b]
-    even_b = y_part_b(early_b[0], late_b[0])
-    even_b, late_b[1] = lax.optimization_barrier((even_b, late_b[1]))
-    odd_b = y_part_b(early_b[1], late_b[1])
-    group = [second_a, from_partner(second_a, "gx", 0)]
-    even_a, odd_a = [y_dft([(value, lane) for value in group], coefs_a, y_table, twist) for lane in (0, width)]
+    second_b = from_partner(first_b, "gx", 1)
+    group = [second_b, from_partner(second_b, "gx", 0), first_b, from_partner(first_b, "gx", 0)]
+    even_b, odd_b = y_dft(group, True, coefs_b, y_table, twist)
+    even_a, odd_a = y_dft([second_a, from_partner(second_a, "gx", 0)], False, coefs_a, y_table, twist)
     latent, tile = x_dft([even_b, even_a], [odd_b, odd_a], even_table, odd_table, row_pair, col_trio)
     tile = tile + fixed / tile.size
     modes = length * columns * lax.axis_size("gx") * lax.axis_size("gy")

time: 295 us -> 168 us (0.57)
  Pallas kernels: 174 us -> 34.8 us
  blocking collectives: 11.3 us -> 15.8 us
  waiting for transfers between devices: 69.9 us -> 73.5 us
    pallas_call x7 -> x2, Pallas kernels: 158 us -> 18.7 us  [y_dft(): pl.pallas_call(functools.partial(y_kernel, len(inputs), pick), out_shape=...]
    ppermute x8 -> x5, waiting for transfers between devices: 26.7 us -> 69.1 us  [from_partner(): return lax.ppermute(value, axis, pairs)]
    all_to_all x2, waiting for transfers between devices: 43.2 us -> 4.38 us  [to_planes(): return lax.all_to_all(values, 'gy', split_axis=0, concat_axis=1, tiled=True)]
    all_to_all x1, blocking collectives: 11.3 us -> 15.8 us  [sum_everywhere(): lax.all_to_all(copies, axes, split_axis=0, concat_axis=0, tiled=True)]
    slice x0 -> x2, local copies, waits for them, and re-layouts: none -> 3.44 us  [the longest x1 1.88 us: four_way(): field[:, :, :2 * width]]
  transfers between devices with their start and end apart: 10 -> 7, of which waited for: 4 -> 5; matrix products, arithmetic and copies ran while one was open for 5% -> 11% of each run, Pallas kernels for 30% -> 9%
where the time goes in v7:
time: 168 us
  waiting for transfers between devices  73.5 us (44%)
  Pallas kernels  34.8 us (21%)
  blocking collectives  15.8 us (9%)
  other arithmetic  14.9 us (9%)
  starting transfers between devices  14.6 us (9%)
  local copies, waits for them, and re-layouts  9.89 us (6%)
  between operations  4.08 us (2%)
    ppermute x5, waiting for transfers between devices, from_partner(): return lax.ppermute(value, axis, pairs)  69.1 us
    pallas_call x2, Pallas kernels, y_dft(): pl.pallas_call(functools.partial(y_kernel, len(inputs), pick), out_shape=...  18.7 us
    all_to_all x1, blocking collectives, sum_everywhere(): lax.all_to_all(copies, axes, split_axis=0, concat_axis=0, tiled=True)  15.8 us
    pallas_call x1, Pallas kernels, x_dft(): pl.pallas_call(functools.partial(x_kernel, count), out_shape=(jax.ShapeDt...  11.2 us
    all_to_all x2, starting transfers between devices, to_planes(): return lax.all_to_all(values, 'gy', split_axis=0, concat_axis=1, tiled=True)  10.3 us
    pallas_call x1, Pallas kernels, combine(): pl.pallas_call(combine_kernel, out_shape=jax.ShapeDtypeStruct(late.shape,...  4.95 us
    unnamed x24, local copies, waits for them, and re-layouts  4.44 us
    all_to_all x2, waiting for transfers between devices, to_planes(): return lax.all_to_all(values, 'gy', split_axis=0, concat_axis=1, tiled=True)  4.38 us
  transfers between devices with their start and end apart: 7, of which 5 were waited for; matrix products, arithmetic and copies ran while one was open for 11% of the time, Pallas kernels for 9%

profile of v7, /device:TPU:0, one launch (start us, length us, event | category | flops | bytes accessed | tf_op | source)
XLA Modules:
  0.0 167.6 jit_solution(7140603951362452897)
XLA Ops:
  0.6 1.9 %slice.18.early_ref = f32[8,256,256]{2,1,0:T(8,128)S(1)} slice(f32[8,256,512]{2,1,0:T(8,128)} %param.6), slice={[0:8], [0:256], [0:256]} | slice | bytes 4194304 | tf_op jit(solution)/shard_map/slice | solution.py:271
  2.5 3.0 %collective-permute-start = (f32[8,256,256]{2,1,0:T(8,128)S(1)}, f32[8,256,256]{2,1,0:T(8,128)}, u32[]{:S(2)}, u32[]{:S(2)}) collective-permute-start(f32[8,256,256]{2,1,0:T(8,128)S(1)} %slice.18.early_ref), channel_id=1, source_target_pairs={{0,16},{8,24},{16,0},{24,8},{1,17},{9,25},{17,1},{25,9},{2,18},{10... | collective-permute-start | bytes 6291464 | tf_op jit(solution)/shard_map/ppermute | solution.py:20
  5.6 1.6 slice.19
  7.1 5.8 %all-to-all-start = ((f32[8,256,256]{2,1,0:T(8,128)}), f32[8,256,256]{2,1,0:T(8,128)}, u32[]{:S(2)}, u32[]{:S(2)}) async-start(f32[8,256,256]{2,1,0:T(8,128)} %slice.19), calls=%async_computation | async-start | bytes 4194304 | tf_op jit(solution)/shard_map/all_to_all | solution.py:24
  12.9 0.0 copy-start.7
  12.9 0.0 copy-start.10
  13.0 0.0 copy-start.11
  13.0 0.0 copy-start.9
  13.1 0.5 fusion.8
  13.6 1.0 slice_sine_fusion.1
  14.6 0.7 neg.17
  15.3 0.9 slice_sine_fusion
  16.3 0.7 log_reduce_fusion
  17.0 0.1 pad_maximum_fusion.9
  17.1 0.1 reshape.183.coef_ref
  17.8 0.6 log_reduce_fusion.1
  19.1 1.1 maximum_bitcast_fusion
  20.2 0.1 pad_maximum_fusion.4
  20.3 0.1 maximum_bitcast_fusion.2
  20.4 0.1 pad_maximum_fusion.5
  20.5 1.1 fusion.19
  21.6 0.1 maximum_maximum_fusion
  21.7 0.1 pad_maximum_fusion.8.coef_ref
  21.8 3.2 %fusion.3 = (f32[1,8,256,128]{3,2,1,0:T(8,128)S(1)}, f32[1,8,256,128]{3,2,1,0:T(8,128)S(1)}) fusion(), kind=kLoop, calls=%fused_computation.17 | loop fusion | flops 786432 | bytes 2097152 | tf_op jit(solution)/shard_map/sin | solution.py:290
  25.0 1.5 pad_maximum_fusion.refs_5_.refs_3_
  26.5 0.1 fusion
  26.7 0.1 reduce-precision_convert_fusion.1
  26.8 0.1 reduce-precision_convert_fusion
  26.9 1.2 pad_maximum_fusion.1.refs_4_.refs_2_
  28.2 1.3 pad_maximum_fusion.2.refs_4_
  29.5 1.3 pad_maximum_fusion.3.refs_5_
  30.8 20.5 %collective-permute-done.late_ref = f32[8,256,256]{2,1,0:T(8,128)} collective-permute-done((f32[8,256,256]{2,1,0:T(8,128)S(1)}, f32[8,256,256]{2,1,0:T(8,128)}, u32[]{:S(2)}, u32[]{:S(2)}) %collective-permute-start) | collective-permute-done | bytes 2097184 | tf_op jit(solution)/shard_map/ppermute | solution.py:20
  51.3 4.9 %combine.1 = f32[8,256,256]{2,1,0:T(8,128)S(1)} custom-call(f32[1]{0:T(128)} %bitcast.sign_ref, f32[8,256,256]{2,1,0:T(8,128)} %collective-permute-done.late_ref, f32[8,256,256]{2,1,0:T(8,128)S(1)} %slice.18.early_ref), custom_call_target="tpu_custom_call" | custom-call | flops 1048576 | bytes 6291456 | tf_op jit(solution)/shard_map/combine/pallas_call | solution.py:46
  56.3 1.4 copy-done
  57.7 3.3 %all-to-all-done = f32[8,256,256]{2,1,0:T(8,128)} async-done(((f32[8,256,256]{2,1,0:T(8,128)}), f32[8,256,256]{2,1,0:T(8,128)}, u32[]{:S(2)}, u32[]{:S(2)}) %all-to-all-start) | async-done | bytes 2097184 | tf_op jit(solution)/shard_map/all_to_all | solution.py:24
  61.0 4.5 %all-to-all-start.1 = ((f32[8,256,256]{2,1,0:T(8,128)}), f32[8,256,256]{2,1,0:T(8,128)}, u32[]{:S(2)}, u32[]{:S(2)}) async-start(f32[8,256,256]{2,1,0:T(8,128)} %copy-done), calls=%async_computation.1 | async-start | bytes 4194304 | tf_op jit(solution)/shard_map/all_to_all | solution.py:24
  65.5 1.2 collective-permute-start.1
  66.7 0.0 collective-permute-start.3
  66.7 45.4 %collective-permute-done.1.refs_0_ = f32[2048,256]{1,0:T(8,128)S(1)} collective-permute-done((f32[2048,256]{1,0:T(8,128)}, f32[2048,256]{1,0:T(8,128)S(1)}, u32[]{:S(2)}, u32[]{:S(2)}) %collective-permute-start.1) | collective-permute-done | bytes 2097184 | tf_op jit(solution)/shard_map/ppermute | solution.py:20
  112.1 1.1 all-to-all-done.1
  113.2 3.2 %collective-permute-done.2.refs_1_ = f32[2048,256]{1,0:T(8,128)} collective-permute-done((f32[2048,256]{1,0:T(8,128)S(1)}, f32[2048,256]{1,0:T(8,128)}, u32[]{:S(2)}, u32[]{:S(2)}) %collective-permute-start.2) | collective-permute-done | bytes 2097184 | tf_op jit(solution)/shard_map/ppermute | solution.py:20
  116.4 1.6 copy-done.1
  118.0 1.4 copy-done.3
  119.4 10.0 %y_dft.2 = (bf16[4,2048,128]{2,1,0:T(8,128)(2,1)S(1)}, bf16[4,2048,128]{2,1,0:T(8,128)(2,1)S(1)}) custom-call(f32[2,4]{1,0:T(2,128)S(1)} %pad_maximum_fusion.8.coef_ref, f32[2048,256]{1,0:T(8,128)S(1)} %collective-permute-done.1.refs_0_, f32[2048,256]{1,0:T(8,128)} %collective-permute-done.2.refs_1_, f32[2048,256]{1,0:T(8,128)} %bitcast.1.refs_2_, ...), custom_call_target="tpu_custom_call" | custom-call | flops 3221225472 | bytes 14680064 | tf_op jit(solution)/shard_map/y_dft/pallas_call | solution.py:161
  129.4 8.7 %y_dft.3 = (bf16[4,2048,128]{2,1,0:T(8,128)(2,1)S(1)}, bf16[4,2048,128]{2,1,0:T(8,128)(2,1)S(1)}) custom-call(f32[2,2]{1,0:T(2,128)S(1)} %reshape.183.coef_ref, f32[2048,256]{1,0:T(8,128)} %bitcast.24.refs_0_, f32[2048,256]{1,0:T(8,128)} %collective-permute-done.4.refs_1_, bf16[512,1536]{1,0:T(8,128)(2,1)S(1)} %copy-done.3, f32[2,8,256,128]{3,2,1,0:T(8,128)S(1)} %copy-done.2), custom_call_target="tpu_custom_call" | custom-call | flops 3221225472 | bytes 10485760 | tf_op jit(solution)/shard_map/y_dft/pallas_call | solution.py:161
  138.1 11.2 %x_dft.1 = (f32[2,1,2048,512]{3,2,1,0:T(8,128)}, f32[8,128]{1,0:T(8,128)S(1)}) custom-call(bf16[4,2048,128]{2,1,0:T(8,128)(2,1)S(1)} %get-tuple-element.27.refs_0_, bf16[4,2048,128]{2,1,0:T(8,128)(2,1)S(1)} %get-tuple-element.30.refs_1_, bf16[4,2048,128]{2,1,0:T(8,128)(2,1)S(1)} %get-tuple-element.31.refs_2_, ...), custom_call_target="tpu_custom_call" | custom-call | flops 6442450944 | bytes 16777216 | tf_op jit(solution)/shard_map/x_dft/pallas_call | solution.py:233
  149.3 15.8 %all_to_all.23 = f32[32,8,128]{2,1,0:T(8,128)S(1)} all-to-all(f32[32,8,128]{2,1,0:T(8,128)S(1)} %broadcast_in_dim.2), channel_id=1, replica_groups=mesh['gx'=4,'gy'=8] {'gx','gy'}, dimensions={0} | all-to-all | bytes 262144 | tf_op jit(solution)/shard_map/all_to_all | solution.py:264
  165.2 0.6 reduce_sum.29
  (33 shorter events, 0.1 us)
Async XLA Ops:
  0.6 4.9 %copy-start.6 = (f32[8,256,512]{2,1,0:T(8,128)S(1)}, f32[8,256,512]{2,1,0:T(8,128)}, u32[]{:S(2)}) copy-start(f32[8,256,512]{2,1,0:T(8,128)} %param.6) | copy-start | bytes 12582916
  2.5 48.8 %collective-permute-start = (f32[8,256,256]{2,1,0:T(8,128)S(1)}, f32[8,256,256]{2,1,0:T(8,128)}, u32[]{:S(2)}, u32[]{:S(2)}) collective-permute-start(f32[8,256,256]{2,1,0:T(8,128)S(1)} %slice.18.early_ref), channel_id=1, source_target_pairs={{0,16},{8,24},{16,0},{24,8},{1,17},{9,25},{17,1},{25,9},{2,18},{10... | collective-permute-start | bytes 6291464 | tf_op jit(solution)/shard_map/ppermute | solution.py:20
  7.1 53.9 %all-to-all-start = ((f32[8,256,256]{2,1,0:T(8,128)}), f32[8,256,256]{2,1,0:T(8,128)}, u32[]{:S(2)}, u32[]{:S(2)}) async-start(f32[8,256,256]{2,1,0:T(8,128)} %slice.19), calls=%async_computation | async-start | bytes 4194304 | tf_op jit(solution)/shard_map/all_to_all | solution.py:24
  12.9 3.4 %copy-start.8 = (f32[2048]{0:T(1024)S(1)}, f32[2048]{0:T(1024)}, u32[]{:S(2)}) copy-start(f32[2048]{0:T(1024)} %param.7) | copy-start | bytes 24580
  12.9 4.9 %copy-start.7 = (f32[512]{0:T(512)S(1)}, f32[512]{0:T(512)}, u32[]{:S(2)}) copy-start(f32[512]{0:T(512)} %param.8) | copy-start | bytes 6148
  12.9 6.1 %copy-start.10 = (f32[512]{0:T(512)S(1)}, f32[512]{0:T(512)}, u32[]{:S(2)}) copy-start(f32[512]{0:T(512)} %param.11) | copy-start | bytes 6148
  13.0 6.1 %copy-start.11 = (f32[512]{0:T(512)S(1)}, f32[512]{0:T(512)}, u32[]{:S(2)}) copy-start(f32[512]{0:T(512)} %param.10) | copy-start | bytes 6148
  13.0 6.2 %copy-start.9 = (f32[2048]{0:T(1024)S(1)}, f32[2048]{0:T(1024)}, u32[]{:S(2)}) copy-start(f32[2048]{0:T(1024)} %param.9) | copy-start | bytes 24580
  56.2 1.4 copy-start
  61.0 52.2 %all-to-all-start.1 = ((f32[8,256,256]{2,1,0:T(8,128)}), f32[8,256,256]{2,1,0:T(8,128)}, u32[]{:S(2)}, u32[]{:S(2)}) async-start(f32[8,256,256]{2,1,0:T(8,128)} %copy-done), calls=%async_computation.1 | async-start | bytes 4194304 | tf_op jit(solution)/shard_map/all_to_all | solution.py:24
  65.5 46.6 %collective-permute-start.1 = (f32[2048,256]{1,0:T(8,128)}, f32[2048,256]{1,0:T(8,128)S(1)}, u32[]{:S(2)}, u32[]{:S(2)}) collective-permute-start(f32[2048,256]{1,0:T(8,128)} %bitcast.1.refs_2_), channel_id=1, source_target_pairs={{0,16},{8,24},{16,0},{24,8},{1,17},{9,25},{17,1},{25,9},{2,18},{10... | collective-permute-start | bytes 6291464 | tf_op jit(solution)/shard_map/ppermute | solution.py:20
  66.7 46.4 %collective-permute-start.3 = (f32[2048,256]{1,0:T(8,128)}, f32[2048,256]{1,0:T(8,128)}, u32[]{:S(2)}, u32[]{:S(2)}) collective-permute-start(f32[2048,256]{1,0:T(8,128)} %bitcast.1.refs_2_), channel_id=1, source_target_pairs={{0,8},{8,0},{16,24},{24,16},{1,9},{9,1},{17,25},{25,17},{2,10},{10... | collective-permute-start | bytes 6291464 | tf_op jit(solution)/shard_map/ppermute | solution.py:20
  112.1 4.3 %collective-permute-start.2 = (f32[2048,256]{1,0:T(8,128)S(1)}, f32[2048,256]{1,0:T(8,128)}, u32[]{:S(2)}, u32[]{:S(2)}) collective-permute-start(f32[2048,256]{1,0:T(8,128)S(1)} %collective-permute-done.1.refs_0_), channel_id=1, source_target_pairs={{0,8},{8,0},{16,24},{24,16},{1,9},{9,1},{17,25},{25,17},{2,10},{10... | collective-permute-start | bytes 6291464 | tf_op jit(solution)/shard_map/ppermute | solution.py:20
  113.2 16.3 %collective-permute-start.4 = (f32[2048,256]{1,0:T(8,128)}, f32[2048,256]{1,0:T(8,128)}, u32[]{:S(2)}, u32[]{:S(2)}) collective-permute-start(f32[2048,256]{1,0:T(8,128)} %bitcast.24.refs_0_), channel_id=1, source_target_pairs={{0,8},{8,0},{16,24},{24,16},{1,9},{9,1},{17,25},{25,17},{2,10},{10... | collective-permute-start | bytes 6291464 | tf_op jit(solution)/shard_map/ppermute | solution.py:20
  116.4 1.6 copy-start.1
  118.0 1.4 copy-start.3
  119.4 10.0 %copy-start.2 = (f32[2,8,256,128]{3,2,1,0:T(8,128)S(1)}, f32[2,8,256,128]{3,2,1,0:T(8,128)}, u32[]{:S(2)}) copy-start(f32[2,8,256,128]{3,2,1,0:T(8,128)} %pad_maximum_fusion.refs_5_.refs_3_) | copy-start | bytes 6291460
  129.4 8.7 %copy-start.4 = (bf16[1536,512]{1,0:T(8,128)(2,1)S(1)}, bf16[1536,512]{1,0:T(8,128)(2,1)}, u32[]{:S(2)}) copy-start(bf16[1536,512]{1,0:T(8,128)(2,1)} %pad_maximum_fusion.2.refs_4_) | copy-start | bytes 4718596
  129.4 8.7 %copy-start.5 = (bf16[1536,512]{1,0:T(8,128)(2,1)S(1)}, bf16[1536,512]{1,0:T(8,128)(2,1)}, u32[]{:S(2)}) copy-start(bf16[1536,512]{1,0:T(8,128)(2,1)} %pad_maximum_fusion.3.refs_5_) | copy-start | bytes 4718596

commit v8 on v6

--- a/solution.py
+++ b/solution.py
@@ -11,7 +11,7 @@
 precision_top = lax.Precision.HIGHEST
 RADIX = 8
 LANES = 128
-CUT_BYTES, SMALL_BYTES, Y_BYTES, X_BYTES = [size * 1024 * 1024 for size in (56, 8, 20, 24)]
+SMALL_BYTES, Y_BYTES, X_BYTES = 8 * 1024 * 1024, (0, 20 * 1024 * 1024, 28 * 1024 * 1024), 24 * 1024 * 1024
 
 
 def from_partner(value, axis, stride):
@@ -24,43 +24,16 @@
     return lax.all_to_all(values, "gy", split_axis=0, concat_axis=1, tiled=True)
 
 
-def cut_kernel(place, field_ref, *refs):
-    out_ref, sem = refs[-2:]
-    half = out_ref.shape[2]
-    copy = pltpu.make_async_copy(field_ref.at[:, :, pl.ds(place * half, half)], out_ref, sem)
-    copy.start()
-    copy.wait()
-
-
-def cut_half(field, place, *earlier):
-    planes, rows, columns = field.shape
-    anywhere = pl.BlockSpec(memory_space=pl.ANY)
-    return pl.pallas_call(
-        functools.partial(cut_kernel, place),
-        out_shape=jax.ShapeDtypeStruct((planes, rows, columns // 2), jnp.float32),
-        in_specs=[anywhere] * (1 + len(earlier)),
-        out_specs=anywhere,
-        scratch_shapes=[pltpu.SemaphoreType.DMA],
-        compiler_params=pltpu.CompilerParams(vmem_limit_bytes=CUT_BYTES),
-        cost_estimate=pl.CostEstimate(flops=0, bytes_accessed=4 * field.size, transcendentals=0),
-        name="cut_half",
-    )(field, *earlier)
-
-
-def pick_columns(left, right, odd):
-    lane = lax.broadcasted_iota(jnp.int32, left.shape, 1)
-    index = (2 * lane + odd) % LANES
-    chosen = [jnp.take_along_axis(tile, index, axis=1, mode="promise_in_bounds") for tile in (left, right)]
-    return jnp.where(lane < LANES // 2, *chosen)
+def sort_columns(tile, odd_first):
+    lane = lax.broadcasted_iota(jnp.int32, tile.shape, 1)
+    index = ((2 * lane) & (LANES - 1)) + ((lane >> LANES.bit_length() - 2) ^ odd_first)
+    return jnp.take_along_axis(tile, index, axis=1, mode="promise_in_bounds")
 
 
 def combine_kernel(sign_ref, late_ref, early_ref, out_ref):
-    sign = sign_ref[0]
-    left, right = [
-        late_ref[0, :, pl.ds(lane, LANES)] + sign * early_ref[0, :, pl.ds(lane, LANES)] for lane in (0, LANES)
-    ]
-    for odd in range(2):
-        out_ref[0, :, pl.ds(odd * LANES, LANES)] = pick_columns(left, right, odd)
+    for lane in (0, LANES):
+        cols = pl.ds(lane, LANES)
+        out_ref[0, :, cols] = sort_columns(late_ref[0, :, cols] + sign_ref[0] * early_ref[0, :, cols], 1)
 
 
 def combine(sign, late, early):
@@ -79,9 +52,8 @@
 
 
 def part_kernel(value_ref, *out_refs):
-    left, right = [value_ref[:, pl.ds(lane, LANES)] for lane in (0, LANES)]
-    for odd, out_ref in enumerate(out_refs):
-        out_ref[...] = pick_columns(left, right, odd)
+    for place, out_ref in enumerate(out_refs):
+        out_ref[...] = sort_columns(value_ref[:, pl.ds(place * LANES, LANES)], 0)
 
 
 def part_columns(value):
@@ -89,10 +61,10 @@
     rows = length // 8
     return pl.pallas_call(
         part_kernel,
-        out_shape=[jax.ShapeDtypeStruct((length, columns // 2), jnp.float32)] * 2,
+        out_shape=[jax.ShapeDtypeStruct((length, LANES), jnp.float32)] * (columns // LANES),
         grid=(length // rows,),
         in_specs=[pl.BlockSpec((rows, columns), lambda i: (i, 0))],
-        out_specs=[pl.BlockSpec((rows, columns // 2), lambda i: (i, 0))] * 2,
+        out_specs=[pl.BlockSpec((rows, LANES), lambda i: (i, 0))] * (columns // LANES),
         cost_estimate=pl.CostEstimate(flops=value.size, bytes_accessed=8 * value.size, transcendentals=0),
         compiler_params=pltpu.CompilerParams(vmem_limit_bytes=SMALL_BYTES),
         name="part_columns",
@@ -155,75 +127,95 @@
     return jnp.dot(left, right, preferred_element_type=jnp.float32)
 
 
-def y_kernel(lanes, coef_ref, *refs):
-    count = len(lanes)
-    inputs, (table_ref, twist_ref, out_ref, mix_ref, split_ref, step_ref) = refs[:count], refs[count:]
-    inner = mix_ref.shape[0] // RADIX
-    parts = [ref[:, pl.ds(lane, LANES)] for ref, lane in zip(inputs, lanes)]
-    for which in range(2):
-        mixed = parts[0] * coef_ref[which, 0]
-        for place in range(1, count):
-            mixed = mixed + parts[place] * coef_ref[which, place]
-        mix_ref[...] = mixed
-        for s in range(RADIX):
-            high, low = split_value(mix_ref[pl.ds(s, inner, stride=RADIX), :])
-            for place, value in enumerate((high, high, low)):
-                split_ref[pl.ds((2 * place + which) * inner, inner), pl.ds(s * LANES, LANES)] = value
-    step_ref[...] = dot(table_ref[...], split_ref[...])
-    rows_each = 16
-
-    @pl.loop(0, inner // rows_each, unroll=2)
-    def _(block):
-        start = pl.multiple_of(block * rows_each, rows_each)
-        values = []
-        for s in range(RADIX):
-            cols = pl.ds(s * LANES, LANES)
-            re = step_ref[pl.ds(start, rows_each), cols]
-            im = step_ref[pl.ds(pl.multiple_of(start + inner, rows_each), rows_each), cols]
-            if s:
-                cos, sin = twist_ref[0, s, pl.ds(start, rows_each), :], twist_ref[1, s, pl.ds(start, rows_each), :]
-                re, im = re * cos - im * sin, re * sin + im * cos
-            values.append((re, im))
-        for kb, pair in enumerate(small_fft(values)):
-            rows = pl.ds(pl.multiple_of(kb * inner + start, rows_each), rows_each)
+def y_kernel(count, tiles, coef_ref, *refs):
+    inputs, refs = refs[:count], refs[count:]
+    (table_hbm, twist_hbm), out_refs, scratch = refs[:2], refs[2 : 2 + tiles], refs[2 + tiles :]
+    table_ref, twist_ref, mix_ref, split_ref, step_ref, sems = scratch
+    copies = [
+        pltpu.make_async_copy(source, target, sems.at[place])
+        for place, (source, target) in enumerate(((table_hbm, table_ref), (twist_hbm, twist_ref)))
+    ]
+    for copy in copies:
+        copy.start()
+    length = mix_ref.shape[1]
+    inner = length // RADIX
+    rows_each = 128
+    for tile in range(tiles):
+        cols = pl.ds(tile * LANES, LANES)
+        for start in range(0, length, rows_each):
+            rows = pl.ds(start, rows_each)
+            parts = [ref[rows, cols] for ref in inputs]
             for which in range(2):
-                high, low = split_value(pair[which])
-                out_ref[2 * which, rows, :] = high
-                out_ref[2 * which + 1, rows, :] = low
+                mixed = parts[0] * coef_ref[which, 0]
+                for place in range(1, count):
+                    mixed = mixed + parts[place] * coef_ref[which, place]
+                mix_ref[which, rows, :] = mixed
+        for which in range(2):
+            for s in range(RADIX):
+                high, low = split_value(mix_ref[which, pl.ds(s, inner, stride=RADIX), :])
+                for place, value in enumerate((high, high, low)):
+                    split_ref[tile, pl.ds((2 * place + which) * inner, inner), pl.ds(s * LANES, LANES)] = value
+    for tile, out_ref in enumerate(out_refs):
+        if tile == 0:
+            copies[0].wait()
+        step_ref[tile] = dot(table_ref[...], split_ref[tile])
+        if tile == 0:
+            copies[1].wait()
+        for start in range(0, inner, 16):
+            values = []
+            for s in range(RADIX):
+                cols = pl.ds(s * LANES, LANES)
+                re = step_ref[tile, pl.ds(start, 16), cols]
+                im = step_ref[tile, pl.ds(inner + start, 16), cols]
+                if s:
+                    cos, sin = [twist_ref[k, s, pl.ds(start, 16), :] for k in range(2)]
+                    re, im = re * cos - im * sin, re * sin + im * cos
+                values.append((re, im))
+            for kb, pair in enumerate(small_fft(values)):
+                rows = pl.ds(kb * inner + start, 16)
+                for which in range(2):
+                    high, low = split_value(pair[which])
+                    out_ref[2 * which, rows, :] = high
+                    out_ref[2 * which + 1, rows, :] = low
 
 
 def y_dft(inputs, coefs, table, twist):
-    arrays, lanes = zip(*inputs)
-    length = arrays[0].shape[0]
-    inner = length // RADIX
-    whole = pl.BlockSpec(memory_space=pltpu.VMEM)
+    length, columns = inputs[0].shape
+    tiles, inner = columns // LANES, length // RADIX
+    whole, anywhere = pl.BlockSpec(memory_space=pltpu.VMEM), pl.BlockSpec(memory_space=pl.ANY)
     return pl.pallas_call(
-        functools.partial(y_kernel, lanes),
-        out_shape=jax.ShapeDtypeStruct((4, length, LANES), jnp.bfloat16),
-        in_specs=[pl.BlockSpec(memory_space=pltpu.SMEM)] + [whole] * (len(arrays) + 2),
-        out_specs=whole,
+        functools.partial(y_kernel, len(inputs), tiles),
+        out_shape=[jax.ShapeDtypeStruct((4, length, LANES), jnp.bfloat16)] * tiles,
+        in_specs=[pl.BlockSpec(memory_space=pltpu.SMEM)] + [whole] * len(inputs) + [anywhere] * 2,
+        out_specs=[whole] * tiles,
         scratch_shapes=[
-            pltpu.VMEM((length, LANES), jnp.float32),
-            pltpu.VMEM((6 * inner, RADIX * LANES), jnp.bfloat16),
-            pltpu.VMEM((2 * inner, RADIX * LANES), jnp.float32),
+            pltpu.VMEM(table.shape, table.dtype),
+            pltpu.VMEM(twist.shape, twist.dtype),
+            pltpu.VMEM((2, length, LANES), jnp.float32),
+            pltpu.VMEM((tiles, 6 * inner, RADIX * LANES), jnp.bfloat16),
+            pltpu.VMEM((tiles, 2 * inner, RADIX * LANES), jnp.float32),
+            pltpu.SemaphoreType.DMA((2,)),
         ],
-        compiler_params=pltpu.CompilerParams(vmem_limit_bytes=Y_BYTES),
+        compiler_params=pltpu.CompilerParams(vmem_limit_bytes=Y_BYTES[tiles]),
         cost_estimate=pl.CostEstimate(
-            flops=24 * inner * length * LANES, bytes_accessed=4 * length * LANES * (len(arrays) + 3), transcendentals=0
+            flops=24 * inner * length * columns, bytes_accessed=4 * length * columns * (len(inputs) + 3), transcendentals=0
         ),
         name="y_dft",
-    )(coefs, *arrays, table, twist)
-
-
-def x_product(parts, table_ref):
-    high = [ref[which] for ref in parts for which in (0, 2)]
-    low = [ref[which] for ref in parts for which in (1, 3)]
+    )(coefs, *inputs, table, twist)
+
+
+def x_product(left, right, table_ref):
+    rows = left[0].shape[1]
+    lower = lax.broadcasted_iota(jnp.int32, (rows, LANES), 1) < LANES // 2
+    planes = [[jnp.where(lower, one[which], two[which]) for which in range(4)] for one, two in zip(left, right)]
+    high, low = [[plane[which] for plane in planes for which in (first, first + 2)] for first in range(2)]
     return dot(jnp.concatenate(high + low + high, axis=1), table_ref[...])
 
 
 def x_kernel(count, *refs):
     parts, (even_ref, odd_ref, row_ref, col_ref, out_ref, total_ref) = refs[: 2 * count], refs[2 * count :]
-    even, odd = x_product(parts[:count], even_ref), x_product(parts[count:], odd_ref)
+    odd_first, even_first = parts[:count], parts[count:]
+    even, odd = x_product(even_first, odd_first, even_ref), x_product(odd_first, even_first, odd_ref)
     half = even.shape[1] // 2
     lanes = LANES
     row_scale, row_rate = [
@@ -258,11 +250,11 @@
     total_ref[...] += total
 
 
-def x_dft(even_parts, odd_parts, even_table, odd_table, row_pair, col_trio):
-    parts, count, length = even_parts + odd_parts, len(even_parts), even_parts[0].shape[1]
+def x_dft(odd_first, even_first, even_table, odd_table, row_pair, col_trio):
+    parts, count, length = [*odd_first, *even_first], len(odd_first), odd_first[0].shape[1]
     columns = even_table.shape[1]
     rows = length // row_pair.shape[1]
-    fixed = [pl.BlockSpec(table.shape, lambda i: (0, 0), pipeline_mode=pl.Buffered(1)) for table in (even_table, odd_table)]
+    fixed = [pl.BlockSpec(memory_space=pltpu.VMEM)] * 2
     return pl.pallas_call(
         functools.partial(x_kernel, count),
         out_shape=(
@@ -301,8 +293,8 @@
     position = lax.axis_index("gx")
     planes, rows, columns = field.shape
     length, width = planes * rows, columns // 4
-    field_a = cut_half(field, 0)
-    field_b = cut_half(field, 1, field_a)
+    field_a, field_rest = lax.optimization_barrier((field[:, :, : 2 * width], field))
+    field_b = field_rest[:, :, 2 * width :]
     sign = jnp.where(position < 2, 1.0, -1.0)
 
     own_real = jnp.where(position == 1, -1.0, jnp.where(position == 3, 0.0, 1.0))
@@ -315,21 +307,22 @@
     inner = length // RADIX
     index = jnp.arange(inner, dtype=jnp.int32)
     cos, sin = root_table(index, index, inner)
-    y_table = jnp.concatenate([jnp.concatenate([cos, -sin], 1), jnp.concatenate([sin, cos], 1)], 0)
+    y_table = jnp.concatenate([jnp.concatenate(pair, 1) for pair in ((cos, -sin), (sin, cos))], 0)
     y_table = split_table(y_table, 1, (0, 1, 0))
     grid = [lax.broadcasted_iota(jnp.int32, (RADIX, inner, LANES), axis) for axis in range(2)]
     angle = (grid[0] * grid[1]).astype(jnp.float32) * (-2.0 * math.pi / length)
     twist = jnp.stack([jnp.cos(angle), jnp.sin(angle)])
-    order = jnp.arange(width, dtype=jnp.int32) * 2
+    order = jnp.arange(width // 2, dtype=jnp.int32) * 2
 
     def x_table(odd):
-        rows = jnp.concatenate([order + (2 * width + odd), order + odd])
+        starts = [tile * width + odd + offset for tile in range(2) for offset in ((0, 2 * width) if odd else (2 * width, 0))]
+        rows = jnp.concatenate([start + order for start in starts])
         cos, sin = [part[:, : 2 * width].reshape(2, width, 2 * width) for part in x_tables(rows, columns, 4, position)]
         table = jnp.stack([jnp.concatenate([cos, sin], 2), jnp.concatenate([-sin, cos], 2)], 1)
         return split_table(table.reshape(columns, columns), 0, (0, 0, 1))
 
     norm = 1.0 / math.sqrt(length * columns * 4)
-    row_pair = jnp.stack([row_scale * norm, row_rate]).reshape(2, 4, length // 4 // LANES, LANES)
+    row_pair = jnp.stack([row_scale * norm, row_rate]).reshape(2, 8, length // 8 // LANES, LANES)
     col_trio = jnp.stack([col_scale, col_shift, col_mix])
     fixed = 2.0 * (columns * jnp.sum(jnp.log(row_scale)) + length * jnp.sum(jnp.log(col_scale)))
     fixed = fixed - length * columns * math.log(2.0 * math.pi)
@@ -340,18 +333,18 @@
     first_a, first_b, (y_table, twist, even_table, odd_table, row_pair, col_trio), coefs_a, coefs_b, fixed = state
     second_a = to_planes(first_a)[0]
 
+    early_b = part_columns(first_b)
+    late_b = [from_partner(value, "gx", 1) for value in early_b]
+
     def y_part_b(early, late):
         group = [late, from_partner(late, "gx", 0), early, from_partner(early, "gx", 0)]
-        return y_dft([(value, 0) for value in group], coefs_b, y_table, twist)
-
-    early_b = part_columns(first_b)
-    late_b = [from_partner(value, "gx", 1) for value in early_b]
-    even_b = y_part_b(early_b[0], late_b[0])
-    even_b, late_b[1] = lax.optimization_barrier((even_b, late_b[1]))
-    odd_b = y_part_b(early_b[1], late_b[1])
-    group = [second_a, from_partner(second_a, "gx", 0)]
-    even_a, odd_a = [y_dft([(value, lane) for value in group], coefs_a, y_table, twist) for lane in (0, width)]
-    latent, tile = x_dft([even_b, even_a], [odd_b, odd_a], even_table, odd_table, row_pair, col_trio)
+        return y_dft(group, coefs_b, y_table, twist)[0]
+
+    even_first = [y_part_b(early_b[0], late_b[0])]
+    even_first[0], late_b[1], second_a = lax.optimization_barrier((even_first[0], late_b[1], second_a))
+    odd_first = y_dft([second_a, from_partner(second_a, "gx", 0)], coefs_a, y_table, twist)
+    even_first.append(y_part_b(early_b[1], late_b[1]))
+    latent, tile = x_dft(odd_first, even_first, even_table, odd_table, row_pair, col_trio)
     tile = tile + fixed / tile.size
     modes = length * columns * lax.axis_size("gx") * lax.axis_size("gy")
     return (latent, sum_everywhere(tile) / modes)

time: 295 us -> 181 us (0.61)
  Pallas kernels: 174 us -> 44.5 us
  waiting for transfers between devices: 69.9 us -> 76.4 us
  local copies, waits for them, and re-layouts: 7.52 us -> 10.9 us
  starting transfers between devices: 14.9 us -> 18.2 us
    pallas_call x7 -> x4, Pallas kernels: 158 us -> 27.3 us  [the longest x3 22.6 us: y_dft(): pl.pallas_call(functools.partial(y_kernel, len(inputs), tiles), out_shape...]
    ppermute x8, waiting for transfers between devices: 26.7 us -> 76.4 us  [from_partner(): return lax.ppermute(value, axis, pairs)]
    all_to_all x2, waiting for transfers between devices: 43.2 us -> 0.01 us  [to_planes(): return lax.all_to_all(values, 'gy', split_axis=0, concat_axis=1, tiled=True)]
    slice x0 -> x2, local copies, waits for them, and re-layouts: none -> 4.77 us  [the longest x1 3.2 us: four_way(): field[:, :, :2 * width]]
  transfers between devices with their start and end apart: 10 -> 10, of which waited for: 4 -> 6; matrix products, arithmetic and copies ran while one was open for 5% -> 8% of each run, Pallas kernels for 30% -> 12%
where the time goes in v8:
time: 181 us; the launch traced here: 180 us
  waiting for transfers between devices  76.4 us (42%)
  Pallas kernels  44.5 us (25%)
  starting transfers between devices  18.2 us (10%)
  blocking collectives  13.3 us (7%)
  other arithmetic  12.9 us (7%)
  local copies, waits for them, and re-layouts  10.9 us (6%)
  between operations  4.11 us (2%)
    ppermute x8, waiting for transfers between devices, from_partner(): return lax.ppermute(value, axis, pairs)  76.4 us
    pallas_call x3, Pallas kernels, y_dft(): pl.pallas_call(functools.partial(y_kernel, len(inputs), tiles), out_shape...  22.6 us
    all_to_all x1, blocking collectives, sum_everywhere(): lax.all_to_all(copies, axes, split_axis=0, concat_axis=0, tiled=True)  13.3 us
    all_to_all x2, starting transfers between devices, to_planes(): return lax.all_to_all(values, 'gy', split_axis=0, concat_axis=1, tiled=True)  13 us
    pallas_call x1, Pallas kernels, x_dft(): pl.pallas_call(functools.partial(x_kernel, count), out_shape=(jax.ShapeDt...  12.2 us
    ppermute x8, starting transfers between devices, from_partner(): return lax.ppermute(value, axis, pairs)  5.21 us
    pallas_call x1, Pallas kernels, combine(): pl.pallas_call(combine_kernel, out_shape=jax.ShapeDtypeStruct(late.shape,...  4.96 us
    pallas_call x1, Pallas kernels, part_columns(): pl.pallas_call(part_kernel, out_shape=[jax.ShapeDtypeStruct((length, LANE...  4.7 us
  transfers between devices with their start and end apart: 10, of which 6 were waited for; matrix products, arithmetic and copies ran while one was open for 8% of the time, Pallas kernels for 12%

profile of v8, /device:TPU:0, one launch (start us, length us, event | category | flops | bytes accessed | tf_op | source)
XLA Modules:
  0.0 180.2 jit_solution(11661641279893166921)
XLA Ops:
  0.6 3.2 %slice.18.early_ref = f32[8,256,256]{2,1,0:T(8,128)} slice(f32[8,256,512]{2,1,0:T(8,128)} %param.6), slice={[0:8], [0:256], [0:256]} | slice | bytes 4194304 | tf_op jit(solution)/shard_map/slice | solution.py:296
  3.8 1.6 slice.19
  5.4 7.3 %all-to-all-start = ((f32[8,256,256]{2,1,0:T(8,128)}), f32[8,256,256]{2,1,0:T(8,128)}, u32[]{:S(2)}, u32[]{:S(2)}) async-start(f32[8,256,256]{2,1,0:T(8,128)} %slice.19), calls=%async_computation | async-start | bytes 4194304 | tf_op jit(solution)/shard_map/all_to_all | solution.py:24
  12.7 1.6 collective-permute-start
  14.3 0.1 pad_add_fusion.1
  14.4 0.1 pad_add_fusion
  14.5 0.5 fusion.8
  15.1 1.0 slice_sine_fusion
  16.0 1.0 slice_sine_fusion.1
  17.0 0.1 pad_maximum_fusion.9
  17.1 0.1 reshape.81.coef_ref
  17.2 0.6 log_reduce_fusion.1
  18.5 0.6 log_reduce_fusion
  19.9 1.0 fusion.19
  20.8 1.0 fusion.17
  21.9 0.1 maximum_bitcast_fusion.2
  22.0 0.1 pad_maximum_fusion.5
  22.1 0.1 maximum_bitcast_fusion
  22.2 0.1 pad_maximum_fusion.8.coef_ref
  22.3 0.2 fusion
  22.5 3.2 %fusion.3 = (f32[1,8,256,128]{3,2,1,0:T(8,128)S(1)}, f32[1,8,256,128]{3,2,1,0:T(8,128)S(1)}) fusion(), kind=kLoop, calls=%fused_computation.17 | loop fusion | flops 786432 | bytes 2097152 | tf_op jit(solution)/shard_map/sin | solution.py:314
  25.7 0.2 pad_maximum_fusion.refs_5_.refs_3_
  25.9 0.1 reduce-precision_convert_fusion
  26.1 0.1 reduce-precision_convert_fusion.1
  26.2 1.2 pad_maximum_fusion.1.refs_4_.refs_2_
  27.4 1.4 pad_maximum_fusion.3.refs_5_
  28.8 1.3 pad_maximum_fusion.2.refs_4_
  30.1 30.1 %collective-permute-done.late_ref = f32[8,256,256]{2,1,0:T(8,128)} collective-permute-done((f32[8,256,256]{2,1,0:T(8,128)}, f32[8,256,256]{2,1,0:T(8,128)}, u32[]{:S(2)}, u32[]{:S(2)}) %collective-permute-start) | collective-permute-done | bytes 2097184 | tf_op jit(solution)/shard_map/ppermute | solution.py:20
  60.2 5.0 %combine.1 = f32[8,256,256]{2,1,0:T(8,128)S(1)} custom-call(f32[1]{0:T(128)} %bitcast.sign_ref, f32[8,256,256]{2,1,0:T(8,128)} %collective-permute-done.late_ref, f32[8,256,256]{2,1,0:T(8,128)} %slice.18.early_ref), custom_call_target="tpu_custom_call" | custom-call | flops 1048576 | bytes 6291456 | tf_op jit(solution)/shard_map/combine/pallas_call | solution.py:42
  65.2 1.3 copy-done.3
  66.5 5.7 %all-to-all-start.1 = ((f32[8,256,256]{2,1,0:T(8,128)}), f32[8,256,256]{2,1,0:T(8,128)}, u32[]{:S(2)}, u32[]{:S(2)}) async-start(f32[8,256,256]{2,1,0:T(8,128)} %copy-done.3), calls=%async_computation.1 | async-start | bytes 4194304 | tf_op jit(solution)/shard_map/all_to_all | solution.py:24
  72.2 4.7 %part_columns.1 = (f32[2048,128]{1,0:T(8,128)S(1)}, f32[2048,128]{1,0:T(8,128)S(1)}) custom-call(f32[2048,256]{1,0:T(8,128)} %bitcast.1.value_ref), custom_call_target="tpu_custom_call" | custom-call | flops 524288 | bytes 4194304 | tf_op jit(solution)/shard_map/part_columns/pallas_call | solution.py:62
  76.9 1.6 collective-permute-start.1
  78.5 21.6 %collective-permute-done.1.refs_0_ = f32[2048,128]{1,0:T(8,128)S(1)} collective-permute-done((f32[2048,128]{1,0:T(8,128)S(1)}, f32[2048,128]{1,0:T(8,128)S(1)}, u32[]{:S(2)}, u32[]{:S(2)}) %collective-permute-start.1) | collective-permute-done | bytes 1048608 | tf_op jit(solution)/shard_map/ppermute | solution.py:20
  100.1 1.5 collective-permute-start.4
  101.6 1.1 collective-permute-done.2.refs_1_
  102.8 5.1 %y_dft.3.refs_2_ = bf16[4,2048,128]{2,1,0:T(8,128)(2,1)S(1)} custom-call(f32[2,4]{1,0:T(2,128)S(1)} %pad_maximum_fusion.8.coef_ref, f32[2048,128]{1,0:T(8,128)S(1)} %collective-permute-done.1.refs_0_, f32[2048,128]{1,0:T(8,128)S(1)} %collective-permute-done.2.refs_1_, f32[2048,128]{1,0:T(8,128)S(1)} %get-tuple-element.29.refs_2_, ...), custom_call_target="tpu_custom_call" | custom-call | flops 1610612736 | bytes 7340032 | tf_op jit(solution)/shard_map/y_dft/pallas_call | solution.py:186
  107.9 1.3 copy-done.4
  109.2 16.5 %collective-permute-done.4.refs_0_ = f32[2048,128]{1,0:T(8,128)} collective-permute-done((f32[2048,128]{1,0:T(8,128)S(1)}, f32[2048,128]{1,0:T(8,128)}, u32[]{:S(2)}, u32[]{:S(2)}) %collective-permute-start.4) | collective-permute-done | bytes 1048608 | tf_op jit(solution)/shard_map/ppermute | solution.py:20
  125.8 0.5 collective-permute-start.7
  126.3 6.4 %collective-permute-done.7.refs_3_ = f32[2048,128]{1,0:T(8,128)} collective-permute-done((f32[2048,128]{1,0:T(8,128)S(1)}, f32[2048,128]{1,0:T(8,128)}, u32[]{:S(2)}, u32[]{:S(2)}) %collective-permute-start.7) | collective-permute-done | bytes 1048608 | tf_op jit(solution)/shard_map/ppermute | solution.py:20
  132.7 0.6 collective-permute-done.6.refs_1_
  133.3 1.4 copy-done.1
  134.7 6.5 %y_dft.5.refs_3_ = bf16[4,2048,128]{2,1,0:T(8,128)(2,1)S(1)} custom-call(f32[2,4]{1,0:T(2,128)S(1)} %pad_maximum_fusion.8.coef_ref, f32[2048,128]{1,0:T(8,128)} %collective-permute-done.4.refs_0_, f32[2048,128]{1,0:T(8,128)} %collective-permute-done.6.refs_1_, f32[2048,128]{1,0:T(8,128)S(1)} %get-tuple-element.32.refs_2_, ...), custom_call_target="tpu_custom_call" | custom-call | flops 1610612736 | bytes 7340032 | tf_op jit(solution)/shard_map/y_dft/pallas_call | solution.py:186
  141.3 10.9 %y_dft.4 = (bf16[4,2048,128]{2,1,0:T(8,128)(2,1)S(1)}, bf16[4,2048,128]{2,1,0:T(8,128)(2,1)S(1)}) custom-call(f32[2,2]{1,0:T(2,128)S(1)} %reshape.81.coef_ref, f32[2048,256]{1,0:T(8,128)} %bitcast.23.refs_0_, f32[2048,256]{1,0:T(8,128)} %collective-permute-done.5.refs_1_, bf16[512,1536]{1,0:T(8,128)(2,1)S(1)} %copy-done.2, ...), custom_call_target="tpu_custom_call" | custom-call | flops 3221225472 | bytes 10485760 | tf_op jit(solution)/shard_map/y_dft/pallas_call | solution.py:186
  152.3 12.2 %x_dft.1 = (f32[2,1,2048,512]{3,2,1,0:T(8,128)}, f32[8,128]{1,0:T(8,128)S(1)}) custom-call(bf16[4,2048,128]{2,1,0:T(8,128)(2,1)S(1)} %get-tuple-element.35.refs_0_, bf16[4,2048,128]{2,1,0:T(8,128)(2,1)S(1)} %get-tuple-element.36.refs_1_, bf16[4,2048,128]{2,1,0:T(8,128)(2,1)S(1)} %copy-done.5, bf16[4,2048,128]{2,1,0:T(8,128)(2,1)S(1)} %y_dft.5.refs_3_, ...), custom_call_target="tpu_custom_call" | custom-call | flops 6442450944 | bytes 16777216 | tf_op jit(solution)/shard_map/x_dft/pallas_call | solution.py:258
  164.5 13.3 %all_to_all.23 = f32[32,8,128]{2,1,0:T(8,128)S(1)} all-to-all(f32[32,8,128]{2,1,0:T(8,128)S(1)} %broadcast_in_dim.2), channel_id=1, replica_groups=mesh['gx'=4,'gy'=8] {'gx','gy'}, dimensions={0} | all-to-all | bytes 262144 | tf_op jit(solution)/shard_map/all_to_all | solution.py:289
  177.8 0.6 reduce_sum.29
  (46 shorter events, 0.3 us)
Async XLA Ops:
  0.6 3.2 %copy-start.8 = (f32[8,256,512]{2,1,0:T(8,128)S(1)}, f32[8,256,512]{2,1,0:T(8,128)}, u32[]{:S(2)}) copy-start(f32[8,256,512]{2,1,0:T(8,128)} %param.6) | copy-start | bytes 12582916
  5.4 61.1 %all-to-all-start = ((f32[8,256,256]{2,1,0:T(8,128)}), f32[8,256,256]{2,1,0:T(8,128)}, u32[]{:S(2)}, u32[]{:S(2)}) async-start(f32[8,256,256]{2,1,0:T(8,128)} %slice.19), calls=%async_computation | async-start | bytes 4194304 | tf_op jit(solution)/shard_map/all_to_all | solution.py:24
  12.7 4.6 %copy-start.9 = (f32[512]{0:T(512)S(1)}, f32[512]{0:T(512)}, u32[]{:S(2)}) copy-start(f32[512]{0:T(512)} %param.8) | copy-start | bytes 6148
  12.7 5.8 %copy-start.10 = (f32[2048]{0:T(1024)S(1)}, f32[2048]{0:T(1024)}, u32[]{:S(2)}) copy-start(f32[2048]{0:T(1024)} %param.7) | copy-start | bytes 24580
  12.7 7.1 %copy-start.12 = (f32[512]{0:T(512)S(1)}, f32[512]{0:T(512)}, u32[]{:S(2)}) copy-start(f32[512]{0:T(512)} %param.11) | copy-start | bytes 6148
  12.7 7.1 %copy-start.13 = (f32[512]{0:T(512)S(1)}, f32[512]{0:T(512)}, u32[]{:S(2)}) copy-start(f32[512]{0:T(512)} %param.10) | copy-start | bytes 6148
  12.7 7.1 %copy-start.11 = (f32[2048]{0:T(1024)S(1)}, f32[2048]{0:T(1024)}, u32[]{:S(2)}) copy-start(f32[2048]{0:T(1024)} %param.9) | copy-start | bytes 24580
  12.7 47.5 %collective-permute-start = (f32[8,256,256]{2,1,0:T(8,128)}, f32[8,256,256]{2,1,0:T(8,128)}, u32[]{:S(2)}, u32[]{:S(2)}) collective-permute-start(f32[8,256,256]{2,1,0:T(8,128)} %slice.18.early_ref), channel_id=1, source_target_pairs={{0,16},{8,24},{16,0},{24,8},{1,17},{9,25},{17,1},{25,9},{2,18},{10... | collective-permute-start | bytes 6291464 | tf_op jit(solution)/shard_map/ppermute | solution.py:20
  65.2 1.3 copy-start.3
  66.5 59.3 %all-to-all-start.1 = ((f32[8,256,256]{2,1,0:T(8,128)}), f32[8,256,256]{2,1,0:T(8,128)}, u32[]{:S(2)}, u32[]{:S(2)}) async-start(f32[8,256,256]{2,1,0:T(8,128)} %copy-done.3), calls=%async_computation.1 | async-start | bytes 4194304 | tf_op jit(solution)/shard_map/all_to_all | solution.py:24
  72.2 30.6 %copy-start = (bf16[512,1536]{1,0:T(8,128)(2,1)S(1)}, bf16[512,1536]{1,0:T(8,128)(2,1)}, u32[]{:S(2)}) copy-start(bf16[512,1536]{1,0:T(8,128)(2,1)} %pad_maximum_fusion.1.refs_4_.refs_2_) | copy-start | bytes 4718596
  76.9 23.2 %collective-permute-start.1 = (f32[2048,128]{1,0:T(8,128)S(1)}, f32[2048,128]{1,0:T(8,128)S(1)}, u32[]{:S(2)}, u32[]{:S(2)}) collective-permute-start(f32[2048,128]{1,0:T(8,128)S(1)} %get-tuple-element.29.refs_2_), channel_id=1, source_target_pairs={{0,16},{8,24},{16,0},{24,8},{1,17},{9,25},{17,1},{25,9},{2,18},{10... | collective-permute-start | bytes 3145736 | tf_op jit(solution)/shard_map/ppermute | solution.py:20
  78.5 23.1 %collective-permute-start.3 = (f32[2048,128]{1,0:T(8,128)S(1)}, f32[2048,128]{1,0:T(8,128)S(1)}, u32[]{:S(2)}, u32[]{:S(2)}) collective-permute-start(f32[2048,128]{1,0:T(8,128)S(1)} %get-tuple-element.29.refs_2_), channel_id=1, source_target_pairs={{0,8},{8,0},{16,24},{24,16},{1,9},{9,1},{17,25},{25,17},{2,10},{10... | collective-permute-start | bytes 3145736 | tf_op jit(solution)/shard_map/ppermute | solution.py:20
  100.1 2.7 %collective-permute-start.2 = (f32[2048,128]{1,0:T(8,128)S(1)}, f32[2048,128]{1,0:T(8,128)S(1)}, u32[]{:S(2)}, u32[]{:S(2)}) collective-permute-start(f32[2048,128]{1,0:T(8,128)S(1)} %collective-permute-done.1.refs_0_), channel_id=1, source_target_pairs={{0,8},{8,0},{16,24},{24,16},{1,9},{9,1},{17,25},{25,17},{2,10},{10... | collective-permute-start | bytes 3145736 | tf_op jit(solution)/shard_map/ppermute | solution.py:20
  100.1 25.7 %collective-permute-start.4 = (f32[2048,128]{1,0:T(8,128)S(1)}, f32[2048,128]{1,0:T(8,128)}, u32[]{:S(2)}, u32[]{:S(2)}) collective-permute-start(f32[2048,128]{1,0:T(8,128)S(1)} %get-tuple-element.32.refs_2_), channel_id=1, source_target_pairs={{0,16},{8,24},{16,0},{24,8},{1,17},{9,25},{17,1},{25,9},{2,18},{10... | collective-permute-start | bytes 3145736 | tf_op jit(solution)/shard_map/ppermute | solution.py:20
  107.9 1.3 copy-start.4
  125.8 15.5 %collective-permute-start.5 = (f32[2048,256]{1,0:T(8,128)}, f32[2048,256]{1,0:T(8,128)}, u32[]{:S(2)}, u32[]{:S(2)}) collective-permute-start(f32[2048,256]{1,0:T(8,128)} %bitcast.23.refs_0_), channel_id=1, source_target_pairs={{0,8},{8,0},{16,24},{24,16},{1,9},{9,1},{17,25},{25,17},{2,10},{10... | collective-permute-start | bytes 6291464 | tf_op jit(solution)/shard_map/ppermute | solution.py:20
  125.8 6.9 %collective-permute-start.7 = (f32[2048,128]{1,0:T(8,128)S(1)}, f32[2048,128]{1,0:T(8,128)}, u32[]{:S(2)}, u32[]{:S(2)}) collective-permute-start(f32[2048,128]{1,0:T(8,128)S(1)} %get-tuple-element.32.refs_2_), channel_id=1, source_target_pairs={{0,8},{8,0},{16,24},{24,16},{1,9},{9,1},{17,25},{25,17},{2,10},{10... | collective-permute-start | bytes 3145736 | tf_op jit(solution)/shard_map/ppermute | solution.py:20
  126.3 7.0 %collective-permute-start.6 = (f32[2048,128]{1,0:T(8,128)}, f32[2048,128]{1,0:T(8,128)}, u32[]{:S(2)}, u32[]{:S(2)}) collective-permute-start(f32[2048,128]{1,0:T(8,128)} %collective-permute-done.4.refs_0_), channel_id=1, source_target_pairs={{0,8},{8,0},{16,24},{24,16},{1,9},{9,1},{17,25},{25,17},{2,10},{10... | collective-permute-start | bytes 3145736 | tf_op jit(solution)/shard_map/ppermute | solution.py:20
  133.3 1.4 copy-start.1
  134.7 6.6 %copy-start.2 = (bf16[512,1536]{1,0:T(8,128)(2,1)S(1)}, bf16[512,1536]{1,0:T(8,128)(2,1)}, u32[]{:S(2)}) copy-start(bf16[512,1536]{1,0:T(8,128)(2,1)} %pad_maximum_fusion.1.refs_4_.refs_2_) | copy-start | bytes 4718596
  141.2 11.0 %copy-start.5 = (bf16[4,2048,128]{2,1,0:T(8,128)(2,1)S(1)}, bf16[4,2048,128]{2,1,0:T(8,128)(2,1)}, u32[]{:S(2)}) copy-start(bf16[4,2048,128]{2,1,0:T(8,128)(2,1)} %copy-done.4) | copy-start | bytes 6291460
  141.2 11.0 %copy-start.6 = (bf16[1536,512]{1,0:T(8,128)(2,1)S(1)}, bf16[1536,512]{1,0:T(8,128)(2,1)}, u32[]{:S(2)}) copy-start(bf16[1536,512]{1,0:T(8,128)(2,1)} %pad_maximum_fusion.3.refs_5_) | copy-start | bytes 4718596
  141.2 11.0 %copy-start.7 = (bf16[1536,512]{1,0:T(8,128)(2,1)S(1)}, bf16[1536,512]{1,0:T(8,128)(2,1)}, u32[]{:S(2)}) copy-start(bf16[1536,512]{1,0:T(8,128)(2,1)} %pad_maximum_fusion.2.refs_4_) | copy-start | bytes 4718596

commit v9 on v7

--- a/solution.py
+++ b/solution.py
@@ -11,7 +11,7 @@
 precision_top = lax.Precision.HIGHEST
 RADIX = 8
 LANES = 128
-SMALL_BYTES, Y_BYTES, X_BYTES = [size * 1024 * 1024 for size in (8, 32, 24)]
+SMALL_BYTES, Y_BYTES, X_BYTES = [size * 1024 * 1024 for size in (8, 28, 26)]
 
 
 def from_partner(value, axis, stride):
@@ -49,7 +49,7 @@
         grid=(planes,),
         in_specs=[pl.BlockSpec(memory_space=pltpu.SMEM), block, block],
         out_specs=block,
-        cost_estimate=pl.CostEstimate(flops=2 * late.size, bytes_accessed=12 * late.size, transcendentals=0),
+        cost_estimate=pl.CostEstimate(flops=2 * late.size, bytes_accessed=100 * late.size, transcendentals=0),
         compiler_params=pltpu.CompilerParams(vmem_limit_bytes=SMALL_BYTES),
         name="combine",
     )(sign, late, early)
@@ -111,125 +111,166 @@
     return jnp.dot(left, right, preferred_element_type=jnp.float32)
 
 
-def y_kernel(count, pick, coef_ref, *refs):
-    inputs, (table_ref, twist_ref, *out_refs, mix_ref, split_ref, step_ref) = refs[:count], refs[count:]
+def y_kernel(count, pick, tiles, coef_ref, *refs):
+    inputs, refs = refs[:count], refs[count:]
+    (table_hbm, twist_hbm), out_refs, scratch = refs[:2], refs[2 : 2 + len(tiles)], refs[2 + len(tiles) :]
+    table_ref, twist_ref, mix_ref, split_ref, step_ref, sems = scratch
+    copies = [
+        pltpu.make_async_copy(source, target, sems.at[place])
+        for place, (source, target) in enumerate(((table_hbm, table_ref), (twist_hbm, twist_ref)))
+    ]
+    for copy in copies:
+        copy.start()
     length = mix_ref.shape[1]
     inner = length // RADIX
-    rows_each = 128
-    for start in range(0, length, rows_each):
+    half = inner // 2
+
+    def mix(place, start, rows_each):
         rows = pl.ds(start, rows_each)
+        lanes = (0, LANES) if pick else (tiles[place] * LANES,)
+        parts = [[ref[rows, pl.ds(lane, LANES)] for ref in inputs] for lane in lanes]
         for which in range(2):
-            tiles = []
-            for lane in (0, LANES):
-                mixed = inputs[0][rows, pl.ds(lane, LANES)] * coef_ref[which, 0]
-                for place in range(1, count):
-                    mixed = mixed + inputs[place][rows, pl.ds(lane, LANES)] * coef_ref[which, place]
-                tiles.append(mixed)
-            for tile in range(2):
-                mix_ref[2 * tile + which, rows, :] = pick_columns(*tiles, tile) if pick else tiles[tile]
-    for tile, out_ref in enumerate(out_refs):
+            mixed = [sum(part * coef_ref[which, k] for k, part in enumerate(group)) for group in parts]
+            mix_ref[which, rows, :] = pick_columns(*mixed, tiles[place]) if pick else mixed[0]
+
+    def split(place, s):
         for which in range(2):
-            for s in range(RADIX):
-                high, low = split_value(mix_ref[2 * tile + which, pl.ds(s, inner, stride=RADIX), :])
-                for place, value in enumerate((high, high, low)):
-                    split_ref[tile, pl.ds((2 * place + which) * inner, inner), pl.ds(s * LANES, LANES)] = value
-        half = inner // 2
+            high, low = split_value(mix_ref[which, pl.ds(s, inner, stride=RADIX), :])
+            for k, value in enumerate((high, high, low)):
+                split_ref[place, pl.ds((2 * k + which) * inner, inner), pl.ds(s * LANES, LANES)] = value
+
+    def multiply(place, part, chunk):
+        cols = pl.ds(2 * chunk * LANES, 2 * LANES)
+        step_ref[place, part, :, cols] = dot(table_ref[pl.ds(part * inner, inner), :], split_ref[place, :, cols])
+
+    def finish(place, part, start):
+        values = []
+        for s in range(RADIX):
+            cols = pl.ds(s * LANES, LANES)
+            re = step_ref[place, part, pl.ds(start, 16), cols]
+            im = step_ref[place, part, pl.ds(half + start, 16), cols]
+            if s:
+                cos, sin = [twist_ref[k, s, pl.ds(part * half + start, 16), :] for k in range(2)]
+                re, im = re * cos - im * sin, re * sin + im * cos
+            values.append((re, im))
+        for kb, pair in enumerate(small_fft(values)):
+            rows = pl.ds(kb * inner + part * half + start, 16)
+            for which in range(2):
+                high, low = split_value(pair[which])
+                out_refs[place][2 * which, rows, :] = high
+                out_refs[place][2 * which + 1, rows, :] = low
+
+    before = None
+    for place in range(len(tiles)):
+        for start in range(0, length, 128):
+            mix(place, start, 128)
+        for s in range(RADIX):
+            split(place, s)
         for part in range(2):
-            step_ref[tile, part] = dot(table_ref[pl.ds(part * inner, inner), :], split_ref[tile])
-            for start in range(0, half, 16):
-                values = []
-                for s in range(RADIX):
-                    cols = pl.ds(s * LANES, LANES)
-                    re = step_ref[tile, part, pl.ds(start, 16), cols]
-                    im = step_ref[tile, part, pl.ds(half + start, 16), cols]
-                    if s:
-                        cos, sin = [twist_ref[k, s, pl.ds(part * half + start, 16), :] for k in range(2)]
-                        re, im = re * cos - im * sin, re * sin + im * cos
-                    values.append((re, im))
-                for kb, pair in enumerate(small_fft(values)):
-                    rows = pl.ds(kb * inner + part * half + start, 16)
-                    for which in range(2):
-                        high, low = split_value(pair[which])
-                        out_ref[2 * which, rows, :] = high
-                        out_ref[2 * which + 1, rows, :] = low
-
-
-def y_dft(inputs, pick, coefs, table, twist):
+            if place == part == 0:
+                copies[0].wait()
+            if before == (0, 0):
+                copies[1].wait()
+            for chunk in range(RADIX // 2):
+                multiply(place, part, chunk)
+                if before is not None:
+                    for start in range(chunk * half // 4, (chunk + 1) * half // 4, 16):
+                        finish(*before, start)
+            before = (place, part)
+    for start in range(0, half, 16):
+        finish(*before, start)
+
+
+def y_dft(inputs, pick, tiles, coefs, table, twist):
     length = inputs[0].shape[0]
     inner = length // RADIX
-    whole = pl.BlockSpec(memory_space=pltpu.VMEM)
+    count = len(tiles)
+    whole, anywhere = pl.BlockSpec(memory_space=pltpu.VMEM), pl.BlockSpec(memory_space=pl.ANY)
     return pl.pallas_call(
-        functools.partial(y_kernel, len(inputs), pick),
-        out_shape=[jax.ShapeDtypeStruct((4, length, LANES), jnp.bfloat16)] * 2,
-        in_specs=[pl.BlockSpec(memory_space=pltpu.SMEM)] + [whole] * (len(inputs) + 2),
-        out_specs=[whole] * 2,
+        functools.partial(y_kernel, len(inputs), pick, tiles),
+        out_shape=[jax.ShapeDtypeStruct((4, length, LANES), jnp.bfloat16)] * count,
+        in_specs=[pl.BlockSpec(memory_space=pltpu.SMEM)] + [whole] * len(inputs) + [anywhere] * 2,
+        out_specs=[whole] * count,
         scratch_shapes=[
-            pltpu.VMEM((4, length, LANES), jnp.float32),
-            pltpu.VMEM((2, 6 * inner, RADIX * LANES), jnp.bfloat16),
-            pltpu.VMEM((2, 2, inner, RADIX * LANES), jnp.float32),
+            pltpu.VMEM(table.shape, table.dtype),
+            pltpu.VMEM(twist.shape, twist.dtype),
+            pltpu.VMEM((2, length, LANES), jnp.float32),
+            pltpu.VMEM((count, 6 * inner, RADIX * LANES), jnp.bfloat16),
+            pltpu.VMEM((count, 2, inner, RADIX * LANES), jnp.float32),
+            pltpu.SemaphoreType.DMA((2,)),
         ],
         compiler_params=pltpu.CompilerParams(vmem_limit_bytes=Y_BYTES),
         cost_estimate=pl.CostEstimate(
-            flops=48 * inner * length * LANES, bytes_accessed=8 * length * LANES * (len(inputs) + 3), transcendentals=0
+            flops=80 * inner * length * LANES * count,
+            bytes_accessed=8 * length * LANES * (len(inputs) + 3),
+            transcendentals=0,
         ),
         name="y_dft",
     )(coefs, *inputs, table, twist)
 
 
-def x_product(parts, table_ref, rows):
-    high = [ref[which, rows, :] for ref in parts for which in (0, 2)]
-    low = [ref[which, rows, :] for ref in parts for which in (1, 3)]
-    return dot(jnp.concatenate(high + low + high, axis=1), table_ref[...])
-
-
 def x_kernel(count, *refs):
     parts, (even_ref, odd_ref, row_ref, col_ref, out_ref, total_ref) = refs[: 2 * count], refs[2 * count :]
-    half = even_ref.shape[1] // 2
-    lanes = LANES
-    total = None
-    spans = [pl.ds(start, 2 * lanes) for start in range(0, out_ref.shape[2], 2 * lanes)]
-    products = [(x_product(parts[:count], even_ref, rows), x_product(parts[count:], odd_ref, rows)) for rows in spans]
-    for rows, (even, odd) in zip(spans, products):
+    columns = out_ref.shape[3]
+    lanes, rows_each, tiles = LANES, 2 * LANES, columns // (2 * LANES)
+    totals = []
+
+    def left(refs, rows):
+        high, low = [[ref[k + which, rows, :] for ref in refs for k in (0, 2)] for which in range(2)]
+        return jnp.concatenate(high + low + high, axis=1)
+
+    def multiply(sides, tile):
+        cols = pl.ds(tile * 2 * lanes, 2 * lanes)
+        return [dot(side, table_ref[:, cols]) for side, table_ref in zip(sides, (even_ref, odd_ref))]
+
+    def finish(start, tile, even, odd):
+        rows = pl.ds(start, rows_each)
         row_scale, row_rate = [
             jnp.concatenate(
                 [
                     jnp.broadcast_to(row_ref[which, 0, c : c + 1, :], (lanes, lanes)).T
-                    for c in range(rows.start // lanes, rows.start // lanes + 2)
+                    for c in range(start // lanes, (start + rows_each) // lanes)
                 ],
                 0,
             )
             for which in range(2)
         ]
-        for tile in range(half // lanes):
-            real, imag = [slice(start, start + lanes) for start in (tile * lanes, half + tile * lanes)]
-            for upper in range(2):
-                cols = pl.ds(upper * half + tile * lanes, lanes)
-                spec_real = even[:, real] - odd[:, real] if upper else even[:, real] + odd[:, real]
-                spec_imag = even[:, imag] - odd[:, imag] if upper else even[:, imag] + odd[:, imag]
-                col_scale, col_shift, col_mix = col_ref[0:1, cols], col_ref[1:2, cols], col_ref[2:3, cols]
-                scale = row_scale * col_scale
-                latent_u = spec_real * scale
-                latent_v = spec_imag * scale
-                log_scale = row_rate * jnp.tanh(latent_u + col_shift)
-                latent_w = latent_v * jnp.exp(log_scale) + col_mix * latent_u
-                out_ref[0, 0, rows, cols] = latent_u
-                out_ref[1, 0, rows, cols] = latent_w
-                terms = log_scale - 0.5 * (latent_u * latent_u + latent_w * latent_w)
-                terms = jnp.sum(terms.reshape(-1, 8, lanes), axis=0)
-                total = terms if total is None else total + terms
+        for upper in range(2):
+            cols = pl.ds(upper * columns // 2 + tile * lanes, lanes)
+            spec = even - odd if upper else even + odd
+            col_scale, col_shift, col_mix = col_ref[0:1, cols], col_ref[1:2, cols], col_ref[2:3, cols]
+            scale = row_scale * col_scale
+            latent_u = spec[:, :lanes] * scale
+            latent_v = spec[:, lanes:] * scale
+            log_scale = row_rate * jnp.tanh(latent_u + col_shift)
+            latent_w = latent_v * jnp.exp(log_scale) + col_mix * latent_u
+            out_ref[0, 0, rows, cols] = latent_u
+            out_ref[1, 0, rows, cols] = latent_w
+            terms = log_scale - 0.5 * (latent_u * latent_u + latent_w * latent_w)
+            totals.append(jnp.sum(terms.reshape(-1, 8, lanes), axis=0))
+
+    before = None
+    for start in range(0, out_ref.shape[2], rows_each):
+        sides = [left(group, pl.ds(start, rows_each)) for group in (parts[:count], parts[count:])]
+        for tile in range(tiles):
+            products = multiply(sides, tile)
+            if before is not None:
+                finish(*before)
+            before = (start, tile, *products)
+    finish(*before)
 
     @pl.when(pl.program_id(0) == 0)
     def _():
         total_ref[...] = jnp.zeros_like(total_ref)
 
-    total_ref[...] += total
+    total_ref[...] += sum(totals)
 
 
 def x_dft(even_parts, odd_parts, even_table, odd_table, row_pair, col_trio):
     parts, count, length = even_parts + odd_parts, len(even_parts), even_parts[0].shape[1]
     columns = even_table.shape[1]
     rows = length // row_pair.shape[1]
-    fixed = [pl.BlockSpec(table.shape, lambda i: (0, 0), pipeline_mode=pl.Buffered(1)) for table in (even_table, odd_table)]
+    fixed = [pl.BlockSpec(memory_space=pltpu.VMEM)] * 2
     return pl.pallas_call(
         functools.partial(x_kernel, count),
         out_shape=(
@@ -292,8 +333,8 @@
 
     def x_table(odd):
         rows = jnp.concatenate([order + (2 * width + odd), order + odd])
-        cos, sin = [part[:, : 2 * width].reshape(2, width, 2 * width) for part in x_tables(rows, columns, 4, position)]
-        table = jnp.stack([jnp.concatenate([cos, sin], 2), jnp.concatenate([-sin, cos], 2)], 1)
+        cos, sin = [part[:, : 2 * width].reshape(2, width, 2, width) for part in x_tables(rows, columns, 4, position)]
+        table = jnp.stack([jnp.stack([cos, sin], 3), jnp.stack([-sin, cos], 3)], 1)
         return split_table(table.reshape(columns, columns), 0, (0, 0, 1))
 
     norm = 1.0 / math.sqrt(length * columns * 4)
@@ -310,8 +351,10 @@
 
     second_b = from_partner(first_b, "gx", 1)
     group = [second_b, from_partner(second_b, "gx", 0), first_b, from_partner(first_b, "gx", 0)]
-    even_b, odd_b = y_dft(group, True, coefs_b, y_table, twist)
-    even_a, odd_a = y_dft([second_a, from_partner(second_a, "gx", 0)], False, coefs_a, y_table, twist)
+    even_b = y_dft(group, True, (0,), coefs_b, y_table, twist)[0]
+    even_b, second_a = lax.optimization_barrier((even_b, second_a))
+    odd_b = y_dft(group, True, (1,), coefs_b, y_table, twist)[0]
+    even_a, odd_a = y_dft([second_a, from_partner(second_a, "gx", 0)], False, (0, 1), coefs_a, y_table, twist)
     latent, tile = x_dft([even_b, even_a], [odd_b, odd_a], even_table, odd_table, row_pair, col_trio)
     tile = tile + fixed / tile.size
     modes = length * columns * lax.axis_size("gx") * lax.axis_size("gy")

time: 168 us -> 177 us (1.054)
  local copies, waits for them, and re-layouts: 9.89 us -> 29.8 us
  waiting for transfers between devices: 73.5 us -> 54.2 us
  other arithmetic: 14.9 us -> 20.1 us
  Pallas kernels: 34.8 us -> 38.6 us
  blocking collectives: 15.8 us -> 13 us
    ppermute x5, waiting for transfers between devices: 69.1 us -> 54.2 us  [from_partner(): return lax.ppermute(value, axis, pairs)]
    unnamed x24 -> x40, local copies, waits for them, and re-layouts: 4.44 us -> 13.1 us
    reshape x0 -> x2, local copies, waits for them, and re-layouts: none -> 5.16 us  [x_table(): return split_table(table.reshape(columns, columns), 0, (0, 0, 1))]
    pallas_call x2 -> x3, Pallas kernels: 18.7 us -> 23.7 us  [y_dft(): pl.pallas_call(functools.partial(y_kernel, len(inputs), pick, tiles), out...]
    another operation x0 -> x4, local copies, waits for them, and re-layouts: none -> 4.61 us  [x_table(): table = jnp.stack([jnp.stack([cos, sin], 3), jnp.stack([-sin, cos], 3)], 1)]
    another operation x4, other arithmetic: 1.3 us -> 5.89 us  [x_table(): table = jnp.stack([jnp.stack([cos, sin], 3), jnp.stack([-sin, cos], 3)], 1)]
    all_to_all x2, waiting for transfers between devices: 4.38 us -> 0.01 us  [to_planes(): return lax.all_to_all(values, 'gy', split_axis=0, concat_axis=1, tiled=True)]
    all_to_all x1, blocking collectives: 15.8 us -> 13 us  [sum_everywhere(): lax.all_to_all(copies, axes, split_axis=0, concat_axis=0, tiled=True)]
  transfers between devices with their start and end apart: 7 -> 7, of which waited for: 5 -> 3; matrix products, arithmetic and copies ran while one was open for 11% -> 19% of each run, Pallas kernels for 9% -> 11%
where the time goes in v9:
time: 177 us; the launch traced here: 176 us
  waiting for transfers between devices  54.2 us (31%)
  Pallas kernels  38.6 us (22%)
  local copies, waits for them, and re-layouts  29.8 us (17%)
  other arithmetic  20.1 us (11%)
  starting transfers between devices  16.2 us (9%)
  blocking collectives  13 us (7%)
  between operations  4.05 us (2%)
    ppermute x5, waiting for transfers between devices, from_partner(): return lax.ppermute(value, axis, pairs)  54.2 us
    pallas_call x3, Pallas kernels, y_dft(): pl.pallas_call(functools.partial(y_kernel, len(inputs), pick, tiles), out...  23.7 us
    unnamed x40, local copies, waits for them, and re-layouts  13.1 us
    all_to_all x1, blocking collectives, sum_everywhere(): lax.all_to_all(copies, axes, split_axis=0, concat_axis=0, tiled=True)  13 us
    all_to_all x2, starting transfers between devices, to_planes(): return lax.all_to_all(values, 'gy', split_axis=0, concat_axis=1, tiled=True)  13 us
    pallas_call x1, Pallas kernels, x_dft(): pl.pallas_call(functools.partial(x_kernel, count), out_shape=(jax.ShapeDt...  10 us
    another operation x4, other arithmetic, x_table(): table = jnp.stack([jnp.stack([cos, sin], 3), jnp.stack([-sin, cos], 3)], 1)  5.89 us
    reshape x2, local copies, waits for them, and re-layouts, x_table(): return split_table(table.reshape(columns, columns), 0, (0, 0, 1))  5.16 us
  transfers between devices with their start and end apart: 7, of which 3 were waited for; matrix products, arithmetic and copies ran while one was open for 19% of the time, Pallas kernels for 11%

profile of v9, /device:TPU:0, one launch (start us, length us, event | category | flops | bytes accessed | tf_op | source)
XLA Modules:
  0.0 176.0 jit_solution(15318832520404290492)
XLA Ops:
  0.6 2.0 %slice.18.early_ref = f32[8,256,256]{2,1,0:T(8,128)S(1)} slice(f32[8,256,512]{2,1,0:T(8,128)} %param.6), slice={[0:8], [0:256], [0:256]} | slice | bytes 4194304 | tf_op jit(solution)/shard_map/slice | solution.py:312
  2.6 0.8 copy-done.13
  3.4 1.6 slice.19
  5.0 7.3 %all-to-all-start = ((f32[8,256,256]{2,1,0:T(8,128)}), f32[8,256,256]{2,1,0:T(8,128)}, u32[]{:S(2)}, u32[]{:S(2)}) async-start(f32[8,256,256]{2,1,0:T(8,128)} %slice.19), calls=%async_computation | async-start | bytes 4194304 | tf_op jit(solution)/shard_map/all_to_all | solution.py:24
  12.3 1.5 collective-permute-start
  13.8 0.5 fusion.8
  14.4 1.6 slice_sine_fusion
  16.3 0.3 neg.32
  16.5 1.2 stack_reshape.16
  17.8 1.7 slice_sine_fusion.1
  19.4 0.9 maximum_bitcast_fusion.2
  20.3 1.5 pad_maximum_fusion.5
  22.0 2.1 %reshape.188 = f32[512,512]{1,0:T(8,128)S(1)} reshape(f32[2,2,128,2,2,128]{5,4,3,2,1,0:T(2,128)} %pad_maximum_fusion.5) | data formatting | bytes 2097152 | tf_op jit(solution)/shard_map/reshape | solution.py:338
  24.0 1.2 stack_reshape.15
  25.2 1.0 neg.31
  26.2 1.9 %stack_reshape.14 = f32[2,128,2,1,128]{4,3,2,1,0:T(1,128)} reshape(f32[256,256]{1,0:T(8,128)} %get-tuple-element.49) | data formatting | bytes 524288 | tf_op jit(solution)/shard_map/stack;reshape | solution.py:337
  28.2 2.1 %maximum_bitcast_fusion = (f32[2,1,128,2,2,128]{5,4,3,2,1,0:T(2,128)S(1)}, f32[2,1,128,2,2,128]{5,4,3,2,1,0:T(2,128)S(1)}) fusion(f32[2,128,2,1,128]{4,3,2,1,0:T(1,128)S(1)} %stack_reshape.15, f32[2,128,2,1,128]{4,3,2,1,0:T(1,128)} %stack_reshape.14, f32[2,128,2,1,128]{4,3,2,1,0:T(1,128)} %neg.31), kind=kLoop, calls=%fused_computation.35 | loop fusion | flops 262144 | bytes 1835008 | tf_op jit(solution)/shard_map/stack | solution.py:337
  30.3 1.5 pad_maximum_fusion.4
  31.7 3.1 %reshape.187 = f32[512,512]{1,0:T(8,128)} reshape(f32[2,2,128,2,2,128]{5,4,3,2,1,0:T(2,128)} %pad_maximum_fusion.4) | data formatting | bytes 2097152 | tf_op jit(solution)/shard_map/reshape | solution.py:338
  34.8 0.7 log_reduce_fusion.1
  36.2 0.7 log_reduce_fusion
  37.6 1.1 fusion.19
  38.9 3.2 %fusion.3 = (f32[1,8,256,128]{3,2,1,0:T(8,128)S(1)}, f32[1,8,256,128]{3,2,1,0:T(8,128)S(1)}) fusion(), kind=kLoop, calls=%fused_computation.17 | loop fusion | flops 786432 | bytes 2097152 | tf_op jit(solution)/shard_map/sin | solution.py:331
  42.1 1.5 pad_maximum_fusion.refs_5_.refs_3_
  44.0 0.9 copy-done.14
  45.0 1.3 pad_maximum_fusion.1.refs_4_.refs_2_
  46.3 1.3 pad_maximum_fusion.3.refs_5_
  47.6 1.3 pad_maximum_fusion.2.refs_4_
  48.9 10.6 %collective-permute-done.late_ref = f32[8,256,256]{2,1,0:T(8,128)} collective-permute-done((f32[8,256,256]{2,1,0:T(8,128)S(1)}, f32[8,256,256]{2,1,0:T(8,128)}, u32[]{:S(2)}, u32[]{:S(2)}) %collective-permute-start) | collective-permute-done | bytes 2097184 | tf_op jit(solution)/shard_map/ppermute | solution.py:20
  59.5 4.9 %combine.1 = f32[8,256,256]{2,1,0:T(8,128)S(1)} custom-call(f32[1]{0:T(128)} %bitcast.sign_ref, f32[8,256,256]{2,1,0:T(8,128)} %collective-permute-done.late_ref, f32[8,256,256]{2,1,0:T(8,128)S(1)} %slice.18.early_ref), custom_call_target="tpu_custom_call" | custom-call | flops 1048576 | bytes 52428800 | tf_op jit(solution)/shard_map/combine/pallas_call | solution.py:46
  64.4 1.4 copy-done
  65.8 1.5 collective-permute-start.1
  67.3 5.7 %all-to-all-start.1 = ((f32[8,256,256]{2,1,0:T(8,128)}), f32[8,256,256]{2,1,0:T(8,128)}, u32[]{:S(2)}, u32[]{:S(2)}) async-start(f32[8,256,256]{2,1,0:T(8,128)} %copy-done), calls=%async_computation.1 | async-start | bytes 4194304 | tf_op jit(solution)/shard_map/all_to_all | solution.py:24
  73.0 39.2 %collective-permute-done.1.refs_0_ = f32[2048,256]{1,0:T(8,128)} collective-permute-done((f32[2048,256]{1,0:T(8,128)}, f32[2048,256]{1,0:T(8,128)}, u32[]{:S(2)}, u32[]{:S(2)}) %collective-permute-start.1) | collective-permute-done | bytes 2097184 | tf_op jit(solution)/shard_map/ppermute | solution.py:20
  112.3 4.4 %collective-permute-done.2.refs_1_ = f32[2048,256]{1,0:T(8,128)S(1)} collective-permute-done((f32[2048,256]{1,0:T(8,128)}, f32[2048,256]{1,0:T(8,128)S(1)}, u32[]{:S(2)}, u32[]{:S(2)}) %collective-permute-start.2) | collective-permute-done | bytes 2097184 | tf_op jit(solution)/shard_map/ppermute | solution.py:20
  116.7 1.4 copy-done.4
  118.1 6.8 %y_dft.3.refs_0_ = bf16[4,2048,128]{2,1,0:T(8,128)(2,1)S(1)} custom-call(f32[2,4]{1,0:T(2,128)S(1)} %pad_maximum_fusion.8.coef_ref, f32[2048,256]{1,0:T(8,128)} %collective-permute-done.1.refs_0_, f32[2048,256]{1,0:T(8,128)S(1)} %collective-permute-done.2.refs_1_, f32[2048,256]{1,0:T(8,128)} %bitcast.1.refs_2_, ...), custom_call_target="tpu_custom_call" | custom-call | flops 5368709120 | bytes 14680064 | tf_op jit(solution)/shard_map/y_dft/pallas_call | solution.py:189
  124.9 1.3 copy-done.7
  126.2 1.4 copy-done.9
  127.5 1.3 copy-done.11
  129.0 1.4 copy-done.5
  130.4 1.6 copy-done.8
  132.0 1.6 copy-done.10
  133.6 6.9 %y_dft.5.refs_2_ = bf16[4,2048,128]{2,1,0:T(8,128)(2,1)S(1)} custom-call(f32[2,4]{1,0:T(2,128)S(1)} %pad_maximum_fusion.8.coef_ref, f32[2048,256]{1,0:T(8,128)} %collective-permute-done.1.refs_0_, f32[2048,256]{1,0:T(8,128)S(1)} %copy-done.10, f32[2048,256]{1,0:T(8,128)} %bitcast.1.refs_2_, f32[2048,256]{1,0:T(8,128)S(1)} %copy-done.8, ...), custom_call_target="tpu_custom_call" | custom-call | flops 5368709120 | bytes 14680064 | tf_op jit(solution)/shard_map/y_dft/pallas_call | solution.py:189
  140.6 10.0 %y_dft.4 = (bf16[4,2048,128]{2,1,0:T(8,128)(2,1)S(1)}, bf16[4,2048,128]{2,1,0:T(8,128)(2,1)S(1)}) custom-call(f32[2,2]{1,0:T(2,128)S(1)} %reshape.189.coef_ref, f32[2048,256]{1,0:T(8,128)} %bitcast.18.refs_0_, f32[2048,256]{1,0:T(8,128)} %collective-permute-done.4.refs_1_, bf16[512,1536]{1,0:T(8,128)(2,1)S(1)} %copy-done.6, f32[2,8,256,128]{3,2,1,0:T(8,128)S(1)} %copy-done.1), custom_call_target="tpu_custom_call" | custom-call | flops 10737418240 | bytes 10485760 | tf_op jit(solution)/shard_map/y_dft/pallas_call | solution.py:189
  150.6 10.0 %x_dft.1 = (f32[2,1,2048,512]{3,2,1,0:T(8,128)}, f32[8,128]{1,0:T(8,128)S(1)}) custom-call(bf16[4,2048,128]{2,1,0:T(8,128)(2,1)S(1)} %copy-done.12, bf16[4,2048,128]{2,1,0:T(8,128)(2,1)S(1)} %get-tuple-element.31.refs_1_, bf16[4,2048,128]{2,1,0:T(8,128)(2,1)S(1)} %y_dft.5.refs_2_, bf16[4,2048,128]{2,1,0:T(8,128)(2,1)S(1)} %get-tuple-element.32.refs_3_, ...), custom_call_target="tpu_custom_call" | custom-call | flops 6442450944 | bytes 16777216 | tf_op jit(solution)/shard_map/x_dft/pallas_call | solution.py:274
  160.6 13.0 %all_to_all.23 = f32[32,8,128]{2,1,0:T(8,128)S(1)} all-to-all(f32[32,8,128]{2,1,0:T(8,128)S(1)} %broadcast_in_dim.2), channel_id=1, replica_groups=mesh['gx'=4,'gy'=8] {'gx','gy'}, dimensions={0} | all-to-all | bytes 262144 | tf_op jit(solution)/shard_map/all_to_all | solution.py:305
  173.6 0.6 reduce_sum.29
  (56 shorter events, 1.4 us)
Async XLA Ops:
  0.6 2.8 %copy-start.13 = (f32[8,256,512]{2,1,0:T(8,128)S(1)}, f32[8,256,512]{2,1,0:T(8,128)}, u32[]{:S(2)}) copy-start(f32[8,256,512]{2,1,0:T(8,128)} %param.6) | copy-start | bytes 12582916
  5.0 60.8 %all-to-all-start = ((f32[8,256,256]{2,1,0:T(8,128)}), f32[8,256,256]{2,1,0:T(8,128)}, u32[]{:S(2)}, u32[]{:S(2)}) async-start(f32[8,256,256]{2,1,0:T(8,128)} %slice.19), calls=%async_computation | async-start | bytes 4194304 | tf_op jit(solution)/shard_map/all_to_all | solution.py:24
  12.3 47.2 %collective-permute-start = (f32[8,256,256]{2,1,0:T(8,128)S(1)}, f32[8,256,256]{2,1,0:T(8,128)}, u32[]{:S(2)}, u32[]{:S(2)}) collective-permute-start(f32[8,256,256]{2,1,0:T(8,128)S(1)} %slice.18.early_ref), channel_id=1, source_target_pairs={{0,16},{8,24},{16,0},{24,8},{1,17},{9,25},{17,1},{25,9},{2,18},{10... | collective-permute-start | bytes 6291464 | tf_op jit(solution)/shard_map/ppermute | solution.py:20
  30.2 4.6 %copy-start.15 = (f32[512]{0:T(512)S(1)}, f32[512]{0:T(512)}, u32[]{:S(2)}) copy-start(f32[512]{0:T(512)} %param.8) | copy-start | bytes 6148
  30.2 5.9 %copy-start.16 = (f32[2048]{0:T(1024)S(1)}, f32[2048]{0:T(1024)}, u32[]{:S(2)}) copy-start(f32[2048]{0:T(1024)} %param.7) | copy-start | bytes 24580
  30.2 7.3 %copy-start.18 = (f32[512]{0:T(512)S(1)}, f32[512]{0:T(512)}, u32[]{:S(2)}) copy-start(f32[512]{0:T(512)} %param.11) | copy-start | bytes 6148
  30.2 7.3 %copy-start.19 = (f32[512]{0:T(512)S(1)}, f32[512]{0:T(512)}, u32[]{:S(2)}) copy-start(f32[512]{0:T(512)} %param.10) | copy-start | bytes 6148
  30.3 7.3 %copy-start.17 = (f32[2048]{0:T(1024)S(1)}, f32[2048]{0:T(1024)}, u32[]{:S(2)}) copy-start(f32[2048]{0:T(1024)} %param.9) | copy-start | bytes 24580
  43.6 1.2 copy-start.14
  64.4 1.4 copy-start
  65.8 50.9 %copy-start.1 = (f32[2,8,256,128]{3,2,1,0:T(8,128)S(1)}, f32[2,8,256,128]{3,2,1,0:T(8,128)}, u32[]{:S(2)}) copy-start(f32[2,8,256,128]{3,2,1,0:T(8,128)} %pad_maximum_fusion.refs_5_.refs_3_) | copy-start | bytes 6291460
  65.8 46.5 %collective-permute-start.1 = (f32[2048,256]{1,0:T(8,128)}, f32[2048,256]{1,0:T(8,128)}, u32[]{:S(2)}, u32[]{:S(2)}) collective-permute-start(f32[2048,256]{1,0:T(8,128)} %bitcast.1.refs_2_), channel_id=1, source_target_pairs={{0,16},{8,24},{16,0},{24,8},{1,17},{9,25},{17,1},{25,9},{2,18},{10... | collective-permute-start | bytes 6291464 | tf_op jit(solution)/shard_map/ppermute | solution.py:20
  67.3 61.5 %all-to-all-start.1 = ((f32[8,256,256]{2,1,0:T(8,128)}), f32[8,256,256]{2,1,0:T(8,128)}, u32[]{:S(2)}, u32[]{:S(2)}) async-start(f32[8,256,256]{2,1,0:T(8,128)} %copy-done), calls=%async_computation.1 | async-start | bytes 4194304 | tf_op jit(solution)/shard_map/all_to_all | solution.py:24
  73.0 39.3 %collective-permute-start.3 = (f32[2048,256]{1,0:T(8,128)}, f32[2048,256]{1,0:T(8,128)S(1)}, u32[]{:S(2)}, u32[]{:S(2)}) collective-permute-start(f32[2048,256]{1,0:T(8,128)} %bitcast.1.refs_2_), channel_id=1, source_target_pairs={{0,8},{8,0},{16,24},{24,16},{1,9},{9,1},{17,25},{25,17},{2,10},{10... | collective-permute-start | bytes 6291464 | tf_op jit(solution)/shard_map/ppermute | solution.py:20
  112.3 4.4 %collective-permute-start.2 = (f32[2048,256]{1,0:T(8,128)}, f32[2048,256]{1,0:T(8,128)S(1)}, u32[]{:S(2)}, u32[]{:S(2)}) collective-permute-start(f32[2048,256]{1,0:T(8,128)} %collective-permute-done.1.refs_0_), channel_id=1, source_target_pairs={{0,8},{8,0},{16,24},{24,16},{1,9},{9,1},{17,25},{25,17},{2,10},{10... | collective-permute-start | bytes 6291464 | tf_op jit(solution)/shard_map/ppermute | solution.py:20
  116.7 1.4 copy-start.4
  124.9 1.3 copy-start.7
  126.2 1.4 copy-start.9
  127.5 1.3 copy-start.11
  128.9 11.7 %collective-permute-start.4 = (f32[2048,256]{1,0:T(8,128)}, f32[2048,256]{1,0:T(8,128)}, u32[]{:S(2)}, u32[]{:S(2)}) collective-permute-start(f32[2048,256]{1,0:T(8,128)} %bitcast.18.refs_0_), channel_id=1, source_target_pairs={{0,8},{8,0},{16,24},{24,16},{1,9},{9,1},{17,25},{25,17},{2,10},{10... | collective-permute-start | bytes 6291464 | tf_op jit(solution)/shard_map/ppermute | solution.py:20
  129.0 1.4 copy-start.5
  130.4 1.6 copy-start.8
  132.0 1.6 copy-start.10
  133.6 7.0 %copy-start.6 = (bf16[512,1536]{1,0:T(8,128)(2,1)S(1)}, bf16[512,1536]{1,0:T(8,128)(2,1)}, u32[]{:S(2)}) copy-start(bf16[512,1536]{1,0:T(8,128)(2,1)} %pad_maximum_fusion.1.refs_4_.refs_2_) | copy-start | bytes 4718596
  140.5 10.0 %copy-start.2 = (bf16[1536,512]{1,0:T(8,128)(2,1)S(1)}, bf16[1536,512]{1,0:T(8,128)(2,1)}, u32[]{:S(2)}) copy-start(bf16[1536,512]{1,0:T(8,128)(2,1)} %pad_maximum_fusion.3.refs_5_) | copy-start | bytes 4718596
  140.5 10.0 %copy-start.3 = (bf16[1536,512]{1,0:T(8,128)(2,1)S(1)}, bf16[1536,512]{1,0:T(8,128)(2,1)}, u32[]{:S(2)}) copy-start(bf16[1536,512]{1,0:T(8,128)(2,1)} %pad_maximum_fusion.2.refs_4_) | copy-start | bytes 4718596
  140.5 10.0 %copy-start.12 = (bf16[4,2048,128]{2,1,0:T(8,128)(2,1)S(1)}, bf16[4,2048,128]{2,1,0:T(8,128)(2,1)}, u32[]{:S(2)}) copy-start(bf16[4,2048,128]{2,1,0:T(8,128)(2,1)} %copy-done.11) | copy-start | bytes 6291460

commit v10 on v7

--- a/solution.py
+++ b/solution.py
@@ -11,7 +11,7 @@
 precision_top = lax.Precision.HIGHEST
 RADIX = 8
 LANES = 128
-SMALL_BYTES, Y_BYTES, X_BYTES = [size * 1024 * 1024 for size in (8, 32, 24)]
+SMALL_BYTES, Y_BYTES, X_BYTES = [size * 1024 * 1024 for size in (8, 30, 26)]
 
 
 def from_partner(value, axis, stride):
@@ -135,13 +135,13 @@
                     split_ref[tile, pl.ds((2 * place + which) * inner, inner), pl.ds(s * LANES, LANES)] = value
         half = inner // 2
         for part in range(2):
-            step_ref[tile, part] = dot(table_ref[pl.ds(part * inner, inner), :], split_ref[tile])
+            step_ref[part] = dot(table_ref[pl.ds(part * inner, inner), :], split_ref[tile])
             for start in range(0, half, 16):
                 values = []
                 for s in range(RADIX):
                     cols = pl.ds(s * LANES, LANES)
-                    re = step_ref[tile, part, pl.ds(start, 16), cols]
-                    im = step_ref[tile, part, pl.ds(half + start, 16), cols]
+                    re = step_ref[part, pl.ds(start, 16), cols]
+                    im = step_ref[part, pl.ds(half + start, 16), cols]
                     if s:
                         cos, sin = [twist_ref[k, s, pl.ds(part * half + start, 16), :] for k in range(2)]
                         re, im = re * cos - im * sin, re * sin + im * cos
@@ -166,7 +166,7 @@
         scratch_shapes=[
             pltpu.VMEM((4, length, LANES), jnp.float32),
             pltpu.VMEM((2, 6 * inner, RADIX * LANES), jnp.bfloat16),
-            pltpu.VMEM((2, 2, inner, RADIX * LANES), jnp.float32),
+            pltpu.VMEM((2, inner, RADIX * LANES), jnp.float32),
         ],
         compiler_params=pltpu.CompilerParams(vmem_limit_bytes=Y_BYTES),
         cost_estimate=pl.CostEstimate(
@@ -176,60 +176,68 @@
     )(coefs, *inputs, table, twist)
 
 
-def x_product(parts, table_ref, rows):
-    high = [ref[which, rows, :] for ref in parts for which in (0, 2)]
-    low = [ref[which, rows, :] for ref in parts for which in (1, 3)]
-    return dot(jnp.concatenate(high + low + high, axis=1), table_ref[...])
-
-
 def x_kernel(count, *refs):
     parts, (even_ref, odd_ref, row_ref, col_ref, out_ref, total_ref) = refs[: 2 * count], refs[2 * count :]
-    half = even_ref.shape[1] // 2
-    lanes = LANES
-    total = None
-    spans = [pl.ds(start, 2 * lanes) for start in range(0, out_ref.shape[2], 2 * lanes)]
-    products = [(x_product(parts[:count], even_ref, rows), x_product(parts[count:], odd_ref, rows)) for rows in spans]
-    for rows, (even, odd) in zip(spans, products):
+    columns = out_ref.shape[3]
+    lanes, rows_each, tiles = LANES, 2 * LANES, columns // (2 * LANES)
+    totals = []
+
+    def left(refs, rows):
+        high, low = [[ref[k + which, rows, :] for ref in refs for k in (0, 2)] for which in range(2)]
+        return jnp.concatenate(high + low + high, axis=1)
+
+    def multiply(sides, tile):
+        cols = pl.ds(tile * 2 * lanes, 2 * lanes)
+        return [dot(side, table_ref[:, cols]) for side, table_ref in zip(sides, (even_ref, odd_ref))]
+
+    def finish(start, tile, even, odd):
+        rows = pl.ds(start, rows_each)
         row_scale, row_rate = [
             jnp.concatenate(
                 [
                     jnp.broadcast_to(row_ref[which, 0, c : c + 1, :], (lanes, lanes)).T
-                    for c in range(rows.start // lanes, rows.start // lanes + 2)
+                    for c in range(start // lanes, (start + rows_each) // lanes)
                 ],
                 0,
             )
             for which in range(2)
         ]
-        for tile in range(half // lanes):
-            real, imag = [slice(start, start + lanes) for start in (tile * lanes, half + tile * lanes)]
-            for upper in range(2):
-                cols = pl.ds(upper * half + tile * lanes, lanes)
-                spec_real = even[:, real] - odd[:, real] if upper else even[:, real] + odd[:, real]
-                spec_imag = even[:, imag] - odd[:, imag] if upper else even[:, imag] + odd[:, imag]
-                col_scale, col_shift, col_mix = col_ref[0:1, cols], col_ref[1:2, cols], col_ref[2:3, cols]
-                scale = row_scale * col_scale
-                latent_u = spec_real * scale
-                latent_v = spec_imag * scale
-                log_scale = row_rate * jnp.tanh(latent_u + col_shift)
-                latent_w = latent_v * jnp.exp(log_scale) + col_mix * latent_u
-                out_ref[0, 0, rows, cols] = latent_u
-                out_ref[1, 0, rows, cols] = latent_w
-                terms = log_scale - 0.5 * (latent_u * latent_u + latent_w * latent_w)
-                terms = jnp.sum(terms.reshape(-1, 8, lanes), axis=0)
-                total = terms if total is None else total + terms
+        for upper in range(2):
+            cols = pl.ds(upper * columns // 2 + tile * lanes, lanes)
+            spec = even - odd if upper else even + odd
+            col_scale, col_shift, col_mix = col_ref[0:1, cols], col_ref[1:2, cols], col_ref[2:3, cols]
+            scale = row_scale * col_scale
+            latent_u = spec[:, :lanes] * scale
+            latent_v = spec[:, lanes:] * scale
+            log_scale = row_rate * jnp.tanh(latent_u + col_shift)
+            latent_w = latent_v * jnp.exp(log_scale) + col_mix * latent_u
+            out_ref[0, 0, rows, cols] = latent_u
+            out_ref[1, 0, rows, cols] = latent_w
+            terms = log_scale - 0.5 * (latent_u * latent_u + latent_w * latent_w)
+            totals.append(jnp.sum(terms.reshape(-1, 8, lanes), axis=0))
+
+    before = None
+    for start in range(0, out_ref.shape[2], rows_each):
+        sides = [left(group, pl.ds(start, rows_each)) for group in (parts[:count], parts[count:])]
+        for tile in range(tiles):
+            products = multiply(sides, tile)
+            if before is not None:
+                finish(*before)
+            before = (start, tile, *products)
+    finish(*before)
 
     @pl.when(pl.program_id(0) == 0)
     def _():
         total_ref[...] = jnp.zeros_like(total_ref)
 
-    total_ref[...] += total
+    total_ref[...] += sum(totals)
 
 
 def x_dft(even_parts, odd_parts, even_table, odd_table, row_pair, col_trio):
     parts, count, length = even_parts + odd_parts, len(even_parts), even_parts[0].shape[1]
     columns = even_table.shape[1]
     rows = length // row_pair.shape[1]
-    fixed = [pl.BlockSpec(table.shape, lambda i: (0, 0), pipeline_mode=pl.Buffered(1)) for table in (even_table, odd_table)]
+    fixed = [pl.BlockSpec(memory_space=pltpu.VMEM)] * 2
     return pl.pallas_call(
         functools.partial(x_kernel, count),
         out_shape=(
@@ -290,11 +298,17 @@
     twist = jnp.stack([jnp.cos(angle), jnp.sin(angle)])
     order = jnp.arange(width, dtype=jnp.int32) * 2
 
-    def x_table(odd):
+    def x_table(odd, position):
         rows = jnp.concatenate([order + (2 * width + odd), order + odd])
-        cos, sin = [part[:, : 2 * width].reshape(2, width, 2 * width) for part in x_tables(rows, columns, 4, position)]
-        table = jnp.stack([jnp.concatenate([cos, sin], 2), jnp.concatenate([-sin, cos], 2)], 1)
-        return split_table(table.reshape(columns, columns), 0, (0, 0, 1))
+        cos, sin = [part[:, : 2 * width] for part in x_tables(rows, columns, 4, position)]
+
+        def lay(left, right):
+            spans = [slice(tile * width, (tile + 1) * width) for tile in range(2)]
+            return jnp.concatenate([side[:, span] for span in spans for side in (left, right)], 1)
+
+        real, imag = lay(cos, sin), lay(-sin, cos)
+        table = jnp.concatenate([real[:width], imag[:width], real[width:], imag[width:]], 0)
+        return split_table(table, 0, (0, 0, 1))
 
     norm = 1.0 / math.sqrt(length * columns * 4)
     row_pair = jnp.stack([row_scale * norm, row_rate]).reshape(2, 4, length // 4 // LANES, LANES)
@@ -303,12 +317,13 @@
     fixed = fixed - length * columns * math.log(2.0 * math.pi)
 
     first_a = combine(sign.reshape(1), from_partner(field_a, "gx", 1), field_a)
-    tables = (y_table, twist, x_table(0), x_table(1), row_pair, col_trio)
-    state = lax.optimization_barrier((first_a, to_planes(field_b)[0], tables, coefs_a, coefs_b, fixed))
-    first_a, first_b, (y_table, twist, even_table, odd_table, row_pair, col_trio), coefs_a, coefs_b, fixed = state
+    state = lax.optimization_barrier((first_a, to_planes(field_b)[0], y_table, twist, position))
+    first_a, first_b, y_table, twist, position = state
     second_a = to_planes(first_a)[0]
-
     second_b = from_partner(first_b, "gx", 1)
+    tables = (x_table(0, position), x_table(1, position), row_pair, col_trio, coefs_a, coefs_b, fixed)
+    second_b, tables = lax.optimization_barrier((second_b, tables))
+    even_table, odd_table, row_pair, col_trio, coefs_a, coefs_b, fixed = tables
     group = [second_b, from_partner(second_b, "gx", 0), first_b, from_partner(first_b, "gx", 0)]
     even_b, odd_b = y_dft(group, True, coefs_b, y_table, twist)
     even_a, odd_a = y_dft([second_a, from_partner(second_a, "gx", 0)], False, coefs_a, y_table, twist)

time: 168 us -> 171 us (1.018)
  waiting for transfers between devices: 73.5 us -> 80.9 us
  blocking collectives: 15.8 us -> 10.4 us
  local copies, waits for them, and re-layouts: 9.89 us -> 6.16 us
  other arithmetic: 14.9 us -> 16.8 us
    all_to_all x1, blocking collectives: 15.8 us -> 10.4 us  [sum_everywhere(): lax.all_to_all(copies, axes, split_axis=0, concat_axis=0, tiled=True)]
    all_to_all x2, waiting for transfers between devices: 4.38 us -> 9.76 us  [to_planes(): return lax.all_to_all(values, 'gy', split_axis=0, concat_axis=1, tiled=True)]
    sin x0 -> x1, other arithmetic: none -> 4.15 us  [root_table(): return (jnp.cos(angle), jnp.sin(angle))]
    all_to_all x2, starting transfers between devices: 10.3 us -> 13.1 us  [to_planes(): return lax.all_to_all(values, 'gy', split_axis=0, concat_axis=1, tiled=True)]
    unnamed x24 -> x22, local copies, waits for them, and re-layouts: 4.44 us -> 2.28 us
    ppermute x5, waiting for transfers between devices: 69.1 us -> 71.1 us  [from_partner(): return lax.ppermute(value, axis, pairs)]
    sin x2 -> x0, local copies, waits for them, and re-layouts: 1.91 us -> none  [root_table(): return (jnp.cos(angle), jnp.sin(angle))]
  transfers between devices with their start and end apart: 7 -> 7, of which waited for: 5 -> 3; matrix products, arithmetic and copies ran while one was open for 11% -> 7% of each run, Pallas kernels for 9% -> 10%
where the time goes in v10:
time: 171 us; the launch traced here: 170 us
  waiting for transfers between devices  80.9 us (47%)
  Pallas kernels  35.6 us (21%)
  other arithmetic  16.8 us (10%)
  starting transfers between devices  16.2 us (9%)
  blocking collectives  10.4 us (6%)
  local copies, waits for them, and re-layouts  6.16 us (4%)
  between operations  4.06 us (2%)
    ppermute x5, waiting for transfers between devices, from_partner(): return lax.ppermute(value, axis, pairs)  71.1 us
    pallas_call x2, Pallas kernels, y_dft(): pl.pallas_call(functools.partial(y_kernel, len(inputs), pick), out_shape=...  19.2 us
    all_to_all x2, starting transfers between devices, to_planes(): return lax.all_to_all(values, 'gy', split_axis=0, concat_axis=1, tiled=True)  13.1 us
    all_to_all x1, blocking collectives, sum_everywhere(): lax.all_to_all(copies, axes, split_axis=0, concat_axis=0, tiled=True)  10.4 us
    pallas_call x1, Pallas kernels, x_dft(): pl.pallas_call(functools.partial(x_kernel, count), out_shape=(jax.ShapeDt...  10 us
    all_to_all x2, waiting for transfers between devices, to_planes(): return lax.all_to_all(values, 'gy', split_axis=0, concat_axis=1, tiled=True)  9.76 us
    pallas_call x1, Pallas kernels, combine(): pl.pallas_call(combine_kernel, out_shape=jax.ShapeDtypeStruct(late.shape,...  6.34 us
    sin x1, other arithmetic, root_table(): return (jnp.cos(angle), jnp.sin(angle))  4.15 us
  transfers between devices with their start and end apart: 7, of which 3 were waited for; matrix products, arithmetic and copies ran while one was open for 7% of the time, Pallas kernels for 10%

profile of v10, /device:TPU:0, one launch (start us, length us, event | category | flops | bytes accessed | tf_op | source)
XLA Modules:
  0.0 170.1 jit_solution(18131624928552933769)
XLA Ops:
  0.6 0.0 copy-start.5
  0.6 2.0 %slice.86.early_ref = f32[8,256,256]{2,1,0:T(8,128)S(1)} slice(f32[8,256,512]{2,1,0:T(8,128)} %param.6), slice={[0:8], [0:256], [0:256]} | slice | bytes 4194304 | tf_op jit(solution)/shard_map/slice | solution.py:279
  2.6 0.8 copy-done.5
  3.4 1.6 slice.87
  5.0 0.0 copy-start.8
  5.0 7.4 %all-to-all-start = ((f32[8,256,256]{2,1,0:T(8,128)}), f32[8,256,256]{2,1,0:T(8,128)}, u32[]{:S(2)}, u32[]{:S(2)}) async-start(f32[8,256,256]{2,1,0:T(8,128)} %slice.87), calls=%async_computation | async-start | bytes 4194304 | tf_op jit(solution)/shard_map/all_to_all | solution.py:24
  12.4 1.5 collective-permute-start
  14.0 0.7 log_reduce_fusion.1
  14.6 0.0 copy-done.7
  14.6 0.7 log_reduce_fusion
  15.3 0.1 pad_maximum_fusion.13
  15.4 0.1 reshape.159.coef_ref
  16.8 0.1 pad_maximum_fusion.12.coef_ref
  16.9 0.0 copy-done.9
  16.9 0.0 copy-done.10
  17.0 1.1 fusion.23
  18.1 0.1 maximum_maximum_fusion
  18.2 3.2 %fusion.3 = (f32[1,8,256,128]{3,2,1,0:T(8,128)S(1)}, f32[1,8,256,128]{3,2,1,0:T(8,128)S(1)}) fusion(), kind=kLoop, calls=%fused_computation.17 | loop fusion | flops 786432 | bytes 2097152 | tf_op jit(solution)/shard_map/sin | solution.py:298
  21.4 1.5 pad_maximum_fusion.refs_5_.refs_3_
  22.9 0.1 fusion
  23.1 1.3 pad_maximum_fusion.1.refs_4_.refs_2_
  24.3 35.3 %collective-permute-done.late_ref = f32[8,256,256]{2,1,0:T(8,128)} collective-permute-done((f32[8,256,256]{2,1,0:T(8,128)S(1)}, f32[8,256,256]{2,1,0:T(8,128)}, u32[]{:S(2)}, u32[]{:S(2)}) %collective-permute-start) | collective-permute-done | bytes 2097184 | tf_op jit(solution)/shard_map/ppermute | solution.py:20
  59.6 6.3 %combine.1 = f32[8,256,256]{2,1,0:T(8,128)} custom-call(f32[1]{0:T(128)} %bitcast.sign_ref, f32[8,256,256]{2,1,0:T(8,128)} %collective-permute-done.late_ref, f32[8,256,256]{2,1,0:T(8,128)S(1)} %slice.86.early_ref), custom_call_target="tpu_custom_call" | custom-call | flops 1048576 | bytes 6291456 | tf_op jit(solution)/shard_map/combine/pallas_call | solution.py:46
  66.0 0.0 all-to-all-done
  66.0 4.2 %fusion.14 = (f32[256,512]{1,0:T(8,128)S(1)}, f32[256,512]{1,0:T(8,128)S(1)}, f32[256,512]{1,0:T(8,128)S(1)}, f32[256,512]{1,0:T(8,128)S(1)}) fusion(s32[512]{0:T(512)S(1)} %multiply_add_fusion, s32[256]{0:T(256)S(1)} %pad_add_fusion.1, s32[256]{0:T(256)S(1)} %pad_add_fusion), kind=kLoop, calls=%fused_computation.47 | loop fusion | flops 3670016 | bytes 2101248 | tf_op jit(solution)/shard_map/sin | solution.py:68
  70.2 1.6 collective-permute-start.1
  71.8 0.0 collective-permute-start.3
  71.8 5.7 %all-to-all-start.1 = ((f32[8,256,256]{2,1,0:T(8,128)}), f32[8,256,256]{2,1,0:T(8,128)}, u32[]{:S(2)}, u32[]{:S(2)}) async-start(f32[8,256,256]{2,1,0:T(8,128)} %combine.1), calls=%async_computation.1 | async-start | bytes 4194304 | tf_op jit(solution)/shard_map/all_to_all | solution.py:24
  77.5 0.1 pad_maximum_fusion.6
  77.7 0.2 reduce-precision_convert_fusion.1
  78.0 0.1 pad_maximum_fusion.8
  78.2 0.2 reduce-precision_convert_fusion
  78.3 1.3 pad_maximum_fusion.2.refs_4_
  79.6 1.3 pad_maximum_fusion.3.refs_5_
  80.9 35.8 %collective-permute-done.1.refs_0_ = f32[2048,256]{1,0:T(8,128)} collective-permute-done((f32[2048,256]{1,0:T(8,128)}, f32[2048,256]{1,0:T(8,128)}, u32[]{:S(2)}, u32[]{:S(2)}) %collective-permute-start.1) | collective-permute-done | bytes 2097184 | tf_op jit(solution)/shard_map/ppermute | solution.py:20
  116.7 0.0 collective-permute-start.2
  116.8 9.8 %all-to-all-done.1 = f32[8,256,256]{2,1,0:T(8,128)} async-done(((f32[8,256,256]{2,1,0:T(8,128)}), f32[8,256,256]{2,1,0:T(8,128)}, u32[]{:S(2)}, u32[]{:S(2)}) %all-to-all-start.1) | async-done | bytes 2097184 | tf_op jit(solution)/shard_map/all_to_all | solution.py:24
  126.5 0.0 collective-permute-start.4
  126.5 0.0 collective-permute-done.3.refs_3_
  126.5 0.0 collective-permute-done.2.refs_1_
  126.5 1.4 copy-done.1
  127.9 10.6 %y_dft.2 = (bf16[4,2048,128]{2,1,0:T(8,128)(2,1)S(1)}, bf16[4,2048,128]{2,1,0:T(8,128)(2,1)S(1)}) custom-call(f32[2,4]{1,0:T(2,128)S(1)} %pad_maximum_fusion.12.coef_ref, f32[2048,256]{1,0:T(8,128)} %collective-permute-done.1.refs_0_, f32[2048,256]{1,0:T(8,128)} %collective-permute-done.2.refs_1_, f32[2048,256]{1,0:T(8,128)} %bitcast.1.refs_2_, ...), custom_call_target="tpu_custom_call" | custom-call | flops 3221225472 | bytes 14680064 | tf_op jit(solution)/shard_map/y_dft/pallas_call | solution.py:161
  138.5 0.0 copy-start.3
  138.5 0.0 collective-permute-done.4.refs_1_
  138.5 8.7 %y_dft.3 = (bf16[4,2048,128]{2,1,0:T(8,128)(2,1)S(1)}, bf16[4,2048,128]{2,1,0:T(8,128)(2,1)S(1)}) custom-call(f32[2,2]{1,0:T(2,128)S(1)} %reshape.159.coef_ref, f32[2048,256]{1,0:T(8,128)} %bitcast.12.refs_0_, f32[2048,256]{1,0:T(8,128)} %collective-permute-done.4.refs_1_, bf16[512,1536]{1,0:T(8,128)(2,1)S(1)} %copy-done.2, f32[2,8,256,128]{3,2,1,0:T(8,128)S(1)} %copy-done), custom_call_target="tpu_custom_call" | custom-call | flops 3221225472 | bytes 10485760 | tf_op jit(solution)/shard_map/y_dft/pallas_call | solution.py:161
  147.2 10.0 %x_dft.1 = (f32[2,1,2048,512]{3,2,1,0:T(8,128)}, f32[8,128]{1,0:T(8,128)S(1)}) custom-call(bf16[4,2048,128]{2,1,0:T(8,128)(2,1)S(1)} %get-tuple-element.31.refs_0_, bf16[4,2048,128]{2,1,0:T(8,128)(2,1)S(1)} %get-tuple-element.34.refs_1_, bf16[4,2048,128]{2,1,0:T(8,128)(2,1)S(1)} %get-tuple-element.35.refs_2_, ...), custom_call_target="tpu_custom_call" | custom-call | flops 6442450944 | bytes 16777216 | tf_op jit(solution)/shard_map/x_dft/pallas_call | solution.py:241
  157.3 10.4 %all_to_all.23 = f32[32,8,128]{2,1,0:T(8,128)S(1)} all-to-all(f32[32,8,128]{2,1,0:T(8,128)S(1)} %broadcast_in_dim.2), channel_id=1, replica_groups=mesh['gx'=4,'gy'=8] {'gx','gy'}, dimensions={0} | all-to-all | bytes 262144 | tf_op jit(solution)/shard_map/all_to_all | solution.py:272
  167.7 0.6 reduce_sum.29
  (37 shorter events, 0.4 us)
Async XLA Ops:
  0.6 2.8 %copy-start.5 = (f32[8,256,512]{2,1,0:T(8,128)S(1)}, f32[8,256,512]{2,1,0:T(8,128)}, u32[]{:S(2)}) copy-start(f32[8,256,512]{2,1,0:T(8,128)} %param.6) | copy-start | bytes 12582916
  5.0 9.0 %copy-start.6 = (f32[512]{0:T(512)S(1)}, f32[512]{0:T(512)}, u32[]{:S(2)}) copy-start(f32[512]{0:T(512)} %param.8) | copy-start | bytes 6148
  5.0 9.6 %copy-start.7 = (f32[2048]{0:T(1024)S(1)}, f32[2048]{0:T(1024)}, u32[]{:S(2)}) copy-start(f32[2048]{0:T(1024)} %param.7) | copy-start | bytes 24580
  5.0 11.9 %copy-start.9 = (f32[512]{0:T(512)S(1)}, f32[512]{0:T(512)}, u32[]{:S(2)}) copy-start(f32[512]{0:T(512)} %param.11) | copy-start | bytes 6148
  5.0 11.9 %copy-start.10 = (f32[512]{0:T(512)S(1)}, f32[512]{0:T(512)}, u32[]{:S(2)}) copy-start(f32[512]{0:T(512)} %param.10) | copy-start | bytes 6148
  5.0 11.9 %copy-start.8 = (f32[2048]{0:T(1024)S(1)}, f32[2048]{0:T(1024)}, u32[]{:S(2)}) copy-start(f32[2048]{0:T(1024)} %param.9) | copy-start | bytes 24580
  5.0 60.9 %all-to-all-start = ((f32[8,256,256]{2,1,0:T(8,128)}), f32[8,256,256]{2,1,0:T(8,128)}, u32[]{:S(2)}, u32[]{:S(2)}) async-start(f32[8,256,256]{2,1,0:T(8,128)} %slice.87), calls=%async_computation | async-start | bytes 4194304 | tf_op jit(solution)/shard_map/all_to_all | solution.py:24
  12.4 47.2 %collective-permute-start = (f32[8,256,256]{2,1,0:T(8,128)S(1)}, f32[8,256,256]{2,1,0:T(8,128)}, u32[]{:S(2)}, u32[]{:S(2)}) collective-permute-start(f32[8,256,256]{2,1,0:T(8,128)S(1)} %slice.86.early_ref), channel_id=1, source_target_pairs={{0,16},{8,24},{16,0},{24,8},{1,17},{9,25},{17,1},{25,9},{2,18},{10... | collective-permute-start | bytes 6291464 | tf_op jit(solution)/shard_map/ppermute | solution.py:20
  70.2 46.6 %collective-permute-start.1 = (f32[2048,256]{1,0:T(8,128)}, f32[2048,256]{1,0:T(8,128)}, u32[]{:S(2)}, u32[]{:S(2)}) collective-permute-start(f32[2048,256]{1,0:T(8,128)} %bitcast.1.refs_2_), channel_id=1, source_target_pairs={{0,16},{8,24},{16,0},{24,8},{1,17},{9,25},{17,1},{25,9},{2,18},{10... | collective-permute-start | bytes 6291464 | tf_op jit(solution)/shard_map/ppermute | solution.py:20
  71.8 54.7 %collective-permute-start.3 = (f32[2048,256]{1,0:T(8,128)}, f32[2048,256]{1,0:T(8,128)}, u32[]{:S(2)}, u32[]{:S(2)}) collective-permute-start(f32[2048,256]{1,0:T(8,128)} %bitcast.1.refs_2_), channel_id=1, source_target_pairs={{0,8},{8,0},{16,24},{24,16},{1,9},{9,1},{17,25},{25,17},{2,10},{10... | collective-permute-start | bytes 6291464 | tf_op jit(solution)/shard_map/ppermute | solution.py:20
  71.8 54.7 %all-to-all-start.1 = ((f32[8,256,256]{2,1,0:T(8,128)}), f32[8,256,256]{2,1,0:T(8,128)}, u32[]{:S(2)}, u32[]{:S(2)}) async-start(f32[8,256,256]{2,1,0:T(8,128)} %combine.1), calls=%async_computation.1 | async-start | bytes 4194304 | tf_op jit(solution)/shard_map/all_to_all | solution.py:24
  78.3 48.2 %copy-start = (f32[2,8,256,128]{3,2,1,0:T(8,128)S(1)}, f32[2,8,256,128]{3,2,1,0:T(8,128)}, u32[]{:S(2)}) copy-start(f32[2,8,256,128]{3,2,1,0:T(8,128)} %pad_maximum_fusion.refs_5_.refs_3_) | copy-start | bytes 6291460
  116.7 9.8 %collective-permute-start.2 = (f32[2048,256]{1,0:T(8,128)}, f32[2048,256]{1,0:T(8,128)}, u32[]{:S(2)}, u32[]{:S(2)}) collective-permute-start(f32[2048,256]{1,0:T(8,128)} %collective-permute-done.1.refs_0_), channel_id=1, source_target_pairs={{0,8},{8,0},{16,24},{24,16},{1,9},{9,1},{17,25},{25,17},{2,10},{10... | collective-permute-start | bytes 6291464 | tf_op jit(solution)/shard_map/ppermute | solution.py:20
  126.5 12.0 %collective-permute-start.4 = (f32[2048,256]{1,0:T(8,128)}, f32[2048,256]{1,0:T(8,128)}, u32[]{:S(2)}, u32[]{:S(2)}) collective-permute-start(f32[2048,256]{1,0:T(8,128)} %bitcast.12.refs_0_), channel_id=1, source_target_pairs={{0,8},{8,0},{16,24},{24,16},{1,9},{9,1},{17,25},{25,17},{2,10},{10... | collective-permute-start | bytes 6291464 | tf_op jit(solution)/shard_map/ppermute | solution.py:20
  126.5 1.4 copy-start.1
  127.9 10.6 %copy-start.2 = (bf16[512,1536]{1,0:T(8,128)(2,1)S(1)}, bf16[512,1536]{1,0:T(8,128)(2,1)}, u32[]{:S(2)}) copy-start(bf16[512,1536]{1,0:T(8,128)(2,1)} %pad_maximum_fusion.1.refs_4_.refs_2_) | copy-start | bytes 4718596
  138.5 8.7 %copy-start.3 = (bf16[1536,512]{1,0:T(8,128)(2,1)S(1)}, bf16[1536,512]{1,0:T(8,128)(2,1)}, u32[]{:S(2)}) copy-start(bf16[1536,512]{1,0:T(8,128)(2,1)} %pad_maximum_fusion.2.refs_4_) | copy-start | bytes 4718596
  138.5 8.7 %copy-start.4 = (bf16[1536,512]{1,0:T(8,128)(2,1)S(1)}, bf16[1536,512]{1,0:T(8,128)(2,1)}, u32[]{:S(2)}) copy-start(bf16[1536,512]{1,0:T(8,128)(2,1)} %pad_maximum_fusion.3.refs_5_) | copy-start | bytes 4718596

commit v11 on v10

--- a/solution.py
+++ b/solution.py
@@ -31,28 +31,37 @@
     return jnp.where(lane < LANES // 2, *chosen)
 
 
-def combine_kernel(sign_ref, late_ref, early_ref, out_ref):
+def combine_kernel(sign_ref, late_ref, early_ref, *refs):
+    out_ref = refs[-1]
     sign = sign_ref[0]
-    left, right = [
-        late_ref[0, :, pl.ds(lane, LANES)] + sign * early_ref[0, :, pl.ds(lane, LANES)] for lane in (0, LANES)
-    ]
-    for odd in range(2):
-        out_ref[0, :, pl.ds(odd * LANES, LANES)] = pick_columns(left, right, odd)
-
-
-def combine(sign, late, early):
-    planes, rows, columns = late.shape
-    block = pl.BlockSpec((1, rows, columns), lambda i: (i, 0, 0))
-    return pl.pallas_call(
-        combine_kernel,
-        out_shape=jax.ShapeDtypeStruct(late.shape, jnp.float32),
-        grid=(planes,),
-        in_specs=[pl.BlockSpec(memory_space=pltpu.SMEM), block, block],
-        out_specs=block,
-        cost_estimate=pl.CostEstimate(flops=2 * late.size, bytes_accessed=12 * late.size, transcendentals=0),
-        compiler_params=pltpu.CompilerParams(vmem_limit_bytes=SMALL_BYTES),
-        name="combine",
-    )(sign, late, early)
+    for plane in range(late_ref.shape[0]):
+        left, right = [
+            late_ref[plane, :, pl.ds(lane, LANES)] + sign * early_ref[plane, :, pl.ds(lane, LANES)] for lane in (0, LANES)
+        ]
+        for odd in range(2):
+            out_ref[plane, :, pl.ds(odd * LANES, LANES)] = pick_columns(left, right, odd)
+
+
+def combine(sign, parts):
+    planes, rows, columns = parts[0][0].shape
+    result = ()
+    for place, pair in enumerate(parts):
+        block = pl.BlockSpec((planes // 2, rows, columns), lambda i: (i, 0, 0))
+        result = pl.pallas_call(
+            combine_kernel,
+            out_shape=[jax.ShapeDtypeStruct((planes * len(parts), rows, columns), jnp.float32)],
+            grid=(2,),
+            in_specs=[pl.BlockSpec(memory_space=pltpu.SMEM), block, block]
+            + [pl.BlockSpec(memory_space=pl.ANY)] * len(result),
+            out_specs=[pl.BlockSpec((planes // 2, rows, columns), lambda i, place=place: (2 * place + i, 0, 0))],
+            input_output_aliases={3: 0} if result else {},
+            cost_estimate=pl.CostEstimate(
+                flops=2 * pair[0].size, bytes_accessed=12 * pair[0].size, transcendentals=0
+            ),
+            compiler_params=pltpu.CompilerParams(vmem_limit_bytes=SMALL_BYTES),
+            name="combine",
+        )(sign, *pair, *result)
+    return result[0]
 
 
 def reverse_bits(value, count):
@@ -276,7 +285,8 @@
     position = lax.axis_index("gx")
     planes, rows, columns = field.shape
     length, width = planes * rows, columns // 4
-    field_a, field_rest = lax.optimization_barrier((field[:, :, : 2 * width], field))
+    groups = [slice(0, planes // 2), slice(planes // 2, None)]
+    field_a, field_rest = lax.optimization_barrier(([field[group, :, : 2 * width] for group in groups], field))
     field_b = field_rest[:, :, 2 * width :]
     sign = jnp.where(position < 2, 1.0, -1.0)
 
@@ -298,7 +308,7 @@
     twist = jnp.stack([jnp.cos(angle), jnp.sin(angle)])
     order = jnp.arange(width, dtype=jnp.int32) * 2
 
-    def x_table(odd, position):
+    def x_table(odd):
         rows = jnp.concatenate([order + (2 * width + odd), order + odd])
         cos, sin = [part[:, : 2 * width] for part in x_tables(rows, columns, 4, position)]
 
@@ -316,14 +326,12 @@
     fixed = 2.0 * (columns * jnp.sum(jnp.log(row_scale)) + length * jnp.sum(jnp.log(col_scale)))
     fixed = fixed - length * columns * math.log(2.0 * math.pi)
 
-    first_a = combine(sign.reshape(1), from_partner(field_a, "gx", 1), field_a)
-    state = lax.optimization_barrier((first_a, to_planes(field_b)[0], y_table, twist, position))
-    first_a, first_b, y_table, twist, position = state
+    first_a = combine(sign.reshape(1), [(from_partner(part, "gx", 1), part) for part in field_a])
+    tables = (y_table, twist, x_table(0), x_table(1), row_pair, col_trio, coefs_a, coefs_b, fixed)
+    first_a, first_b, tables = lax.optimization_barrier((first_a, to_planes(field_b)[0], tables))
+    y_table, twist, even_table, odd_table, row_pair, col_trio, coefs_a, coefs_b, fixed = tables
     second_a = to_planes(first_a)[0]
     second_b = from_partner(first_b, "gx", 1)
-    tables = (x_table(0, position), x_table(1, position), row_pair, col_trio, coefs_a, coefs_b, fixed)
-    second_b, tables = lax.optimization_barrier((second_b, tables))
-    even_table, odd_table, row_pair, col_trio, coefs_a, coefs_b, fixed = tables
     group = [second_b, from_partner(second_b, "gx", 0), first_b, from_partner(first_b, "gx", 0)]
     even_b, odd_b = y_dft(group, True, coefs_b, y_table, twist)
     even_a, odd_a = y_dft([second_a, from_partner(second_a, "gx", 0)], False, coefs_a, y_table, twist)

time: 171 us -> 165 us (0.965)
  waiting for transfers between devices: 80.9 us -> 55.2 us
  other arithmetic: 16.8 us -> 30.7 us
  local copies, waits for them, and re-layouts: 6.16 us -> 12.4 us
  blocking collectives: 10.4 us -> 13.3 us
  Pallas kernels: 35.6 us -> 33.8 us
    ppermute x5 -> x6, waiting for transfers between devices: 71.1 us -> 49.6 us  [from_partner(): return lax.ppermute(value, axis, pairs)]
    convert_element_type x3, other arithmetic: 0.48 us -> 4.72 us  [split_table(): parts = [high.astype(jnp.bfloat16), (table - high).astype(jnp.bfloat16)]]
    all_to_all x2, waiting for transfers between devices: 9.76 us -> 5.65 us  [to_planes(): return lax.all_to_all(values, 'gy', split_axis=0, concat_axis=1, tiled=True)]
    all_to_all x1, blocking collectives: 10.4 us -> 13.3 us  [sum_everywhere(): lax.all_to_all(copies, axes, split_axis=0, concat_axis=0, tiled=True)]
    slice x6, local copies, waits for them, and re-layouts: 0.12 us -> 2.69 us  [lay(): side[:, span]]
    all_to_all x2, starting transfers between devices: 13.1 us -> 10.8 us  [to_planes(): return lax.all_to_all(values, 'gy', split_axis=0, concat_axis=1, tiled=True)]
    concatenate x1, other arithmetic: 0.1 us -> 2.25 us  [four_way(): y_table = jnp.concatenate(y_table, 1).reshape(2 * inner, 2 * inner)]
    ppermute x5 -> x6, starting transfers between devices: 3.11 us -> 4.6 us  [from_partner(): return lax.ppermute(value, axis, pairs)]
  transfers between devices with their start and end apart: 7 -> 8, of which waited for: 3 -> 5; matrix products, arithmetic and copies ran while one was open for 7% -> 22% of each run, Pallas kernels for 10% -> 9%
where the time goes in v11:
time: 165 us
  waiting for transfers between devices  55.2 us (33%)
  Pallas kernels  33.8 us (20%)
  other arithmetic  30.7 us (19%)
  starting transfers between devices  15.4 us (9%)
  blocking collectives  13.3 us (8%)
  local copies, waits for them, and re-layouts  12.4 us (8%)
  between operations  4.03 us (2%)
    ppermute x6, waiting for transfers between devices, from_partner(): return lax.ppermute(value, axis, pairs)  49.6 us
    pallas_call x2, Pallas kernels, y_dft(): pl.pallas_call(functools.partial(y_kernel, len(inputs), pick), out_shape=...  18.4 us
    all_to_all x1, blocking collectives, sum_everywhere(): lax.all_to_all(copies, axes, split_axis=0, concat_axis=0, tiled=True)  13.3 us
    all_to_all x2, starting transfers between devices, to_planes(): return lax.all_to_all(values, 'gy', split_axis=0, concat_axis=1, tiled=True)  10.8 us
    pallas_call x1, Pallas kernels, x_dft(): pl.pallas_call(functools.partial(x_kernel, count), out_shape=(jax.ShapeDt...  9.99 us
    all_to_all x2, waiting for transfers between devices, to_planes(): return lax.all_to_all(values, 'gy', split_axis=0, concat_axis=1, tiled=True)  5.65 us
    sin x1, other arithmetic, root_table(): return (jnp.cos(angle), jnp.sin(angle))  5.55 us
    pallas_call x2, Pallas kernels, combine(): pl.pallas_call(combine_kernel, out_shape=[jax.ShapeDtypeStruct((planes *...  5.33 us
  transfers between devices with their start and end apart: 8, of which 5 were waited for; matrix products, arithmetic and copies ran while one was open for 22% of the time, Pallas kernels for 9%

profile of v11, /device:TPU:0, one launch (start us, length us, event | category | flops | bytes accessed | tf_op | source)
XLA Modules:
  0.0 164.8 jit_solution(18006398246194015801)
XLA Ops:
  0.6 2.9 %fusion.24 = (f32[4,256,256]{2,1,0:T(8,128)S(1)}, f32[4,256,256]{2,1,0:T(8,128)}) fusion(f32[8,256,512]{2,1,0:T(8,128)} %param.6), kind=kLoop, calls=%fused_computation.74 | loop fusion | bytes 4194304 | tf_op jit(solution)/shard_map/slice | solution.py:289
  3.5 3.0 %collective-permute-start = (f32[4,256,256]{2,1,0:T(8,128)S(1)}, f32[4,256,256]{2,1,0:T(8,128)}, u32[]{:S(2)}, u32[]{:S(2)}) collective-permute-start(f32[4,256,256]{2,1,0:T(8,128)S(1)} %get-tuple-element.22.early_ref), channel_id=1, source_target_pairs={{0,16},{8,24},{16,0},{24,8},{1,17},{9,25},{17,1},{25,9},{2,18},{10... | collective-permute-start | bytes 3145736 | tf_op jit(solution)/shard_map/ppermute | solution.py:20
  6.5 0.0 collective-permute-start.1
  6.5 1.6 slice.91
  8.1 6.3 %all-to-all-start = ((f32[8,256,256]{2,1,0:T(8,128)}), f32[8,256,256]{2,1,0:T(8,128)S(1)}, u32[]{:S(2)}, u32[]{:S(2)}) async-start(f32[8,256,256]{2,1,0:T(8,128)} %slice.91), calls=%async_computation | async-start | bytes 4194304 | tf_op jit(solution)/shard_map/all_to_all | solution.py:24
  14.4 5.5 %fusion.14 = (f32[256,512]{1,0:T(8,128)}, f32[256,512]{1,0:T(8,128)}, f32[256,512]{1,0:T(8,128)}, f32[256,512]{1,0:T(8,128)S(1)}) fusion(s32[512]{0:T(512)S(1)} %multiply_add_fusion, s32[256]{0:T(256)S(1)} %pad_add_fusion.1, s32[256]{0:T(256)S(1)} %pad_add_fusion), kind=kLoop, calls=%fused_computation.47 | loop fusion | flops 3670016 | bytes 2101248 | tf_op jit(solution)/shard_map/sin | solution.py:77
  20.0 0.7 fusion.31
  20.6 0.7 slice_negate_fusion.1
  21.4 1.9 %fusion.23 = (f32[2,1,128,256]{3,2,1,0:T(8,128)S(1)}, f32[2,1,128,256]{3,2,1,0:T(8,128)}, f32[2,1,128,256]{3,2,1,0:T(8,128)}) fusion(s32[2,128]{1,0:T(2,128)S(1)} %multiply_add_fusion.1), kind=kLoop, calls=%fused_computation.56 | loop fusion | flops 983040 | bytes 787456 | tf_op jit(solution)/shard_map/neg | solution.py:303
  23.3 1.0 fusion.32
  24.3 1.0 fusion.34
  25.3 0.0 copy-start.18
  25.3 1.0 pad_maximum_fusion.6
  26.3 0.8 fusion.30
  27.2 0.9 fusion.29
  28.0 0.6 log_reduce_fusion
  28.7 0.7 log_reduce_fusion.1
  29.3 0.7 pad_maximum_fusion.10.refs_6_
  30.0 2.3 %maximum_maximum_fusion = f32[2,2,128,512]{3,2,1,0:T(8,128)} fusion(f32[2,1,128,256]{3,2,1,0:T(8,128)} %get-tuple-element.84, f32[2,1,128,256]{3,2,1,0:T(8,128)} %get-tuple-element.83, f32[2,1,128,256]{3,2,1,0:T(8,128)S(1)} %get-tuple-element.82), kind=kLoop, calls=%fused_computation.13 | loop fusion | flops 786432 | bytes 1835008 | tf_op jit(solution)/shard_map/concatenate | solution.py:304
  32.3 0.1 pad_maximum_fusion.13
  32.4 0.1 reshape.159.coef_ref
  32.5 2.5 %reduce-precision_convert_fusion.1 = (bf16[512,512]{1,0:T(8,128)(2,1)}, bf16[512,512]{1,0:T(8,128)(2,1)}) fusion(f32[128,512]{1,0:T(8,128)} %get-tuple-element.61, f32[128,512]{1,0:T(8,128)} %get-tuple-element.59, f32[128,512]{1,0:T(8,128)} %get-tuple-element.60, f32[128,512]{1,0:T(8,128)} %get-tuple-element.58), kind=kLoop, calls=%fused_computation.7 | loop fusion | flops 1835008 | bytes 2097152 | tf_op jit(solution)/shard_map/convert_element_type | solution.py:89
  35.1 0.1 pad_maximum_fusion.8
  35.3 1.1 reduce-precision_convert_fusion
  36.4 4.6 %fusion.3 = (f32[1,8,256,128]{3,2,1,0:T(8,128)}, f32[1,8,256,128]{3,2,1,0:T(8,128)}) fusion(), kind=kLoop, calls=%fused_computation.17 | loop fusion | flops 786432 | bytes 2097152 | tf_op jit(solution)/shard_map/sin | solution.py:308
  41.0 1.1 fusion
  42.1 0.1 pad_maximum_fusion.12.coef_ref
  43.5 3.2 %pad_maximum_fusion.refs_5_.refs_3_ = f32[2,8,256,128]{3,2,1,0:T(8,128)} fusion(f32[1,8,256,128]{3,2,1,0:T(8,128)} %get-tuple-element.85, f32[1,8,256,128]{3,2,1,0:T(8,128)} %get-tuple-element.86), kind=kLoop, calls=%fused_computation | loop fusion | flops 524288 | bytes 4194304 | tf_op jit(solution)/shard_map/stack | solution.py:308
  46.7 1.3 pad_maximum_fusion.1.refs_4_.refs_2_
  48.0 0.3 copy-done.9
  48.3 1.3 pad_maximum_fusion.2.refs_4_
  49.6 1.3 pad_maximum_fusion.3.refs_5_
  50.9 1.4 collective-permute-done.1.late_ref
  52.2 2.8 %combine.2.refs_0_ = f32[8,256,256]{2,1,0:T(8,128)} custom-call(f32[1]{0:T(128)} %bitcast.sign_ref, f32[4,256,256]{2,1,0:T(8,128)} %collective-permute-done.1.late_ref, f32[4,256,256]{2,1,0:T(8,128)} %get-tuple-element.23.early_ref), custom_call_target="tpu_custom_call" | custom-call | flops 524288 | bytes 3145728 | tf_op jit(solution)/shard_map/combine/pallas_call | solution.py:50
  55.0 2.6 %combine.3 = f32[8,256,256]{2,1,0:T(8,128)} custom-call(f32[1]{0:T(128)} %bitcast.sign_ref, f32[4,256,256]{2,1,0:T(8,128)} %collective-permute-done.late_ref, f32[4,256,256]{2,1,0:T(8,128)S(1)} %get-tuple-element.22.early_ref, f32[8,256,256]{2,1,0:T(8,128)} %combine.2.refs_0_), custom_call_target="tpu_custom_call", output_to_operand_aliasing={{}: (3, {})} | custom-call | flops 524288 | bytes 3145728 | tf_op jit(solution)/shard_map/combine/pallas_call | solution.py:50
  57.5 4.5 %all-to-all-done = f32[8,256,256]{2,1,0:T(8,128)S(1)} async-done(((f32[8,256,256]{2,1,0:T(8,128)}), f32[8,256,256]{2,1,0:T(8,128)S(1)}, u32[]{:S(2)}, u32[]{:S(2)}) %all-to-all-start) | async-done | bytes 2097184 | tf_op jit(solution)/shard_map/all_to_all | solution.py:24
  62.0 4.5 %all-to-all-start.1 = ((f32[8,256,256]{2,1,0:T(8,128)}), f32[8,256,256]{2,1,0:T(8,128)}, u32[]{:S(2)}, u32[]{:S(2)}) async-start(f32[8,256,256]{2,1,0:T(8,128)} %combine.3), calls=%async_computation.1 | async-start | bytes 4194304 | tf_op jit(solution)/shard_map/all_to_all | solution.py:24
  66.6 1.6 collective-permute-start.2
  68.2 44.9 %collective-permute-done.2.refs_0_ = f32[2048,256]{1,0:T(8,128)} collective-permute-done((f32[2048,256]{1,0:T(8,128)S(1)}, f32[2048,256]{1,0:T(8,128)}, u32[]{:S(2)}, u32[]{:S(2)}) %collective-permute-start.2) | collective-permute-done | bytes 2097184 | tf_op jit(solution)/shard_map/ppermute | solution.py:20
  113.0 1.2 all-to-all-done.1
  114.2 3.3 %collective-permute-done.3.refs_1_ = f32[2048,256]{1,0:T(8,128)} collective-permute-done((f32[2048,256]{1,0:T(8,128)}, f32[2048,256]{1,0:T(8,128)}, u32[]{:S(2)}, u32[]{:S(2)}) %collective-permute-start.3) | collective-permute-done | bytes 2097184 | tf_op jit(solution)/shard_map/ppermute | solution.py:20
  117.6 1.6 copy-done
  119.1 1.4 copy-done.2
  120.6 10.0 %y_dft.2 = (bf16[4,2048,128]{2,1,0:T(8,128)(2,1)S(1)}, bf16[4,2048,128]{2,1,0:T(8,128)(2,1)S(1)}) custom-call(f32[2,4]{1,0:T(2,128)S(1)} %pad_maximum_fusion.12.coef_ref, f32[2048,256]{1,0:T(8,128)} %collective-permute-done.2.refs_0_, f32[2048,256]{1,0:T(8,128)} %collective-permute-done.3.refs_1_, f32[2048,256]{1,0:T(8,128)S(1)} %bitcast.17, ...), custom_call_target="tpu_custom_call" | custom-call | flops 3221225472 | bytes 14680064 | tf_op jit(solution)/shard_map/y_dft/pallas_call | solution.py:170
  130.6 8.5 %y_dft.3 = (bf16[4,2048,128]{2,1,0:T(8,128)(2,1)S(1)}, bf16[4,2048,128]{2,1,0:T(8,128)(2,1)S(1)}) custom-call(f32[2,2]{1,0:T(2,128)S(1)} %reshape.159.coef_ref, f32[2048,256]{1,0:T(8,128)} %bitcast.12.refs_0_, f32[2048,256]{1,0:T(8,128)} %collective-permute-done.5.refs_1_, bf16[512,1536]{1,0:T(8,128)(2,1)S(1)} %copy-done.3, f32[2,8,256,128]{3,2,1,0:T(8,128)S(1)} %copy-done.1), custom_call_target="tpu_custom_call" | custom-call | flops 3221225472 | bytes 10485760 | tf_op jit(solution)/shard_map/y_dft/pallas_call | solution.py:170
  139.1 10.0 %x_dft.1 = (f32[2,1,2048,512]{3,2,1,0:T(8,128)}, f32[8,128]{1,0:T(8,128)S(1)}) custom-call(bf16[4,2048,128]{2,1,0:T(8,128)(2,1)S(1)} %get-tuple-element.29.refs_0_, bf16[4,2048,128]{2,1,0:T(8,128)(2,1)S(1)} %get-tuple-element.32.refs_1_, bf16[4,2048,128]{2,1,0:T(8,128)(2,1)S(1)} %get-tuple-element.33.refs_2_, ...), custom_call_target="tpu_custom_call" | custom-call | flops 6442450944 | bytes 16777216 | tf_op jit(solution)/shard_map/x_dft/pallas_call | solution.py:250
  149.1 13.3 %all_to_all.23 = f32[32,8,128]{2,1,0:T(8,128)S(1)} all-to-all(f32[32,8,128]{2,1,0:T(8,128)S(1)} %broadcast_in_dim.2), channel_id=1, replica_groups=mesh['gx'=4,'gy'=8] {'gx','gy'}, dimensions={0} | all-to-all | bytes 262144 | tf_op jit(solution)/shard_map/all_to_all | solution.py:281
  162.4 0.6 reduce_sum.29
  (60 shorter events, 0.3 us)
Async XLA Ops:
  0.6 5.9 %copy-start.7 = (f32[8,256,512]{2,1,0:T(8,128)S(1)}, f32[8,256,512]{2,1,0:T(8,128)}, u32[]{:S(2)}) copy-start(f32[8,256,512]{2,1,0:T(8,128)} %param.6) | copy-start | bytes 12582916
  3.5 51.5 %collective-permute-start = (f32[4,256,256]{2,1,0:T(8,128)S(1)}, f32[4,256,256]{2,1,0:T(8,128)}, u32[]{:S(2)}, u32[]{:S(2)}) collective-permute-start(f32[4,256,256]{2,1,0:T(8,128)S(1)} %get-tuple-element.22.early_ref), channel_id=1, source_target_pairs={{0,16},{8,24},{16,0},{24,8},{1,17},{9,25},{17,1},{25,9},{2,18},{10... | collective-permute-start | bytes 3145736 | tf_op jit(solution)/shard_map/ppermute | solution.py:20
  6.5 45.7 %collective-permute-start.1 = (f32[4,256,256]{2,1,0:T(8,128)}, f32[4,256,256]{2,1,0:T(8,128)}, u32[]{:S(2)}, u32[]{:S(2)}) collective-permute-start(f32[4,256,256]{2,1,0:T(8,128)} %get-tuple-element.23.early_ref), channel_id=1, source_target_pairs={{0,16},{8,24},{16,0},{24,8},{1,17},{9,25},{17,1},{25,9},{2,18},{10... | collective-permute-start | bytes 3145736 | tf_op jit(solution)/shard_map/ppermute | solution.py:20
  8.1 54.0 %all-to-all-start = ((f32[8,256,256]{2,1,0:T(8,128)}), f32[8,256,256]{2,1,0:T(8,128)S(1)}, u32[]{:S(2)}, u32[]{:S(2)}) async-start(f32[8,256,256]{2,1,0:T(8,128)} %slice.91), calls=%async_computation | async-start | bytes 4194304 | tf_op jit(solution)/shard_map/all_to_all | solution.py:24
  25.3 2.8 %copy-start.18 = (f32[2048]{0:T(1024)S(1)}, f32[2048]{0:T(1024)}, u32[]{:S(2)}) copy-start(f32[2048]{0:T(1024)} %param.7) | copy-start | bytes 24580
  25.3 3.4 %copy-start.16 = (f32[512]{0:T(512)S(1)}, f32[512]{0:T(512)}, u32[]{:S(2)}) copy-start(f32[512]{0:T(512)} %param.8) | copy-start | bytes 6148
  26.3 6.0 %copy-start.17 = (f32[512]{0:T(512)S(1)}, f32[512]{0:T(512)}, u32[]{:S(2)}) copy-start(f32[512]{0:T(512)} %param.8) | copy-start | bytes 6148
  26.3 6.0 %copy-start.19 = (f32[512]{0:T(512)S(1)}, f32[512]{0:T(512)}, u32[]{:S(2)}) copy-start(f32[512]{0:T(512)} %param.11) | copy-start | bytes 6148
  26.3 6.0 %copy-start.20 = (f32[512]{0:T(512)S(1)}, f32[512]{0:T(512)}, u32[]{:S(2)}) copy-start(f32[512]{0:T(512)} %param.10) | copy-start | bytes 6148
  32.5 2.5 %copy-start.14 = (f32[256,512]{1,0:T(8,128)S(1)}, f32[256,512]{1,0:T(8,128)}, u32[]{:S(2)}) copy-start(f32[256,512]{1,0:T(8,128)} %get-tuple-element.76) | copy-start | bytes 1572868
  32.5 2.5 %copy-start.15 = (f32[256,512]{1,0:T(8,128)S(1)}, f32[256,512]{1,0:T(8,128)}, u32[]{:S(2)}) copy-start(f32[256,512]{1,0:T(8,128)} %get-tuple-element.77) | copy-start | bytes 1572868
  35.3 5.7 %copy-start.6 = (f32[2,2,128,512]{3,2,1,0:T(8,128)S(1)}, f32[2,2,128,512]{3,2,1,0:T(8,128)}, u32[]{:S(2)}) copy-start(f32[2,2,128,512]{3,2,1,0:T(8,128)} %maximum_maximum_fusion) | copy-start | bytes 3145732
  43.5 3.2 %copy-start.12 = (bf16[512,512]{1,0:T(8,128)(2,1)S(1)}, bf16[512,512]{1,0:T(8,128)(2,1)}, u32[]{:S(2)}) copy-start(bf16[512,512]{1,0:T(8,128)(2,1)} %get-tuple-element.48) | copy-start | bytes 1572868
  43.5 3.2 %copy-start.13 = (bf16[512,512]{1,0:T(8,128)(2,1)S(1)}, bf16[512,512]{1,0:T(8,128)(2,1)}, u32[]{:S(2)}) copy-start(bf16[512,512]{1,0:T(8,128)(2,1)} %get-tuple-element.49) | copy-start | bytes 1572868
  46.7 1.3 copy-start.8
  46.7 1.6 copy-start.9
  46.7 2.9 %copy-start.10 = (bf16[512,512]{1,0:T(8,128)(2,1)S(1)}, bf16[512,512]{1,0:T(8,128)(2,1)}, u32[]{:S(2)}) copy-start(bf16[512,512]{1,0:T(8,128)(2,1)} %get-tuple-element.44) | copy-start | bytes 1572868
  46.7 2.9 %copy-start.11 = (bf16[512,512]{1,0:T(8,128)(2,1)S(1)}, bf16[512,512]{1,0:T(8,128)(2,1)}, u32[]{:S(2)}) copy-start(bf16[512,512]{1,0:T(8,128)(2,1)} %get-tuple-element.45) | copy-start | bytes 1572868
  62.0 52.2 %all-to-all-start.1 = ((f32[8,256,256]{2,1,0:T(8,128)}), f32[8,256,256]{2,1,0:T(8,128)}, u32[]{:S(2)}, u32[]{:S(2)}) async-start(f32[8,256,256]{2,1,0:T(8,128)} %combine.3), calls=%async_computation.1 | async-start | bytes 4194304 | tf_op jit(solution)/shard_map/all_to_all | solution.py:24
  66.6 46.5 %collective-permute-start.2 = (f32[2048,256]{1,0:T(8,128)S(1)}, f32[2048,256]{1,0:T(8,128)}, u32[]{:S(2)}, u32[]{:S(2)}) collective-permute-start(f32[2048,256]{1,0:T(8,128)S(1)} %bitcast.15), channel_id=1, source_target_pairs={{0,16},{8,24},{16,0},{24,8},{1,17},{9,25},{17,1},{25,9},{2,18},{10... | collective-permute-start | bytes 6291464 | tf_op jit(solution)/shard_map/ppermute | solution.py:20
  68.2 46.0 %collective-permute-start.4 = (f32[2048,256]{1,0:T(8,128)S(1)}, f32[2048,256]{1,0:T(8,128)}, u32[]{:S(2)}, u32[]{:S(2)}) collective-permute-start(f32[2048,256]{1,0:T(8,128)S(1)} %bitcast.16), channel_id=1, source_target_pairs={{0,8},{8,0},{16,24},{24,16},{1,9},{9,1},{17,25},{25,17},{2,10},{10... | collective-permute-start | bytes 6291464 | tf_op jit(solution)/shard_map/ppermute | solution.py:20
  113.0 4.5 %collective-permute-start.3 = (f32[2048,256]{1,0:T(8,128)}, f32[2048,256]{1,0:T(8,128)}, u32[]{:S(2)}, u32[]{:S(2)}) collective-permute-start(f32[2048,256]{1,0:T(8,128)} %collective-permute-done.2.refs_0_), channel_id=1, source_target_pairs={{0,8},{8,0},{16,24},{24,16},{1,9},{9,1},{17,25},{25,17},{2,10},{10... | collective-permute-start | bytes 6291464 | tf_op jit(solution)/shard_map/ppermute | solution.py:20
  114.2 16.4 %collective-permute-start.5 = (f32[2048,256]{1,0:T(8,128)}, f32[2048,256]{1,0:T(8,128)}, u32[]{:S(2)}, u32[]{:S(2)}) collective-permute-start(f32[2048,256]{1,0:T(8,128)} %bitcast.12.refs_0_), channel_id=1, source_target_pairs={{0,8},{8,0},{16,24},{24,16},{1,9},{9,1},{17,25},{25,17},{2,10},{10... | collective-permute-start | bytes 6291464 | tf_op jit(solution)/shard_map/ppermute | solution.py:20
  117.5 1.6 copy-start
  119.1 1.4 copy-start.2
  120.5 10.0 %copy-start.1 = (f32[2,8,256,128]{3,2,1,0:T(8,128)S(1)}, f32[2,8,256,128]{3,2,1,0:T(8,128)}, u32[]{:S(2)}) copy-start(f32[2,8,256,128]{3,2,1,0:T(8,128)} %pad_maximum_fusion.refs_5_.refs_3_) | copy-start | bytes 6291460
  120.6 10.0 %copy-start.3 = (bf16[512,1536]{1,0:T(8,128)(2,1)S(1)}, bf16[512,1536]{1,0:T(8,128)(2,1)}, u32[]{:S(2)}) copy-start(bf16[512,1536]{1,0:T(8,128)(2,1)} %pad_maximum_fusion.1.refs_4_.refs_2_) | copy-start | bytes 4718596
  130.5 8.5 %copy-start.4 = (bf16[1536,512]{1,0:T(8,128)(2,1)S(1)}, bf16[1536,512]{1,0:T(8,128)(2,1)}, u32[]{:S(2)}) copy-start(bf16[1536,512]{1,0:T(8,128)(2,1)} %pad_maximum_fusion.2.refs_4_) | copy-start | bytes 4718596
  130.6 8.5 %copy-start.5 = (bf16[1536,512]{1,0:T(8,128)(2,1)S(1)}, bf16[1536,512]{1,0:T(8,128)(2,1)}, u32[]{:S(2)}) copy-start(bf16[1536,512]{1,0:T(8,128)(2,1)} %pad_maximum_fusion.3.refs_5_) | copy-start | bytes 4718596

commit v12 on v11

--- a/solution.py
+++ b/solution.py
@@ -11,7 +11,7 @@
 precision_top = lax.Precision.HIGHEST
 RADIX = 8
 LANES = 128
-SMALL_BYTES, Y_BYTES, X_BYTES = [size * 1024 * 1024 for size in (8, 30, 26)]
+SMALL_BYTES, Y_BYTES, X_BYTES = [size * 1024 * 1024 for size in (8, 27, 26)]
 
 
 def from_partner(value, axis, stride):
@@ -84,10 +84,9 @@
     return root_table(rows, freqs, devices * width)
 
 
-def split_table(table, axis, order):
+def split_table(table):
     high = lax.reduce_precision(table, 8, 7)
-    parts = [high.astype(jnp.bfloat16), (table - high).astype(jnp.bfloat16)]
-    return jnp.concatenate([parts[which] for which in order], axis)
+    return jnp.stack([high.astype(jnp.bfloat16), (table - high).astype(jnp.bfloat16)])
 
 
 def split_value(value):
@@ -139,12 +138,14 @@
     for tile, out_ref in enumerate(out_refs):
         for which in range(2):
             for s in range(RADIX):
-                high, low = split_value(mix_ref[2 * tile + which, pl.ds(s, inner, stride=RADIX), :])
-                for place, value in enumerate((high, high, low)):
-                    split_ref[tile, pl.ds((2 * place + which) * inner, inner), pl.ds(s * LANES, LANES)] = value
+                parts = split_value(mix_ref[2 * tile + which, pl.ds(s, inner, stride=RADIX), :])
+                for place, value in enumerate(parts):
+                    split_ref[tile, place, pl.ds(which * inner, inner), pl.ds(s * LANES, LANES)] = value
         half = inner // 2
         for part in range(2):
-            step_ref[part] = dot(table_ref[pl.ds(part * inner, inner), :], split_ref[tile])
+            table = [table_ref[place, pl.ds(part * inner, inner), :] for place in (0, 1, 0)]
+            values = [split_ref[tile, place] for place in (0, 0, 1)]
+            step_ref[part] = dot(jnp.concatenate(table, axis=1), jnp.concatenate(values, axis=0))
             for start in range(0, half, 16):
                 values = []
                 for s in range(RADIX):
@@ -174,7 +175,7 @@
         out_specs=[whole] * 2,
         scratch_shapes=[
             pltpu.VMEM((4, length, LANES), jnp.float32),
-            pltpu.VMEM((2, 6 * inner, RADIX * LANES), jnp.bfloat16),
+            pltpu.VMEM((2, 2, 2 * inner, RADIX * LANES), jnp.bfloat16),
             pltpu.VMEM((2, inner, RADIX * LANES), jnp.float32),
         ],
         compiler_params=pltpu.CompilerParams(vmem_limit_bytes=Y_BYTES),
@@ -192,12 +193,17 @@
     totals = []
 
     def left(refs, rows):
+        first = pl.multiple_of(pl.program_id(0) * out_ref.shape[2], out_ref.shape[2])
+        rows = pl.ds(first + rows, rows_each)
         high, low = [[ref[k + which, rows, :] for ref in refs for k in (0, 2)] for which in range(2)]
         return jnp.concatenate(high + low + high, axis=1)
 
     def multiply(sides, tile):
         cols = pl.ds(tile * 2 * lanes, 2 * lanes)
-        return [dot(side, table_ref[:, cols]) for side, table_ref in zip(sides, (even_ref, odd_ref))]
+        return [
+            dot(side, jnp.concatenate([table_ref[place, :, cols] for place in (0, 0, 1)], axis=0))
+            for side, table_ref in zip(sides, (even_ref, odd_ref))
+        ]
 
     def finish(start, tile, even, odd):
         rows = pl.ds(start, rows_each)
@@ -227,7 +233,7 @@
 
     before = None
     for start in range(0, out_ref.shape[2], rows_each):
-        sides = [left(group, pl.ds(start, rows_each)) for group in (parts[:count], parts[count:])]
+        sides = [left(group, start) for group in (parts[:count], parts[count:])]
         for tile in range(tiles):
             products = multiply(sides, tile)
             if before is not None:
@@ -244,9 +250,9 @@
 
 def x_dft(even_parts, odd_parts, even_table, odd_table, row_pair, col_trio):
     parts, count, length = even_parts + odd_parts, len(even_parts), even_parts[0].shape[1]
-    columns = even_table.shape[1]
+    columns = even_table.shape[2]
     rows = length // row_pair.shape[1]
-    fixed = [pl.BlockSpec(memory_space=pltpu.VMEM)] * 2
+    whole = [pl.BlockSpec(memory_space=pltpu.VMEM)] * (len(parts) + 2)
     return pl.pallas_call(
         functools.partial(x_kernel, count),
         out_shape=(
@@ -254,8 +260,7 @@
             jax.ShapeDtypeStruct((8, LANES), jnp.float32),
         ),
         grid=(length // rows,),
-        in_specs=[pl.BlockSpec((4, rows, part.shape[2]), lambda i: (0, i, 0)) for part in parts]
-        + fixed
+        in_specs=whole
         + [
             pl.BlockSpec((2, 1, rows // LANES, LANES), lambda i: (0, i, 0, 0)),
             pl.BlockSpec(col_trio.shape, lambda i: (0, 0)),
@@ -266,7 +271,7 @@
         ),
         compiler_params=pltpu.CompilerParams(vmem_limit_bytes=X_BYTES),
         cost_estimate=pl.CostEstimate(
-            flops=4 * length * even_table.size,
+            flops=6 * length * even_table.size,
             bytes_accessed=16 * length * columns,
             transcendentals=2 * length * columns,
         ),
@@ -302,7 +307,7 @@
     cos, sin = root_table(index, index, inner)
     y_table = [jnp.concatenate(pair, 1).reshape(2, 1, inner // 2, 2 * inner) for pair in ((cos, -sin), (sin, cos))]
     y_table = jnp.concatenate(y_table, 1).reshape(2 * inner, 2 * inner)
-    y_table = split_table(y_table, 1, (0, 1, 0))
+    y_table = split_table(y_table)
     grid = [lax.broadcasted_iota(jnp.int32, (RADIX, inner, LANES), axis) for axis in range(2)]
     angle = (grid[0] * grid[1]).astype(jnp.float32) * (-2.0 * math.pi / length)
     twist = jnp.stack([jnp.cos(angle), jnp.sin(angle)])
@@ -318,7 +323,7 @@
 
         real, imag = lay(cos, sin), lay(-sin, cos)
         table = jnp.concatenate([real[:width], imag[:width], real[width:], imag[width:]], 0)
-        return split_table(table, 0, (0, 0, 1))
+        return split_table(table)
 
     norm = 1.0 / math.sqrt(length * columns * 4)
     row_pair = jnp.stack([row_scale * norm, row_rate]).reshape(2, 4, length // 4 // LANES, LANES)

time: 165 us -> 161 us (0.976)
  waiting for transfers between devices: 55.2 us -> 69.2 us
  other arithmetic: 30.7 us -> 21.4 us
  local copies, waits for them, and re-layouts: 12.4 us -> 5.25 us
  Pallas kernels: 33.8 us -> 31.9 us
    ppermute x6, waiting for transfers between devices: 49.6 us -> 62.3 us  [from_partner(): return lax.ppermute(value, axis, pairs)]
    another operation x0 -> x3, other arithmetic: none -> 4.4 us  [split_table(): jnp.stack([high.astype(jnp.bfloat16), (table - high).astype(jnp.bfloat16)])]
    concatenate x3 -> x0, other arithmetic: 3.82 us -> none  [split_table(): return jnp.concatenate([parts[which] for which in order], axis)]
    convert_element_type x3, other arithmetic: 4.72 us -> 1.5 us  [split_table(): high.astype(jnp.bfloat16)]
    unnamed x42 -> x26, local copies, waits for them, and re-layouts: 3.39 us -> 0.82 us
    concatenate x1, other arithmetic: 2.25 us -> 0.1 us  [four_way(): y_table = jnp.concatenate(y_table, 1).reshape(2 * inner, 2 * inner)]
    slice x6, local copies, waits for them, and re-layouts: 2.69 us -> 0.8 us  [lay(): side[:, span]]
    slice x4 -> x0, local copies, waits for them, and re-layouts: 1.78 us -> none  [the longest x2 0.9 us: x_table(): real[:width]]
  transfers between devices with their start and end apart: 8 -> 8, of which waited for: 5 -> 5; matrix products, arithmetic and copies ran while one was open for 22% -> 15% of each run, Pallas kernels for 9% -> 9%
where the time goes in v12:
time: 161 us
  waiting for transfers between devices  69.2 us (43%)
  Pallas kernels  31.9 us (20%)
  other arithmetic  21.4 us (13%)
  starting transfers between devices  15.7 us (10%)
  blocking collectives  13.3 us (8%)
  local copies, waits for them, and re-layouts  5.25 us (3%)
  between operations  4.02 us (2%)
    ppermute x6, waiting for transfers between devices, from_partner(): return lax.ppermute(value, axis, pairs)  62.3 us
    pallas_call x2, Pallas kernels, y_dft(): pl.pallas_call(functools.partial(y_kernel, len(inputs), pick), out_shape=...  18.2 us
    all_to_all x1, blocking collectives, sum_everywhere(): lax.all_to_all(copies, axes, split_axis=0, concat_axis=0, tiled=True)  13.3 us
    all_to_all x2, starting transfers between devices, to_planes(): return lax.all_to_all(values, 'gy', split_axis=0, concat_axis=1, tiled=True)  11 us
    pallas_call x1, Pallas kernels, x_dft(): pl.pallas_call(functools.partial(x_kernel, count), out_shape=(jax.ShapeDt...  9.61 us
    all_to_all x2, waiting for transfers between devices, to_planes(): return lax.all_to_all(values, 'gy', split_axis=0, concat_axis=1, tiled=True)  6.89 us
    sin x1, other arithmetic, root_table(): return (jnp.cos(angle), jnp.sin(angle))  5.16 us
    ppermute x6, starting transfers between devices, from_partner(): return lax.ppermute(value, axis, pairs)  4.71 us
  transfers between devices with their start and end apart: 8, of which 5 were waited for; matrix products, arithmetic and copies ran while one was open for 15% of the time, Pallas kernels for 9%

profile of v12, /device:TPU:0, one launch (start us, length us, event | category | flops | bytes accessed | tf_op | source)
XLA Modules:
  0.0 160.8 jit_solution(13585214798326274811)
XLA Ops:
  0.6 0.0 copy-start.4
  0.6 1.8 %fusion.24 = (f32[4,256,256]{2,1,0:T(8,128)S(1)}, f32[4,256,256]{2,1,0:T(8,128)S(1)}) fusion(f32[8,256,512]{2,1,0:T(8,128)} %param.6), kind=kLoop, calls=%fused_computation.82 | loop fusion | bytes 4194304 | tf_op jit(solution)/shard_map/slice | solution.py:294
  2.5 3.0 %collective-permute-start = (f32[4,256,256]{2,1,0:T(8,128)S(1)}, f32[4,256,256]{2,1,0:T(8,128)S(1)}, u32[]{:S(2)}, u32[]{:S(2)}) collective-permute-start(f32[4,256,256]{2,1,0:T(8,128)S(1)} %get-tuple-element.22.early_ref), channel_id=1, source_target_pairs={{0,16},{8,24},{16,0},{24,8},{1,17},{9,25},{17,1},{25,9},{2,18},{10... | collective-permute-start | bytes 3145736 | tf_op jit(solution)/shard_map/ppermute | solution.py:20
  5.5 0.1 collective-permute-start.1
  5.6 0.0 copy-done.4
  5.6 1.6 slice.91
  7.1 6.2 %all-to-all-start = ((f32[8,256,256]{2,1,0:T(8,128)}), f32[8,256,256]{2,1,0:T(8,128)}, u32[]{:S(2)}, u32[]{:S(2)}) async-start(f32[8,256,256]{2,1,0:T(8,128)} %slice.91), calls=%async_computation | async-start | bytes 4194304 | tf_op jit(solution)/shard_map/all_to_all | solution.py:24
  13.4 1.1 fusion.23
  14.6 0.1 maximum_maximum_fusion
  14.7 1.2 reduce-precision_convert_fusion.2
  15.9 5.2 %fusion.14 = (f32[256,512]{1,0:T(8,128)}, f32[256,512]{1,0:T(8,128)}, f32[256,512]{1,0:T(8,128)S(1)}, f32[256,512]{1,0:T(8,128)S(1)}) fusion(s32[512]{0:T(512)S(1)} %multiply_add_fusion, s32[256]{0:T(256)S(1)} %pad_add_fusion.1, s32[256]{0:T(256)S(1)} %pad_add_fusion), kind=kLoop, calls=%fused_computation.55 | loop fusion | flops 3670016 | bytes 2101248 | tf_op jit(solution)/shard_map/sin | solution.py:77
  21.1 0.8 copy-done.6
  21.9 0.7 fusion.28
  22.6 0.7 log_reduce_fusion
  23.2 0.1 pad_maximum_fusion.13
  23.3 0.1 reshape.444.coef_ref
  23.4 0.6 log_reduce_fusion.1
  24.0 2.3 %pad_maximum_fusion.1.refs_4_.refs_2_ = bf16[2,512,512]{2,1,0:T(8,128)(2,1)} fusion(bf16[1,512,512]{2,1,0:T(8,128)(2,1)} %get-tuple-element.49, bf16[1,512,512]{2,1,0:T(8,128)(2,1)} %get-tuple-element.48), kind=kLoop, calls=%fused_computation.11 | loop fusion | flops 524288 | bytes 2097152 | tf_op jit(solution)/shard_map/stack | solution.py:89
  26.3 0.1 pad_maximum_fusion.12.coef_ref
  27.7 1.0 slice_negate_fusion.1
  28.7 1.2 pad_maximum_fusion.6
  30.0 0.2 reduce-precision_convert_fusion.1
  30.1 1.1 pad_maximum_fusion.3.refs_4_
  31.3 0.1 pad_maximum_fusion.8
  31.5 0.2 reduce-precision_convert_fusion
  31.7 1.1 pad_maximum_fusion.5.refs_5_
  32.7 3.2 %fusion.3 = (f32[1,8,256,128]{3,2,1,0:T(8,128)S(1)}, f32[1,8,256,128]{3,2,1,0:T(8,128)S(1)}) fusion(), kind=kLoop, calls=%fused_computation.17 | loop fusion | flops 786432 | bytes 2097152 | tf_op jit(solution)/shard_map/sin | solution.py:313
  36.0 1.5 pad_maximum_fusion.refs_5_.refs_3_
  37.5 13.7 %collective-permute-done.1.late_ref = f32[4,256,256]{2,1,0:T(8,128)} collective-permute-done((f32[4,256,256]{2,1,0:T(8,128)S(1)}, f32[4,256,256]{2,1,0:T(8,128)}, u32[]{:S(2)}, u32[]{:S(2)}) %collective-permute-start.1) | collective-permute-done | bytes 1048608 | tf_op jit(solution)/shard_map/ppermute | solution.py:20
  51.2 2.6 %combine.2.refs_0_ = f32[8,256,256]{2,1,0:T(8,128)} custom-call(f32[1]{0:T(128)} %bitcast.sign_ref, f32[4,256,256]{2,1,0:T(8,128)} %collective-permute-done.1.late_ref, f32[4,256,256]{2,1,0:T(8,128)S(1)} %get-tuple-element.23.early_ref), custom_call_target="tpu_custom_call" | custom-call | flops 524288 | bytes 3145728 | tf_op jit(solution)/shard_map/combine/pallas_call | solution.py:50
  53.8 0.0 collective-permute-done.late_ref
  53.8 1.5 combine.3
  55.3 5.9 %all-to-all-done = f32[8,256,256]{2,1,0:T(8,128)} async-done(((f32[8,256,256]{2,1,0:T(8,128)}), f32[8,256,256]{2,1,0:T(8,128)}, u32[]{:S(2)}, u32[]{:S(2)}) %all-to-all-start) | async-done | bytes 2097184 | tf_op jit(solution)/shard_map/all_to_all | solution.py:24
  61.2 4.8 %all-to-all-start.1 = ((f32[8,256,256]{2,1,0:T(8,128)}), f32[8,256,256]{2,1,0:T(8,128)}, u32[]{:S(2)}, u32[]{:S(2)}) async-start(f32[8,256,256]{2,1,0:T(8,128)} %combine.3), calls=%async_computation.1 | async-start | bytes 4194304 | tf_op jit(solution)/shard_map/all_to_all | solution.py:24
  66.0 1.6 collective-permute-start.2
  67.6 0.0 collective-permute-start.4
  67.6 45.1 %collective-permute-done.2.refs_0_ = f32[2048,256]{1,0:T(8,128)} collective-permute-done((f32[2048,256]{1,0:T(8,128)}, f32[2048,256]{1,0:T(8,128)}, u32[]{:S(2)}, u32[]{:S(2)}) %collective-permute-start.2) | collective-permute-done | bytes 2097184 | tf_op jit(solution)/shard_map/ppermute | solution.py:20
  112.7 0.0 collective-permute-start.3
  112.7 1.0 all-to-all-done.1
  113.7 0.0 collective-permute-start.5
  113.7 0.0 collective-permute-done.4.refs_3_
  113.7 3.5 %collective-permute-done.3.refs_1_ = f32[2048,256]{1,0:T(8,128)} collective-permute-done((f32[2048,256]{1,0:T(8,128)}, f32[2048,256]{1,0:T(8,128)}, u32[]{:S(2)}, u32[]{:S(2)}) %collective-permute-start.3) | collective-permute-done | bytes 2097184 | tf_op jit(solution)/shard_map/ppermute | solution.py:20
  117.2 10.2 %y_dft.2 = (bf16[4,2048,128]{2,1,0:T(8,128)(2,1)S(1)}, bf16[4,2048,128]{2,1,0:T(8,128)(2,1)S(1)}) custom-call(f32[2,4]{1,0:T(2,128)S(1)} %pad_maximum_fusion.12.coef_ref, f32[2048,256]{1,0:T(8,128)} %collective-permute-done.2.refs_0_, f32[2048,256]{1,0:T(8,128)} %collective-permute-done.3.refs_1_, f32[2048,256]{1,0:T(8,128)} %bitcast.1.refs_2_, ...), custom_call_target="tpu_custom_call" | custom-call | flops 3221225472 | bytes 14680064 | tf_op jit(solution)/shard_map/y_dft/pallas_call | solution.py:171
  127.4 0.0 collective-permute-done.5.refs_1_
  127.4 8.1 %y_dft.3 = (bf16[4,2048,128]{2,1,0:T(8,128)(2,1)S(1)}, bf16[4,2048,128]{2,1,0:T(8,128)(2,1)S(1)}) custom-call(f32[2,2]{1,0:T(2,128)S(1)} %reshape.444.coef_ref, f32[2048,256]{1,0:T(8,128)} %bitcast.20.refs_0_, f32[2048,256]{1,0:T(8,128)} %collective-permute-done.5.refs_1_, bf16[2,512,512]{2,1,0:T(8,128)(2,1)S(1)} %copy-done.1, f32[2,8,256,128]{3,2,1,0:T(8,128)S(1)} %copy-done), custom_call_target="tpu_custom_call" | custom-call | flops 3221225472 | bytes 10485760 | tf_op jit(solution)/shard_map/y_dft/pallas_call | solution.py:171
  135.5 9.6 %x_dft.1 = (f32[2,1,2048,512]{3,2,1,0:T(8,128)}, f32[8,128]{1,0:T(8,128)S(1)}) custom-call(bf16[4,2048,128]{2,1,0:T(8,128)(2,1)S(1)} %get-tuple-element.29.refs_0_, bf16[4,2048,128]{2,1,0:T(8,128)(2,1)S(1)} %get-tuple-element.32.refs_1_, bf16[4,2048,128]{2,1,0:T(8,128)(2,1)S(1)} %get-tuple-element.33.refs_2_, ...), custom_call_target="tpu_custom_call" | custom-call | flops 6442450944 | bytes 16777216 | tf_op jit(solution)/shard_map/x_dft/pallas_call | solution.py:256
  145.1 13.3 %all_to_all.23 = f32[32,8,128]{2,1,0:T(8,128)S(1)} all-to-all(f32[32,8,128]{2,1,0:T(8,128)S(1)} %broadcast_in_dim.2), channel_id=1, replica_groups=mesh['gx'=4,'gy'=8] {'gx','gy'}, dimensions={0} | all-to-all | bytes 262144 | tf_op jit(solution)/shard_map/all_to_all | solution.py:286
  158.4 0.6 reduce_sum.29
  (44 shorter events, 0.4 us)
Async XLA Ops:
  0.6 5.0 %copy-start.4 = (f32[8,256,512]{2,1,0:T(8,128)S(1)}, f32[8,256,512]{2,1,0:T(8,128)}, u32[]{:S(2)}) copy-start(f32[8,256,512]{2,1,0:T(8,128)} %param.6) | copy-start | bytes 12582916
  2.5 51.3 %collective-permute-start = (f32[4,256,256]{2,1,0:T(8,128)S(1)}, f32[4,256,256]{2,1,0:T(8,128)S(1)}, u32[]{:S(2)}, u32[]{:S(2)}) collective-permute-start(f32[4,256,256]{2,1,0:T(8,128)S(1)} %get-tuple-element.22.early_ref), channel_id=1, source_target_pairs={{0,16},{8,24},{16,0},{24,8},{1,17},{9,25},{17,1},{25,9},{2,18},{10... | collective-permute-start | bytes 3145736 | tf_op jit(solution)/shard_map/ppermute | solution.py:20
  5.5 45.7 %collective-permute-start.1 = (f32[4,256,256]{2,1,0:T(8,128)S(1)}, f32[4,256,256]{2,1,0:T(8,128)}, u32[]{:S(2)}, u32[]{:S(2)}) collective-permute-start(f32[4,256,256]{2,1,0:T(8,128)S(1)} %get-tuple-element.23.early_ref), channel_id=1, source_target_pairs={{0,16},{8,24},{16,0},{24,8},{1,17},{9,25},{17,1},{25,9},{2,18},{10... | collective-permute-start | bytes 3145736 | tf_op jit(solution)/shard_map/ppermute | solution.py:20
  7.1 54.0 %all-to-all-start = ((f32[8,256,256]{2,1,0:T(8,128)}), f32[8,256,256]{2,1,0:T(8,128)}, u32[]{:S(2)}, u32[]{:S(2)}) async-start(f32[8,256,256]{2,1,0:T(8,128)} %slice.91), calls=%async_computation | async-start | bytes 4194304 | tf_op jit(solution)/shard_map/all_to_all | solution.py:24
  15.9 6.7 %copy-start.9 = (f32[2048]{0:T(1024)S(1)}, f32[2048]{0:T(1024)}, u32[]{:S(2)}) copy-start(f32[2048]{0:T(1024)} %param.7) | copy-start | bytes 24580
  15.9 7.5 %copy-start.8 = (f32[512]{0:T(512)S(1)}, f32[512]{0:T(512)}, u32[]{:S(2)}) copy-start(f32[512]{0:T(512)} %param.8) | copy-start | bytes 6148
  21.1 0.8 copy-start.6
  21.1 5.2 %copy-start.11 = (f32[512]{0:T(512)S(1)}, f32[512]{0:T(512)}, u32[]{:S(2)}) copy-start(f32[512]{0:T(512)} %param.11) | copy-start | bytes 6148
  21.1 5.2 %copy-start.12 = (f32[512]{0:T(512)S(1)}, f32[512]{0:T(512)}, u32[]{:S(2)}) copy-start(f32[512]{0:T(512)} %param.10) | copy-start | bytes 6148
  21.1 6.6 %copy-start.10 = (f32[2048]{0:T(1024)S(1)}, f32[2048]{0:T(1024)}, u32[]{:S(2)}) copy-start(f32[2048]{0:T(1024)} %param.9) | copy-start | bytes 24580
  30.0 1.2 copy-start.5
  30.0 1.3 copy-start.7
  61.2 56.0 %copy-start = (f32[2,8,256,128]{3,2,1,0:T(8,128)S(1)}, f32[2,8,256,128]{3,2,1,0:T(8,128)}, u32[]{:S(2)}) copy-start(f32[2,8,256,128]{3,2,1,0:T(8,128)} %pad_maximum_fusion.refs_5_.refs_3_) | copy-start | bytes 6291460
  61.2 56.0 %copy-start.1 = (bf16[2,512,512]{2,1,0:T(8,128)(2,1)S(1)}, bf16[2,512,512]{2,1,0:T(8,128)(2,1)}, u32[]{:S(2)}) copy-start(bf16[2,512,512]{2,1,0:T(8,128)(2,1)} %pad_maximum_fusion.1.refs_4_.refs_2_) | copy-start | bytes 3145732
  61.2 52.5 %all-to-all-start.1 = ((f32[8,256,256]{2,1,0:T(8,128)}), f32[8,256,256]{2,1,0:T(8,128)}, u32[]{:S(2)}, u32[]{:S(2)}) async-start(f32[8,256,256]{2,1,0:T(8,128)} %combine.3), calls=%async_computation.1 | async-start | bytes 4194304 | tf_op jit(solution)/shard_map/all_to_all | solution.py:24
  66.0 46.7 %collective-permute-start.2 = (f32[2048,256]{1,0:T(8,128)}, f32[2048,256]{1,0:T(8,128)}, u32[]{:S(2)}, u32[]{:S(2)}) collective-permute-start(f32[2048,256]{1,0:T(8,128)} %bitcast.1.refs_2_), channel_id=1, source_target_pairs={{0,16},{8,24},{16,0},{24,8},{1,17},{9,25},{17,1},{25,9},{2,18},{10... | collective-permute-start | bytes 6291464 | tf_op jit(solution)/shard_map/ppermute | solution.py:20
  67.6 46.1 %collective-permute-start.4 = (f32[2048,256]{1,0:T(8,128)}, f32[2048,256]{1,0:T(8,128)}, u32[]{:S(2)}, u32[]{:S(2)}) collective-permute-start(f32[2048,256]{1,0:T(8,128)} %bitcast.1.refs_2_), channel_id=1, source_target_pairs={{0,8},{8,0},{16,24},{24,16},{1,9},{9,1},{17,25},{25,17},{2,10},{10... | collective-permute-start | bytes 6291464 | tf_op jit(solution)/shard_map/ppermute | solution.py:20
  112.7 4.5 %collective-permute-start.3 = (f32[2048,256]{1,0:T(8,128)}, f32[2048,256]{1,0:T(8,128)}, u32[]{:S(2)}, u32[]{:S(2)}) collective-permute-start(f32[2048,256]{1,0:T(8,128)} %collective-permute-done.2.refs_0_), channel_id=1, source_target_pairs={{0,8},{8,0},{16,24},{24,16},{1,9},{9,1},{17,25},{25,17},{2,10},{10... | collective-permute-start | bytes 6291464 | tf_op jit(solution)/shard_map/ppermute | solution.py:20
  113.7 13.7 %collective-permute-start.5 = (f32[2048,256]{1,0:T(8,128)}, f32[2048,256]{1,0:T(8,128)}, u32[]{:S(2)}, u32[]{:S(2)}) collective-permute-start(f32[2048,256]{1,0:T(8,128)} %bitcast.20.refs_0_), channel_id=1, source_target_pairs={{0,8},{8,0},{16,24},{24,16},{1,9},{9,1},{17,25},{25,17},{2,10},{10... | collective-permute-start | bytes 6291464 | tf_op jit(solution)/shard_map/ppermute | solution.py:20
  127.3 8.1 %copy-start.2 = (bf16[2,512,512]{2,1,0:T(8,128)(2,1)S(1)}, bf16[2,512,512]{2,1,0:T(8,128)(2,1)}, u32[]{:S(2)}) copy-start(bf16[2,512,512]{2,1,0:T(8,128)(2,1)} %pad_maximum_fusion.3.refs_4_) | copy-start | bytes 3145732
  127.3 8.1 %copy-start.3 = (bf16[2,512,512]{2,1,0:T(8,128)(2,1)S(1)}, bf16[2,512,512]{2,1,0:T(8,128)(2,1)}, u32[]{:S(2)}) copy-start(bf16[2,512,512]{2,1,0:T(8,128)(2,1)} %pad_maximum_fusion.5.refs_5_) | copy-start | bytes 3145732

commit v13 on v12

--- a/solution.py
+++ b/solution.py
@@ -11,7 +11,7 @@
 precision_top = lax.Precision.HIGHEST
 RADIX = 8
 LANES = 128
-SMALL_BYTES, Y_BYTES, X_BYTES = [size * 1024 * 1024 for size in (8, 27, 26)]
+SMALL_BYTES, Y_BYTES, X_BYTES = [size * 1024 * 1024 for size in (8, 25, 26)]
 
 
 def from_partner(value, axis, stride):
@@ -64,6 +64,28 @@
     return result[0]
 
 
+def cut_kernel(field_ref, out_ref):
+    for plane in range(field_ref.shape[0]):
+        left, right = [field_ref[plane, :, pl.ds(lane, LANES)] for lane in (0, LANES)]
+        for odd in range(2):
+            out_ref[plane, :, pl.ds(odd * LANES, LANES)] = pick_columns(left, right, odd)
+
+
+def cut_right(field):
+    planes, rows, columns = field.shape
+    block = (planes // 4, rows, columns // 2)
+    return pl.pallas_call(
+        cut_kernel,
+        out_shape=jax.ShapeDtypeStruct((planes, rows, columns // 2), jnp.float32),
+        grid=(4,),
+        in_specs=[pl.BlockSpec(block, lambda i: (i, 0, 1))],
+        out_specs=pl.BlockSpec(block, lambda i: (i, 0, 0)),
+        cost_estimate=pl.CostEstimate(flops=field.size, bytes_accessed=4 * field.size, transcendentals=0),
+        compiler_params=pltpu.CompilerParams(vmem_limit_bytes=SMALL_BYTES),
+        name="cut_right",
+    )(field)
+
+
 def reverse_bits(value, count):
     result = value * 0
     for place in range(count):
@@ -119,22 +141,20 @@
     return jnp.dot(left, right, preferred_element_type=jnp.float32)
 
 
-def y_kernel(count, pick, coef_ref, *refs):
+def y_kernel(count, tiles, coef_ref, *refs):
     inputs, (table_ref, twist_ref, *out_refs, mix_ref, split_ref, step_ref) = refs[:count], refs[count:]
     length = mix_ref.shape[1]
     inner = length // RADIX
     rows_each = 128
-    for start in range(0, length, rows_each):
-        rows = pl.ds(start, rows_each)
-        for which in range(2):
-            tiles = []
-            for lane in (0, LANES):
-                mixed = inputs[0][rows, pl.ds(lane, LANES)] * coef_ref[which, 0]
-                for place in range(1, count):
-                    mixed = mixed + inputs[place][rows, pl.ds(lane, LANES)] * coef_ref[which, place]
-                tiles.append(mixed)
-            for tile in range(2):
-                mix_ref[2 * tile + which, rows, :] = pick_columns(*tiles, tile) if pick else tiles[tile]
+    for place, tile in enumerate(tiles):
+        cols = pl.ds(tile * LANES, LANES)
+        for start in range(0, length, rows_each):
+            rows = pl.ds(start, rows_each)
+            for which in range(2):
+                mixed = inputs[0][rows, cols] * coef_ref[which, 0]
+                for k in range(1, count):
+                    mixed = mixed + inputs[k][rows, cols] * coef_ref[which, k]
+                mix_ref[2 * place + which, rows, :] = mixed
     for tile, out_ref in enumerate(out_refs):
         for which in range(2):
             for s in range(RADIX):
@@ -164,23 +184,26 @@
                         out_ref[2 * which + 1, rows, :] = low
 
 
-def y_dft(inputs, pick, coefs, table, twist):
+def y_dft(inputs, tiles, coefs, table, twist):
     length = inputs[0].shape[0]
     inner = length // RADIX
+    count = len(tiles)
     whole = pl.BlockSpec(memory_space=pltpu.VMEM)
     return pl.pallas_call(
-        functools.partial(y_kernel, len(inputs), pick),
-        out_shape=[jax.ShapeDtypeStruct((4, length, LANES), jnp.bfloat16)] * 2,
+        functools.partial(y_kernel, len(inputs), tiles),
+        out_shape=[jax.ShapeDtypeStruct((4, length, LANES), jnp.bfloat16)] * count,
         in_specs=[pl.BlockSpec(memory_space=pltpu.SMEM)] + [whole] * (len(inputs) + 2),
-        out_specs=[whole] * 2,
+        out_specs=[whole] * count,
         scratch_shapes=[
-            pltpu.VMEM((4, length, LANES), jnp.float32),
-            pltpu.VMEM((2, 2, 2 * inner, RADIX * LANES), jnp.bfloat16),
+            pltpu.VMEM((2 * count, length, LANES), jnp.float32),
+            pltpu.VMEM((count, 2, 2 * inner, RADIX * LANES), jnp.bfloat16),
             pltpu.VMEM((2, inner, RADIX * LANES), jnp.float32),
         ],
         compiler_params=pltpu.CompilerParams(vmem_limit_bytes=Y_BYTES),
         cost_estimate=pl.CostEstimate(
-            flops=48 * inner * length * LANES, bytes_accessed=8 * length * LANES * (len(inputs) + 3), transcendentals=0
+            flops=80 * inner * length * LANES * count,
+            bytes_accessed=8 * length * LANES * (len(inputs) + 3),
+            transcendentals=0,
         ),
         name="y_dft",
     )(coefs, *inputs, table, twist)
@@ -292,7 +315,7 @@
     length, width = planes * rows, columns // 4
     groups = [slice(0, planes // 2), slice(planes // 2, None)]
     field_a, field_rest = lax.optimization_barrier(([field[group, :, : 2 * width] for group in groups], field))
-    field_b = field_rest[:, :, 2 * width :]
+    field_b = cut_right(field_rest)
     sign = jnp.where(position < 2, 1.0, -1.0)
 
     own_real = jnp.where(position == 1, -1.0, jnp.where(position == 3, 0.0, 1.0))
@@ -338,8 +361,10 @@
     second_a = to_planes(first_a)[0]
     second_b = from_partner(first_b, "gx", 1)
     group = [second_b, from_partner(second_b, "gx", 0), first_b, from_partner(first_b, "gx", 0)]
-    even_b, odd_b = y_dft(group, True, coefs_b, y_table, twist)
-    even_a, odd_a = y_dft([second_a, from_partner(second_a, "gx", 0)], False, coefs_a, y_table, twist)
+    even_b = y_dft(group, (0,), coefs_b, y_table, twist)[0]
+    even_b, second_a = lax.optimization_barrier((even_b, second_a))
+    odd_b = y_dft(group, (1,), coefs_b, y_table, twist)[0]
+    even_a, odd_a = y_dft([second_a, from_partner(second_a, "gx", 0)], (0, 1), coefs_a, y_table, twist)
     latent, tile = x_dft([even_b, even_a], [odd_b, odd_a], even_table, odd_table, row_pair, col_trio)
     tile = tile + fixed / tile.size
     modes = length * columns * lax.axis_size("gx") * lax.axis_size("gy")

time: 161 us -> 165 us (1.025)
  local copies, waits for them, and re-layouts: 5.25 us -> 11.1 us
  Pallas kernels: 31.9 us -> 35.7 us
  other arithmetic: 21.4 us -> 18.5 us
  waiting for transfers between devices: 69.2 us -> 66.4 us
    unnamed x26 -> x36, local copies, waits for them, and re-layouts: 0.82 us -> 7.24 us
    pallas_call x2 -> x4, Pallas kernels: 18.2 us -> 22 us  [the longest x3 19.2 us: y_dft(): pl.pallas_call(functools.partial(y_kernel, len(inputs), tiles), out_shape...]
    ppermute x6, waiting for transfers between devices: 62.3 us -> 59.3 us  [from_partner(): return lax.ppermute(value, axis, pairs)]
  transfers between devices with their start and end apart: 8 -> 8, of which waited for: 5 -> 4; matrix products, arithmetic and copies ran while one was open for 15% -> 12% of each run, Pallas kernels for 9% -> 11%
where the time goes in v13:
time: 165 us
  waiting for transfers between devices  66.4 us (40%)
  Pallas kernels  35.7 us (22%)
  other arithmetic  18.5 us (11%)
  starting transfers between devices  15.6 us (9%)
  blocking collectives  13.1 us (8%)
  local copies, waits for them, and re-layouts  11.1 us (7%)
  between operations  4.11 us (2%)
    ppermute x6, waiting for transfers between devices, from_partner(): return lax.ppermute(value, axis, pairs)  59.3 us
    pallas_call x3, Pallas kernels, y_dft(): pl.pallas_call(functools.partial(y_kernel, len(inputs), tiles), out_shape...  19.2 us
    all_to_all x1, blocking collectives, sum_everywhere(): lax.all_to_all(copies, axes, split_axis=0, concat_axis=0, tiled=True)  13.1 us
    all_to_all x2, starting transfers between devices, to_planes(): return lax.all_to_all(values, 'gy', split_axis=0, concat_axis=1, tiled=True)  10.8 us
    pallas_call x1, Pallas kernels, x_dft(): pl.pallas_call(functools.partial(x_kernel, count), out_shape=(jax.ShapeDt...  9.62 us
    unnamed x36, local copies, waits for them, and re-layouts  7.24 us
    all_to_all x2, waiting for transfers between devices, to_planes(): return lax.all_to_all(values, 'gy', split_axis=0, concat_axis=1, tiled=True)  7.05 us
    sin x1, other arithmetic, root_table(): return (jnp.cos(angle), jnp.sin(angle))  5.55 us
  transfers between devices with their start and end apart: 8, of which 4 were waited for; matrix products, arithmetic and copies ran while one was open for 12% of the time, Pallas kernels for 11%

profile of v13, /device:TPU:0, one launch (start us, length us, event | category | flops | bytes accessed | tf_op | source)
XLA Modules:
  0.0 164.6 jit_solution(1178858593079203053)
XLA Ops:
  0.6 1.8 %fusion.24 = (f32[4,256,256]{2,1,0:T(8,128)S(1)}, f32[4,256,256]{2,1,0:T(8,128)S(1)}) fusion(f32[8,256,512]{2,1,0:T(8,128)} %field_ref), kind=kLoop, calls=%fused_computation.82 | loop fusion | bytes 4194304 | tf_op jit(solution)/shard_map/slice | solution.py:317
  2.5 3.0 %collective-permute-start = (f32[4,256,256]{2,1,0:T(8,128)S(1)}, f32[4,256,256]{2,1,0:T(8,128)S(1)}, u32[]{:S(2)}, u32[]{:S(2)}) collective-permute-start(f32[4,256,256]{2,1,0:T(8,128)S(1)} %get-tuple-element.22.early_ref), channel_id=1, source_target_pairs={{0,16},{8,24},{16,0},{24,8},{1,17},{9,25},{17,1},{25,9},{2,18},{10... | collective-permute-start | bytes 3145736 | tf_op jit(solution)/shard_map/ppermute | solution.py:20
  5.5 0.1 collective-permute-start.1
  5.6 2.8 %cut_right.1 = f32[8,256,256]{2,1,0:T(8,128)} custom-call(f32[8,256,512]{2,1,0:T(8,128)S(1)} %copy-done), custom_call_target="tpu_custom_call" | custom-call | flops 1048576 | bytes 4194304 | tf_op jit(solution)/shard_map/cut_right/pallas_call | solution.py:77
  8.4 6.2 %all-to-all-start = ((f32[8,256,256]{2,1,0:T(8,128)}), f32[8,256,256]{2,1,0:T(8,128)}, u32[]{:S(2)}, u32[]{:S(2)}) async-start(f32[8,256,256]{2,1,0:T(8,128)} %cut_right.1), calls=%async_computation | async-start | bytes 4194304 | tf_op jit(solution)/shard_map/all_to_all | solution.py:24
  14.7 5.5 %fusion.14 = (f32[256,512]{1,0:T(8,128)}, f32[256,512]{1,0:T(8,128)}, f32[256,512]{1,0:T(8,128)}, f32[256,512]{1,0:T(8,128)S(1)}) fusion(s32[512]{0:T(512)S(1)} %multiply_add_fusion, s32[256]{0:T(256)S(1)} %pad_add_fusion.1, s32[256]{0:T(256)S(1)} %pad_add_fusion), kind=kLoop, calls=%fused_computation.55 | loop fusion | flops 3670016 | bytes 2101248 | tf_op jit(solution)/shard_map/sin | solution.py:99
  20.3 0.7 fusion.27
  21.0 0.6 log_reduce_fusion.1
  21.6 0.1 pad_maximum_fusion.13
  21.7 0.1 reshape.444.coef_ref
  21.8 0.6 log_reduce_fusion
  22.4 1.1 fusion.23
  23.5 0.1 maximum_maximum_fusion
  23.6 0.0 copy-start.16
  23.7 0.2 reduce-precision_convert_fusion.2
  23.9 1.1 pad_maximum_fusion.1.refs_4_.refs_2_
  24.9 0.1 pad_maximum_fusion.12.coef_ref
  26.4 1.0 fusion.28
  27.3 1.1 pad_maximum_fusion.6
  28.5 0.2 reduce-precision_convert_fusion.1
  28.7 1.1 pad_maximum_fusion.3.refs_4_
  29.9 0.1 pad_maximum_fusion.8
  30.1 0.2 reduce-precision_convert_fusion
  30.2 1.1 pad_maximum_fusion.5.refs_5_
  31.3 3.2 %fusion.3 = (f32[1,8,256,128]{3,2,1,0:T(8,128)S(1)}, f32[1,8,256,128]{3,2,1,0:T(8,128)S(1)}) fusion(), kind=kLoop, calls=%fused_computation.17 | loop fusion | flops 786432 | bytes 2097152 | tf_op jit(solution)/shard_map/sin | solution.py:336
  34.6 1.6 pad_maximum_fusion.refs_5_.refs_3_
  36.1 15.1 %collective-permute-done.1.late_ref = f32[4,256,256]{2,1,0:T(8,128)} collective-permute-done((f32[4,256,256]{2,1,0:T(8,128)S(1)}, f32[4,256,256]{2,1,0:T(8,128)}, u32[]{:S(2)}, u32[]{:S(2)}) %collective-permute-start.1) | collective-permute-done | bytes 1048608 | tf_op jit(solution)/shard_map/ppermute | solution.py:20
  51.2 2.6 %combine.2.refs_0_ = f32[8,256,256]{2,1,0:T(8,128)} custom-call(f32[1]{0:T(128)} %bitcast.sign_ref, f32[4,256,256]{2,1,0:T(8,128)} %collective-permute-done.1.late_ref, f32[4,256,256]{2,1,0:T(8,128)S(1)} %get-tuple-element.23.early_ref), custom_call_target="tpu_custom_call" | custom-call | flops 524288 | bytes 3145728 | tf_op jit(solution)/shard_map/combine/pallas_call | solution.py:50
  53.8 1.5 combine.3
  55.3 7.0 %all-to-all-done = f32[8,256,256]{2,1,0:T(8,128)} async-done(((f32[8,256,256]{2,1,0:T(8,128)}), f32[8,256,256]{2,1,0:T(8,128)}, u32[]{:S(2)}, u32[]{:S(2)}) %all-to-all-start) | async-done | bytes 2097184 | tf_op jit(solution)/shard_map/all_to_all | solution.py:24
  62.4 1.5 collective-permute-start.2
  63.9 4.5 %all-to-all-start.1 = ((f32[8,256,256]{2,1,0:T(8,128)}), f32[8,256,256]{2,1,0:T(8,128)}, u32[]{:S(2)}, u32[]{:S(2)}) async-start(f32[8,256,256]{2,1,0:T(8,128)} %combine.3), calls=%async_computation.1 | async-start | bytes 4194304 | tf_op jit(solution)/shard_map/all_to_all | solution.py:24
  68.4 0.1 collective-permute-start.4
  68.5 39.8 %collective-permute-done.2.refs_0_ = f32[2048,256]{1,0:T(8,128)} collective-permute-done((f32[2048,256]{1,0:T(8,128)}, f32[2048,256]{1,0:T(8,128)}, u32[]{:S(2)}, u32[]{:S(2)}) %collective-permute-start.2) | collective-permute-done | bytes 2097184 | tf_op jit(solution)/shard_map/ppermute | solution.py:20
  108.4 4.4 %collective-permute-done.3.refs_1_ = f32[2048,256]{1,0:T(8,128)S(1)} collective-permute-done((f32[2048,256]{1,0:T(8,128)}, f32[2048,256]{1,0:T(8,128)S(1)}, u32[]{:S(2)}, u32[]{:S(2)}) %collective-permute-start.3) | collective-permute-done | bytes 2097184 | tf_op jit(solution)/shard_map/ppermute | solution.py:20
  112.7 5.6 %y_dft.3.refs_0_ = bf16[4,2048,128]{2,1,0:T(8,128)(2,1)S(1)} custom-call(f32[2,4]{1,0:T(2,128)S(1)} %pad_maximum_fusion.12.coef_ref, f32[2048,256]{1,0:T(8,128)} %collective-permute-done.2.refs_0_, f32[2048,256]{1,0:T(8,128)S(1)} %collective-permute-done.3.refs_1_, f32[2048,256]{1,0:T(8,128)} %bitcast.1.refs_2_, ...), custom_call_target="tpu_custom_call" | custom-call | flops 5368709120 | bytes 14680064 | tf_op jit(solution)/shard_map/y_dft/pallas_call | solution.py:192
  118.3 1.3 copy-done.5
  119.6 1.4 copy-done.7
  121.0 1.3 copy-done.9
  122.3 0.1 collective-permute-start.5
  122.5 1.6 copy-done.6
  124.0 1.6 copy-done.8
  125.6 5.6 %y_dft.5.refs_2_ = bf16[4,2048,128]{2,1,0:T(8,128)(2,1)S(1)} custom-call(f32[2,4]{1,0:T(2,128)S(1)} %pad_maximum_fusion.12.coef_ref, f32[2048,256]{1,0:T(8,128)} %collective-permute-done.2.refs_0_, f32[2048,256]{1,0:T(8,128)S(1)} %copy-done.8, f32[2048,256]{1,0:T(8,128)} %bitcast.1.refs_2_, f32[2048,256]{1,0:T(8,128)S(1)} %copy-done.6, ...), custom_call_target="tpu_custom_call" | custom-call | flops 5368709120 | bytes 14680064 | tf_op jit(solution)/shard_map/y_dft/pallas_call | solution.py:192
  131.2 0.0 copy-start.10
  131.3 8.1 %y_dft.4 = (bf16[4,2048,128]{2,1,0:T(8,128)(2,1)S(1)}, bf16[4,2048,128]{2,1,0:T(8,128)(2,1)S(1)}) custom-call(f32[2,2]{1,0:T(2,128)S(1)} %reshape.444.coef_ref, f32[2048,256]{1,0:T(8,128)} %bitcast.20.refs_0_, f32[2048,256]{1,0:T(8,128)} %collective-permute-done.5.refs_1_, bf16[2,512,512]{2,1,0:T(8,128)(2,1)S(1)} %copy-done.2, f32[2,8,256,128]{3,2,1,0:T(8,128)S(1)} %copy-done.1), custom_call_target="tpu_custom_call" | custom-call | flops 10737418240 | bytes 10485760 | tf_op jit(solution)/shard_map/y_dft/pallas_call | solution.py:192
  139.4 9.6 %x_dft.1 = (f32[2,1,2048,512]{3,2,1,0:T(8,128)}, f32[8,128]{1,0:T(8,128)S(1)}) custom-call(bf16[4,2048,128]{2,1,0:T(8,128)(2,1)S(1)} %copy-done.10, bf16[4,2048,128]{2,1,0:T(8,128)(2,1)S(1)} %get-tuple-element.33.refs_1_, bf16[4,2048,128]{2,1,0:T(8,128)(2,1)S(1)} %y_dft.5.refs_2_, bf16[4,2048,128]{2,1,0:T(8,128)(2,1)S(1)} %get-tuple-element.34.refs_3_, ...), custom_call_target="tpu_custom_call" | custom-call | flops 6442450944 | bytes 16777216 | tf_op jit(solution)/shard_map/x_dft/pallas_call | solution.py:279
  149.0 13.1 %all_to_all.23 = f32[32,8,128]{2,1,0:T(8,128)S(1)} all-to-all(f32[32,8,128]{2,1,0:T(8,128)S(1)} %broadcast_in_dim.2), channel_id=1, replica_groups=mesh['gx'=4,'gy'=8] {'gx','gy'}, dimensions={0} | all-to-all | bytes 262144 | tf_op jit(solution)/shard_map/all_to_all | solution.py:309
  162.2 0.6 reduce_sum.29
  (55 shorter events, 0.4 us)
Async XLA Ops:
  0.6 5.0 %copy-start = (f32[8,256,512]{2,1,0:T(8,128)S(1)}, f32[8,256,512]{2,1,0:T(8,128)}, u32[]{:S(2)}) copy-start(f32[8,256,512]{2,1,0:T(8,128)} %field_ref) | copy-start | bytes 12582916
  2.5 51.3 %collective-permute-start = (f32[4,256,256]{2,1,0:T(8,128)S(1)}, f32[4,256,256]{2,1,0:T(8,128)S(1)}, u32[]{:S(2)}, u32[]{:S(2)}) collective-permute-start(f32[4,256,256]{2,1,0:T(8,128)S(1)} %get-tuple-element.22.early_ref), channel_id=1, source_target_pairs={{0,16},{8,24},{16,0},{24,8},{1,17},{9,25},{17,1},{25,9},{2,18},{10... | collective-permute-start | bytes 3145736 | tf_op jit(solution)/shard_map/ppermute | solution.py:20
  5.5 45.7 %collective-permute-start.1 = (f32[4,256,256]{2,1,0:T(8,128)S(1)}, f32[4,256,256]{2,1,0:T(8,128)}, u32[]{:S(2)}, u32[]{:S(2)}) collective-permute-start(f32[4,256,256]{2,1,0:T(8,128)S(1)} %get-tuple-element.23.early_ref), channel_id=1, source_target_pairs={{0,16},{8,24},{16,0},{24,8},{1,17},{9,25},{17,1},{25,9},{2,18},{10... | collective-permute-start | bytes 3145736 | tf_op jit(solution)/shard_map/ppermute | solution.py:20
  8.4 54.0 %all-to-all-start = ((f32[8,256,256]{2,1,0:T(8,128)}), f32[8,256,256]{2,1,0:T(8,128)}, u32[]{:S(2)}, u32[]{:S(2)}) async-start(f32[8,256,256]{2,1,0:T(8,128)} %cut_right.1), calls=%async_computation | async-start | bytes 4194304 | tf_op jit(solution)/shard_map/all_to_all | solution.py:24
  14.6 6.4 %copy-start.13 = (f32[512]{0:T(512)S(1)}, f32[512]{0:T(512)}, u32[]{:S(2)}) copy-start(f32[512]{0:T(512)} %param.8) | copy-start | bytes 6148
  14.6 7.2 %copy-start.14 = (f32[2048]{0:T(1024)S(1)}, f32[2048]{0:T(1024)}, u32[]{:S(2)}) copy-start(f32[2048]{0:T(1024)} %param.7) | copy-start | bytes 24580
  23.6 1.3 copy-start.16
  23.6 1.3 copy-start.17
  23.7 2.6 %copy-start.15 = (f32[2048]{0:T(1024)S(1)}, f32[2048]{0:T(1024)}, u32[]{:S(2)}) copy-start(f32[2048]{0:T(1024)} %param.9) | copy-start | bytes 24580
  28.5 1.3 copy-start.12
  28.5 1.3 copy-start.11
  62.4 50.3 %copy-start.1 = (f32[2,8,256,128]{3,2,1,0:T(8,128)S(1)}, f32[2,8,256,128]{3,2,1,0:T(8,128)}, u32[]{:S(2)}) copy-start(f32[2,8,256,128]{3,2,1,0:T(8,128)} %pad_maximum_fusion.refs_5_.refs_3_) | copy-start | bytes 6291460
  62.4 50.3 %copy-start.2 = (bf16[2,512,512]{2,1,0:T(8,128)(2,1)S(1)}, bf16[2,512,512]{2,1,0:T(8,128)(2,1)}, u32[]{:S(2)}) copy-start(bf16[2,512,512]{2,1,0:T(8,128)(2,1)} %pad_maximum_fusion.1.refs_4_.refs_2_) | copy-start | bytes 3145732
  62.4 46.0 %collective-permute-start.2 = (f32[2048,256]{1,0:T(8,128)}, f32[2048,256]{1,0:T(8,128)}, u32[]{:S(2)}, u32[]{:S(2)}) collective-permute-start(f32[2048,256]{1,0:T(8,128)} %bitcast.1.refs_2_), channel_id=1, source_target_pairs={{0,16},{8,24},{16,0},{24,8},{1,17},{9,25},{17,1},{25,9},{2,18},{10... | collective-permute-start | bytes 6291464 | tf_op jit(solution)/shard_map/ppermute | solution.py:20
  63.9 58.4 %all-to-all-start.1 = ((f32[8,256,256]{2,1,0:T(8,128)}), f32[8,256,256]{2,1,0:T(8,128)}, u32[]{:S(2)}, u32[]{:S(2)}) async-start(f32[8,256,256]{2,1,0:T(8,128)} %combine.3), calls=%async_computation.1 | async-start | bytes 4194304 | tf_op jit(solution)/shard_map/all_to_all | solution.py:24
  68.4 39.9 %collective-permute-start.4 = (f32[2048,256]{1,0:T(8,128)}, f32[2048,256]{1,0:T(8,128)S(1)}, u32[]{:S(2)}, u32[]{:S(2)}) collective-permute-start(f32[2048,256]{1,0:T(8,128)} %bitcast.1.refs_2_), channel_id=1, source_target_pairs={{0,8},{8,0},{16,24},{24,16},{1,9},{9,1},{17,25},{25,17},{2,10},{10... | collective-permute-start | bytes 6291464 | tf_op jit(solution)/shard_map/ppermute | solution.py:20
  108.4 4.4 %collective-permute-start.3 = (f32[2048,256]{1,0:T(8,128)}, f32[2048,256]{1,0:T(8,128)S(1)}, u32[]{:S(2)}, u32[]{:S(2)}) collective-permute-start(f32[2048,256]{1,0:T(8,128)} %collective-permute-done.2.refs_0_), channel_id=1, source_target_pairs={{0,8},{8,0},{16,24},{24,16},{1,9},{9,1},{17,25},{25,17},{2,10},{10... | collective-permute-start | bytes 6291464 | tf_op jit(solution)/shard_map/ppermute | solution.py:20
  118.3 1.3 copy-start.5
  119.6 1.4 copy-start.7
  121.0 1.3 copy-start.9
  122.3 8.9 %collective-permute-start.5 = (f32[2048,256]{1,0:T(8,128)}, f32[2048,256]{1,0:T(8,128)}, u32[]{:S(2)}, u32[]{:S(2)}) collective-permute-start(f32[2048,256]{1,0:T(8,128)} %bitcast.20.refs_0_), channel_id=1, source_target_pairs={{0,8},{8,0},{16,24},{24,16},{1,9},{9,1},{17,25},{25,17},{2,10},{10... | collective-permute-start | bytes 6291464 | tf_op jit(solution)/shard_map/ppermute | solution.py:20
  122.5 1.6 copy-start.6
  124.0 1.6 copy-start.8
  131.2 8.1 %copy-start.3 = (bf16[2,512,512]{2,1,0:T(8,128)(2,1)S(1)}, bf16[2,512,512]{2,1,0:T(8,128)(2,1)}, u32[]{:S(2)}) copy-start(bf16[2,512,512]{2,1,0:T(8,128)(2,1)} %pad_maximum_fusion.3.refs_4_) | copy-start | bytes 3145732
  131.2 8.1 %copy-start.4 = (bf16[2,512,512]{2,1,0:T(8,128)(2,1)S(1)}, bf16[2,512,512]{2,1,0:T(8,128)(2,1)}, u32[]{:S(2)}) copy-start(bf16[2,512,512]{2,1,0:T(8,128)(2,1)} %pad_maximum_fusion.5.refs_5_) | copy-start | bytes 3145732
  131.2 8.1 %copy-start.10 = (bf16[4,2048,128]{2,1,0:T(8,128)(2,1)S(1)}, bf16[4,2048,128]{2,1,0:T(8,128)(2,1)}, u32[]{:S(2)}) copy-start(bf16[4,2048,128]{2,1,0:T(8,128)(2,1)} %copy-done.9) | copy-start | bytes 6291460

commit v14 on v13

--- a/solution.py
+++ b/solution.py
@@ -11,7 +11,7 @@
 precision_top = lax.Precision.HIGHEST
 RADIX = 8
 LANES = 128
-SMALL_BYTES, Y_BYTES, X_BYTES = [size * 1024 * 1024 for size in (8, 25, 26)]
+SMALL_BYTES, Y_BYTES, X_BYTES = [size * 1024 * 1024 for size in (8, 28, 26)]
 
 
 def from_partner(value, axis, stride):
@@ -141,31 +141,55 @@
     return jnp.dot(left, right, preferred_element_type=jnp.float32)
 
 
-def y_kernel(count, tiles, coef_ref, *refs):
-    inputs, (table_ref, twist_ref, *out_refs, mix_ref, split_ref, step_ref) = refs[:count], refs[count:]
+def y_kernel(count, coef_ref, *refs):
+    inputs, (table_hbm, twist_hbm, *refs) = refs[:count], refs[count:]
+    *out_refs, table_ref, twist_ref, in_ref, mix_ref, split_ref, step_ref, table_sems, sems = refs
     length = mix_ref.shape[1]
     inner = length // RADIX
-    rows_each = 128
-    for place, tile in enumerate(tiles):
-        cols = pl.ds(tile * LANES, LANES)
+    rows_each, rows_half = 128, length // 2
+
+    def fetch(tile, half):
+        rows, cols = pl.ds(half * rows_half, rows_half), pl.ds(tile * LANES, LANES)
+        return [
+            pltpu.make_async_copy(ref.at[rows, cols], in_ref.at[tile, k, rows, :], sems.at[tile, half, k])
+            for k, ref in enumerate(inputs)
+        ]
+
+    table_copies = [
+        pltpu.make_async_copy(source, target, table_sems.at[place])
+        for place, (source, target) in enumerate(((table_hbm, table_ref), (twist_hbm, twist_ref)))
+    ]
+    copies = {(tile, half): fetch(tile, half) for tile in range(len(out_refs)) for half in range(2)}
+    for copy in (*copies[0, 0], *copies[0, 1], *table_copies):
+        copy.start()
+    for tile in range(1, len(out_refs)):
+        for copy in (*copies[tile, 0], *copies[tile, 1]):
+            copy.start()
+    for tile, out_ref in enumerate(out_refs):
         for start in range(0, length, rows_each):
+            if start % rows_half == 0:
+                for copy in copies[tile, start // rows_half]:
+                    copy.wait()
             rows = pl.ds(start, rows_each)
             for which in range(2):
-                mixed = inputs[0][rows, cols] * coef_ref[which, 0]
+                mixed = in_ref[tile, 0, rows, :] * coef_ref[which, 0]
                 for k in range(1, count):
-                    mixed = mixed + inputs[k][rows, cols] * coef_ref[which, k]
-                mix_ref[2 * place + which, rows, :] = mixed
-    for tile, out_ref in enumerate(out_refs):
+                    mixed = mixed + in_ref[tile, k, rows, :] * coef_ref[which, k]
+                mix_ref[which, rows, :] = mixed
         for which in range(2):
             for s in range(RADIX):
-                parts = split_value(mix_ref[2 * tile + which, pl.ds(s, inner, stride=RADIX), :])
+                parts = split_value(mix_ref[which, pl.ds(s, inner, stride=RADIX), :])
                 for place, value in enumerate(parts):
                     split_ref[tile, place, pl.ds(which * inner, inner), pl.ds(s * LANES, LANES)] = value
         half = inner // 2
         for part in range(2):
+            if tile == part == 0:
+                table_copies[0].wait()
             table = [table_ref[place, pl.ds(part * inner, inner), :] for place in (0, 1, 0)]
             values = [split_ref[tile, place] for place in (0, 0, 1)]
             step_ref[part] = dot(jnp.concatenate(table, axis=1), jnp.concatenate(values, axis=0))
+            if tile == part == 0:
+                table_copies[1].wait()
             for start in range(0, half, 16):
                 values = []
                 for s in range(RADIX):
@@ -184,25 +208,30 @@
                         out_ref[2 * which + 1, rows, :] = low
 
 
-def y_dft(inputs, tiles, coefs, table, twist):
-    length = inputs[0].shape[0]
+def y_dft(inputs, coefs, table, twist):
+    length, columns = inputs[0].shape
     inner = length // RADIX
-    count = len(tiles)
-    whole = pl.BlockSpec(memory_space=pltpu.VMEM)
+    tiles, count = columns // LANES, len(inputs)
+    whole, anywhere = pl.BlockSpec(memory_space=pltpu.VMEM), pl.BlockSpec(memory_space=pl.ANY)
     return pl.pallas_call(
-        functools.partial(y_kernel, len(inputs), tiles),
-        out_shape=[jax.ShapeDtypeStruct((4, length, LANES), jnp.bfloat16)] * count,
-        in_specs=[pl.BlockSpec(memory_space=pltpu.SMEM)] + [whole] * (len(inputs) + 2),
-        out_specs=[whole] * count,
+        functools.partial(y_kernel, count),
+        out_shape=[jax.ShapeDtypeStruct((4, length, LANES), jnp.bfloat16)] * tiles,
+        in_specs=[pl.BlockSpec(memory_space=pltpu.SMEM)] + [anywhere] * (count + 2),
+        out_specs=[whole] * tiles,
         scratch_shapes=[
-            pltpu.VMEM((2 * count, length, LANES), jnp.float32),
-            pltpu.VMEM((count, 2, 2 * inner, RADIX * LANES), jnp.bfloat16),
+            pltpu.VMEM(table.shape, table.dtype),
+            pltpu.VMEM(twist.shape, twist.dtype),
+            pltpu.VMEM((tiles, count, length, LANES), jnp.float32),
+            pltpu.VMEM((2, length, LANES), jnp.float32),
+            pltpu.VMEM((tiles, 2, 2 * inner, RADIX * LANES), jnp.bfloat16),
             pltpu.VMEM((2, inner, RADIX * LANES), jnp.float32),
+            pltpu.SemaphoreType.DMA((2,)),
+            pltpu.SemaphoreType.DMA((tiles, 2, count)),
         ],
         compiler_params=pltpu.CompilerParams(vmem_limit_bytes=Y_BYTES),
         cost_estimate=pl.CostEstimate(
-            flops=80 * inner * length * LANES * count,
-            bytes_accessed=8 * length * LANES * (len(inputs) + 3),
+            flops=24 * inner * length * columns,
+            bytes_accessed=4 * length * columns * (count + 3),
             transcendentals=0,
         ),
         name="y_dft",
@@ -361,10 +390,8 @@
     second_a = to_planes(first_a)[0]
     second_b = from_partner(first_b, "gx", 1)
     group = [second_b, from_partner(second_b, "gx", 0), first_b, from_partner(first_b, "gx", 0)]
-    even_b = y_dft(group, (0,), coefs_b, y_table, twist)[0]
-    even_b, second_a = lax.optimization_barrier((even_b, second_a))
-    odd_b = y_dft(group, (1,), coefs_b, y_table, twist)[0]
-    even_a, odd_a = y_dft([second_a, from_partner(second_a, "gx", 0)], (0, 1), coefs_a, y_table, twist)
+    even_b, odd_b = y_dft(group, coefs_b, y_table, twist)
+    even_a, odd_a = y_dft([second_a, from_partner(second_a, "gx", 0)], coefs_a, y_table, twist)
     latent, tile = x_dft([even_b, even_a], [odd_b, odd_a], even_table, odd_table, row_pair, col_trio)
     tile = tile + fixed / tile.size
     modes = length * columns * lax.axis_size("gx") * lax.axis_size("gy")

time: 165 us -> 163 us (0.988)
  local copies, waits for them, and re-layouts: 11.1 us -> 3.7 us
  other arithmetic: 18.5 us -> 21.4 us
  waiting for transfers between devices: 66.4 us -> 69.2 us
    unnamed x36 -> x26, local copies, waits for them, and re-layouts: 7.24 us -> 0.82 us
    ppermute x6, waiting for transfers between devices: 59.3 us -> 61.1 us  [from_partner(): return lax.ppermute(value, axis, pairs)]
    pallas_call x3 -> x2, Pallas kernels: 19.2 us -> 18.7 us  [y_dft(): pl.pallas_call(functools.partial(y_kernel, count), out_shape=[jax.ShapeDt...]
  transfers between devices with their start and end apart: 8 -> 8, of which waited for: 4 -> 5; matrix products, arithmetic and copies ran while one was open for 12% -> 13% of each run, Pallas kernels for 11% -> 10%
where the time goes in v14:
time: 163 us; the launch traced here: 162 us
  waiting for transfers between devices  69.2 us (42%)
  Pallas kernels  35.1 us (22%)
  other arithmetic  21.4 us (13%)
  starting transfers between devices  15.7 us (10%)
  blocking collectives  13.3 us (8%)
  between operations  4.02 us (2%)
  local copies, waits for them, and re-layouts  3.7 us (2%)
    ppermute x6, waiting for transfers between devices, from_partner(): return lax.ppermute(value, axis, pairs)  61.1 us
    pallas_call x2, Pallas kernels, y_dft(): pl.pallas_call(functools.partial(y_kernel, count), out_shape=[jax.ShapeDt...  18.7 us
    all_to_all x1, blocking collectives, sum_everywhere(): lax.all_to_all(copies, axes, split_axis=0, concat_axis=0, tiled=True)  13.3 us
    all_to_all x2, starting transfers between devices, to_planes(): return lax.all_to_all(values, 'gy', split_axis=0, concat_axis=1, tiled=True)  11 us
    pallas_call x1, Pallas kernels, x_dft(): pl.pallas_call(functools.partial(x_kernel, count), out_shape=(jax.ShapeDt...  9.61 us
    all_to_all x2, waiting for transfers between devices, to_planes(): return lax.all_to_all(values, 'gy', split_axis=0, concat_axis=1, tiled=True)  8.1 us
    sin x1, other arithmetic, root_table(): return (jnp.cos(angle), jnp.sin(angle))  5.16 us
    ppermute x6, starting transfers between devices, from_partner(): return lax.ppermute(value, axis, pairs)  4.7 us
  transfers between devices with their start and end apart: 8, of which 5 were waited for; matrix products, arithmetic and copies ran while one was open for 13% of the time, Pallas kernels for 10%

profile of v14, /device:TPU:0, one launch (start us, length us, event | category | flops | bytes accessed | tf_op | source)
XLA Modules:
  0.0 162.5 jit_solution(9299104771564511098)
XLA Ops:
  0.6 0.0 copy-start
  0.6 1.8 %fusion.24 = (f32[4,256,256]{2,1,0:T(8,128)S(1)}, f32[4,256,256]{2,1,0:T(8,128)S(1)}) fusion(f32[8,256,512]{2,1,0:T(8,128)} %field_ref), kind=kLoop, calls=%fused_computation.82 | loop fusion | bytes 4194304 | tf_op jit(solution)/shard_map/slice | solution.py:346
  2.5 3.0 %collective-permute-start = (f32[4,256,256]{2,1,0:T(8,128)S(1)}, f32[4,256,256]{2,1,0:T(8,128)S(1)}, u32[]{:S(2)}, u32[]{:S(2)}) collective-permute-start(f32[4,256,256]{2,1,0:T(8,128)S(1)} %get-tuple-element.22.early_ref), channel_id=1, source_target_pairs={{0,16},{8,24},{16,0},{24,8},{1,17},{9,25},{17,1},{25,9},{2,18},{10... | collective-permute-start | bytes 3145736 | tf_op jit(solution)/shard_map/ppermute | solution.py:20
  5.5 0.1 collective-permute-start.1
  5.6 0.0 copy-done
  5.6 2.8 %cut_right.1 = f32[8,256,256]{2,1,0:T(8,128)} custom-call(f32[8,256,512]{2,1,0:T(8,128)S(1)} %copy-done), custom_call_target="tpu_custom_call" | custom-call | flops 1048576 | bytes 4194304 | tf_op jit(solution)/shard_map/cut_right/pallas_call | solution.py:77
  8.4 6.2 %all-to-all-start = ((f32[8,256,256]{2,1,0:T(8,128)}), f32[8,256,256]{2,1,0:T(8,128)}, u32[]{:S(2)}, u32[]{:S(2)}) async-start(f32[8,256,256]{2,1,0:T(8,128)} %cut_right.1), calls=%async_computation | async-start | bytes 4194304 | tf_op jit(solution)/shard_map/all_to_all | solution.py:24
  14.7 1.1 fusion.23
  15.8 0.1 maximum_maximum_fusion
  15.9 1.2 reduce-precision_convert_fusion.2
  17.1 5.2 %fusion.14 = (f32[256,512]{1,0:T(8,128)}, f32[256,512]{1,0:T(8,128)}, f32[256,512]{1,0:T(8,128)S(1)}, f32[256,512]{1,0:T(8,128)S(1)}) fusion(s32[512]{0:T(512)S(1)} %multiply_add_fusion, s32[256]{0:T(256)S(1)} %pad_add_fusion.1, s32[256]{0:T(256)S(1)} %pad_add_fusion), kind=kLoop, calls=%fused_computation.55 | loop fusion | flops 3670016 | bytes 2101248 | tf_op jit(solution)/shard_map/sin | solution.py:99
  22.3 0.8 copy-done.6
  23.1 0.7 fusion.28
  23.8 0.7 log_reduce_fusion
  24.4 0.1 pad_maximum_fusion.13
  24.5 0.1 reshape.444.coef_ref
  24.6 0.6 log_reduce_fusion.1
  25.2 2.3 %pad_maximum_fusion.1.refs_4_.refs_2_ = bf16[2,512,512]{2,1,0:T(8,128)(2,1)} fusion(bf16[1,512,512]{2,1,0:T(8,128)(2,1)} %get-tuple-element.49, bf16[1,512,512]{2,1,0:T(8,128)(2,1)} %get-tuple-element.48), kind=kLoop, calls=%fused_computation.11 | loop fusion | flops 524288 | bytes 2097152 | tf_op jit(solution)/shard_map/stack | solution.py:111
  27.5 0.1 pad_maximum_fusion.12.coef_ref
  28.9 1.0 slice_negate_fusion.1
  29.9 1.2 pad_maximum_fusion.6
  31.2 0.2 reduce-precision_convert_fusion.1
  31.4 1.1 pad_maximum_fusion.3.refs_4_
  32.5 0.1 pad_maximum_fusion.8
  32.7 0.2 reduce-precision_convert_fusion
  32.9 1.1 pad_maximum_fusion.5.refs_5_
  33.9 3.2 %fusion.3 = (f32[1,8,256,128]{3,2,1,0:T(8,128)S(1)}, f32[1,8,256,128]{3,2,1,0:T(8,128)S(1)}) fusion(), kind=kLoop, calls=%fused_computation.17 | loop fusion | flops 786432 | bytes 2097152 | tf_op jit(solution)/shard_map/sin | solution.py:365
  37.2 1.5 pad_maximum_fusion.refs_5_.refs_3_
  38.7 12.5 %collective-permute-done.1.late_ref = f32[4,256,256]{2,1,0:T(8,128)} collective-permute-done((f32[4,256,256]{2,1,0:T(8,128)S(1)}, f32[4,256,256]{2,1,0:T(8,128)}, u32[]{:S(2)}, u32[]{:S(2)}) %collective-permute-start.1) | collective-permute-done | bytes 1048608 | tf_op jit(solution)/shard_map/ppermute | solution.py:20
  51.2 2.6 %combine.2.refs_0_ = f32[8,256,256]{2,1,0:T(8,128)} custom-call(f32[1]{0:T(128)} %bitcast.sign_ref, f32[4,256,256]{2,1,0:T(8,128)} %collective-permute-done.1.late_ref, f32[4,256,256]{2,1,0:T(8,128)S(1)} %get-tuple-element.23.early_ref), custom_call_target="tpu_custom_call" | custom-call | flops 524288 | bytes 3145728 | tf_op jit(solution)/shard_map/combine/pallas_call | solution.py:50
  53.8 0.0 collective-permute-done.late_ref
  53.8 1.5 combine.3
  55.3 7.1 %all-to-all-done = f32[8,256,256]{2,1,0:T(8,128)} async-done(((f32[8,256,256]{2,1,0:T(8,128)}), f32[8,256,256]{2,1,0:T(8,128)}, u32[]{:S(2)}, u32[]{:S(2)}) %all-to-all-start) | async-done | bytes 2097184 | tf_op jit(solution)/shard_map/all_to_all | solution.py:24
  62.4 4.8 %all-to-all-start.1 = ((f32[8,256,256]{2,1,0:T(8,128)}), f32[8,256,256]{2,1,0:T(8,128)}, u32[]{:S(2)}, u32[]{:S(2)}) async-start(f32[8,256,256]{2,1,0:T(8,128)} %combine.3), calls=%async_computation.1 | async-start | bytes 4194304 | tf_op jit(solution)/shard_map/all_to_all | solution.py:24
  67.2 1.6 collective-permute-start.2
  68.8 0.0 collective-permute-start.4
  68.8 45.1 %collective-permute-done.2.refs_0_ = f32[2048,256]{1,0:T(8,128)} collective-permute-done((f32[2048,256]{1,0:T(8,128)}, f32[2048,256]{1,0:T(8,128)}, u32[]{:S(2)}, u32[]{:S(2)}) %collective-permute-start.2) | collective-permute-done | bytes 2097184 | tf_op jit(solution)/shard_map/ppermute | solution.py:20
  113.9 0.0 collective-permute-start.3
  113.9 1.0 all-to-all-done.1
  114.9 0.0 collective-permute-start.5
  114.9 0.0 collective-permute-done.4.refs_3_
  114.9 3.5 %collective-permute-done.3.refs_1_ = f32[2048,256]{1,0:T(8,128)} collective-permute-done((f32[2048,256]{1,0:T(8,128)}, f32[2048,256]{1,0:T(8,128)}, u32[]{:S(2)}, u32[]{:S(2)}) %collective-permute-start.3) | collective-permute-done | bytes 2097184 | tf_op jit(solution)/shard_map/ppermute | solution.py:20
  118.4 9.9 %y_dft.2 = (bf16[4,2048,128]{2,1,0:T(8,128)(2,1)S(1)}, bf16[4,2048,128]{2,1,0:T(8,128)(2,1)S(1)}) custom-call(f32[2,4]{1,0:T(2,128)S(1)} %pad_maximum_fusion.12.coef_ref, f32[2048,256]{1,0:T(8,128)} %collective-permute-done.2.refs_0_, f32[2048,256]{1,0:T(8,128)} %collective-permute-done.3.refs_1_, f32[2048,256]{1,0:T(8,128)} %bitcast.1.refs_2_, ...), custom_call_target="tpu_custom_call" | custom-call | flops 3221225472 | bytes 14680064 | tf_op jit(solution)/shard_map/y_dft/pallas_call | solution.py:216
  128.3 0.0 collective-permute-done.5.refs_1_
  128.3 8.8 %y_dft.3 = (bf16[4,2048,128]{2,1,0:T(8,128)(2,1)S(1)}, bf16[4,2048,128]{2,1,0:T(8,128)(2,1)S(1)}) custom-call(f32[2,2]{1,0:T(2,128)S(1)} %reshape.444.coef_ref, f32[2048,256]{1,0:T(8,128)} %bitcast.20.refs_0_, f32[2048,256]{1,0:T(8,128)} %collective-permute-done.5.refs_1_, bf16[2,512,512]{2,1,0:T(8,128)(2,1)S(1)} %copy-done.2, f32[2,8,256,128]{3,2,1,0:T(8,128)S(1)} %copy-done.1), custom_call_target="tpu_custom_call" | custom-call | flops 3221225472 | bytes 10485760 | tf_op jit(solution)/shard_map/y_dft/pallas_call | solution.py:216
  137.1 9.6 %x_dft.1 = (f32[2,1,2048,512]{3,2,1,0:T(8,128)}, f32[8,128]{1,0:T(8,128)S(1)}) custom-call(bf16[4,2048,128]{2,1,0:T(8,128)(2,1)S(1)} %get-tuple-element.29.refs_0_, bf16[4,2048,128]{2,1,0:T(8,128)(2,1)S(1)} %get-tuple-element.32.refs_1_, bf16[4,2048,128]{2,1,0:T(8,128)(2,1)S(1)} %get-tuple-element.33.refs_2_, ...), custom_call_target="tpu_custom_call" | custom-call | flops 6442450944 | bytes 16777216 | tf_op jit(solution)/shard_map/x_dft/pallas_call | solution.py:308
  146.8 13.3 %all_to_all.23 = f32[32,8,128]{2,1,0:T(8,128)S(1)} all-to-all(f32[32,8,128]{2,1,0:T(8,128)S(1)} %broadcast_in_dim.2), channel_id=1, replica_groups=mesh['gx'=4,'gy'=8] {'gx','gy'}, dimensions={0} | all-to-all | bytes 262144 | tf_op jit(solution)/shard_map/all_to_all | solution.py:338
  160.1 0.6 reduce_sum.29
  (44 shorter events, 0.4 us)
Async XLA Ops:
  0.6 5.0 %copy-start = (f32[8,256,512]{2,1,0:T(8,128)S(1)}, f32[8,256,512]{2,1,0:T(8,128)}, u32[]{:S(2)}) copy-start(f32[8,256,512]{2,1,0:T(8,128)} %field_ref) | copy-start | bytes 12582916
  2.5 51.3 %collective-permute-start = (f32[4,256,256]{2,1,0:T(8,128)S(1)}, f32[4,256,256]{2,1,0:T(8,128)S(1)}, u32[]{:S(2)}, u32[]{:S(2)}) collective-permute-start(f32[4,256,256]{2,1,0:T(8,128)S(1)} %get-tuple-element.22.early_ref), channel_id=1, source_target_pairs={{0,16},{8,24},{16,0},{24,8},{1,17},{9,25},{17,1},{25,9},{2,18},{10... | collective-permute-start | bytes 3145736 | tf_op jit(solution)/shard_map/ppermute | solution.py:20
  5.5 45.7 %collective-permute-start.1 = (f32[4,256,256]{2,1,0:T(8,128)S(1)}, f32[4,256,256]{2,1,0:T(8,128)}, u32[]{:S(2)}, u32[]{:S(2)}) collective-permute-start(f32[4,256,256]{2,1,0:T(8,128)S(1)} %get-tuple-element.23.early_ref), channel_id=1, source_target_pairs={{0,16},{8,24},{16,0},{24,8},{1,17},{9,25},{17,1},{25,9},{2,18},{10... | collective-permute-start | bytes 3145736 | tf_op jit(solution)/shard_map/ppermute | solution.py:20
  8.4 54.0 %all-to-all-start = ((f32[8,256,256]{2,1,0:T(8,128)}), f32[8,256,256]{2,1,0:T(8,128)}, u32[]{:S(2)}, u32[]{:S(2)}) async-start(f32[8,256,256]{2,1,0:T(8,128)} %cut_right.1), calls=%async_computation | async-start | bytes 4194304 | tf_op jit(solution)/shard_map/all_to_all | solution.py:24
  17.1 6.7 %copy-start.9 = (f32[2048]{0:T(1024)S(1)}, f32[2048]{0:T(1024)}, u32[]{:S(2)}) copy-start(f32[2048]{0:T(1024)} %param.7) | copy-start | bytes 24580
  17.1 7.5 %copy-start.8 = (f32[512]{0:T(512)S(1)}, f32[512]{0:T(512)}, u32[]{:S(2)}) copy-start(f32[512]{0:T(512)} %param.8) | copy-start | bytes 6148
  22.3 0.8 copy-start.6
  22.3 5.2 %copy-start.11 = (f32[512]{0:T(512)S(1)}, f32[512]{0:T(512)}, u32[]{:S(2)}) copy-start(f32[512]{0:T(512)} %param.11) | copy-start | bytes 6148
  22.3 5.2 %copy-start.12 = (f32[512]{0:T(512)S(1)}, f32[512]{0:T(512)}, u32[]{:S(2)}) copy-start(f32[512]{0:T(512)} %param.10) | copy-start | bytes 6148
  22.3 6.6 %copy-start.10 = (f32[2048]{0:T(1024)S(1)}, f32[2048]{0:T(1024)}, u32[]{:S(2)}) copy-start(f32[2048]{0:T(1024)} %param.9) | copy-start | bytes 24580
  31.2 1.2 copy-start.5
  31.2 1.3 copy-start.7
  62.4 56.0 %copy-start.1 = (f32[2,8,256,128]{3,2,1,0:T(8,128)S(1)}, f32[2,8,256,128]{3,2,1,0:T(8,128)}, u32[]{:S(2)}) copy-start(f32[2,8,256,128]{3,2,1,0:T(8,128)} %pad_maximum_fusion.refs_5_.refs_3_) | copy-start | bytes 6291460
  62.4 56.0 %copy-start.2 = (bf16[2,512,512]{2,1,0:T(8,128)(2,1)S(1)}, bf16[2,512,512]{2,1,0:T(8,128)(2,1)}, u32[]{:S(2)}) copy-start(bf16[2,512,512]{2,1,0:T(8,128)(2,1)} %pad_maximum_fusion.1.refs_4_.refs_2_) | copy-start | bytes 3145732
  62.4 52.5 %all-to-all-start.1 = ((f32[8,256,256]{2,1,0:T(8,128)}), f32[8,256,256]{2,1,0:T(8,128)}, u32[]{:S(2)}, u32[]{:S(2)}) async-start(f32[8,256,256]{2,1,0:T(8,128)} %combine.3), calls=%async_computation.1 | async-start | bytes 4194304 | tf_op jit(solution)/shard_map/all_to_all | solution.py:24
  67.2 46.7 %collective-permute-start.2 = (f32[2048,256]{1,0:T(8,128)}, f32[2048,256]{1,0:T(8,128)}, u32[]{:S(2)}, u32[]{:S(2)}) collective-permute-start(f32[2048,256]{1,0:T(8,128)} %bitcast.1.refs_2_), channel_id=1, source_target_pairs={{0,16},{8,24},{16,0},{24,8},{1,17},{9,25},{17,1},{25,9},{2,18},{10... | collective-permute-start | bytes 6291464 | tf_op jit(solution)/shard_map/ppermute | solution.py:20
  68.8 46.1 %collective-permute-start.4 = (f32[2048,256]{1,0:T(8,128)}, f32[2048,256]{1,0:T(8,128)}, u32[]{:S(2)}, u32[]{:S(2)}) collective-permute-start(f32[2048,256]{1,0:T(8,128)} %bitcast.1.refs_2_), channel_id=1, source_target_pairs={{0,8},{8,0},{16,24},{24,16},{1,9},{9,1},{17,25},{25,17},{2,10},{10... | collective-permute-start | bytes 6291464 | tf_op jit(solution)/shard_map/ppermute | solution.py:20
  113.9 4.5 %collective-permute-start.3 = (f32[2048,256]{1,0:T(8,128)}, f32[2048,256]{1,0:T(8,128)}, u32[]{:S(2)}, u32[]{:S(2)}) collective-permute-start(f32[2048,256]{1,0:T(8,128)} %collective-permute-done.2.refs_0_), channel_id=1, source_target_pairs={{0,8},{8,0},{16,24},{24,16},{1,9},{9,1},{17,25},{25,17},{2,10},{10... | collective-permute-start | bytes 6291464 | tf_op jit(solution)/shard_map/ppermute | solution.py:20
  114.9 13.4 %collective-permute-start.5 = (f32[2048,256]{1,0:T(8,128)}, f32[2048,256]{1,0:T(8,128)}, u32[]{:S(2)}, u32[]{:S(2)}) collective-permute-start(f32[2048,256]{1,0:T(8,128)} %bitcast.20.refs_0_), channel_id=1, source_target_pairs={{0,8},{8,0},{16,24},{24,16},{1,9},{9,1},{17,25},{25,17},{2,10},{10... | collective-permute-start | bytes 6291464 | tf_op jit(solution)/shard_map/ppermute | solution.py:20
  128.3 8.8 %copy-start.3 = (bf16[2,512,512]{2,1,0:T(8,128)(2,1)S(1)}, bf16[2,512,512]{2,1,0:T(8,128)(2,1)}, u32[]{:S(2)}) copy-start(bf16[2,512,512]{2,1,0:T(8,128)(2,1)} %pad_maximum_fusion.3.refs_4_) | copy-start | bytes 3145732
  128.3 8.8 %copy-start.4 = (bf16[2,512,512]{2,1,0:T(8,128)(2,1)S(1)}, bf16[2,512,512]{2,1,0:T(8,128)(2,1)}, u32[]{:S(2)}) copy-start(bf16[2,512,512]{2,1,0:T(8,128)(2,1)} %pad_maximum_fusion.5.refs_5_) | copy-start | bytes 3145732

commit v15 on v12

--- a/solution.py
+++ b/solution.py
@@ -180,7 +180,7 @@
         ],
         compiler_params=pltpu.CompilerParams(vmem_limit_bytes=Y_BYTES),
         cost_estimate=pl.CostEstimate(
-            flops=48 * inner * length * LANES, bytes_accessed=8 * length * LANES * (len(inputs) + 3), transcendentals=0
+            flops=160 * inner * length * LANES, bytes_accessed=8 * length * LANES * (len(inputs) + 3), transcendentals=0
         ),
         name="y_dft",
     )(coefs, *inputs, table, twist)
@@ -291,8 +291,8 @@
     planes, rows, columns = field.shape
     length, width = planes * rows, columns // 4
     groups = [slice(0, planes // 2), slice(planes // 2, None)]
-    field_a, field_rest = lax.optimization_barrier(([field[group, :, : 2 * width] for group in groups], field))
-    field_b = field_rest[:, :, 2 * width :]
+    field_b, field_rest = lax.optimization_barrier((field[:, :, 2 * width :], field))
+    field_a = [field_rest[group, :, : 2 * width] for group in groups]
     sign = jnp.where(position < 2, 1.0, -1.0)
 
     own_real = jnp.where(position == 1, -1.0, jnp.where(position == 3, 0.0, 1.0))

time: 161 us -> 161 us (level)
  transfers between devices with their start and end apart: 8 -> 8, of which waited for: 5 -> 5; matrix products, arithmetic and copies ran while one was open for 15% -> 14% of each run, Pallas kernels for 9% -> 9%
where the time goes in v15:
time: 161 us
  waiting for transfers between devices  69.2 us (43%)
  Pallas kernels  31.9 us (20%)
  other arithmetic  21.4 us (13%)
  starting transfers between devices  15.7 us (10%)
  blocking collectives  13.3 us (8%)
  local copies, waits for them, and re-layouts  5.31 us (3%)
  between operations  4.02 us (2%)
    ppermute x6, waiting for transfers between devices, from_partner(): return lax.ppermute(value, axis, pairs)  63.9 us
    pallas_call x2, Pallas kernels, y_dft(): pl.pallas_call(functools.partial(y_kernel, len(inputs), pick), out_shape=...  18.2 us
    all_to_all x1, blocking collectives, sum_everywhere(): lax.all_to_all(copies, axes, split_axis=0, concat_axis=0, tiled=True)  13.3 us
    all_to_all x2, starting transfers between devices, to_planes(): return lax.all_to_all(values, 'gy', split_axis=0, concat_axis=1, tiled=True)  11 us
    pallas_call x1, Pallas kernels, x_dft(): pl.pallas_call(functools.partial(x_kernel, count), out_shape=(jax.ShapeDt...  9.61 us
    all_to_all x2, waiting for transfers between devices, to_planes(): return lax.all_to_all(values, 'gy', split_axis=0, concat_axis=1, tiled=True)  5.33 us
    sin x1, other arithmetic, root_table(): return (jnp.cos(angle), jnp.sin(angle))  5.16 us
    ppermute x6, starting transfers between devices, from_partner(): return lax.ppermute(value, axis, pairs)  4.7 us
  transfers between devices with their start and end apart: 8, of which 5 were waited for; matrix products, arithmetic and copies ran while one was open for 14% of the time, Pallas kernels for 9%

profile of v15, /device:TPU:0, one launch (start us, length us, event | category | flops | bytes accessed | tf_op | source)
XLA Modules:
  0.0 160.9 jit_solution(11621263167255969511)
XLA Ops:
  0.6 0.0 copy-start.4
  0.6 3.2 %slice.89 = f32[8,256,256]{2,1,0:T(8,128)} slice(f32[8,256,512]{2,1,0:T(8,128)} %param.6), slice={[0:8], [0:256], [256:512]} | slice | bytes 4194304 | tf_op jit(solution)/shard_map/slice | solution.py:294
  3.8 0.0 copy-done.4
  3.8 0.2 fusion.24
  4.1 3.0 %collective-permute-start = (f32[4,256,256]{2,1,0:T(8,128)S(1)}, f32[4,256,256]{2,1,0:T(8,128)S(1)}, u32[]{:S(2)}, u32[]{:S(2)}) collective-permute-start(f32[4,256,256]{2,1,0:T(8,128)S(1)} %get-tuple-element.41.early_ref), channel_id=1, source_target_pairs={{0,16},{8,24},{16,0},{24,8},{1,17},{9,25},{17,1},{25,9},{2,18},{10... | collective-permute-start | bytes 3145736 | tf_op jit(solution)/shard_map/ppermute | solution.py:20
  7.1 0.1 collective-permute-start.1
  7.2 6.2 %all-to-all-start = ((f32[8,256,256]{2,1,0:T(8,128)}), f32[8,256,256]{2,1,0:T(8,128)}, u32[]{:S(2)}, u32[]{:S(2)}) async-start(f32[8,256,256]{2,1,0:T(8,128)} %slice.89), calls=%async_computation | async-start | bytes 4194304 | tf_op jit(solution)/shard_map/all_to_all | solution.py:24
  13.5 1.1 fusion.23
  14.6 0.1 maximum_maximum_fusion
  14.7 1.2 reduce-precision_convert_fusion.2
  15.9 5.2 %fusion.14 = (f32[256,512]{1,0:T(8,128)}, f32[256,512]{1,0:T(8,128)}, f32[256,512]{1,0:T(8,128)S(1)}, f32[256,512]{1,0:T(8,128)S(1)}) fusion(s32[512]{0:T(512)S(1)} %multiply_add_fusion, s32[256]{0:T(256)S(1)} %pad_add_fusion.1, s32[256]{0:T(256)S(1)} %pad_add_fusion), kind=kLoop, calls=%fused_computation.55 | loop fusion | flops 3670016 | bytes 2101248 | tf_op jit(solution)/shard_map/sin | solution.py:77
  21.1 0.8 copy-done.6
  21.9 0.7 fusion.28
  22.6 0.7 log_reduce_fusion
  23.3 0.1 pad_maximum_fusion.13
  23.4 0.1 reshape.444.coef_ref
  23.4 0.6 log_reduce_fusion.1
  24.1 2.3 %pad_maximum_fusion.1.refs_4_.refs_2_ = bf16[2,512,512]{2,1,0:T(8,128)(2,1)} fusion(bf16[1,512,512]{2,1,0:T(8,128)(2,1)} %get-tuple-element.47, bf16[1,512,512]{2,1,0:T(8,128)(2,1)} %get-tuple-element.46), kind=kLoop, calls=%fused_computation.11 | loop fusion | flops 524288 | bytes 2097152 | tf_op jit(solution)/shard_map/stack | solution.py:89
  26.4 0.1 pad_maximum_fusion.12.coef_ref
  27.7 1.0 slice_negate_fusion.1
  28.7 1.2 pad_maximum_fusion.6
  30.0 0.2 reduce-precision_convert_fusion.1
  30.2 1.1 pad_maximum_fusion.3.refs_4_
  31.4 0.1 pad_maximum_fusion.8
  31.6 0.2 reduce-precision_convert_fusion
  31.7 1.1 pad_maximum_fusion.5.refs_5_
  32.8 3.2 %fusion.3 = (f32[1,8,256,128]{3,2,1,0:T(8,128)S(1)}, f32[1,8,256,128]{3,2,1,0:T(8,128)S(1)}) fusion(), kind=kLoop, calls=%fused_computation.17 | loop fusion | flops 786432 | bytes 2097152 | tf_op jit(solution)/shard_map/sin | solution.py:313
  36.0 1.5 pad_maximum_fusion.refs_5_.refs_3_
  37.6 15.3 %collective-permute-done.1.late_ref = f32[4,256,256]{2,1,0:T(8,128)} collective-permute-done((f32[4,256,256]{2,1,0:T(8,128)S(1)}, f32[4,256,256]{2,1,0:T(8,128)}, u32[]{:S(2)}, u32[]{:S(2)}) %collective-permute-start.1) | collective-permute-done | bytes 1048608 | tf_op jit(solution)/shard_map/ppermute | solution.py:20
  52.9 2.6 %combine.2.refs_0_ = f32[8,256,256]{2,1,0:T(8,128)} custom-call(f32[1]{0:T(128)} %bitcast.sign_ref, f32[4,256,256]{2,1,0:T(8,128)} %collective-permute-done.1.late_ref, f32[4,256,256]{2,1,0:T(8,128)S(1)} %get-tuple-element.40.early_ref), custom_call_target="tpu_custom_call" | custom-call | flops 524288 | bytes 3145728 | tf_op jit(solution)/shard_map/combine/pallas_call | solution.py:50
  55.4 0.0 collective-permute-done.late_ref
  55.4 1.5 combine.3
  56.9 4.3 %all-to-all-done = f32[8,256,256]{2,1,0:T(8,128)} async-done(((f32[8,256,256]{2,1,0:T(8,128)}), f32[8,256,256]{2,1,0:T(8,128)}, u32[]{:S(2)}, u32[]{:S(2)}) %all-to-all-start) | async-done | bytes 2097184 | tf_op jit(solution)/shard_map/all_to_all | solution.py:24
  61.2 4.8 %all-to-all-start.1 = ((f32[8,256,256]{2,1,0:T(8,128)}), f32[8,256,256]{2,1,0:T(8,128)}, u32[]{:S(2)}, u32[]{:S(2)}) async-start(f32[8,256,256]{2,1,0:T(8,128)} %combine.3), calls=%async_computation.1 | async-start | bytes 4194304 | tf_op jit(solution)/shard_map/all_to_all | solution.py:24
  66.0 1.6 collective-permute-start.2
  67.6 0.0 collective-permute-start.4
  67.6 45.1 %collective-permute-done.2.refs_0_ = f32[2048,256]{1,0:T(8,128)} collective-permute-done((f32[2048,256]{1,0:T(8,128)}, f32[2048,256]{1,0:T(8,128)}, u32[]{:S(2)}, u32[]{:S(2)}) %collective-permute-start.2) | collective-permute-done | bytes 2097184 | tf_op jit(solution)/shard_map/ppermute | solution.py:20
  112.7 0.0 collective-permute-start.3
  112.7 1.0 all-to-all-done.1
  113.8 0.0 collective-permute-start.5
  113.8 0.0 collective-permute-done.4.refs_3_
  113.8 3.5 %collective-permute-done.3.refs_1_ = f32[2048,256]{1,0:T(8,128)} collective-permute-done((f32[2048,256]{1,0:T(8,128)}, f32[2048,256]{1,0:T(8,128)}, u32[]{:S(2)}, u32[]{:S(2)}) %collective-permute-start.3) | collective-permute-done | bytes 2097184 | tf_op jit(solution)/shard_map/ppermute | solution.py:20
  117.2 10.2 %y_dft.2 = (bf16[4,2048,128]{2,1,0:T(8,128)(2,1)S(1)}, bf16[4,2048,128]{2,1,0:T(8,128)(2,1)S(1)}) custom-call(f32[2,4]{1,0:T(2,128)S(1)} %pad_maximum_fusion.12.coef_ref, f32[2048,256]{1,0:T(8,128)} %collective-permute-done.2.refs_0_, f32[2048,256]{1,0:T(8,128)} %collective-permute-done.3.refs_1_, f32[2048,256]{1,0:T(8,128)} %bitcast.1.refs_2_, ...), custom_call_target="tpu_custom_call" | custom-call | flops 10737418240 | bytes 14680064 | tf_op jit(solution)/shard_map/y_dft/pallas_call | solution.py:171
  127.4 0.0 collective-permute-done.5.refs_1_
  127.4 8.1 %y_dft.3 = (bf16[4,2048,128]{2,1,0:T(8,128)(2,1)S(1)}, bf16[4,2048,128]{2,1,0:T(8,128)(2,1)S(1)}) custom-call(f32[2,2]{1,0:T(2,128)S(1)} %reshape.444.coef_ref, f32[2048,256]{1,0:T(8,128)} %bitcast.20.refs_0_, f32[2048,256]{1,0:T(8,128)} %collective-permute-done.5.refs_1_, bf16[2,512,512]{2,1,0:T(8,128)(2,1)S(1)} %copy-done.1, f32[2,8,256,128]{3,2,1,0:T(8,128)S(1)} %copy-done), custom_call_target="tpu_custom_call" | custom-call | flops 10737418240 | bytes 10485760 | tf_op jit(solution)/shard_map/y_dft/pallas_call | solution.py:171
  135.5 9.6 %x_dft.1 = (f32[2,1,2048,512]{3,2,1,0:T(8,128)}, f32[8,128]{1,0:T(8,128)S(1)}) custom-call(bf16[4,2048,128]{2,1,0:T(8,128)(2,1)S(1)} %get-tuple-element.27.refs_0_, bf16[4,2048,128]{2,1,0:T(8,128)(2,1)S(1)} %get-tuple-element.30.refs_1_, bf16[4,2048,128]{2,1,0:T(8,128)(2,1)S(1)} %get-tuple-element.31.refs_2_, ...), custom_call_target="tpu_custom_call" | custom-call | flops 6442450944 | bytes 16777216 | tf_op jit(solution)/shard_map/x_dft/pallas_call | solution.py:256
  145.2 13.3 %all_to_all.23 = f32[32,8,128]{2,1,0:T(8,128)S(1)} all-to-all(f32[32,8,128]{2,1,0:T(8,128)S(1)} %broadcast_in_dim.2), channel_id=1, replica_groups=mesh['gx'=4,'gy'=8] {'gx','gy'}, dimensions={0} | all-to-all | bytes 262144 | tf_op jit(solution)/shard_map/all_to_all | solution.py:286
  158.5 0.6 reduce_sum.29
  (44 shorter events, 0.4 us)
Async XLA Ops:
  0.6 3.2 %copy-start.4 = (f32[8,256,512]{2,1,0:T(8,128)S(1)}, f32[8,256,512]{2,1,0:T(8,128)}, u32[]{:S(2)}) copy-start(f32[8,256,512]{2,1,0:T(8,128)} %param.6) | copy-start | bytes 12582916
  4.1 51.3 %collective-permute-start = (f32[4,256,256]{2,1,0:T(8,128)S(1)}, f32[4,256,256]{2,1,0:T(8,128)S(1)}, u32[]{:S(2)}, u32[]{:S(2)}) collective-permute-start(f32[4,256,256]{2,1,0:T(8,128)S(1)} %get-tuple-element.41.early_ref), channel_id=1, source_target_pairs={{0,16},{8,24},{16,0},{24,8},{1,17},{9,25},{17,1},{25,9},{2,18},{10... | collective-permute-start | bytes 3145736 | tf_op jit(solution)/shard_map/ppermute | solution.py:20
  7.1 45.7 %collective-permute-start.1 = (f32[4,256,256]{2,1,0:T(8,128)S(1)}, f32[4,256,256]{2,1,0:T(8,128)}, u32[]{:S(2)}, u32[]{:S(2)}) collective-permute-start(f32[4,256,256]{2,1,0:T(8,128)S(1)} %get-tuple-element.40.early_ref), channel_id=1, source_target_pairs={{0,16},{8,24},{16,0},{24,8},{1,17},{9,25},{17,1},{25,9},{2,18},{10... | collective-permute-start | bytes 3145736 | tf_op jit(solution)/shard_map/ppermute | solution.py:20
  7.2 54.0 %all-to-all-start = ((f32[8,256,256]{2,1,0:T(8,128)}), f32[8,256,256]{2,1,0:T(8,128)}, u32[]{:S(2)}, u32[]{:S(2)}) async-start(f32[8,256,256]{2,1,0:T(8,128)} %slice.89), calls=%async_computation | async-start | bytes 4194304 | tf_op jit(solution)/shard_map/all_to_all | solution.py:24
  15.9 6.7 %copy-start.9 = (f32[2048]{0:T(1024)S(1)}, f32[2048]{0:T(1024)}, u32[]{:S(2)}) copy-start(f32[2048]{0:T(1024)} %param.7) | copy-start | bytes 24580
  15.9 7.5 %copy-start.8 = (f32[512]{0:T(512)S(1)}, f32[512]{0:T(512)}, u32[]{:S(2)}) copy-start(f32[512]{0:T(512)} %param.8) | copy-start | bytes 6148
  21.1 0.8 copy-start.6
  21.1 5.2 %copy-start.11 = (f32[512]{0:T(512)S(1)}, f32[512]{0:T(512)}, u32[]{:S(2)}) copy-start(f32[512]{0:T(512)} %param.11) | copy-start | bytes 6148
  21.1 5.2 %copy-start.12 = (f32[512]{0:T(512)S(1)}, f32[512]{0:T(512)}, u32[]{:S(2)}) copy-start(f32[512]{0:T(512)} %param.10) | copy-start | bytes 6148
  21.1 6.6 %copy-start.10 = (f32[2048]{0:T(1024)S(1)}, f32[2048]{0:T(1024)}, u32[]{:S(2)}) copy-start(f32[2048]{0:T(1024)} %param.9) | copy-start | bytes 24580
  30.0 1.2 copy-start.5
  30.0 1.3 copy-start.7
  61.2 56.0 %copy-start = (f32[2,8,256,128]{3,2,1,0:T(8,128)S(1)}, f32[2,8,256,128]{3,2,1,0:T(8,128)}, u32[]{:S(2)}) copy-start(f32[2,8,256,128]{3,2,1,0:T(8,128)} %pad_maximum_fusion.refs_5_.refs_3_) | copy-start | bytes 6291460
  61.2 56.0 %copy-start.1 = (bf16[2,512,512]{2,1,0:T(8,128)(2,1)S(1)}, bf16[2,512,512]{2,1,0:T(8,128)(2,1)}, u32[]{:S(2)}) copy-start(bf16[2,512,512]{2,1,0:T(8,128)(2,1)} %pad_maximum_fusion.1.refs_4_.refs_2_) | copy-start | bytes 3145732
  61.2 52.5 %all-to-all-start.1 = ((f32[8,256,256]{2,1,0:T(8,128)}), f32[8,256,256]{2,1,0:T(8,128)}, u32[]{:S(2)}, u32[]{:S(2)}) async-start(f32[8,256,256]{2,1,0:T(8,128)} %combine.3), calls=%async_computation.1 | async-start | bytes 4194304 | tf_op jit(solution)/shard_map/all_to_all | solution.py:24
  66.0 46.7 %collective-permute-start.2 = (f32[2048,256]{1,0:T(8,128)}, f32[2048,256]{1,0:T(8,128)}, u32[]{:S(2)}, u32[]{:S(2)}) collective-permute-start(f32[2048,256]{1,0:T(8,128)} %bitcast.1.refs_2_), channel_id=1, source_target_pairs={{0,16},{8,24},{16,0},{24,8},{1,17},{9,25},{17,1},{25,9},{2,18},{10... | collective-permute-start | bytes 6291464 | tf_op jit(solution)/shard_map/ppermute | solution.py:20
  67.6 46.1 %collective-permute-start.4 = (f32[2048,256]{1,0:T(8,128)}, f32[2048,256]{1,0:T(8,128)}, u32[]{:S(2)}, u32[]{:S(2)}) collective-permute-start(f32[2048,256]{1,0:T(8,128)} %bitcast.1.refs_2_), channel_id=1, source_target_pairs={{0,8},{8,0},{16,24},{24,16},{1,9},{9,1},{17,25},{25,17},{2,10},{10... | collective-permute-start | bytes 6291464 | tf_op jit(solution)/shard_map/ppermute | solution.py:20
  112.7 4.5 %collective-permute-start.3 = (f32[2048,256]{1,0:T(8,128)}, f32[2048,256]{1,0:T(8,128)}, u32[]{:S(2)}, u32[]{:S(2)}) collective-permute-start(f32[2048,256]{1,0:T(8,128)} %collective-permute-done.2.refs_0_), channel_id=1, source_target_pairs={{0,8},{8,0},{16,24},{24,16},{1,9},{9,1},{17,25},{25,17},{2,10},{10... | collective-permute-start | bytes 6291464 | tf_op jit(solution)/shard_map/ppermute | solution.py:20
  113.8 13.7 %collective-permute-start.5 = (f32[2048,256]{1,0:T(8,128)}, f32[2048,256]{1,0:T(8,128)}, u32[]{:S(2)}, u32[]{:S(2)}) collective-permute-start(f32[2048,256]{1,0:T(8,128)} %bitcast.20.refs_0_), channel_id=1, source_target_pairs={{0,8},{8,0},{16,24},{24,16},{1,9},{9,1},{17,25},{25,17},{2,10},{10... | collective-permute-start | bytes 6291464 | tf_op jit(solution)/shard_map/ppermute | solution.py:20
  127.4 8.1 %copy-start.2 = (bf16[2,512,512]{2,1,0:T(8,128)(2,1)S(1)}, bf16[2,512,512]{2,1,0:T(8,128)(2,1)}, u32[]{:S(2)}) copy-start(bf16[2,512,512]{2,1,0:T(8,128)(2,1)} %pad_maximum_fusion.3.refs_4_) | copy-start | bytes 3145732
  127.4 8.1 %copy-start.3 = (bf16[2,512,512]{2,1,0:T(8,128)(2,1)S(1)}, bf16[2,512,512]{2,1,0:T(8,128)(2,1)}, u32[]{:S(2)}) copy-start(bf16[2,512,512]{2,1,0:T(8,128)(2,1)} %pad_maximum_fusion.5.refs_5_) | copy-start | bytes 3145732

commit v16 on v15

--- a/solution.py
+++ b/solution.py
@@ -135,33 +135,48 @@
                 tiles.append(mixed)
             for tile in range(2):
                 mix_ref[2 * tile + which, rows, :] = pick_columns(*tiles, tile) if pick else tiles[tile]
-    for tile, out_ref in enumerate(out_refs):
+    half = inner // 2
+
+    def split(tile):
         for which in range(2):
             for s in range(RADIX):
                 parts = split_value(mix_ref[2 * tile + which, pl.ds(s, inner, stride=RADIX), :])
                 for place, value in enumerate(parts):
                     split_ref[tile, place, pl.ds(which * inner, inner), pl.ds(s * LANES, LANES)] = value
-        half = inner // 2
-        for part in range(2):
-            table = [table_ref[place, pl.ds(part * inner, inner), :] for place in (0, 1, 0)]
-            values = [split_ref[tile, place] for place in (0, 0, 1)]
-            step_ref[part] = dot(jnp.concatenate(table, axis=1), jnp.concatenate(values, axis=0))
-            for start in range(0, half, 16):
-                values = []
-                for s in range(RADIX):
-                    cols = pl.ds(s * LANES, LANES)
-                    re = step_ref[part, pl.ds(start, 16), cols]
-                    im = step_ref[part, pl.ds(half + start, 16), cols]
-                    if s:
-                        cos, sin = [twist_ref[k, s, pl.ds(part * half + start, 16), :] for k in range(2)]
-                        re, im = re * cos - im * sin, re * sin + im * cos
-                    values.append((re, im))
-                for kb, pair in enumerate(small_fft(values)):
-                    rows = pl.ds(kb * inner + part * half + start, 16)
-                    for which in range(2):
-                        high, low = split_value(pair[which])
-                        out_ref[2 * which, rows, :] = high
-                        out_ref[2 * which + 1, rows, :] = low
+
+    def multiply(tile, part):
+        table = [table_ref[place, pl.ds(part * inner, inner), :] for place in (0, 1, 0)]
+        values = [split_ref[tile, place] for place in (0, 0, 1)]
+        step_ref[part] = dot(jnp.concatenate(table, axis=1), jnp.concatenate(values, axis=0))
+
+    def finish(tile, part):
+        for start in range(0, half, 16):
+            values = []
+            for s in range(RADIX):
+                cols = pl.ds(s * LANES, LANES)
+                re = step_ref[part, pl.ds(start, 16), cols]
+                im = step_ref[part, pl.ds(half + start, 16), cols]
+                if s:
+                    cos, sin = [twist_ref[k, s, pl.ds(part * half + start, 16), :] for k in range(2)]
+                    re, im = re * cos - im * sin, re * sin + im * cos
+                values.append((re, im))
+            for kb, pair in enumerate(small_fft(values)):
+                rows = pl.ds(kb * inner + part * half + start, 16)
+                for which in range(2):
+                    high, low = split_value(pair[which])
+                    out_refs[tile][2 * which, rows, :] = high
+                    out_refs[tile][2 * which + 1, rows, :] = low
+
+    jobs = [(tile, part) for tile in range(len(out_refs)) for part in range(2)]
+    split(0)
+    multiply(*jobs[0])
+    for before, job in zip(jobs, jobs[1:]):
+        if job[1]:
+            if job[0] + 1 < len(out_refs):
+                split(job[0] + 1)
+        multiply(*job)
+        finish(*before)
+    finish(*jobs[-1])
 
 
 def y_dft(inputs, pick, coefs, table, twist):

time: 161 us -> 161 us (level)
  no operation moved by 1% of the time
where the time goes in v16:
time: 161 us
  waiting for transfers between devices  69.2 us (43%)
  Pallas kernels  31.9 us (20%)
  other arithmetic  21.4 us (13%)
  starting transfers between devices  15.7 us (10%)
  blocking collectives  13.3 us (8%)
  local copies, waits for them, and re-layouts  5.31 us (3%)
  between operations  4.02 us (2%)
    ppermute x6, waiting for transfers between devices, from_partner(): return lax.ppermute(value, axis, pairs)  63.9 us
    pallas_call x2, Pallas kernels, y_dft(): pl.pallas_call(functools.partial(y_kernel, len(inputs), pick), out_shape=...  18.2 us
    all_to_all x1, blocking collectives, sum_everywhere(): lax.all_to_all(copies, axes, split_axis=0, concat_axis=0, tiled=True)  13.3 us
    all_to_all x2, starting transfers between devices, to_planes(): return lax.all_to_all(values, 'gy', split_axis=0, concat_axis=1, tiled=True)  11 us
    pallas_call x1, Pallas kernels, x_dft(): pl.pallas_call(functools.partial(x_kernel, count), out_shape=(jax.ShapeDt...  9.61 us
    all_to_all x2, waiting for transfers between devices, to_planes(): return lax.all_to_all(values, 'gy', split_axis=0, concat_axis=1, tiled=True)  5.33 us
    sin x1, other arithmetic, root_table(): return (jnp.cos(angle), jnp.sin(angle))  5.16 us
    ppermute x6, starting transfers between devices, from_partner(): return lax.ppermute(value, axis, pairs)  4.7 us
  transfers between devices with their start and end apart: 8, of which 5 were waited for; matrix products, arithmetic and copies ran while one was open for 14% of the time, Pallas kernels for 9%

profile of v16, /device:TPU:0, one launch (start us, length us, event | category | flops | bytes accessed | tf_op | source)
XLA Modules:
  0.0 160.9 jit_solution(11621263167255969511)
XLA Ops:
  0.6 0.0 copy-start.4
  0.6 3.2 %slice.89 = f32[8,256,256]{2,1,0:T(8,128)} slice(f32[8,256,512]{2,1,0:T(8,128)} %param.6), slice={[0:8], [0:256], [256:512]} | slice | bytes 4194304 | tf_op jit(solution)/shard_map/slice | solution.py:309
  3.8 0.0 copy-done.4
  3.8 0.2 fusion.24
  4.1 3.0 %collective-permute-start = (f32[4,256,256]{2,1,0:T(8,128)S(1)}, f32[4,256,256]{2,1,0:T(8,128)S(1)}, u32[]{:S(2)}, u32[]{:S(2)}) collective-permute-start(f32[4,256,256]{2,1,0:T(8,128)S(1)} %get-tuple-element.41.early_ref), channel_id=1, source_target_pairs={{0,16},{8,24},{16,0},{24,8},{1,17},{9,25},{17,1},{25,9},{2,18},{10... | collective-permute-start | bytes 3145736 | tf_op jit(solution)/shard_map/ppermute | solution.py:20
  7.1 0.1 collective-permute-start.1
  7.2 6.2 %all-to-all-start = ((f32[8,256,256]{2,1,0:T(8,128)}), f32[8,256,256]{2,1,0:T(8,128)}, u32[]{:S(2)}, u32[]{:S(2)}) async-start(f32[8,256,256]{2,1,0:T(8,128)} %slice.89), calls=%async_computation | async-start | bytes 4194304 | tf_op jit(solution)/shard_map/all_to_all | solution.py:24
  13.5 1.1 fusion.23
  14.6 0.1 maximum_maximum_fusion
  14.7 1.2 reduce-precision_convert_fusion.2
  15.9 5.2 %fusion.14 = (f32[256,512]{1,0:T(8,128)}, f32[256,512]{1,0:T(8,128)}, f32[256,512]{1,0:T(8,128)S(1)}, f32[256,512]{1,0:T(8,128)S(1)}) fusion(s32[512]{0:T(512)S(1)} %multiply_add_fusion, s32[256]{0:T(256)S(1)} %pad_add_fusion.1, s32[256]{0:T(256)S(1)} %pad_add_fusion), kind=kLoop, calls=%fused_computation.55 | loop fusion | flops 3670016 | bytes 2101248 | tf_op jit(solution)/shard_map/sin | solution.py:77
  21.1 0.8 copy-done.6
  21.9 0.7 fusion.28
  22.6 0.7 log_reduce_fusion
  23.3 0.1 pad_maximum_fusion.13
  23.4 0.1 reshape.444.coef_ref
  23.4 0.6 log_reduce_fusion.1
  24.1 2.3 %pad_maximum_fusion.1.refs_4_.refs_2_ = bf16[2,512,512]{2,1,0:T(8,128)(2,1)} fusion(bf16[1,512,512]{2,1,0:T(8,128)(2,1)} %get-tuple-element.47, bf16[1,512,512]{2,1,0:T(8,128)(2,1)} %get-tuple-element.46), kind=kLoop, calls=%fused_computation.11 | loop fusion | flops 524288 | bytes 2097152 | tf_op jit(solution)/shard_map/stack | solution.py:89
  26.4 0.1 pad_maximum_fusion.12.coef_ref
  27.7 1.0 slice_negate_fusion.1
  28.7 1.2 pad_maximum_fusion.6
  30.0 0.2 reduce-precision_convert_fusion.1
  30.2 1.1 pad_maximum_fusion.3.refs_4_
  31.4 0.1 pad_maximum_fusion.8
  31.6 0.2 reduce-precision_convert_fusion
  31.7 1.1 pad_maximum_fusion.5.refs_5_
  32.8 3.2 %fusion.3 = (f32[1,8,256,128]{3,2,1,0:T(8,128)S(1)}, f32[1,8,256,128]{3,2,1,0:T(8,128)S(1)}) fusion(), kind=kLoop, calls=%fused_computation.17 | loop fusion | flops 786432 | bytes 2097152 | tf_op jit(solution)/shard_map/sin | solution.py:328
  36.0 1.5 pad_maximum_fusion.refs_5_.refs_3_
  37.6 15.3 %collective-permute-done.1.late_ref = f32[4,256,256]{2,1,0:T(8,128)} collective-permute-done((f32[4,256,256]{2,1,0:T(8,128)S(1)}, f32[4,256,256]{2,1,0:T(8,128)}, u32[]{:S(2)}, u32[]{:S(2)}) %collective-permute-start.1) | collective-permute-done | bytes 1048608 | tf_op jit(solution)/shard_map/ppermute | solution.py:20
  52.9 2.6 %combine.2.refs_0_ = f32[8,256,256]{2,1,0:T(8,128)} custom-call(f32[1]{0:T(128)} %bitcast.sign_ref, f32[4,256,256]{2,1,0:T(8,128)} %collective-permute-done.1.late_ref, f32[4,256,256]{2,1,0:T(8,128)S(1)} %get-tuple-element.40.early_ref), custom_call_target="tpu_custom_call" | custom-call | flops 524288 | bytes 3145728 | tf_op jit(solution)/shard_map/combine/pallas_call | solution.py:50
  55.4 0.0 collective-permute-done.late_ref
  55.4 1.5 combine.3
  56.9 4.3 %all-to-all-done = f32[8,256,256]{2,1,0:T(8,128)} async-done(((f32[8,256,256]{2,1,0:T(8,128)}), f32[8,256,256]{2,1,0:T(8,128)}, u32[]{:S(2)}, u32[]{:S(2)}) %all-to-all-start) | async-done | bytes 2097184 | tf_op jit(solution)/shard_map/all_to_all | solution.py:24
  61.2 4.8 %all-to-all-start.1 = ((f32[8,256,256]{2,1,0:T(8,128)}), f32[8,256,256]{2,1,0:T(8,128)}, u32[]{:S(2)}, u32[]{:S(2)}) async-start(f32[8,256,256]{2,1,0:T(8,128)} %combine.3), calls=%async_computation.1 | async-start | bytes 4194304 | tf_op jit(solution)/shard_map/all_to_all | solution.py:24
  66.0 1.6 collective-permute-start.2
  67.6 0.0 collective-permute-start.4
  67.6 45.1 %collective-permute-done.2.refs_0_ = f32[2048,256]{1,0:T(8,128)} collective-permute-done((f32[2048,256]{1,0:T(8,128)}, f32[2048,256]{1,0:T(8,128)}, u32[]{:S(2)}, u32[]{:S(2)}) %collective-permute-start.2) | collective-permute-done | bytes 2097184 | tf_op jit(solution)/shard_map/ppermute | solution.py:20
  112.7 0.0 collective-permute-start.3
  112.7 1.0 all-to-all-done.1
  113.8 0.0 collective-permute-start.5
  113.8 0.0 collective-permute-done.4.refs_3_
  113.8 3.5 %collective-permute-done.3.refs_1_ = f32[2048,256]{1,0:T(8,128)} collective-permute-done((f32[2048,256]{1,0:T(8,128)}, f32[2048,256]{1,0:T(8,128)}, u32[]{:S(2)}, u32[]{:S(2)}) %collective-permute-start.3) | collective-permute-done | bytes 2097184 | tf_op jit(solution)/shard_map/ppermute | solution.py:20
  117.2 10.2 %y_dft.2 = (bf16[4,2048,128]{2,1,0:T(8,128)(2,1)S(1)}, bf16[4,2048,128]{2,1,0:T(8,128)(2,1)S(1)}) custom-call(f32[2,4]{1,0:T(2,128)S(1)} %pad_maximum_fusion.12.coef_ref, f32[2048,256]{1,0:T(8,128)} %collective-permute-done.2.refs_0_, f32[2048,256]{1,0:T(8,128)} %collective-permute-done.3.refs_1_, f32[2048,256]{1,0:T(8,128)} %bitcast.1.refs_2_, ...), custom_call_target="tpu_custom_call" | custom-call | flops 10737418240 | bytes 14680064 | tf_op jit(solution)/shard_map/y_dft/pallas_call | solution.py:186
  127.4 0.0 collective-permute-done.5.refs_1_
  127.4 8.1 %y_dft.3 = (bf16[4,2048,128]{2,1,0:T(8,128)(2,1)S(1)}, bf16[4,2048,128]{2,1,0:T(8,128)(2,1)S(1)}) custom-call(f32[2,2]{1,0:T(2,128)S(1)} %reshape.444.coef_ref, f32[2048,256]{1,0:T(8,128)} %bitcast.20.refs_0_, f32[2048,256]{1,0:T(8,128)} %collective-permute-done.5.refs_1_, bf16[2,512,512]{2,1,0:T(8,128)(2,1)S(1)} %copy-done.1, f32[2,8,256,128]{3,2,1,0:T(8,128)S(1)} %copy-done), custom_call_target="tpu_custom_call" | custom-call | flops 10737418240 | bytes 10485760 | tf_op jit(solution)/shard_map/y_dft/pallas_call | solution.py:186
  135.5 9.6 %x_dft.1 = (f32[2,1,2048,512]{3,2,1,0:T(8,128)}, f32[8,128]{1,0:T(8,128)S(1)}) custom-call(bf16[4,2048,128]{2,1,0:T(8,128)(2,1)S(1)} %get-tuple-element.27.refs_0_, bf16[4,2048,128]{2,1,0:T(8,128)(2,1)S(1)} %get-tuple-element.30.refs_1_, bf16[4,2048,128]{2,1,0:T(8,128)(2,1)S(1)} %get-tuple-element.31.refs_2_, ...), custom_call_target="tpu_custom_call" | custom-call | flops 6442450944 | bytes 16777216 | tf_op jit(solution)/shard_map/x_dft/pallas_call | solution.py:271
  145.2 13.3 %all_to_all.23 = f32[32,8,128]{2,1,0:T(8,128)S(1)} all-to-all(f32[32,8,128]{2,1,0:T(8,128)S(1)} %broadcast_in_dim.2), channel_id=1, replica_groups=mesh['gx'=4,'gy'=8] {'gx','gy'}, dimensions={0} | all-to-all | bytes 262144 | tf_op jit(solution)/shard_map/all_to_all | solution.py:301
  158.5 0.6 reduce_sum.29
  (44 shorter events, 0.4 us)
Async XLA Ops:
  0.6 3.2 %copy-start.4 = (f32[8,256,512]{2,1,0:T(8,128)S(1)}, f32[8,256,512]{2,1,0:T(8,128)}, u32[]{:S(2)}) copy-start(f32[8,256,512]{2,1,0:T(8,128)} %param.6) | copy-start | bytes 12582916
  4.1 51.3 %collective-permute-start = (f32[4,256,256]{2,1,0:T(8,128)S(1)}, f32[4,256,256]{2,1,0:T(8,128)S(1)}, u32[]{:S(2)}, u32[]{:S(2)}) collective-permute-start(f32[4,256,256]{2,1,0:T(8,128)S(1)} %get-tuple-element.41.early_ref), channel_id=1, source_target_pairs={{0,16},{8,24},{16,0},{24,8},{1,17},{9,25},{17,1},{25,9},{2,18},{10... | collective-permute-start | bytes 3145736 | tf_op jit(solution)/shard_map/ppermute | solution.py:20
  7.1 45.7 %collective-permute-start.1 = (f32[4,256,256]{2,1,0:T(8,128)S(1)}, f32[4,256,256]{2,1,0:T(8,128)}, u32[]{:S(2)}, u32[]{:S(2)}) collective-permute-start(f32[4,256,256]{2,1,0:T(8,128)S(1)} %get-tuple-element.40.early_ref), channel_id=1, source_target_pairs={{0,16},{8,24},{16,0},{24,8},{1,17},{9,25},{17,1},{25,9},{2,18},{10... | collective-permute-start | bytes 3145736 | tf_op jit(solution)/shard_map/ppermute | solution.py:20
  7.2 54.0 %all-to-all-start = ((f32[8,256,256]{2,1,0:T(8,128)}), f32[8,256,256]{2,1,0:T(8,128)}, u32[]{:S(2)}, u32[]{:S(2)}) async-start(f32[8,256,256]{2,1,0:T(8,128)} %slice.89), calls=%async_computation | async-start | bytes 4194304 | tf_op jit(solution)/shard_map/all_to_all | solution.py:24
  15.9 6.7 %copy-start.9 = (f32[2048]{0:T(1024)S(1)}, f32[2048]{0:T(1024)}, u32[]{:S(2)}) copy-start(f32[2048]{0:T(1024)} %param.7) | copy-start | bytes 24580
  15.9 7.5 %copy-start.8 = (f32[512]{0:T(512)S(1)}, f32[512]{0:T(512)}, u32[]{:S(2)}) copy-start(f32[512]{0:T(512)} %param.8) | copy-start | bytes 6148
  21.1 0.8 copy-start.6
  21.1 5.2 %copy-start.11 = (f32[512]{0:T(512)S(1)}, f32[512]{0:T(512)}, u32[]{:S(2)}) copy-start(f32[512]{0:T(512)} %param.11) | copy-start | bytes 6148
  21.1 5.2 %copy-start.12 = (f32[512]{0:T(512)S(1)}, f32[512]{0:T(512)}, u32[]{:S(2)}) copy-start(f32[512]{0:T(512)} %param.10) | copy-start | bytes 6148
  21.1 6.6 %copy-start.10 = (f32[2048]{0:T(1024)S(1)}, f32[2048]{0:T(1024)}, u32[]{:S(2)}) copy-start(f32[2048]{0:T(1024)} %param.9) | copy-start | bytes 24580
  30.0 1.2 copy-start.5
  30.0 1.3 copy-start.7
  61.2 56.0 %copy-start = (f32[2,8,256,128]{3,2,1,0:T(8,128)S(1)}, f32[2,8,256,128]{3,2,1,0:T(8,128)}, u32[]{:S(2)}) copy-start(f32[2,8,256,128]{3,2,1,0:T(8,128)} %pad_maximum_fusion.refs_5_.refs_3_) | copy-start | bytes 6291460
  61.2 56.0 %copy-start.1 = (bf16[2,512,512]{2,1,0:T(8,128)(2,1)S(1)}, bf16[2,512,512]{2,1,0:T(8,128)(2,1)}, u32[]{:S(2)}) copy-start(bf16[2,512,512]{2,1,0:T(8,128)(2,1)} %pad_maximum_fusion.1.refs_4_.refs_2_) | copy-start | bytes 3145732
  61.2 52.5 %all-to-all-start.1 = ((f32[8,256,256]{2,1,0:T(8,128)}), f32[8,256,256]{2,1,0:T(8,128)}, u32[]{:S(2)}, u32[]{:S(2)}) async-start(f32[8,256,256]{2,1,0:T(8,128)} %combine.3), calls=%async_computation.1 | async-start | bytes 4194304 | tf_op jit(solution)/shard_map/all_to_all | solution.py:24
  66.0 46.7 %collective-permute-start.2 = (f32[2048,256]{1,0:T(8,128)}, f32[2048,256]{1,0:T(8,128)}, u32[]{:S(2)}, u32[]{:S(2)}) collective-permute-start(f32[2048,256]{1,0:T(8,128)} %bitcast.1.refs_2_), channel_id=1, source_target_pairs={{0,16},{8,24},{16,0},{24,8},{1,17},{9,25},{17,1},{25,9},{2,18},{10... | collective-permute-start | bytes 6291464 | tf_op jit(solution)/shard_map/ppermute | solution.py:20
  67.6 46.1 %collective-permute-start.4 = (f32[2048,256]{1,0:T(8,128)}, f32[2048,256]{1,0:T(8,128)}, u32[]{:S(2)}, u32[]{:S(2)}) collective-permute-start(f32[2048,256]{1,0:T(8,128)} %bitcast.1.refs_2_), channel_id=1, source_target_pairs={{0,8},{8,0},{16,24},{24,16},{1,9},{9,1},{17,25},{25,17},{2,10},{10... | collective-permute-start | bytes 6291464 | tf_op jit(solution)/shard_map/ppermute | solution.py:20
  112.7 4.5 %collective-permute-start.3 = (f32[2048,256]{1,0:T(8,128)}, f32[2048,256]{1,0:T(8,128)}, u32[]{:S(2)}, u32[]{:S(2)}) collective-permute-start(f32[2048,256]{1,0:T(8,128)} %collective-permute-done.2.refs_0_), channel_id=1, source_target_pairs={{0,8},{8,0},{16,24},{24,16},{1,9},{9,1},{17,25},{25,17},{2,10},{10... | collective-permute-start | bytes 6291464 | tf_op jit(solution)/shard_map/ppermute | solution.py:20
  113.8 13.7 %collective-permute-start.5 = (f32[2048,256]{1,0:T(8,128)}, f32[2048,256]{1,0:T(8,128)}, u32[]{:S(2)}, u32[]{:S(2)}) collective-permute-start(f32[2048,256]{1,0:T(8,128)} %bitcast.20.refs_0_), channel_id=1, source_target_pairs={{0,8},{8,0},{16,24},{24,16},{1,9},{9,1},{17,25},{25,17},{2,10},{10... | collective-permute-start | bytes 6291464 | tf_op jit(solution)/shard_map/ppermute | solution.py:20
  127.4 8.1 %copy-start.2 = (bf16[2,512,512]{2,1,0:T(8,128)(2,1)S(1)}, bf16[2,512,512]{2,1,0:T(8,128)(2,1)}, u32[]{:S(2)}) copy-start(bf16[2,512,512]{2,1,0:T(8,128)(2,1)} %pad_maximum_fusion.3.refs_4_) | copy-start | bytes 3145732
  127.4 8.1 %copy-start.3 = (bf16[2,512,512]{2,1,0:T(8,128)(2,1)S(1)}, bf16[2,512,512]{2,1,0:T(8,128)(2,1)}, u32[]{:S(2)}) copy-start(bf16[2,512,512]{2,1,0:T(8,128)(2,1)} %pad_maximum_fusion.5.refs_5_) | copy-start | bytes 3145732

commit v17 on v16

--- a/solution.py
+++ b/solution.py
@@ -348,7 +348,7 @@
 
     first_a = combine(sign.reshape(1), [(from_partner(part, "gx", 1), part) for part in field_a])
     tables = (y_table, twist, x_table(0), x_table(1), row_pair, col_trio, coefs_a, coefs_b, fixed)
-    first_a, first_b, tables = lax.optimization_barrier((first_a, to_planes(field_b)[0], tables))
+    first_b, tables = lax.optimization_barrier((to_planes(field_b)[0], tables))
     y_table, twist, even_table, odd_table, row_pair, col_trio, coefs_a, coefs_b, fixed = tables
     second_a = to_planes(first_a)[0]
     second_b = from_partner(first_b, "gx", 1)

time: 161 us -> 171 us (1.062)
  local copies, waits for them, and re-layouts: 5.31 us -> 10.4 us
  waiting for transfers between devices: 69.2 us -> 71.7 us
    all_to_all x2, waiting for transfers between devices: 5.33 us -> 36.3 us  [to_planes(): return lax.all_to_all(values, 'gy', split_axis=0, concat_axis=1, tiled=True)]
    ppermute x6, waiting for transfers between devices: 63.9 us -> 35.4 us  [from_partner(): return lax.ppermute(value, axis, pairs)]
    all_to_all x2, starting transfers between devices: 11 us -> 13 us  [to_planes(): return lax.all_to_all(values, 'gy', split_axis=0, concat_axis=1, tiled=True)]
  transfers between devices with their start and end apart: 8 -> 8, of which waited for: 5 -> 3; matrix products, arithmetic and copies ran while one was open for 14% -> 16% of each run, Pallas kernels for 9% -> 7%
where the time goes in v17:
time: 171 us
  waiting for transfers between devices  71.7 us (42%)
  Pallas kernels  32.4 us (19%)
  other arithmetic  21.6 us (13%)
  starting transfers between devices  17.1 us (10%)
  blocking collectives  13.4 us (8%)
  local copies, waits for them, and re-layouts  10.4 us (6%)
  between operations  3.92 us (2%)
    all_to_all x2, waiting for transfers between devices, to_planes(): return lax.all_to_all(values, 'gy', split_axis=0, concat_axis=1, tiled=True)  36.3 us
    ppermute x6, waiting for transfers between devices, from_partner(): return lax.ppermute(value, axis, pairs)  35.4 us
    pallas_call x2, Pallas kernels, y_dft(): pl.pallas_call(functools.partial(y_kernel, len(inputs), pick), out_shape=...  18.4 us
    all_to_all x1, blocking collectives, sum_everywhere(): lax.all_to_all(copies, axes, split_axis=0, concat_axis=0, tiled=True)  13.4 us
    all_to_all x2, starting transfers between devices, to_planes(): return lax.all_to_all(values, 'gy', split_axis=0, concat_axis=1, tiled=True)  13 us
    pallas_call x1, Pallas kernels, x_dft(): pl.pallas_call(functools.partial(x_kernel, count), out_shape=(jax.ShapeDt...  9.87 us
    sin x1, other arithmetic, root_table(): return (jnp.cos(angle), jnp.sin(angle))  5.18 us
    ppermute x6, starting transfers between devices, from_partner(): return lax.ppermute(value, axis, pairs)  4.12 us
  transfers between devices with their start and end apart: 8, of which 3 were waited for; matrix products, arithmetic and copies ran while one was open for 16% of the time, Pallas kernels for 7%

profile of v17, /device:TPU:0, one launch (start us, length us, event | category | flops | bytes accessed | tf_op | source)
XLA Modules:
  0.0 170.5 jit_solution(16836872084606339899)
XLA Ops:
  0.6 3.0 %slice.89 = f32[8,256,256]{2,1,0:T(8,128)} slice(f32[8,256,512]{2,1,0:T(8,128)} %param.6), slice={[0:8], [0:256], [256:512]} | slice | bytes 4194304 | tf_op jit(solution)/shard_map/slice | solution.py:309
  3.7 7.3 %all-to-all-start = ((f32[8,256,256]{2,1,0:T(8,128)}), f32[8,256,256]{2,1,0:T(8,128)}, u32[]{:S(2)}, u32[]{:S(2)}) async-start(f32[8,256,256]{2,1,0:T(8,128)} %slice.89), calls=%async_computation | async-start | bytes 4194304 | tf_op jit(solution)/shard_map/all_to_all | solution.py:24
  10.9 0.0 copy-start.12
  10.9 0.0 copy-start.13
  11.0 0.0 copy-start.10
  11.0 0.0 copy-start.11
  11.0 1.7 fusion.24
  12.7 1.6 collective-permute-start.3
  14.3 0.5 collective-permute-start.4
  14.8 0.1 pad_maximum_fusion.13
  14.9 0.1 reshape.443.coef_ref
  15.0 0.6 log_reduce_fusion.1
  15.7 0.6 log_reduce_fusion
  16.3 5.2 %fusion.14 = (f32[256,512]{1,0:T(8,128)}, f32[256,512]{1,0:T(8,128)}, f32[256,512]{1,0:T(8,128)S(1)}, f32[256,512]{1,0:T(8,128)S(1)}) fusion(s32[512]{0:T(512)S(1)} %multiply_add_fusion, s32[256]{0:T(256)S(1)} %pad_add_fusion.1, s32[256]{0:T(256)S(1)} %pad_add_fusion), kind=kLoop, calls=%fused_computation.55 | loop fusion | flops 3670016 | bytes 2101248 | tf_op jit(solution)/shard_map/sin | solution.py:77
  21.5 0.7 fusion.27
  22.2 0.7 fusion.28
  23.0 0.7 fusion.30
  23.7 1.9 %fusion.23 = (f32[2,1,128,256]{3,2,1,0:T(8,128)S(1)}, f32[2,1,128,256]{3,2,1,0:T(8,128)}, f32[2,1,128,256]{3,2,1,0:T(8,128)}) fusion(s32[2,128]{1,0:T(2,128)S(1)} %multiply_add_fusion.1), kind=kLoop, calls=%fused_computation.64 | loop fusion | flops 983040 | bytes 787456 | tf_op jit(solution)/shard_map/neg | solution.py:323
  25.6 0.1 pad_maximum_fusion.12.coef_ref
  26.8 1.2 maximum_maximum_fusion
  28.1 1.4 pad_maximum_fusion.6
  29.4 0.7 slice_bitcast_fusion.6
  30.2 0.9 slice_bitcast_fusion.7
  31.0 1.1 reduce-precision_convert_fusion.2
  32.2 27.8 %collective-permute-done.4.late_ref = f32[4,256,256]{2,1,0:T(8,128)} collective-permute-done((f32[4,256,256]{2,1,0:T(8,128)S(1)}, f32[4,256,256]{2,1,0:T(8,128)}, u32[]{:S(2)}, u32[]{:S(2)}) %collective-permute-start.4) | collective-permute-done | bytes 1048608 | tf_op jit(solution)/shard_map/ppermute | solution.py:20
  59.9 2.6 %combine.2.refs_0_ = f32[8,256,256]{2,1,0:T(8,128)} custom-call(f32[1]{0:T(128)} %bitcast.19.sign_ref, f32[4,256,256]{2,1,0:T(8,128)} %collective-permute-done.4.late_ref, f32[4,256,256]{2,1,0:T(8,128)S(1)} %get-tuple-element.38.early_ref), custom_call_target="tpu_custom_call" | custom-call | flops 524288 | bytes 3145728 | tf_op jit(solution)/shard_map/combine/pallas_call | solution.py:50
  62.5 1.5 combine.3
  64.1 5.7 %all-to-all-start.1 = ((f32[8,256,256]{2,1,0:T(8,128)}), f32[8,256,256]{2,1,0:T(8,128)S(1)}, u32[]{:S(2)}, u32[]{:S(2)}) async-start(f32[8,256,256]{2,1,0:T(8,128)} %combine.3), calls=%async_computation.1 | async-start | bytes 4194304 | tf_op jit(solution)/shard_map/all_to_all | solution.py:24
  69.8 1.4 pad_maximum_fusion.1.refs_4_.refs_2_
  71.2 0.0 copy-done.8
  71.2 0.2 reduce-precision_convert_fusion.1
  71.4 1.1 pad_maximum_fusion.3.refs_4_
  72.6 0.1 pad_maximum_fusion.8
  72.8 0.2 reduce-precision_convert_fusion
  72.9 1.1 pad_maximum_fusion.5.refs_5_
  74.1 3.2 %fusion.3 = (f32[1,8,256,128]{3,2,1,0:T(8,128)S(1)}, f32[1,8,256,128]{3,2,1,0:T(8,128)S(1)}) fusion(), kind=kLoop, calls=%fused_computation.17 | loop fusion | flops 786432 | bytes 2097152 | tf_op jit(solution)/shard_map/sin | solution.py:328
  77.3 1.5 pad_maximum_fusion.refs_5_.refs_3_
  78.8 1.5 collective-permute-start
  80.3 36.3 %all-to-all-done.1 = f32[8,256,256]{2,1,0:T(8,128)S(1)} async-done(((f32[8,256,256]{2,1,0:T(8,128)}), f32[8,256,256]{2,1,0:T(8,128)S(1)}, u32[]{:S(2)}, u32[]{:S(2)}) %all-to-all-start.1) | async-done | bytes 2097184 | tf_op jit(solution)/shard_map/all_to_all | solution.py:24
  116.6 0.5 collective-permute-start.2
  117.1 7.6 %collective-permute-done.refs_0_ = f32[2048,256]{1,0:T(8,128)} collective-permute-done((f32[2048,256]{1,0:T(8,128)}, f32[2048,256]{1,0:T(8,128)}, u32[]{:S(2)}, u32[]{:S(2)}) %collective-permute-start) | collective-permute-done | bytes 2097184 | tf_op jit(solution)/shard_map/ppermute | solution.py:20
  124.7 0.0 collective-permute-start.1
  124.7 1.6 copy-done
  126.3 7.7 %y_dft.3 = (bf16[4,2048,128]{2,1,0:T(8,128)(2,1)S(1)}, bf16[4,2048,128]{2,1,0:T(8,128)(2,1)S(1)}) custom-call(f32[2,2]{1,0:T(2,128)S(1)} %reshape.443.coef_ref, f32[2048,256]{1,0:T(8,128)S(1)} %bitcast.30, f32[2048,256]{1,0:T(8,128)} %collective-permute-done.5.refs_1_, bf16[2,512,512]{2,1,0:T(8,128)(2,1)S(1)} %pad_maximum_fusion.1.refs_4_.refs_2_, ...), custom_call_target="tpu_custom_call" | custom-call | flops 10737418240 | bytes 10485760 | tf_op jit(solution)/shard_map/y_dft/pallas_call | solution.py:186
  134.0 10.8 %y_dft.2 = (bf16[4,2048,128]{2,1,0:T(8,128)(2,1)S(1)}, bf16[4,2048,128]{2,1,0:T(8,128)(2,1)S(1)}) custom-call(f32[2,4]{1,0:T(2,128)S(1)} %pad_maximum_fusion.12.coef_ref, f32[2048,256]{1,0:T(8,128)} %collective-permute-done.refs_0_, f32[2048,256]{1,0:T(8,128)} %collective-permute-done.1.refs_1_, f32[2048,256]{1,0:T(8,128)} %bitcast.refs_2_, ...), custom_call_target="tpu_custom_call" | custom-call | flops 10737418240 | bytes 14680064 | tf_op jit(solution)/shard_map/y_dft/pallas_call | solution.py:186
  144.8 9.9 %x_dft.1 = (f32[2,1,2048,512]{3,2,1,0:T(8,128)}, f32[8,128]{1,0:T(8,128)S(1)}) custom-call(bf16[4,2048,128]{2,1,0:T(8,128)(2,1)S(1)} %get-tuple-element.25.refs_0_, bf16[4,2048,128]{2,1,0:T(8,128)(2,1)S(1)} %get-tuple-element.28.refs_1_, bf16[4,2048,128]{2,1,0:T(8,128)(2,1)S(1)} %get-tuple-element.29.refs_2_, ...), custom_call_target="tpu_custom_call" | custom-call | flops 6442450944 | bytes 16777216 | tf_op jit(solution)/shard_map/x_dft/pallas_call | solution.py:271
  154.7 13.4 %all_to_all.23 = f32[32,8,128]{2,1,0:T(8,128)S(1)} all-to-all(f32[32,8,128]{2,1,0:T(8,128)S(1)} %broadcast_in_dim.2), channel_id=1, replica_groups=mesh['gx'=4,'gy'=8] {'gx','gy'}, dimensions={0} | all-to-all | bytes 262144 | tf_op jit(solution)/shard_map/all_to_all | solution.py:301
  168.1 0.6 reduce_sum.29
  (46 shorter events, 0.3 us)
Async XLA Ops:
  3.7 60.4 %all-to-all-start = ((f32[8,256,256]{2,1,0:T(8,128)}), f32[8,256,256]{2,1,0:T(8,128)}, u32[]{:S(2)}, u32[]{:S(2)}) async-start(f32[8,256,256]{2,1,0:T(8,128)} %slice.89), calls=%async_computation | async-start | bytes 4194304 | tf_op jit(solution)/shard_map/all_to_all | solution.py:24
  10.9 4.1 %copy-start.9 = (f32[512]{0:T(512)S(1)}, f32[512]{0:T(512)}, u32[]{:S(2)}) copy-start(f32[512]{0:T(512)} %param.8) | copy-start | bytes 6148
  10.9 4.7 %copy-start.12 = (f32[512]{0:T(512)S(1)}, f32[512]{0:T(512)}, u32[]{:S(2)}) copy-start(f32[512]{0:T(512)} %param.11) | copy-start | bytes 6148
  10.9 4.7 %copy-start.13 = (f32[512]{0:T(512)S(1)}, f32[512]{0:T(512)}, u32[]{:S(2)}) copy-start(f32[512]{0:T(512)} %param.10) | copy-start | bytes 6148
  11.0 4.7 %copy-start.10 = (f32[2048]{0:T(1024)S(1)}, f32[2048]{0:T(1024)}, u32[]{:S(2)}) copy-start(f32[2048]{0:T(1024)} %param.7) | copy-start | bytes 24580
  11.0 5.3 %copy-start.11 = (f32[2048]{0:T(1024)S(1)}, f32[2048]{0:T(1024)}, u32[]{:S(2)}) copy-start(f32[2048]{0:T(1024)} %param.9) | copy-start | bytes 24580
  12.7 49.9 %collective-permute-start.3 = (f32[4,256,256]{2,1,0:T(8,128)S(1)}, f32[4,256,256]{2,1,0:T(8,128)S(1)}, u32[]{:S(2)}, u32[]{:S(2)}) collective-permute-start(f32[4,256,256]{2,1,0:T(8,128)S(1)} %get-tuple-element.39.early_ref), channel_id=1, source_target_pairs={{0,16},{8,24},{16,0},{24,8},{1,17},{9,25},{17,1},{25,9},{2,18},{10... | collective-permute-start | bytes 3145736 | tf_op jit(solution)/shard_map/ppermute | solution.py:20
  14.3 45.7 %collective-permute-start.4 = (f32[4,256,256]{2,1,0:T(8,128)S(1)}, f32[4,256,256]{2,1,0:T(8,128)}, u32[]{:S(2)}, u32[]{:S(2)}) collective-permute-start(f32[4,256,256]{2,1,0:T(8,128)S(1)} %get-tuple-element.38.early_ref), channel_id=1, source_target_pairs={{0,16},{8,24},{16,0},{24,8},{1,17},{9,25},{17,1},{25,9},{2,18},{10... | collective-permute-start | bytes 3145736 | tf_op jit(solution)/shard_map/ppermute | solution.py:20
  64.1 52.5 %all-to-all-start.1 = ((f32[8,256,256]{2,1,0:T(8,128)}), f32[8,256,256]{2,1,0:T(8,128)S(1)}, u32[]{:S(2)}, u32[]{:S(2)}) async-start(f32[8,256,256]{2,1,0:T(8,128)} %combine.3), calls=%async_computation.1 | async-start | bytes 4194304 | tf_op jit(solution)/shard_map/all_to_all | solution.py:24
  69.8 1.4 copy-start.6
  69.8 1.4 copy-start.7
  69.8 1.4 copy-start.8
  71.2 1.3 copy-start.4
  71.2 1.3 copy-start.5
  78.8 45.9 %collective-permute-start = (f32[2048,256]{1,0:T(8,128)}, f32[2048,256]{1,0:T(8,128)}, u32[]{:S(2)}, u32[]{:S(2)}) collective-permute-start(f32[2048,256]{1,0:T(8,128)} %bitcast.refs_2_), channel_id=1, source_target_pairs={{0,16},{8,24},{16,0},{24,8},{1,17},{9,25},{17,1},{25,9},{2,18},{10... | collective-permute-start | bytes 6291464 | tf_op jit(solution)/shard_map/ppermute | solution.py:20
  116.6 8.1 %collective-permute-start.5 = (f32[2048,256]{1,0:T(8,128)S(1)}, f32[2048,256]{1,0:T(8,128)}, u32[]{:S(2)}, u32[]{:S(2)}) collective-permute-start(f32[2048,256]{1,0:T(8,128)S(1)} %bitcast.29), channel_id=1, source_target_pairs={{0,8},{8,0},{16,24},{24,16},{1,9},{9,1},{17,25},{25,17},{2,10},{10... | collective-permute-start | bytes 6291464 | tf_op jit(solution)/shard_map/ppermute | solution.py:20
  116.6 17.4 %collective-permute-start.2 = (f32[2048,256]{1,0:T(8,128)}, f32[2048,256]{1,0:T(8,128)}, u32[]{:S(2)}, u32[]{:S(2)}) collective-permute-start(f32[2048,256]{1,0:T(8,128)} %bitcast.refs_2_), channel_id=1, source_target_pairs={{0,8},{8,0},{16,24},{24,16},{1,9},{9,1},{17,25},{25,17},{2,10},{10... | collective-permute-start | bytes 6291464 | tf_op jit(solution)/shard_map/ppermute | solution.py:20
  124.7 9.3 %collective-permute-start.1 = (f32[2048,256]{1,0:T(8,128)}, f32[2048,256]{1,0:T(8,128)}, u32[]{:S(2)}, u32[]{:S(2)}) collective-permute-start(f32[2048,256]{1,0:T(8,128)} %collective-permute-done.refs_0_), channel_id=1, source_target_pairs={{0,8},{8,0},{16,24},{24,16},{1,9},{9,1},{17,25},{25,17},{2,10},{10... | collective-permute-start | bytes 6291464 | tf_op jit(solution)/shard_map/ppermute | solution.py:20
  124.7 1.6 copy-start
  126.3 7.7 %copy-start.1 = (f32[2,8,256,128]{3,2,1,0:T(8,128)S(1)}, f32[2,8,256,128]{3,2,1,0:T(8,128)}, u32[]{:S(2)}) copy-start(f32[2,8,256,128]{3,2,1,0:T(8,128)} %pad_maximum_fusion.refs_5_.refs_3_) | copy-start | bytes 6291460
  134.0 10.8 %copy-start.2 = (bf16[2,512,512]{2,1,0:T(8,128)(2,1)S(1)}, bf16[2,512,512]{2,1,0:T(8,128)(2,1)}, u32[]{:S(2)}) copy-start(bf16[2,512,512]{2,1,0:T(8,128)(2,1)} %pad_maximum_fusion.3.refs_4_) | copy-start | bytes 3145732
  134.0 10.8 %copy-start.3 = (bf16[2,512,512]{2,1,0:T(8,128)(2,1)S(1)}, bf16[2,512,512]{2,1,0:T(8,128)(2,1)}, u32[]{:S(2)}) copy-start(bf16[2,512,512]{2,1,0:T(8,128)(2,1)} %pad_maximum_fusion.5.refs_5_) | copy-start | bytes 3145732

commit v18 on v16

--- a/solution.py
+++ b/solution.py
@@ -123,7 +123,7 @@
     inputs, (table_ref, twist_ref, *out_refs, mix_ref, split_ref, step_ref) = refs[:count], refs[count:]
     length = mix_ref.shape[1]
     inner = length // RADIX
-    rows_each = 128
+    rows_each = 32
     for start in range(0, length, rows_each):
         rows = pl.ds(start, rows_each)
         for which in range(2):
@@ -140,9 +140,10 @@
     def split(tile):
         for which in range(2):
             for s in range(RADIX):
-                parts = split_value(mix_ref[2 * tile + which, pl.ds(s, inner, stride=RADIX), :])
-                for place, value in enumerate(parts):
-                    split_ref[tile, place, pl.ds(which * inner, inner), pl.ds(s * LANES, LANES)] = value
+                for start in range(0, inner, 64):
+                    parts = split_value(mix_ref[2 * tile + which, pl.ds(s + start * RADIX, 64, stride=RADIX), :])
+                    for place, value in enumerate(parts):
+                        split_ref[tile, place, pl.ds(which * inner + start, 64), pl.ds(s * LANES, LANES)] = value
 
     def multiply(tile, part):
         table = [table_ref[place, pl.ds(part * inner, inner), :] for place in (0, 1, 0)]
@@ -220,9 +221,8 @@
             for side, table_ref in zip(sides, (even_ref, odd_ref))
         ]
 
-    def finish(start, tile, even, odd):
-        rows = pl.ds(start, rows_each)
-        row_scale, row_rate = [
+    def row_factors(start):
+        return [
             jnp.concatenate(
                 [
                     jnp.broadcast_to(row_ref[which, 0, c : c + 1, :], (lanes, lanes)).T
@@ -232,28 +232,36 @@
             )
             for which in range(2)
         ]
+
+    def finish(start, tile, factors, even, odd):
         for upper in range(2):
             cols = pl.ds(upper * columns // 2 + tile * lanes, lanes)
-            spec = even - odd if upper else even + odd
             col_scale, col_shift, col_mix = col_ref[0:1, cols], col_ref[1:2, cols], col_ref[2:3, cols]
-            scale = row_scale * col_scale
-            latent_u = spec[:, :lanes] * scale
-            latent_v = spec[:, lanes:] * scale
-            log_scale = row_rate * jnp.tanh(latent_u + col_shift)
-            latent_w = latent_v * jnp.exp(log_scale) + col_mix * latent_u
-            out_ref[0, 0, rows, cols] = latent_u
-            out_ref[1, 0, rows, cols] = latent_w
-            terms = log_scale - 0.5 * (latent_u * latent_u + latent_w * latent_w)
-            totals.append(jnp.sum(terms.reshape(-1, 8, lanes), axis=0))
+            total = None
+            for first in range(0, rows_each, 32):
+                rows, span = pl.ds(start + first, 32), slice(first, first + 32)
+                spec = even[span] - odd[span] if upper else even[span] + odd[span]
+                scale = factors[0][span] * col_scale
+                latent_u = spec[:, :lanes] * scale
+                latent_v = spec[:, lanes:] * scale
+                log_scale = factors[1][span] * jnp.tanh(latent_u + col_shift)
+                latent_w = latent_v * jnp.exp(log_scale) + col_mix * latent_u
+                out_ref[0, 0, rows, cols] = latent_u
+                out_ref[1, 0, rows, cols] = latent_w
+                terms = log_scale - 0.5 * (latent_u * latent_u + latent_w * latent_w)
+                terms = jnp.sum(terms.reshape(-1, 8, lanes), axis=0)
+                total = terms if total is None else total + terms
+            totals.append(total)
 
     before = None
     for start in range(0, out_ref.shape[2], rows_each):
         sides = [left(group, start) for group in (parts[:count], parts[count:])]
+        factors = row_factors(start)
         for tile in range(tiles):
             products = multiply(sides, tile)
             if before is not None:
                 finish(*before)
-            before = (start, tile, *products)
+            before = (start, tile, factors, *products)
     finish(*before)
 
     @pl.when(pl.program_id(0) == 0)

time: 161 us -> 161 us (level)
  no operation moved by 1% of the time
where the time goes in v18:
time: 161 us
  waiting for transfers between devices  69.2 us (43%)
  Pallas kernels  32 us (20%)
  other arithmetic  21.4 us (13%)
  starting transfers between devices  15.7 us (10%)
  blocking collectives  13.3 us (8%)
  local copies, waits for them, and re-layouts  5.31 us (3%)
  between operations  4.02 us (2%)
    ppermute x6, waiting for transfers between devices, from_partner(): return lax.ppermute(value, axis, pairs)  63.9 us
    pallas_call x2, Pallas kernels, y_dft(): pl.pallas_call(functools.partial(y_kernel, len(inputs), pick), out_shape=...  18.2 us
    all_to_all x1, blocking collectives, sum_everywhere(): lax.all_to_all(copies, axes, split_axis=0, concat_axis=0, tiled=True)  13.3 us
    all_to_all x2, starting transfers between devices, to_planes(): return lax.all_to_all(values, 'gy', split_axis=0, concat_axis=1, tiled=True)  11 us
    pallas_call x1, Pallas kernels, x_dft(): pl.pallas_call(functools.partial(x_kernel, count), out_shape=(jax.ShapeDt...  9.72 us
    all_to_all x2, waiting for transfers between devices, to_planes(): return lax.all_to_all(values, 'gy', split_axis=0, concat_axis=1, tiled=True)  5.33 us
    sin x1, other arithmetic, root_table(): return (jnp.cos(angle), jnp.sin(angle))  5.16 us
    ppermute x6, starting transfers between devices, from_partner(): return lax.ppermute(value, axis, pairs)  4.7 us
  transfers between devices with their start and end apart: 8, of which 5 were waited for; matrix products, arithmetic and copies ran while one was open for 14% of the time, Pallas kernels for 9%

profile of v18, /device:TPU:0, one launch (start us, length us, event | category | flops | bytes accessed | tf_op | source)
XLA Modules:
  0.0 160.9 jit_solution(13443386295349185591)
XLA Ops:
  0.6 0.0 copy-start.4
  0.6 3.2 %slice.89 = f32[8,256,256]{2,1,0:T(8,128)} slice(f32[8,256,512]{2,1,0:T(8,128)} %param.6), slice={[0:8], [0:256], [256:512]} | slice | bytes 4194304 | tf_op jit(solution)/shard_map/slice | solution.py:317
  3.8 0.0 copy-done.4
  3.8 0.2 fusion.24
  4.1 3.0 %collective-permute-start = (f32[4,256,256]{2,1,0:T(8,128)S(1)}, f32[4,256,256]{2,1,0:T(8,128)S(1)}, u32[]{:S(2)}, u32[]{:S(2)}) collective-permute-start(f32[4,256,256]{2,1,0:T(8,128)S(1)} %get-tuple-element.41.early_ref), channel_id=1, source_target_pairs={{0,16},{8,24},{16,0},{24,8},{1,17},{9,25},{17,1},{25,9},{2,18},{10... | collective-permute-start | bytes 3145736 | tf_op jit(solution)/shard_map/ppermute | solution.py:20
  7.1 0.1 collective-permute-start.1
  7.2 6.2 %all-to-all-start = ((f32[8,256,256]{2,1,0:T(8,128)}), f32[8,256,256]{2,1,0:T(8,128)}, u32[]{:S(2)}, u32[]{:S(2)}) async-start(f32[8,256,256]{2,1,0:T(8,128)} %slice.89), calls=%async_computation | async-start | bytes 4194304 | tf_op jit(solution)/shard_map/all_to_all | solution.py:24
  13.5 1.1 fusion.23
  14.6 0.1 maximum_maximum_fusion
  14.7 1.2 reduce-precision_convert_fusion.2
  15.9 5.2 %fusion.14 = (f32[256,512]{1,0:T(8,128)}, f32[256,512]{1,0:T(8,128)}, f32[256,512]{1,0:T(8,128)S(1)}, f32[256,512]{1,0:T(8,128)S(1)}) fusion(s32[512]{0:T(512)S(1)} %multiply_add_fusion, s32[256]{0:T(256)S(1)} %pad_add_fusion.1, s32[256]{0:T(256)S(1)} %pad_add_fusion), kind=kLoop, calls=%fused_computation.55 | loop fusion | flops 3670016 | bytes 2101248 | tf_op jit(solution)/shard_map/sin | solution.py:77
  21.1 0.8 copy-done.6
  21.9 0.7 fusion.28
  22.6 0.7 log_reduce_fusion
  23.3 0.1 pad_maximum_fusion.13
  23.4 0.1 reshape.444.coef_ref
  23.4 0.6 log_reduce_fusion.1
  24.1 2.3 %pad_maximum_fusion.1.refs_4_.refs_2_ = bf16[2,512,512]{2,1,0:T(8,128)(2,1)} fusion(bf16[1,512,512]{2,1,0:T(8,128)(2,1)} %get-tuple-element.47, bf16[1,512,512]{2,1,0:T(8,128)(2,1)} %get-tuple-element.46), kind=kLoop, calls=%fused_computation.11 | loop fusion | flops 524288 | bytes 2097152 | tf_op jit(solution)/shard_map/stack | solution.py:89
  26.4 0.1 pad_maximum_fusion.12.coef_ref
  27.7 1.0 slice_negate_fusion.1
  28.7 1.2 pad_maximum_fusion.6
  30.0 0.2 reduce-precision_convert_fusion.1
  30.2 1.1 pad_maximum_fusion.3.refs_4_
  31.4 0.1 pad_maximum_fusion.8
  31.6 0.2 reduce-precision_convert_fusion
  31.7 1.1 pad_maximum_fusion.5.refs_5_
  32.8 3.2 %fusion.3 = (f32[1,8,256,128]{3,2,1,0:T(8,128)S(1)}, f32[1,8,256,128]{3,2,1,0:T(8,128)S(1)}) fusion(), kind=kLoop, calls=%fused_computation.17 | loop fusion | flops 786432 | bytes 2097152 | tf_op jit(solution)/shard_map/sin | solution.py:336
  36.0 1.5 pad_maximum_fusion.refs_5_.refs_3_
  37.6 15.3 %collective-permute-done.1.late_ref = f32[4,256,256]{2,1,0:T(8,128)} collective-permute-done((f32[4,256,256]{2,1,0:T(8,128)S(1)}, f32[4,256,256]{2,1,0:T(8,128)}, u32[]{:S(2)}, u32[]{:S(2)}) %collective-permute-start.1) | collective-permute-done | bytes 1048608 | tf_op jit(solution)/shard_map/ppermute | solution.py:20
  52.9 2.6 %combine.2.refs_0_ = f32[8,256,256]{2,1,0:T(8,128)} custom-call(f32[1]{0:T(128)} %bitcast.sign_ref, f32[4,256,256]{2,1,0:T(8,128)} %collective-permute-done.1.late_ref, f32[4,256,256]{2,1,0:T(8,128)S(1)} %get-tuple-element.40.early_ref), custom_call_target="tpu_custom_call" | custom-call | flops 524288 | bytes 3145728 | tf_op jit(solution)/shard_map/combine/pallas_call | solution.py:50
  55.4 0.0 collective-permute-done.late_ref
  55.4 1.5 combine.3
  56.9 4.3 %all-to-all-done = f32[8,256,256]{2,1,0:T(8,128)} async-done(((f32[8,256,256]{2,1,0:T(8,128)}), f32[8,256,256]{2,1,0:T(8,128)}, u32[]{:S(2)}, u32[]{:S(2)}) %all-to-all-start) | async-done | bytes 2097184 | tf_op jit(solution)/shard_map/all_to_all | solution.py:24
  61.2 4.8 %all-to-all-start.1 = ((f32[8,256,256]{2,1,0:T(8,128)}), f32[8,256,256]{2,1,0:T(8,128)}, u32[]{:S(2)}, u32[]{:S(2)}) async-start(f32[8,256,256]{2,1,0:T(8,128)} %combine.3), calls=%async_computation.1 | async-start | bytes 4194304 | tf_op jit(solution)/shard_map/all_to_all | solution.py:24
  66.0 1.6 collective-permute-start.2
  67.6 0.0 collective-permute-start.4
  67.6 45.1 %collective-permute-done.2.refs_0_ = f32[2048,256]{1,0:T(8,128)} collective-permute-done((f32[2048,256]{1,0:T(8,128)}, f32[2048,256]{1,0:T(8,128)}, u32[]{:S(2)}, u32[]{:S(2)}) %collective-permute-start.2) | collective-permute-done | bytes 2097184 | tf_op jit(solution)/shard_map/ppermute | solution.py:20
  112.7 0.0 collective-permute-start.3
  112.7 1.0 all-to-all-done.1
  113.8 0.0 collective-permute-start.5
  113.8 0.0 collective-permute-done.4.refs_3_
  113.8 3.5 %collective-permute-done.3.refs_1_ = f32[2048,256]{1,0:T(8,128)} collective-permute-done((f32[2048,256]{1,0:T(8,128)}, f32[2048,256]{1,0:T(8,128)}, u32[]{:S(2)}, u32[]{:S(2)}) %collective-permute-start.3) | collective-permute-done | bytes 2097184 | tf_op jit(solution)/shard_map/ppermute | solution.py:20
  117.2 10.2 %y_dft.2 = (bf16[4,2048,128]{2,1,0:T(8,128)(2,1)S(1)}, bf16[4,2048,128]{2,1,0:T(8,128)(2,1)S(1)}) custom-call(f32[2,4]{1,0:T(2,128)S(1)} %pad_maximum_fusion.12.coef_ref, f32[2048,256]{1,0:T(8,128)} %collective-permute-done.2.refs_0_, f32[2048,256]{1,0:T(8,128)} %collective-permute-done.3.refs_1_, f32[2048,256]{1,0:T(8,128)} %bitcast.1.refs_2_, ...), custom_call_target="tpu_custom_call" | custom-call | flops 10737418240 | bytes 14680064 | tf_op jit(solution)/shard_map/y_dft/pallas_call | solution.py:187
  127.4 0.0 collective-permute-done.5.refs_1_
  127.4 8.0 %y_dft.3 = (bf16[4,2048,128]{2,1,0:T(8,128)(2,1)S(1)}, bf16[4,2048,128]{2,1,0:T(8,128)(2,1)S(1)}) custom-call(f32[2,2]{1,0:T(2,128)S(1)} %reshape.444.coef_ref, f32[2048,256]{1,0:T(8,128)} %bitcast.20.refs_0_, f32[2048,256]{1,0:T(8,128)} %collective-permute-done.5.refs_1_, bf16[2,512,512]{2,1,0:T(8,128)(2,1)S(1)} %copy-done.1, f32[2,8,256,128]{3,2,1,0:T(8,128)S(1)} %copy-done), custom_call_target="tpu_custom_call" | custom-call | flops 10737418240 | bytes 10485760 | tf_op jit(solution)/shard_map/y_dft/pallas_call | solution.py:187
  135.5 9.7 %x_dft.1 = (f32[2,1,2048,512]{3,2,1,0:T(8,128)}, f32[8,128]{1,0:T(8,128)S(1)}) custom-call(bf16[4,2048,128]{2,1,0:T(8,128)(2,1)S(1)} %get-tuple-element.27.refs_0_, bf16[4,2048,128]{2,1,0:T(8,128)(2,1)S(1)} %get-tuple-element.30.refs_1_, bf16[4,2048,128]{2,1,0:T(8,128)(2,1)S(1)} %get-tuple-element.31.refs_2_, ...), custom_call_target="tpu_custom_call" | custom-call | flops 6442450944 | bytes 16777216 | tf_op jit(solution)/shard_map/x_dft/pallas_call | solution.py:279
  145.2 13.3 %all_to_all.23 = f32[32,8,128]{2,1,0:T(8,128)S(1)} all-to-all(f32[32,8,128]{2,1,0:T(8,128)S(1)} %broadcast_in_dim.2), channel_id=1, replica_groups=mesh['gx'=4,'gy'=8] {'gx','gy'}, dimensions={0} | all-to-all | bytes 262144 | tf_op jit(solution)/shard_map/all_to_all | solution.py:309
  158.5 0.6 reduce_sum.29
  (44 shorter events, 0.4 us)
Async XLA Ops:
  0.6 3.2 %copy-start.4 = (f32[8,256,512]{2,1,0:T(8,128)S(1)}, f32[8,256,512]{2,1,0:T(8,128)}, u32[]{:S(2)}) copy-start(f32[8,256,512]{2,1,0:T(8,128)} %param.6) | copy-start | bytes 12582916
  4.1 51.3 %collective-permute-start = (f32[4,256,256]{2,1,0:T(8,128)S(1)}, f32[4,256,256]{2,1,0:T(8,128)S(1)}, u32[]{:S(2)}, u32[]{:S(2)}) collective-permute-start(f32[4,256,256]{2,1,0:T(8,128)S(1)} %get-tuple-element.41.early_ref), channel_id=1, source_target_pairs={{0,16},{8,24},{16,0},{24,8},{1,17},{9,25},{17,1},{25,9},{2,18},{10... | collective-permute-start | bytes 3145736 | tf_op jit(solution)/shard_map/ppermute | solution.py:20
  7.1 45.7 %collective-permute-start.1 = (f32[4,256,256]{2,1,0:T(8,128)S(1)}, f32[4,256,256]{2,1,0:T(8,128)}, u32[]{:S(2)}, u32[]{:S(2)}) collective-permute-start(f32[4,256,256]{2,1,0:T(8,128)S(1)} %get-tuple-element.40.early_ref), channel_id=1, source_target_pairs={{0,16},{8,24},{16,0},{24,8},{1,17},{9,25},{17,1},{25,9},{2,18},{10... | collective-permute-start | bytes 3145736 | tf_op jit(solution)/shard_map/ppermute | solution.py:20
  7.2 54.0 %all-to-all-start = ((f32[8,256,256]{2,1,0:T(8,128)}), f32[8,256,256]{2,1,0:T(8,128)}, u32[]{:S(2)}, u32[]{:S(2)}) async-start(f32[8,256,256]{2,1,0:T(8,128)} %slice.89), calls=%async_computation | async-start | bytes 4194304 | tf_op jit(solution)/shard_map/all_to_all | solution.py:24
  15.9 6.7 %copy-start.9 = (f32[2048]{0:T(1024)S(1)}, f32[2048]{0:T(1024)}, u32[]{:S(2)}) copy-start(f32[2048]{0:T(1024)} %param.7) | copy-start | bytes 24580
  15.9 7.5 %copy-start.8 = (f32[512]{0:T(512)S(1)}, f32[512]{0:T(512)}, u32[]{:S(2)}) copy-start(f32[512]{0:T(512)} %param.8) | copy-start | bytes 6148
  21.1 0.8 copy-start.6
  21.1 5.2 %copy-start.11 = (f32[512]{0:T(512)S(1)}, f32[512]{0:T(512)}, u32[]{:S(2)}) copy-start(f32[512]{0:T(512)} %param.11) | copy-start | bytes 6148
  21.1 5.2 %copy-start.12 = (f32[512]{0:T(512)S(1)}, f32[512]{0:T(512)}, u32[]{:S(2)}) copy-start(f32[512]{0:T(512)} %param.10) | copy-start | bytes 6148
  21.1 6.6 %copy-start.10 = (f32[2048]{0:T(1024)S(1)}, f32[2048]{0:T(1024)}, u32[]{:S(2)}) copy-start(f32[2048]{0:T(1024)} %param.9) | copy-start | bytes 24580
  30.0 1.2 copy-start.5
  30.0 1.3 copy-start.7
  61.2 56.0 %copy-start = (f32[2,8,256,128]{3,2,1,0:T(8,128)S(1)}, f32[2,8,256,128]{3,2,1,0:T(8,128)}, u32[]{:S(2)}) copy-start(f32[2,8,256,128]{3,2,1,0:T(8,128)} %pad_maximum_fusion.refs_5_.refs_3_) | copy-start | bytes 6291460
  61.2 56.0 %copy-start.1 = (bf16[2,512,512]{2,1,0:T(8,128)(2,1)S(1)}, bf16[2,512,512]{2,1,0:T(8,128)(2,1)}, u32[]{:S(2)}) copy-start(bf16[2,512,512]{2,1,0:T(8,128)(2,1)} %pad_maximum_fusion.1.refs_4_.refs_2_) | copy-start | bytes 3145732
  61.2 52.5 %all-to-all-start.1 = ((f32[8,256,256]{2,1,0:T(8,128)}), f32[8,256,256]{2,1,0:T(8,128)}, u32[]{:S(2)}, u32[]{:S(2)}) async-start(f32[8,256,256]{2,1,0:T(8,128)} %combine.3), calls=%async_computation.1 | async-start | bytes 4194304 | tf_op jit(solution)/shard_map/all_to_all | solution.py:24
  66.0 46.7 %collective-permute-start.2 = (f32[2048,256]{1,0:T(8,128)}, f32[2048,256]{1,0:T(8,128)}, u32[]{:S(2)}, u32[]{:S(2)}) collective-permute-start(f32[2048,256]{1,0:T(8,128)} %bitcast.1.refs_2_), channel_id=1, source_target_pairs={{0,16},{8,24},{16,0},{24,8},{1,17},{9,25},{17,1},{25,9},{2,18},{10... | collective-permute-start | bytes 6291464 | tf_op jit(solution)/shard_map/ppermute | solution.py:20
  67.6 46.1 %collective-permute-start.4 = (f32[2048,256]{1,0:T(8,128)}, f32[2048,256]{1,0:T(8,128)}, u32[]{:S(2)}, u32[]{:S(2)}) collective-permute-start(f32[2048,256]{1,0:T(8,128)} %bitcast.1.refs_2_), channel_id=1, source_target_pairs={{0,8},{8,0},{16,24},{24,16},{1,9},{9,1},{17,25},{25,17},{2,10},{10... | collective-permute-start | bytes 6291464 | tf_op jit(solution)/shard_map/ppermute | solution.py:20
  112.7 4.5 %collective-permute-start.3 = (f32[2048,256]{1,0:T(8,128)}, f32[2048,256]{1,0:T(8,128)}, u32[]{:S(2)}, u32[]{:S(2)}) collective-permute-start(f32[2048,256]{1,0:T(8,128)} %collective-permute-done.2.refs_0_), channel_id=1, source_target_pairs={{0,8},{8,0},{16,24},{24,16},{1,9},{9,1},{17,25},{25,17},{2,10},{10... | collective-permute-start | bytes 6291464 | tf_op jit(solution)/shard_map/ppermute | solution.py:20
  113.8 13.7 %collective-permute-start.5 = (f32[2048,256]{1,0:T(8,128)}, f32[2048,256]{1,0:T(8,128)}, u32[]{:S(2)}, u32[]{:S(2)}) collective-permute-start(f32[2048,256]{1,0:T(8,128)} %bitcast.20.refs_0_), channel_id=1, source_target_pairs={{0,8},{8,0},{16,24},{24,16},{1,9},{9,1},{17,25},{25,17},{2,10},{10... | collective-permute-start | bytes 6291464 | tf_op jit(solution)/shard_map/ppermute | solution.py:20
  127.4 8.1 %copy-start.2 = (bf16[2,512,512]{2,1,0:T(8,128)(2,1)S(1)}, bf16[2,512,512]{2,1,0:T(8,128)(2,1)}, u32[]{:S(2)}) copy-start(bf16[2,512,512]{2,1,0:T(8,128)(2,1)} %pad_maximum_fusion.3.refs_4_) | copy-start | bytes 3145732
  127.4 8.1 %copy-start.3 = (bf16[2,512,512]{2,1,0:T(8,128)(2,1)S(1)}, bf16[2,512,512]{2,1,0:T(8,128)(2,1)}, u32[]{:S(2)}) copy-start(bf16[2,512,512]{2,1,0:T(8,128)(2,1)} %pad_maximum_fusion.5.refs_5_) | copy-start | bytes 3145732

commit v19 on v18

--- a/solution.py
+++ b/solution.py
@@ -120,18 +120,31 @@
 
 
 def y_kernel(count, pick, coef_ref, *refs):
-    inputs, (table_ref, twist_ref, *out_refs, mix_ref, split_ref, step_ref) = refs[:count], refs[count:]
+    sources, (table_ref, twist_ref, *out_refs, in_ref, mix_ref, split_ref, step_ref, sems) = refs[:count], refs[count:]
     length = mix_ref.shape[1]
     inner = length // RADIX
-    rows_each = 32
+    chunks, rows_each = sems.shape[0], 32
+    copies = []
+    for chunk in range(chunks):
+        rows = pl.ds(chunk * length // chunks, length // chunks)
+        copies.append([
+            pltpu.make_async_copy(source.at[rows, :], in_ref.at[place, rows, :], sems.at[chunk, place])
+            for place, source in enumerate(sources)
+        ])
+    for group in copies:
+        for copy in group:
+            copy.start()
     for start in range(0, length, rows_each):
+        if start % (length // chunks) == 0:
+            for copy in copies[start * chunks // length]:
+                copy.wait()
         rows = pl.ds(start, rows_each)
         for which in range(2):
             tiles = []
             for lane in (0, LANES):
-                mixed = inputs[0][rows, pl.ds(lane, LANES)] * coef_ref[which, 0]
+                mixed = in_ref[0, rows, pl.ds(lane, LANES)] * coef_ref[which, 0]
                 for place in range(1, count):
-                    mixed = mixed + inputs[place][rows, pl.ds(lane, LANES)] * coef_ref[which, place]
+                    mixed = mixed + in_ref[place, rows, pl.ds(lane, LANES)] * coef_ref[which, place]
                 tiles.append(mixed)
             for tile in range(2):
                 mix_ref[2 * tile + which, rows, :] = pick_columns(*tiles, tile) if pick else tiles[tile]
@@ -183,16 +196,18 @@
 def y_dft(inputs, pick, coefs, table, twist):
     length = inputs[0].shape[0]
     inner = length // RADIX
-    whole = pl.BlockSpec(memory_space=pltpu.VMEM)
+    whole, anywhere = pl.BlockSpec(memory_space=pltpu.VMEM), pl.BlockSpec(memory_space=pl.ANY)
     return pl.pallas_call(
         functools.partial(y_kernel, len(inputs), pick),
         out_shape=[jax.ShapeDtypeStruct((4, length, LANES), jnp.bfloat16)] * 2,
-        in_specs=[pl.BlockSpec(memory_space=pltpu.SMEM)] + [whole] * (len(inputs) + 2),
+        in_specs=[pl.BlockSpec(memory_space=pltpu.SMEM)] + [anywhere] * len(inputs) + [whole] * 2,
         out_specs=[whole] * 2,
         scratch_shapes=[
+            pltpu.VMEM((len(inputs), length, 2 * LANES), jnp.float32),
             pltpu.VMEM((4, length, LANES), jnp.float32),
             pltpu.VMEM((2, 2, 2 * inner, RADIX * LANES), jnp.bfloat16),
             pltpu.VMEM((2, inner, RADIX * LANES), jnp.float32),
+            pltpu.SemaphoreType.DMA((4, len(inputs))),
         ],
         compiler_params=pltpu.CompilerParams(vmem_limit_bytes=Y_BYTES),
         cost_estimate=pl.CostEstimate(

time: 161 us -> 162 us (level)
  no operation moved by 1% of the time
where the time goes in v19:
time: 162 us; the launch traced here: 161 us
  waiting for transfers between devices  69.2 us (43%)
  Pallas kernels  32.3 us (20%)
  other arithmetic  21.4 us (13%)
  starting transfers between devices  15.7 us (10%)
  blocking collectives  13.3 us (8%)
  local copies, waits for them, and re-layouts  5.31 us (3%)
  between operations  4.02 us (2%)
    ppermute x6, waiting for transfers between devices, from_partner(): return lax.ppermute(value, axis, pairs)  63.9 us
    pallas_call x2, Pallas kernels, y_dft(): pl.pallas_call(functools.partial(y_kernel, len(inputs), pick), out_shape=...  18.5 us
    all_to_all x1, blocking collectives, sum_everywhere(): lax.all_to_all(copies, axes, split_axis=0, concat_axis=0, tiled=True)  13.3 us
    all_to_all x2, starting transfers between devices, to_planes(): return lax.all_to_all(values, 'gy', split_axis=0, concat_axis=1, tiled=True)  11 us
    pallas_call x1, Pallas kernels, x_dft(): pl.pallas_call(functools.partial(x_kernel, count), out_shape=(jax.ShapeDt...  9.72 us
    all_to_all x2, waiting for transfers between devices, to_planes(): return lax.all_to_all(values, 'gy', split_axis=0, concat_axis=1, tiled=True)  5.24 us
    sin x1, other arithmetic, root_table(): return (jnp.cos(angle), jnp.sin(angle))  5.16 us
    ppermute x6, starting transfers between devices, from_partner(): return lax.ppermute(value, axis, pairs)  4.7 us
  transfers between devices with their start and end apart: 8, of which 5 were waited for; matrix products, arithmetic and copies ran while one was open for 14% of the time, Pallas kernels for 9%

profile of v19, /device:TPU:0, one launch (start us, length us, event | category | flops | bytes accessed | tf_op | source)
XLA Modules:
  0.0 161.2 jit_solution(8484321939369222106)
XLA Ops:
  0.6 0.0 copy-start.4
  0.6 3.2 %slice.89 = f32[8,256,256]{2,1,0:T(8,128)} slice(f32[8,256,512]{2,1,0:T(8,128)} %param.6), slice={[0:8], [0:256], [256:512]} | slice | bytes 4194304 | tf_op jit(solution)/shard_map/slice | solution.py:332
  3.8 0.0 copy-done.4
  3.8 0.2 fusion.24
  4.1 3.0 %collective-permute-start = (f32[4,256,256]{2,1,0:T(8,128)S(1)}, f32[4,256,256]{2,1,0:T(8,128)S(1)}, u32[]{:S(2)}, u32[]{:S(2)}) collective-permute-start(f32[4,256,256]{2,1,0:T(8,128)S(1)} %get-tuple-element.41.early_ref), channel_id=1, source_target_pairs={{0,16},{8,24},{16,0},{24,8},{1,17},{9,25},{17,1},{25,9},{2,18},{10... | collective-permute-start | bytes 3145736 | tf_op jit(solution)/shard_map/ppermute | solution.py:20
  7.1 0.1 collective-permute-start.1
  7.2 6.2 %all-to-all-start = ((f32[8,256,256]{2,1,0:T(8,128)}), f32[8,256,256]{2,1,0:T(8,128)}, u32[]{:S(2)}, u32[]{:S(2)}) async-start(f32[8,256,256]{2,1,0:T(8,128)} %slice.89), calls=%async_computation | async-start | bytes 4194304 | tf_op jit(solution)/shard_map/all_to_all | solution.py:24
  13.5 1.1 fusion.23
  14.6 0.1 maximum_maximum_fusion
  14.7 1.2 reduce-precision_convert_fusion.2
  15.9 5.2 %fusion.14 = (f32[256,512]{1,0:T(8,128)}, f32[256,512]{1,0:T(8,128)}, f32[256,512]{1,0:T(8,128)S(1)}, f32[256,512]{1,0:T(8,128)S(1)}) fusion(s32[512]{0:T(512)S(1)} %multiply_add_fusion, s32[256]{0:T(256)S(1)} %pad_add_fusion.1, s32[256]{0:T(256)S(1)} %pad_add_fusion), kind=kLoop, calls=%fused_computation.55 | loop fusion | flops 3670016 | bytes 2101248 | tf_op jit(solution)/shard_map/sin | solution.py:77
  21.1 0.8 copy-done.6
  21.9 0.7 fusion.28
  22.6 0.7 log_reduce_fusion
  23.3 0.1 pad_maximum_fusion.13
  23.4 0.1 reshape.444.coef_ref
  23.4 0.6 log_reduce_fusion.1
  24.1 2.3 %pad_maximum_fusion.1.refs_4_.refs_2_ = bf16[2,512,512]{2,1,0:T(8,128)(2,1)} fusion(bf16[1,512,512]{2,1,0:T(8,128)(2,1)} %get-tuple-element.47, bf16[1,512,512]{2,1,0:T(8,128)(2,1)} %get-tuple-element.46), kind=kLoop, calls=%fused_computation.11 | loop fusion | flops 524288 | bytes 2097152 | tf_op jit(solution)/shard_map/stack | solution.py:89
  26.4 0.1 pad_maximum_fusion.12.coef_ref
  27.7 1.0 slice_negate_fusion.1
  28.7 1.2 pad_maximum_fusion.6
  30.0 0.2 reduce-precision_convert_fusion.1
  30.2 1.1 pad_maximum_fusion.3.refs_4_
  31.4 0.1 pad_maximum_fusion.8
  31.6 0.2 reduce-precision_convert_fusion
  31.7 1.1 pad_maximum_fusion.5.refs_5_
  32.8 3.2 %fusion.3 = (f32[1,8,256,128]{3,2,1,0:T(8,128)S(1)}, f32[1,8,256,128]{3,2,1,0:T(8,128)S(1)}) fusion(), kind=kLoop, calls=%fused_computation.17 | loop fusion | flops 786432 | bytes 2097152 | tf_op jit(solution)/shard_map/sin | solution.py:351
  36.0 1.5 pad_maximum_fusion.refs_5_.refs_3_
  37.6 15.3 %collective-permute-done.1.late_ref = f32[4,256,256]{2,1,0:T(8,128)} collective-permute-done((f32[4,256,256]{2,1,0:T(8,128)S(1)}, f32[4,256,256]{2,1,0:T(8,128)}, u32[]{:S(2)}, u32[]{:S(2)}) %collective-permute-start.1) | collective-permute-done | bytes 1048608 | tf_op jit(solution)/shard_map/ppermute | solution.py:20
  52.9 2.6 %combine.2.refs_0_ = f32[8,256,256]{2,1,0:T(8,128)} custom-call(f32[1]{0:T(128)} %bitcast.sign_ref, f32[4,256,256]{2,1,0:T(8,128)} %collective-permute-done.1.late_ref, f32[4,256,256]{2,1,0:T(8,128)S(1)} %get-tuple-element.40.early_ref), custom_call_target="tpu_custom_call" | custom-call | flops 524288 | bytes 3145728 | tf_op jit(solution)/shard_map/combine/pallas_call | solution.py:50
  55.4 0.0 collective-permute-done.late_ref
  55.4 1.5 combine.3
  56.9 4.3 %all-to-all-done = f32[8,256,256]{2,1,0:T(8,128)} async-done(((f32[8,256,256]{2,1,0:T(8,128)}), f32[8,256,256]{2,1,0:T(8,128)}, u32[]{:S(2)}, u32[]{:S(2)}) %all-to-all-start) | async-done | bytes 2097184 | tf_op jit(solution)/shard_map/all_to_all | solution.py:24
  61.2 4.8 %all-to-all-start.1 = ((f32[8,256,256]{2,1,0:T(8,128)}), f32[8,256,256]{2,1,0:T(8,128)}, u32[]{:S(2)}, u32[]{:S(2)}) async-start(f32[8,256,256]{2,1,0:T(8,128)} %combine.3), calls=%async_computation.1 | async-start | bytes 4194304 | tf_op jit(solution)/shard_map/all_to_all | solution.py:24
  66.0 1.6 collective-permute-start.2
  67.6 0.0 collective-permute-start.4
  67.6 45.1 %collective-permute-done.2.refs_0_ = f32[2048,256]{1,0:T(8,128)} collective-permute-done((f32[2048,256]{1,0:T(8,128)}, f32[2048,256]{1,0:T(8,128)}, u32[]{:S(2)}, u32[]{:S(2)}) %collective-permute-start.2) | collective-permute-done | bytes 2097184 | tf_op jit(solution)/shard_map/ppermute | solution.py:20
  112.7 0.0 collective-permute-start.3
  112.7 0.9 all-to-all-done.1
  113.7 0.0 collective-permute-start.5
  113.7 0.0 collective-permute-done.4.refs_3_
  113.7 3.5 %collective-permute-done.3.refs_1_ = f32[2048,256]{1,0:T(8,128)} collective-permute-done((f32[2048,256]{1,0:T(8,128)}, f32[2048,256]{1,0:T(8,128)}, u32[]{:S(2)}, u32[]{:S(2)}) %collective-permute-start.3) | collective-permute-done | bytes 2097184 | tf_op jit(solution)/shard_map/ppermute | solution.py:20
  117.2 10.2 %y_dft.2 = (bf16[4,2048,128]{2,1,0:T(8,128)(2,1)S(1)}, bf16[4,2048,128]{2,1,0:T(8,128)(2,1)S(1)}) custom-call(f32[2,4]{1,0:T(2,128)S(1)} %pad_maximum_fusion.12.coef_ref, f32[2048,256]{1,0:T(8,128)} %collective-permute-done.2.refs_0_, f32[2048,256]{1,0:T(8,128)} %collective-permute-done.3.refs_1_, f32[2048,256]{1,0:T(8,128)} %bitcast.1.refs_2_, ...), custom_call_target="tpu_custom_call" | custom-call | flops 10737418240 | bytes 14680064 | tf_op jit(solution)/shard_map/y_dft/pallas_call | solution.py:200
  127.4 0.0 collective-permute-done.5.refs_1_
  127.4 8.3 %y_dft.3 = (bf16[4,2048,128]{2,1,0:T(8,128)(2,1)S(1)}, bf16[4,2048,128]{2,1,0:T(8,128)(2,1)S(1)}) custom-call(f32[2,2]{1,0:T(2,128)S(1)} %reshape.444.coef_ref, f32[2048,256]{1,0:T(8,128)} %bitcast.20.refs_0_, f32[2048,256]{1,0:T(8,128)} %collective-permute-done.5.refs_1_, bf16[2,512,512]{2,1,0:T(8,128)(2,1)S(1)} %copy-done.1, f32[2,8,256,128]{3,2,1,0:T(8,128)S(1)} %copy-done), custom_call_target="tpu_custom_call" | custom-call | flops 10737418240 | bytes 10485760 | tf_op jit(solution)/shard_map/y_dft/pallas_call | solution.py:200
  135.8 9.7 %x_dft.1 = (f32[2,1,2048,512]{3,2,1,0:T(8,128)}, f32[8,128]{1,0:T(8,128)S(1)}) custom-call(bf16[4,2048,128]{2,1,0:T(8,128)(2,1)S(1)} %get-tuple-element.27.refs_0_, bf16[4,2048,128]{2,1,0:T(8,128)(2,1)S(1)} %get-tuple-element.30.refs_1_, bf16[4,2048,128]{2,1,0:T(8,128)(2,1)S(1)} %get-tuple-element.31.refs_2_, ...), custom_call_target="tpu_custom_call" | custom-call | flops 6442450944 | bytes 16777216 | tf_op jit(solution)/shard_map/x_dft/pallas_call | solution.py:294
  145.5 13.3 %all_to_all.23 = f32[32,8,128]{2,1,0:T(8,128)S(1)} all-to-all(f32[32,8,128]{2,1,0:T(8,128)S(1)} %broadcast_in_dim.2), channel_id=1, replica_groups=mesh['gx'=4,'gy'=8] {'gx','gy'}, dimensions={0} | all-to-all | bytes 262144 | tf_op jit(solution)/shard_map/all_to_all | solution.py:324
  158.8 0.6 reduce_sum.29
  (44 shorter events, 0.4 us)
Async XLA Ops:
  0.6 3.2 %copy-start.4 = (f32[8,256,512]{2,1,0:T(8,128)S(1)}, f32[8,256,512]{2,1,0:T(8,128)}, u32[]{:S(2)}) copy-start(f32[8,256,512]{2,1,0:T(8,128)} %param.6) | copy-start | bytes 12582916
  4.1 51.3 %collective-permute-start = (f32[4,256,256]{2,1,0:T(8,128)S(1)}, f32[4,256,256]{2,1,0:T(8,128)S(1)}, u32[]{:S(2)}, u32[]{:S(2)}) collective-permute-start(f32[4,256,256]{2,1,0:T(8,128)S(1)} %get-tuple-element.41.early_ref), channel_id=1, source_target_pairs={{0,16},{8,24},{16,0},{24,8},{1,17},{9,25},{17,1},{25,9},{2,18},{10... | collective-permute-start | bytes 3145736 | tf_op jit(solution)/shard_map/ppermute | solution.py:20
  7.1 45.7 %collective-permute-start.1 = (f32[4,256,256]{2,1,0:T(8,128)S(1)}, f32[4,256,256]{2,1,0:T(8,128)}, u32[]{:S(2)}, u32[]{:S(2)}) collective-permute-start(f32[4,256,256]{2,1,0:T(8,128)S(1)} %get-tuple-element.40.early_ref), channel_id=1, source_target_pairs={{0,16},{8,24},{16,0},{24,8},{1,17},{9,25},{17,1},{25,9},{2,18},{10... | collective-permute-start | bytes 3145736 | tf_op jit(solution)/shard_map/ppermute | solution.py:20
  7.2 54.0 %all-to-all-start = ((f32[8,256,256]{2,1,0:T(8,128)}), f32[8,256,256]{2,1,0:T(8,128)}, u32[]{:S(2)}, u32[]{:S(2)}) async-start(f32[8,256,256]{2,1,0:T(8,128)} %slice.89), calls=%async_computation | async-start | bytes 4194304 | tf_op jit(solution)/shard_map/all_to_all | solution.py:24
  15.9 6.7 %copy-start.9 = (f32[2048]{0:T(1024)S(1)}, f32[2048]{0:T(1024)}, u32[]{:S(2)}) copy-start(f32[2048]{0:T(1024)} %param.7) | copy-start | bytes 24580
  15.9 7.5 %copy-start.8 = (f32[512]{0:T(512)S(1)}, f32[512]{0:T(512)}, u32[]{:S(2)}) copy-start(f32[512]{0:T(512)} %param.8) | copy-start | bytes 6148
  21.1 0.8 copy-start.6
  21.1 5.2 %copy-start.11 = (f32[512]{0:T(512)S(1)}, f32[512]{0:T(512)}, u32[]{:S(2)}) copy-start(f32[512]{0:T(512)} %param.11) | copy-start | bytes 6148
  21.1 5.2 %copy-start.12 = (f32[512]{0:T(512)S(1)}, f32[512]{0:T(512)}, u32[]{:S(2)}) copy-start(f32[512]{0:T(512)} %param.10) | copy-start | bytes 6148
  21.1 6.6 %copy-start.10 = (f32[2048]{0:T(1024)S(1)}, f32[2048]{0:T(1024)}, u32[]{:S(2)}) copy-start(f32[2048]{0:T(1024)} %param.9) | copy-start | bytes 24580
  30.0 1.2 copy-start.5
  30.0 1.3 copy-start.7
  61.2 56.0 %copy-start = (f32[2,8,256,128]{3,2,1,0:T(8,128)S(1)}, f32[2,8,256,128]{3,2,1,0:T(8,128)}, u32[]{:S(2)}) copy-start(f32[2,8,256,128]{3,2,1,0:T(8,128)} %pad_maximum_fusion.refs_5_.refs_3_) | copy-start | bytes 6291460
  61.2 56.0 %copy-start.1 = (bf16[2,512,512]{2,1,0:T(8,128)(2,1)S(1)}, bf16[2,512,512]{2,1,0:T(8,128)(2,1)}, u32[]{:S(2)}) copy-start(bf16[2,512,512]{2,1,0:T(8,128)(2,1)} %pad_maximum_fusion.1.refs_4_.refs_2_) | copy-start | bytes 3145732
  61.2 52.4 %all-to-all-start.1 = ((f32[8,256,256]{2,1,0:T(8,128)}), f32[8,256,256]{2,1,0:T(8,128)}, u32[]{:S(2)}, u32[]{:S(2)}) async-start(f32[8,256,256]{2,1,0:T(8,128)} %combine.3), calls=%async_computation.1 | async-start | bytes 4194304 | tf_op jit(solution)/shard_map/all_to_all | solution.py:24
  66.0 46.7 %collective-permute-start.2 = (f32[2048,256]{1,0:T(8,128)}, f32[2048,256]{1,0:T(8,128)}, u32[]{:S(2)}, u32[]{:S(2)}) collective-permute-start(f32[2048,256]{1,0:T(8,128)} %bitcast.1.refs_2_), channel_id=1, source_target_pairs={{0,16},{8,24},{16,0},{24,8},{1,17},{9,25},{17,1},{25,9},{2,18},{10... | collective-permute-start | bytes 6291464 | tf_op jit(solution)/shard_map/ppermute | solution.py:20
  67.6 46.1 %collective-permute-start.4 = (f32[2048,256]{1,0:T(8,128)}, f32[2048,256]{1,0:T(8,128)}, u32[]{:S(2)}, u32[]{:S(2)}) collective-permute-start(f32[2048,256]{1,0:T(8,128)} %bitcast.1.refs_2_), channel_id=1, source_target_pairs={{0,8},{8,0},{16,24},{24,16},{1,9},{9,1},{17,25},{25,17},{2,10},{10... | collective-permute-start | bytes 6291464 | tf_op jit(solution)/shard_map/ppermute | solution.py:20
  112.7 4.5 %collective-permute-start.3 = (f32[2048,256]{1,0:T(8,128)}, f32[2048,256]{1,0:T(8,128)}, u32[]{:S(2)}, u32[]{:S(2)}) collective-permute-start(f32[2048,256]{1,0:T(8,128)} %collective-permute-done.2.refs_0_), channel_id=1, source_target_pairs={{0,8},{8,0},{16,24},{24,16},{1,9},{9,1},{17,25},{25,17},{2,10},{10... | collective-permute-start | bytes 6291464 | tf_op jit(solution)/shard_map/ppermute | solution.py:20
  113.7 13.7 %collective-permute-start.5 = (f32[2048,256]{1,0:T(8,128)}, f32[2048,256]{1,0:T(8,128)}, u32[]{:S(2)}, u32[]{:S(2)}) collective-permute-start(f32[2048,256]{1,0:T(8,128)} %bitcast.20.refs_0_), channel_id=1, source_target_pairs={{0,8},{8,0},{16,24},{24,16},{1,9},{9,1},{17,25},{25,17},{2,10},{10... | collective-permute-start | bytes 6291464 | tf_op jit(solution)/shard_map/ppermute | solution.py:20
  127.4 8.4 %copy-start.2 = (bf16[2,512,512]{2,1,0:T(8,128)(2,1)S(1)}, bf16[2,512,512]{2,1,0:T(8,128)(2,1)}, u32[]{:S(2)}) copy-start(bf16[2,512,512]{2,1,0:T(8,128)(2,1)} %pad_maximum_fusion.3.refs_4_) | copy-start | bytes 3145732
  127.4 8.4 %copy-start.3 = (bf16[2,512,512]{2,1,0:T(8,128)(2,1)S(1)}, bf16[2,512,512]{2,1,0:T(8,128)(2,1)}, u32[]{:S(2)}) copy-start(bf16[2,512,512]{2,1,0:T(8,128)(2,1)} %pad_maximum_fusion.5.refs_5_) | copy-start | bytes 3145732

commit v20 on v18

--- a/solution.py
+++ b/solution.py
@@ -359,7 +359,9 @@
     first_a, first_b, tables = lax.optimization_barrier((first_a, to_planes(field_b)[0], tables))
     y_table, twist, even_table, odd_table, row_pair, col_trio, coefs_a, coefs_b, fixed = tables
     second_a = to_planes(first_a)[0]
-    second_b = from_partner(first_b, "gx", 1)
+    late = (even_table, odd_table, row_pair, col_trio, fixed)
+    second_b, late = lax.optimization_barrier((from_partner(first_b, "gx", 1), late))
+    even_table, odd_table, row_pair, col_trio, fixed = late
     group = [second_b, from_partner(second_b, "gx", 0), first_b, from_partner(first_b, "gx", 0)]
     even_b, odd_b = y_dft(group, True, coefs_b, y_table, twist)
     even_a, odd_a = y_dft([second_a, from_partner(second_a, "gx", 0)], False, coefs_a, y_table, twist)

time: 161 us -> 161 us (level)
  no operation moved by 1% of the time
where the time goes in v20:
time: 161 us
  waiting for transfers between devices  69.2 us (43%)
  Pallas kernels  32 us (20%)
  other arithmetic  21.4 us (13%)
  starting transfers between devices  15.7 us (10%)
  blocking collectives  13.3 us (8%)
  local copies, waits for them, and re-layouts  5.31 us (3%)
  between operations  4.02 us (2%)
    ppermute x6, waiting for transfers between devices, from_partner(): return lax.ppermute(value, axis, pairs)  63.9 us
    pallas_call x2, Pallas kernels, y_dft(): pl.pallas_call(functools.partial(y_kernel, len(inputs), pick), out_shape=...  18.2 us
    all_to_all x1, blocking collectives, sum_everywhere(): lax.all_to_all(copies, axes, split_axis=0, concat_axis=0, tiled=True)  13.3 us
    all_to_all x2, starting transfers between devices, to_planes(): return lax.all_to_all(values, 'gy', split_axis=0, concat_axis=1, tiled=True)  11 us
    pallas_call x1, Pallas kernels, x_dft(): pl.pallas_call(functools.partial(x_kernel, count), out_shape=(jax.ShapeDt...  9.72 us
    all_to_all x2, waiting for transfers between devices, to_planes(): return lax.all_to_all(values, 'gy', split_axis=0, concat_axis=1, tiled=True)  5.33 us
    sin x1, other arithmetic, root_table(): return (jnp.cos(angle), jnp.sin(angle))  5.16 us
    ppermute x6, starting transfers between devices, from_partner(): return lax.ppermute(value, axis, pairs)  4.7 us
  transfers between devices with their start and end apart: 8, of which 5 were waited for; matrix products, arithmetic and copies ran while one was open for 14% of the time, Pallas kernels for 9%

profile of v20, /device:TPU:0, one launch (start us, length us, event | category | flops | bytes accessed | tf_op | source)
XLA Modules:
  0.0 160.9 jit_solution(13443386295349185591)
XLA Ops:
  0.6 0.0 copy-start.4
  0.6 3.2 %slice.89 = f32[8,256,256]{2,1,0:T(8,128)} slice(f32[8,256,512]{2,1,0:T(8,128)} %param.6), slice={[0:8], [0:256], [256:512]} | slice | bytes 4194304 | tf_op jit(solution)/shard_map/slice | solution.py:317
  3.8 0.0 copy-done.4
  3.8 0.2 fusion.24
  4.1 3.0 %collective-permute-start = (f32[4,256,256]{2,1,0:T(8,128)S(1)}, f32[4,256,256]{2,1,0:T(8,128)S(1)}, u32[]{:S(2)}, u32[]{:S(2)}) collective-permute-start(f32[4,256,256]{2,1,0:T(8,128)S(1)} %get-tuple-element.53.early_ref), channel_id=1, source_target_pairs={{0,16},{8,24},{16,0},{24,8},{1,17},{9,25},{17,1},{25,9},{2,18},{10... | collective-permute-start | bytes 3145736 | tf_op jit(solution)/shard_map/ppermute | solution.py:20
  7.1 0.1 collective-permute-start.1
  7.2 6.2 %all-to-all-start = ((f32[8,256,256]{2,1,0:T(8,128)}), f32[8,256,256]{2,1,0:T(8,128)}, u32[]{:S(2)}, u32[]{:S(2)}) async-start(f32[8,256,256]{2,1,0:T(8,128)} %slice.89), calls=%async_computation | async-start | bytes 4194304 | tf_op jit(solution)/shard_map/all_to_all | solution.py:24
  13.5 1.1 fusion.23
  14.6 0.1 maximum_maximum_fusion
  14.7 1.2 reduce-precision_convert_fusion.2
  15.9 5.2 %fusion.14 = (f32[256,512]{1,0:T(8,128)}, f32[256,512]{1,0:T(8,128)}, f32[256,512]{1,0:T(8,128)S(1)}, f32[256,512]{1,0:T(8,128)S(1)}) fusion(s32[512]{0:T(512)S(1)} %multiply_add_fusion, s32[256]{0:T(256)S(1)} %pad_add_fusion.1, s32[256]{0:T(256)S(1)} %pad_add_fusion), kind=kLoop, calls=%fused_computation.55 | loop fusion | flops 3670016 | bytes 2101248 | tf_op jit(solution)/shard_map/sin | solution.py:77
  21.1 0.8 copy-done.6
  21.9 0.7 fusion.28
  22.6 0.7 log_reduce_fusion
  23.3 0.1 pad_maximum_fusion.13
  23.4 0.1 reshape.444.coef_ref
  23.4 0.6 log_reduce_fusion.1
  24.1 2.3 %pad_maximum_fusion.1.refs_4_.refs_2_ = bf16[2,512,512]{2,1,0:T(8,128)(2,1)} fusion(bf16[1,512,512]{2,1,0:T(8,128)(2,1)} %get-tuple-element.59, bf16[1,512,512]{2,1,0:T(8,128)(2,1)} %get-tuple-element.58), kind=kLoop, calls=%fused_computation.11 | loop fusion | flops 524288 | bytes 2097152 | tf_op jit(solution)/shard_map/stack | solution.py:89
  26.4 0.1 pad_maximum_fusion.12.coef_ref
  27.7 1.0 slice_negate_fusion.1
  28.7 1.2 pad_maximum_fusion.6
  30.0 0.2 reduce-precision_convert_fusion.1
  30.2 1.1 pad_maximum_fusion.3.refs_4_
  31.4 0.1 pad_maximum_fusion.8
  31.6 0.2 reduce-precision_convert_fusion
  31.7 1.1 pad_maximum_fusion.5.refs_5_
  32.8 3.2 %fusion.3 = (f32[1,8,256,128]{3,2,1,0:T(8,128)S(1)}, f32[1,8,256,128]{3,2,1,0:T(8,128)S(1)}) fusion(), kind=kLoop, calls=%fused_computation.17 | loop fusion | flops 786432 | bytes 2097152 | tf_op jit(solution)/shard_map/sin | solution.py:336
  36.0 1.5 pad_maximum_fusion.refs_5_.refs_3_
  37.6 15.3 %collective-permute-done.1.late_ref = f32[4,256,256]{2,1,0:T(8,128)} collective-permute-done((f32[4,256,256]{2,1,0:T(8,128)S(1)}, f32[4,256,256]{2,1,0:T(8,128)}, u32[]{:S(2)}, u32[]{:S(2)}) %collective-permute-start.1) | collective-permute-done | bytes 1048608 | tf_op jit(solution)/shard_map/ppermute | solution.py:20
  52.9 2.6 %combine.2.refs_0_ = f32[8,256,256]{2,1,0:T(8,128)} custom-call(f32[1]{0:T(128)} %bitcast.sign_ref, f32[4,256,256]{2,1,0:T(8,128)} %collective-permute-done.1.late_ref, f32[4,256,256]{2,1,0:T(8,128)S(1)} %get-tuple-element.52.early_ref), custom_call_target="tpu_custom_call" | custom-call | flops 524288 | bytes 3145728 | tf_op jit(solution)/shard_map/combine/pallas_call | solution.py:50
  55.4 0.0 collective-permute-done.late_ref
  55.4 1.5 combine.3
  56.9 4.3 %all-to-all-done = f32[8,256,256]{2,1,0:T(8,128)} async-done(((f32[8,256,256]{2,1,0:T(8,128)}), f32[8,256,256]{2,1,0:T(8,128)}, u32[]{:S(2)}, u32[]{:S(2)}) %all-to-all-start) | async-done | bytes 2097184 | tf_op jit(solution)/shard_map/all_to_all | solution.py:24
  61.2 4.8 %all-to-all-start.1 = ((f32[8,256,256]{2,1,0:T(8,128)}), f32[8,256,256]{2,1,0:T(8,128)}, u32[]{:S(2)}, u32[]{:S(2)}) async-start(f32[8,256,256]{2,1,0:T(8,128)} %combine.3), calls=%async_computation.1 | async-start | bytes 4194304 | tf_op jit(solution)/shard_map/all_to_all | solution.py:24
  66.0 1.6 collective-permute-start.2
  67.6 0.0 collective-permute-start.4
  67.6 45.1 %collective-permute-done.2.refs_0_ = f32[2048,256]{1,0:T(8,128)} collective-permute-done((f32[2048,256]{1,0:T(8,128)}, f32[2048,256]{1,0:T(8,128)}, u32[]{:S(2)}, u32[]{:S(2)}) %collective-permute-start.2) | collective-permute-done | bytes 2097184 | tf_op jit(solution)/shard_map/ppermute | solution.py:20
  112.7 0.0 collective-permute-start.3
  112.7 1.0 all-to-all-done.1
  113.8 0.0 collective-permute-start.5
  113.8 0.0 collective-permute-done.4.refs_3_
  113.8 3.5 %collective-permute-done.3.refs_1_ = f32[2048,256]{1,0:T(8,128)} collective-permute-done((f32[2048,256]{1,0:T(8,128)}, f32[2048,256]{1,0:T(8,128)}, u32[]{:S(2)}, u32[]{:S(2)}) %collective-permute-start.3) | collective-permute-done | bytes 2097184 | tf_op jit(solution)/shard_map/ppermute | solution.py:20
  117.2 10.2 %y_dft.2 = (bf16[4,2048,128]{2,1,0:T(8,128)(2,1)S(1)}, bf16[4,2048,128]{2,1,0:T(8,128)(2,1)S(1)}) custom-call(f32[2,4]{1,0:T(2,128)S(1)} %pad_maximum_fusion.12.coef_ref, f32[2048,256]{1,0:T(8,128)} %collective-permute-done.2.refs_0_, f32[2048,256]{1,0:T(8,128)} %collective-permute-done.3.refs_1_, f32[2048,256]{1,0:T(8,128)} %bitcast.1.refs_2_, ...), custom_call_target="tpu_custom_call" | custom-call | flops 10737418240 | bytes 14680064 | tf_op jit(solution)/shard_map/y_dft/pallas_call | solution.py:187
  127.4 0.0 collective-permute-done.5.refs_1_
  127.4 8.0 %y_dft.3 = (bf16[4,2048,128]{2,1,0:T(8,128)(2,1)S(1)}, bf16[4,2048,128]{2,1,0:T(8,128)(2,1)S(1)}) custom-call(f32[2,2]{1,0:T(2,128)S(1)} %reshape.444.coef_ref, f32[2048,256]{1,0:T(8,128)} %bitcast.20.refs_0_, f32[2048,256]{1,0:T(8,128)} %collective-permute-done.5.refs_1_, bf16[2,512,512]{2,1,0:T(8,128)(2,1)S(1)} %copy-done.1, f32[2,8,256,128]{3,2,1,0:T(8,128)S(1)} %copy-done), custom_call_target="tpu_custom_call" | custom-call | flops 10737418240 | bytes 10485760 | tf_op jit(solution)/shard_map/y_dft/pallas_call | solution.py:187
  135.5 9.7 %x_dft.1 = (f32[2,1,2048,512]{3,2,1,0:T(8,128)}, f32[8,128]{1,0:T(8,128)S(1)}) custom-call(bf16[4,2048,128]{2,1,0:T(8,128)(2,1)S(1)} %get-tuple-element.39.refs_0_, bf16[4,2048,128]{2,1,0:T(8,128)(2,1)S(1)} %get-tuple-element.42.refs_1_, bf16[4,2048,128]{2,1,0:T(8,128)(2,1)S(1)} %get-tuple-element.43.refs_2_, ...), custom_call_target="tpu_custom_call" | custom-call | flops 6442450944 | bytes 16777216 | tf_op jit(solution)/shard_map/x_dft/pallas_call | solution.py:279
  145.2 13.3 %all_to_all.23 = f32[32,8,128]{2,1,0:T(8,128)S(1)} all-to-all(f32[32,8,128]{2,1,0:T(8,128)S(1)} %broadcast_in_dim.2), channel_id=1, replica_groups=mesh['gx'=4,'gy'=8] {'gx','gy'}, dimensions={0} | all-to-all | bytes 262144 | tf_op jit(solution)/shard_map/all_to_all | solution.py:309
  158.5 0.6 reduce_sum.29
  (44 shorter events, 0.4 us)
Async XLA Ops:
  0.6 3.2 %copy-start.4 = (f32[8,256,512]{2,1,0:T(8,128)S(1)}, f32[8,256,512]{2,1,0:T(8,128)}, u32[]{:S(2)}) copy-start(f32[8,256,512]{2,1,0:T(8,128)} %param.6) | copy-start | bytes 12582916
  4.1 51.3 %collective-permute-start = (f32[4,256,256]{2,1,0:T(8,128)S(1)}, f32[4,256,256]{2,1,0:T(8,128)S(1)}, u32[]{:S(2)}, u32[]{:S(2)}) collective-permute-start(f32[4,256,256]{2,1,0:T(8,128)S(1)} %get-tuple-element.53.early_ref), channel_id=1, source_target_pairs={{0,16},{8,24},{16,0},{24,8},{1,17},{9,25},{17,1},{25,9},{2,18},{10... | collective-permute-start | bytes 3145736 | tf_op jit(solution)/shard_map/ppermute | solution.py:20
  7.1 45.7 %collective-permute-start.1 = (f32[4,256,256]{2,1,0:T(8,128)S(1)}, f32[4,256,256]{2,1,0:T(8,128)}, u32[]{:S(2)}, u32[]{:S(2)}) collective-permute-start(f32[4,256,256]{2,1,0:T(8,128)S(1)} %get-tuple-element.52.early_ref), channel_id=1, source_target_pairs={{0,16},{8,24},{16,0},{24,8},{1,17},{9,25},{17,1},{25,9},{2,18},{10... | collective-permute-start | bytes 3145736 | tf_op jit(solution)/shard_map/ppermute | solution.py:20
  7.2 54.0 %all-to-all-start = ((f32[8,256,256]{2,1,0:T(8,128)}), f32[8,256,256]{2,1,0:T(8,128)}, u32[]{:S(2)}, u32[]{:S(2)}) async-start(f32[8,256,256]{2,1,0:T(8,128)} %slice.89), calls=%async_computation | async-start | bytes 4194304 | tf_op jit(solution)/shard_map/all_to_all | solution.py:24
  15.9 6.7 %copy-start.9 = (f32[2048]{0:T(1024)S(1)}, f32[2048]{0:T(1024)}, u32[]{:S(2)}) copy-start(f32[2048]{0:T(1024)} %param.7) | copy-start | bytes 24580
  15.9 7.5 %copy-start.8 = (f32[512]{0:T(512)S(1)}, f32[512]{0:T(512)}, u32[]{:S(2)}) copy-start(f32[512]{0:T(512)} %param.8) | copy-start | bytes 6148
  21.1 0.8 copy-start.6
  21.1 5.2 %copy-start.11 = (f32[512]{0:T(512)S(1)}, f32[512]{0:T(512)}, u32[]{:S(2)}) copy-start(f32[512]{0:T(512)} %param.11) | copy-start | bytes 6148
  21.1 5.2 %copy-start.12 = (f32[512]{0:T(512)S(1)}, f32[512]{0:T(512)}, u32[]{:S(2)}) copy-start(f32[512]{0:T(512)} %param.10) | copy-start | bytes 6148
  21.1 6.6 %copy-start.10 = (f32[2048]{0:T(1024)S(1)}, f32[2048]{0:T(1024)}, u32[]{:S(2)}) copy-start(f32[2048]{0:T(1024)} %param.9) | copy-start | bytes 24580
  30.0 1.2 copy-start.5
  30.0 1.3 copy-start.7
  61.2 56.0 %copy-start = (f32[2,8,256,128]{3,2,1,0:T(8,128)S(1)}, f32[2,8,256,128]{3,2,1,0:T(8,128)}, u32[]{:S(2)}) copy-start(f32[2,8,256,128]{3,2,1,0:T(8,128)} %pad_maximum_fusion.refs_5_.refs_3_) | copy-start | bytes 6291460
  61.2 56.0 %copy-start.1 = (bf16[2,512,512]{2,1,0:T(8,128)(2,1)S(1)}, bf16[2,512,512]{2,1,0:T(8,128)(2,1)}, u32[]{:S(2)}) copy-start(bf16[2,512,512]{2,1,0:T(8,128)(2,1)} %pad_maximum_fusion.1.refs_4_.refs_2_) | copy-start | bytes 3145732
  61.2 52.5 %all-to-all-start.1 = ((f32[8,256,256]{2,1,0:T(8,128)}), f32[8,256,256]{2,1,0:T(8,128)}, u32[]{:S(2)}, u32[]{:S(2)}) async-start(f32[8,256,256]{2,1,0:T(8,128)} %combine.3), calls=%async_computation.1 | async-start | bytes 4194304 | tf_op jit(solution)/shard_map/all_to_all | solution.py:24
  66.0 46.7 %collective-permute-start.2 = (f32[2048,256]{1,0:T(8,128)}, f32[2048,256]{1,0:T(8,128)}, u32[]{:S(2)}, u32[]{:S(2)}) collective-permute-start(f32[2048,256]{1,0:T(8,128)} %bitcast.1.refs_2_), channel_id=1, source_target_pairs={{0,16},{8,24},{16,0},{24,8},{1,17},{9,25},{17,1},{25,9},{2,18},{10... | collective-permute-start | bytes 6291464 | tf_op jit(solution)/shard_map/ppermute | solution.py:20
  67.6 46.1 %collective-permute-start.4 = (f32[2048,256]{1,0:T(8,128)}, f32[2048,256]{1,0:T(8,128)}, u32[]{:S(2)}, u32[]{:S(2)}) collective-permute-start(f32[2048,256]{1,0:T(8,128)} %bitcast.1.refs_2_), channel_id=1, source_target_pairs={{0,8},{8,0},{16,24},{24,16},{1,9},{9,1},{17,25},{25,17},{2,10},{10... | collective-permute-start | bytes 6291464 | tf_op jit(solution)/shard_map/ppermute | solution.py:20
  112.7 4.5 %collective-permute-start.3 = (f32[2048,256]{1,0:T(8,128)}, f32[2048,256]{1,0:T(8,128)}, u32[]{:S(2)}, u32[]{:S(2)}) collective-permute-start(f32[2048,256]{1,0:T(8,128)} %collective-permute-done.2.refs_0_), channel_id=1, source_target_pairs={{0,8},{8,0},{16,24},{24,16},{1,9},{9,1},{17,25},{25,17},{2,10},{10... | collective-permute-start | bytes 6291464 | tf_op jit(solution)/shard_map/ppermute | solution.py:20
  113.8 13.7 %collective-permute-start.5 = (f32[2048,256]{1,0:T(8,128)}, f32[2048,256]{1,0:T(8,128)}, u32[]{:S(2)}, u32[]{:S(2)}) collective-permute-start(f32[2048,256]{1,0:T(8,128)} %bitcast.20.refs_0_), channel_id=1, source_target_pairs={{0,8},{8,0},{16,24},{24,16},{1,9},{9,1},{17,25},{25,17},{2,10},{10... | collective-permute-start | bytes 6291464 | tf_op jit(solution)/shard_map/ppermute | solution.py:20
  127.4 8.1 %copy-start.2 = (bf16[2,512,512]{2,1,0:T(8,128)(2,1)S(1)}, bf16[2,512,512]{2,1,0:T(8,128)(2,1)}, u32[]{:S(2)}) copy-start(bf16[2,512,512]{2,1,0:T(8,128)(2,1)} %pad_maximum_fusion.3.refs_4_) | copy-start | bytes 3145732
  127.4 8.1 %copy-start.3 = (bf16[2,512,512]{2,1,0:T(8,128)(2,1)S(1)}, bf16[2,512,512]{2,1,0:T(8,128)(2,1)}, u32[]{:S(2)}) copy-start(bf16[2,512,512]{2,1,0:T(8,128)(2,1)} %pad_maximum_fusion.5.refs_5_) | copy-start | bytes 3145732

commit v21 on v18

--- a/solution.py
+++ b/solution.py
@@ -303,10 +303,16 @@
 
 
 def sum_everywhere(tile):
-    axes = ("gx", "gy")
-    devices = lax.axis_size("gx") * lax.axis_size("gy")
-    copies = jnp.broadcast_to(tile[None], (devices,) + tile.shape)
-    return jnp.sum(lax.all_to_all(copies, axes, split_axis=0, concat_axis=0, tiled=True))
+    for axis in ("gx", "gy"):
+        devices = lax.axis_size(axis)
+        place = devices
+        while place > 1:
+            low = max(place // 4, 1)
+            masks = range(low, place, low)
+            others = [lax.ppermute(tile, axis, [(s, s ^ mask) for s in range(devices)]) for mask in masks]
+            tile = functools.reduce(jnp.add, others, tile)
+            place = low
+    return jnp.sum(tile)
 
 
 def four_way(field, row_scale, col_scale, row_rate, col_shift, col_mix):

time: 161 us -> 164 us (1.019)
  blocking collectives: 13.3 us -> 0 us
  waiting for transfers between devices: 69.2 us -> 78.1 us
  starting transfers between devices: 15.7 us -> 23.6 us
    all_to_all x1 -> x0, blocking collectives: 13.3 us -> none  [sum_everywhere(): lax.all_to_all(copies, axes, split_axis=0, concat_axis=0, tiled=True)]
    ppermute x0 -> x7, waiting for transfers between devices: none -> 8.84 us  [sum_everywhere(): lax.ppermute(tile, axis, [(s, s ^ mask) for s in range(devices)])]
    ppermute x0 -> x7, starting transfers between devices: none -> 7.83 us  [sum_everywhere(): lax.ppermute(tile, axis, [(s, s ^ mask) for s in range(devices)])]
  transfers between devices with their start and end apart: 8 -> 15, of which waited for: 5 -> 10; matrix products, arithmetic and copies ran while one was open for 14% -> 13% of each run, Pallas kernels for 9% -> 9%
where the time goes in v21:
time: 164 us
  waiting for transfers between devices  78.1 us (48%)
  Pallas kernels  31.7 us (19%)
  starting transfers between devices  23.6 us (14%)
  other arithmetic  21.4 us (13%)
  local copies, waits for them, and re-layouts  5.32 us (3%)
  between operations  3.95 us (2%)
    ppermute x6, waiting for transfers between devices, from_partner(): return lax.ppermute(value, axis, pairs)  63.9 us
    pallas_call x2, Pallas kernels, y_dft(): pl.pallas_call(functools.partial(y_kernel, len(inputs), pick), out_shape=...  18.2 us
    all_to_all x2, starting transfers between devices, to_planes(): return lax.all_to_all(values, 'gy', split_axis=0, concat_axis=1, tiled=True)  11 us
    pallas_call x1, Pallas kernels, x_dft(): pl.pallas_call(functools.partial(x_kernel, count), out_shape=(jax.ShapeDt...  9.39 us
    ppermute x7, waiting for transfers between devices, sum_everywhere(): lax.ppermute(tile, axis, [(s, s ^ mask) for s in range(devices)])  8.84 us
    ppermute x7, starting transfers between devices, sum_everywhere(): lax.ppermute(tile, axis, [(s, s ^ mask) for s in range(devices)])  7.83 us
    all_to_all x2, waiting for transfers between devices, to_planes(): return lax.all_to_all(values, 'gy', split_axis=0, concat_axis=1, tiled=True)  5.31 us
    sin x1, other arithmetic, root_table(): return (jnp.cos(angle), jnp.sin(angle))  5.16 us
  transfers between devices with their start and end apart: 15, of which 10 were waited for; matrix products, arithmetic and copies ran while one was open for 13% of the time, Pallas kernels for 9%

profile of v21, /device:TPU:0, one launch (start us, length us, event | category | flops | bytes accessed | tf_op | source)
XLA Modules:
  0.0 164.0 jit_solution(18296468695360690262)
XLA Ops:
  0.6 3.2 %slice.89 = f32[8,256,256]{2,1,0:T(8,128)} slice(f32[8,256,512]{2,1,0:T(8,128)} %param.6), slice={[0:8], [0:256], [256:512]} | slice | bytes 4194304 | tf_op jit(solution)/shard_map/slice | solution.py:323
  3.8 0.2 fusion.24
  4.1 3.0 %collective-permute-start = (f32[4,256,256]{2,1,0:T(8,128)S(1)}, f32[4,256,256]{2,1,0:T(8,128)S(1)}, u32[]{:S(2)}, u32[]{:S(2)}) collective-permute-start(f32[4,256,256]{2,1,0:T(8,128)S(1)} %get-tuple-element.41.early_ref), channel_id=1, source_target_pairs={{0,16},{8,24},{16,0},{24,8},{1,17},{9,25},{17,1},{25,9},{2,18},{10... | collective-permute-start | bytes 3145736 | tf_op jit(solution)/shard_map/ppermute | solution.py:20
  7.1 0.1 collective-permute-start.1
  7.2 6.2 %all-to-all-start = ((f32[8,256,256]{2,1,0:T(8,128)}), f32[8,256,256]{2,1,0:T(8,128)}, u32[]{:S(2)}, u32[]{:S(2)}) async-start(f32[8,256,256]{2,1,0:T(8,128)} %slice.89), calls=%async_computation | async-start | bytes 4194304 | tf_op jit(solution)/shard_map/all_to_all | solution.py:24
  13.5 1.1 fusion.23
  14.6 0.1 maximum_maximum_fusion
  14.7 1.2 reduce-precision_convert_fusion.2
  15.9 5.2 %fusion.14 = (f32[256,512]{1,0:T(8,128)}, f32[256,512]{1,0:T(8,128)}, f32[256,512]{1,0:T(8,128)S(1)}, f32[256,512]{1,0:T(8,128)S(1)}) fusion(s32[512]{0:T(512)S(1)} %multiply_add_fusion, s32[256]{0:T(256)S(1)} %pad_add_fusion.1, s32[256]{0:T(256)S(1)} %pad_add_fusion), kind=kLoop, calls=%fused_computation.55 | loop fusion | flops 3670016 | bytes 2101248 | tf_op jit(solution)/shard_map/sin | solution.py:77
  21.1 0.8 copy-done.6
  21.9 0.7 fusion.28
  22.6 0.6 log_reduce_fusion
  23.3 0.1 reshape.443.coef_ref
  23.4 0.6 log_reduce_fusion.1
  24.0 2.3 %pad_maximum_fusion.1.refs_4_.refs_2_ = bf16[2,512,512]{2,1,0:T(8,128)(2,1)} fusion(bf16[1,512,512]{2,1,0:T(8,128)(2,1)} %get-tuple-element.47, bf16[1,512,512]{2,1,0:T(8,128)(2,1)} %get-tuple-element.46), kind=kLoop, calls=%fused_computation.11 | loop fusion | flops 524288 | bytes 2097152 | tf_op jit(solution)/shard_map/stack | solution.py:89
  27.7 1.0 slice_negate_fusion.1
  28.7 1.2 pad_maximum_fusion.6
  30.0 0.2 reduce-precision_convert_fusion.1
  30.1 1.1 pad_maximum_fusion.3.refs_4_
  31.3 0.1 pad_maximum_fusion.8
  31.5 0.2 reduce-precision_convert_fusion
  31.7 1.1 pad_maximum_fusion.5.refs_5_
  32.8 3.2 %fusion.3 = (f32[1,8,256,128]{3,2,1,0:T(8,128)S(1)}, f32[1,8,256,128]{3,2,1,0:T(8,128)S(1)}) fusion(), kind=kLoop, calls=%fused_computation.17 | loop fusion | flops 786432 | bytes 2097152 | tf_op jit(solution)/shard_map/sin | solution.py:342
  36.0 1.5 pad_maximum_fusion.refs_5_.refs_3_
  37.5 15.3 %collective-permute-done.1.late_ref = f32[4,256,256]{2,1,0:T(8,128)} collective-permute-done((f32[4,256,256]{2,1,0:T(8,128)S(1)}, f32[4,256,256]{2,1,0:T(8,128)}, u32[]{:S(2)}, u32[]{:S(2)}) %collective-permute-start.1) | collective-permute-done | bytes 1048608 | tf_op jit(solution)/shard_map/ppermute | solution.py:20
  52.9 2.6 %combine.2.refs_0_ = f32[8,256,256]{2,1,0:T(8,128)} custom-call(f32[1]{0:T(128)} %bitcast.sign_ref, f32[4,256,256]{2,1,0:T(8,128)} %collective-permute-done.1.late_ref, f32[4,256,256]{2,1,0:T(8,128)S(1)} %get-tuple-element.40.early_ref), custom_call_target="tpu_custom_call" | custom-call | flops 524288 | bytes 3145728 | tf_op jit(solution)/shard_map/combine/pallas_call | solution.py:50
  55.4 1.5 combine.3
  56.9 4.3 %all-to-all-done = f32[8,256,256]{2,1,0:T(8,128)} async-done(((f32[8,256,256]{2,1,0:T(8,128)}), f32[8,256,256]{2,1,0:T(8,128)}, u32[]{:S(2)}, u32[]{:S(2)}) %all-to-all-start) | async-done | bytes 2097184 | tf_op jit(solution)/shard_map/all_to_all | solution.py:24
  61.2 4.8 %all-to-all-start.1 = ((f32[8,256,256]{2,1,0:T(8,128)}), f32[8,256,256]{2,1,0:T(8,128)}, u32[]{:S(2)}, u32[]{:S(2)}) async-start(f32[8,256,256]{2,1,0:T(8,128)} %combine.3), calls=%async_computation.1 | async-start | bytes 4194304 | tf_op jit(solution)/shard_map/all_to_all | solution.py:24
  66.0 1.6 collective-permute-start.2
  67.6 45.1 %collective-permute-done.2.refs_0_ = f32[2048,256]{1,0:T(8,128)} collective-permute-done((f32[2048,256]{1,0:T(8,128)}, f32[2048,256]{1,0:T(8,128)}, u32[]{:S(2)}, u32[]{:S(2)}) %collective-permute-start.2) | collective-permute-done | bytes 2097184 | tf_op jit(solution)/shard_map/ppermute | solution.py:20
  112.7 1.0 all-to-all-done.1
  113.8 3.5 %collective-permute-done.3.refs_1_ = f32[2048,256]{1,0:T(8,128)} collective-permute-done((f32[2048,256]{1,0:T(8,128)}, f32[2048,256]{1,0:T(8,128)}, u32[]{:S(2)}, u32[]{:S(2)}) %collective-permute-start.3) | collective-permute-done | bytes 2097184 | tf_op jit(solution)/shard_map/ppermute | solution.py:20
  117.2 10.2 %y_dft.2 = (bf16[4,2048,128]{2,1,0:T(8,128)(2,1)S(1)}, bf16[4,2048,128]{2,1,0:T(8,128)(2,1)S(1)}) custom-call(f32[2,4]{1,0:T(2,128)S(1)} %pad_maximum_fusion.12.coef_ref, f32[2048,256]{1,0:T(8,128)} %collective-permute-done.2.refs_0_, f32[2048,256]{1,0:T(8,128)} %collective-permute-done.3.refs_1_, f32[2048,256]{1,0:T(8,128)} %bitcast.1.refs_2_, ...), custom_call_target="tpu_custom_call" | custom-call | flops 10737418240 | bytes 14680064 | tf_op jit(solution)/shard_map/y_dft/pallas_call | solution.py:187
  127.4 8.0 %y_dft.3 = (bf16[4,2048,128]{2,1,0:T(8,128)(2,1)S(1)}, bf16[4,2048,128]{2,1,0:T(8,128)(2,1)S(1)}) custom-call(f32[2,2]{1,0:T(2,128)S(1)} %reshape.443.coef_ref, f32[2048,256]{1,0:T(8,128)} %bitcast.20.refs_0_, f32[2048,256]{1,0:T(8,128)} %collective-permute-done.5.refs_1_, bf16[2,512,512]{2,1,0:T(8,128)(2,1)S(1)} %copy-done.1, f32[2,8,256,128]{3,2,1,0:T(8,128)S(1)} %copy-done), custom_call_target="tpu_custom_call" | custom-call | flops 10737418240 | bytes 10485760 | tf_op jit(solution)/shard_map/y_dft/pallas_call | solution.py:187
  135.5 9.4 %x_dft.1 = (f32[2,1,2048,512]{3,2,1,0:T(8,128)}, f32[8,128]{1,0:T(8,128)S(1)}) custom-call(bf16[4,2048,128]{2,1,0:T(8,128)(2,1)S(1)} %get-tuple-element.27.refs_0_, bf16[4,2048,128]{2,1,0:T(8,128)(2,1)S(1)} %get-tuple-element.30.refs_1_, bf16[4,2048,128]{2,1,0:T(8,128)(2,1)S(1)} %get-tuple-element.31.refs_2_, ...), custom_call_target="tpu_custom_call" | custom-call | flops 6442450944 | bytes 16777216 | tf_op jit(solution)/shard_map/x_dft/pallas_call | solution.py:279
  144.9 1.3 collective-permute-start.8
  146.1 0.5 collective-permute-start.7
  146.7 0.1 collective-permute-start.6
  146.7 1.2 collective-permute-done.8
  147.9 1.8 %collective-permute-done.7 = f32[8,128]{1,0:T(8,128)S(1)} collective-permute-done((f32[8,128]{1,0:T(8,128)S(1)}, f32[8,128]{1,0:T(8,128)S(1)}, u32[]{:S(2)}, u32[]{:S(2)}) %collective-permute-start.7) | collective-permute-done | bytes 4128 | tf_op jit(solution)/shard_map/ppermute | solution.py:312
  149.8 3.6 %collective-permute-start.11 = (f32[8,128]{1,0:T(8,128)S(1)}, f32[8,128]{1,0:T(8,128)S(1)}, u32[]{:S(2)}, u32[]{:S(2)}) collective-permute-start(f32[8,128]{1,0:T(8,128)S(1)} %add_add_fusion.1), channel_id=1, source_target_pairs={{0,6},{1,7},{2,4},{3,5},{4,2},{5,3},{6,0},{7,1},{8,14},{9,15},{10,... | collective-permute-start | bytes 12296 | tf_op jit(solution)/shard_map/ppermute | solution.py:312
  153.4 0.8 collective-permute-start.9
  154.2 1.0 collective-permute-done.11
  155.2 2.7 %collective-permute-done.10 = f32[8,128]{1,0:T(8,128)S(1)} collective-permute-done((f32[8,128]{1,0:T(8,128)S(1)}, f32[8,128]{1,0:T(8,128)S(1)}, u32[]{:S(2)}, u32[]{:S(2)}) %collective-permute-start.10) | collective-permute-done | bytes 4128 | tf_op jit(solution)/shard_map/ppermute | solution.py:312
  157.9 1.5 collective-permute-start.12
  159.4 2.2 %collective-permute-done.12 = f32[8,128]{1,0:T(8,128)S(1)} collective-permute-done((f32[8,128]{1,0:T(8,128)S(1)}, f32[8,128]{1,0:T(8,128)S(1)}, u32[]{:S(2)}, u32[]{:S(2)}) %collective-permute-start.12) | collective-permute-done | bytes 4128 | tf_op jit(solution)/shard_map/ppermute | solution.py:312
  161.6 0.6 add_reduce_fusion
  (58 shorter events, 0.6 us)
Async XLA Ops:
  0.6 3.2 %copy-start.4 = (f32[8,256,512]{2,1,0:T(8,128)S(1)}, f32[8,256,512]{2,1,0:T(8,128)}, u32[]{:S(2)}) copy-start(f32[8,256,512]{2,1,0:T(8,128)} %param.6) | copy-start | bytes 12582916
  4.1 51.3 %collective-permute-start = (f32[4,256,256]{2,1,0:T(8,128)S(1)}, f32[4,256,256]{2,1,0:T(8,128)S(1)}, u32[]{:S(2)}, u32[]{:S(2)}) collective-permute-start(f32[4,256,256]{2,1,0:T(8,128)S(1)} %get-tuple-element.41.early_ref), channel_id=1, source_target_pairs={{0,16},{8,24},{16,0},{24,8},{1,17},{9,25},{17,1},{25,9},{2,18},{10... | collective-permute-start | bytes 3145736 | tf_op jit(solution)/shard_map/ppermute | solution.py:20
  7.1 45.7 %collective-permute-start.1 = (f32[4,256,256]{2,1,0:T(8,128)S(1)}, f32[4,256,256]{2,1,0:T(8,128)}, u32[]{:S(2)}, u32[]{:S(2)}) collective-permute-start(f32[4,256,256]{2,1,0:T(8,128)S(1)} %get-tuple-element.40.early_ref), channel_id=1, source_target_pairs={{0,16},{8,24},{16,0},{24,8},{1,17},{9,25},{17,1},{25,9},{2,18},{10... | collective-permute-start | bytes 3145736 | tf_op jit(solution)/shard_map/ppermute | solution.py:20
  7.2 54.0 %all-to-all-start = ((f32[8,256,256]{2,1,0:T(8,128)}), f32[8,256,256]{2,1,0:T(8,128)}, u32[]{:S(2)}, u32[]{:S(2)}) async-start(f32[8,256,256]{2,1,0:T(8,128)} %slice.89), calls=%async_computation | async-start | bytes 4194304 | tf_op jit(solution)/shard_map/all_to_all | solution.py:24
  15.9 6.8 %copy-start.9 = (f32[2048]{0:T(1024)S(1)}, f32[2048]{0:T(1024)}, u32[]{:S(2)}) copy-start(f32[2048]{0:T(1024)} %param.7) | copy-start | bytes 24580
  15.9 7.5 %copy-start.8 = (f32[512]{0:T(512)S(1)}, f32[512]{0:T(512)}, u32[]{:S(2)}) copy-start(f32[512]{0:T(512)} %param.8) | copy-start | bytes 6148
  21.1 0.8 copy-start.6
  21.1 5.2 %copy-start.11 = (f32[512]{0:T(512)S(1)}, f32[512]{0:T(512)}, u32[]{:S(2)}) copy-start(f32[512]{0:T(512)} %param.11) | copy-start | bytes 6148
  21.1 5.2 %copy-start.12 = (f32[512]{0:T(512)S(1)}, f32[512]{0:T(512)}, u32[]{:S(2)}) copy-start(f32[512]{0:T(512)} %param.10) | copy-start | bytes 6148
  21.1 6.6 %copy-start.10 = (f32[2048]{0:T(1024)S(1)}, f32[2048]{0:T(1024)}, u32[]{:S(2)}) copy-start(f32[2048]{0:T(1024)} %param.9) | copy-start | bytes 24580
  29.9 1.3 copy-start.5
  29.9 1.3 copy-start.7
  61.2 56.0 %copy-start = (f32[2,8,256,128]{3,2,1,0:T(8,128)S(1)}, f32[2,8,256,128]{3,2,1,0:T(8,128)}, u32[]{:S(2)}) copy-start(f32[2,8,256,128]{3,2,1,0:T(8,128)} %pad_maximum_fusion.refs_5_.refs_3_) | copy-start | bytes 6291460
  61.2 56.0 %copy-start.1 = (bf16[2,512,512]{2,1,0:T(8,128)(2,1)S(1)}, bf16[2,512,512]{2,1,0:T(8,128)(2,1)}, u32[]{:S(2)}) copy-start(bf16[2,512,512]{2,1,0:T(8,128)(2,1)} %pad_maximum_fusion.1.refs_4_.refs_2_) | copy-start | bytes 3145732
  61.2 52.5 %all-to-all-start.1 = ((f32[8,256,256]{2,1,0:T(8,128)}), f32[8,256,256]{2,1,0:T(8,128)}, u32[]{:S(2)}, u32[]{:S(2)}) async-start(f32[8,256,256]{2,1,0:T(8,128)} %combine.3), calls=%async_computation.1 | async-start | bytes 4194304 | tf_op jit(solution)/shard_map/all_to_all | solution.py:24
  66.0 46.7 %collective-permute-start.2 = (f32[2048,256]{1,0:T(8,128)}, f32[2048,256]{1,0:T(8,128)}, u32[]{:S(2)}, u32[]{:S(2)}) collective-permute-start(f32[2048,256]{1,0:T(8,128)} %bitcast.1.refs_2_), channel_id=1, source_target_pairs={{0,16},{8,24},{16,0},{24,8},{1,17},{9,25},{17,1},{25,9},{2,18},{10... | collective-permute-start | bytes 6291464 | tf_op jit(solution)/shard_map/ppermute | solution.py:20
  67.6 46.1 %collective-permute-start.4 = (f32[2048,256]{1,0:T(8,128)}, f32[2048,256]{1,0:T(8,128)}, u32[]{:S(2)}, u32[]{:S(2)}) collective-permute-start(f32[2048,256]{1,0:T(8,128)} %bitcast.1.refs_2_), channel_id=1, source_target_pairs={{0,8},{8,0},{16,24},{24,16},{1,9},{9,1},{17,25},{25,17},{2,10},{10... | collective-permute-start | bytes 6291464 | tf_op jit(solution)/shard_map/ppermute | solution.py:20
  112.7 4.5 %collective-permute-start.3 = (f32[2048,256]{1,0:T(8,128)}, f32[2048,256]{1,0:T(8,128)}, u32[]{:S(2)}, u32[]{:S(2)}) collective-permute-start(f32[2048,256]{1,0:T(8,128)} %collective-permute-done.2.refs_0_), channel_id=1, source_target_pairs={{0,8},{8,0},{16,24},{24,16},{1,9},{9,1},{17,25},{25,17},{2,10},{10... | collective-permute-start | bytes 6291464 | tf_op jit(solution)/shard_map/ppermute | solution.py:20
  113.7 13.7 %collective-permute-start.5 = (f32[2048,256]{1,0:T(8,128)}, f32[2048,256]{1,0:T(8,128)}, u32[]{:S(2)}, u32[]{:S(2)}) collective-permute-start(f32[2048,256]{1,0:T(8,128)} %bitcast.20.refs_0_), channel_id=1, source_target_pairs={{0,8},{8,0},{16,24},{24,16},{1,9},{9,1},{17,25},{25,17},{2,10},{10... | collective-permute-start | bytes 6291464 | tf_op jit(solution)/shard_map/ppermute | solution.py:20
  127.4 8.1 %copy-start.2 = (bf16[2,512,512]{2,1,0:T(8,128)(2,1)S(1)}, bf16[2,512,512]{2,1,0:T(8,128)(2,1)}, u32[]{:S(2)}) copy-start(bf16[2,512,512]{2,1,0:T(8,128)(2,1)} %pad_maximum_fusion.3.refs_4_) | copy-start | bytes 3145732
  127.4 8.1 %copy-start.3 = (bf16[2,512,512]{2,1,0:T(8,128)(2,1)S(1)}, bf16[2,512,512]{2,1,0:T(8,128)(2,1)}, u32[]{:S(2)}) copy-start(bf16[2,512,512]{2,1,0:T(8,128)(2,1)} %pad_maximum_fusion.5.refs_5_) | copy-start | bytes 3145732
  144.9 3.0 %collective-permute-start.8 = (f32[8,128]{1,0:T(8,128)S(1)}, f32[8,128]{1,0:T(8,128)S(1)}, u32[]{:S(2)}, u32[]{:S(2)}) collective-permute-start(f32[8,128]{1,0:T(8,128)S(1)} %broadcast_add_fusion), channel_id=1, source_target_pairs={{0,24},{8,16},{16,8},{24,0},{1,25},{9,17},{17,9},{25,1},{2,26},{10... | collective-permute-start | bytes 12296 | tf_op jit(solution)/shard_map/ppermute | solution.py:312
  146.1 3.6 %collective-permute-start.7 = (f32[8,128]{1,0:T(8,128)S(1)}, f32[8,128]{1,0:T(8,128)S(1)}, u32[]{:S(2)}, u32[]{:S(2)}) collective-permute-start(f32[8,128]{1,0:T(8,128)S(1)} %broadcast_add_fusion), channel_id=1, source_target_pairs={{0,16},{8,24},{16,0},{24,8},{1,17},{9,25},{17,1},{25,9},{2,18},{10... | collective-permute-start | bytes 12296 | tf_op jit(solution)/shard_map/ppermute | solution.py:312
  146.7 3.1 %collective-permute-start.6 = (f32[8,128]{1,0:T(8,128)S(1)}, f32[8,128]{1,0:T(8,128)S(1)}, u32[]{:S(2)}, u32[]{:S(2)}) collective-permute-start(f32[8,128]{1,0:T(8,128)S(1)} %broadcast_add_fusion), channel_id=1, source_target_pairs={{0,8},{8,0},{16,24},{24,16},{1,9},{9,1},{17,25},{25,17},{2,10},{10... | collective-permute-start | bytes 12296 | tf_op jit(solution)/shard_map/ppermute | solution.py:312
  149.8 5.5 %collective-permute-start.11 = (f32[8,128]{1,0:T(8,128)S(1)}, f32[8,128]{1,0:T(8,128)S(1)}, u32[]{:S(2)}, u32[]{:S(2)}) collective-permute-start(f32[8,128]{1,0:T(8,128)S(1)} %add_add_fusion.1), channel_id=1, source_target_pairs={{0,6},{1,7},{2,4},{3,5},{4,2},{5,3},{6,0},{7,1},{8,14},{9,15},{10,... | collective-permute-start | bytes 12296 | tf_op jit(solution)/shard_map/ppermute | solution.py:312
  153.4 4.5 %collective-permute-start.10 = (f32[8,128]{1,0:T(8,128)S(1)}, f32[8,128]{1,0:T(8,128)S(1)}, u32[]{:S(2)}, u32[]{:S(2)}) collective-permute-start(f32[8,128]{1,0:T(8,128)S(1)} %add_add_fusion.1), channel_id=1, source_target_pairs={{0,4},{1,5},{2,6},{3,7},{4,0},{5,1},{6,2},{7,3},{8,12},{9,13},{10,... | collective-permute-start | bytes 12296 | tf_op jit(solution)/shard_map/ppermute | solution.py:312
  153.4 4.5 %collective-permute-start.9 = (f32[8,128]{1,0:T(8,128)S(1)}, f32[8,128]{1,0:T(8,128)S(1)}, u32[]{:S(2)}, u32[]{:S(2)}) collective-permute-start(f32[8,128]{1,0:T(8,128)S(1)} %add_add_fusion.1), channel_id=1, source_target_pairs={{0,2},{1,3},{2,0},{3,1},{4,6},{5,7},{6,4},{7,5},{8,10},{9,11},{10,... | collective-permute-start | bytes 12296 | tf_op jit(solution)/shard_map/ppermute | solution.py:312
  157.9 3.7 %collective-permute-start.12 = (f32[8,128]{1,0:T(8,128)S(1)}, f32[8,128]{1,0:T(8,128)S(1)}, u32[]{:S(2)}, u32[]{:S(2)}) collective-permute-start(f32[8,128]{1,0:T(8,128)S(1)} %add_add_fusion), channel_id=1, source_target_pairs={{0,1},{1,0},{2,3},{3,2},{4,5},{5,4},{6,7},{7,6},{8,9},{9,8},{10,11... | collective-permute-start | bytes 12296 | tf_op jit(solution)/shard_map/ppermute | solution.py:312

commit v22 on v18

--- a/solution.py
+++ b/solution.py
@@ -305,7 +305,8 @@
 def sum_everywhere(tile):
     axes = ("gx", "gy")
     devices = lax.axis_size("gx") * lax.axis_size("gy")
-    copies = jnp.broadcast_to(tile[None], (devices,) + tile.shape)
+    row = jnp.sum(tile, axis=0, keepdims=True)
+    copies = jnp.broadcast_to(row[None], (devices,) + row.shape)
     return jnp.sum(lax.all_to_all(copies, axes, split_axis=0, concat_axis=0, tiled=True))
 
 

time: 161 us -> 161 us (level)
  no operation moved by 1% of the time
where the time goes in v22:
time: 161 us; the launch traced here: 160 us
  waiting for transfers between devices  69 us (43%)
  Pallas kernels  32 us (20%)
  other arithmetic  21.5 us (13%)
  starting transfers between devices  15.7 us (10%)
  blocking collectives  12.7 us (8%)
  local copies, waits for them, and re-layouts  5.33 us (3%)
  between operations  4.07 us (3%)
    ppermute x6, waiting for transfers between devices, from_partner(): return lax.ppermute(value, axis, pairs)  63.7 us
    pallas_call x2, Pallas kernels, y_dft(): pl.pallas_call(functools.partial(y_kernel, len(inputs), pick), out_shape=...  18.2 us
    all_to_all x1, blocking collectives, sum_everywhere(): lax.all_to_all(copies, axes, split_axis=0, concat_axis=0, tiled=True)  12.7 us
    all_to_all x2, starting transfers between devices, to_planes(): return lax.all_to_all(values, 'gy', split_axis=0, concat_axis=1, tiled=True)  11 us
    pallas_call x1, Pallas kernels, x_dft(): pl.pallas_call(functools.partial(x_kernel, count), out_shape=(jax.ShapeDt...  9.72 us
    all_to_all x2, waiting for transfers between devices, to_planes(): return lax.all_to_all(values, 'gy', split_axis=0, concat_axis=1, tiled=True)  5.33 us
    sin x1, other arithmetic, root_table(): return (jnp.cos(angle), jnp.sin(angle))  5.17 us
    ppermute x6, starting transfers between devices, from_partner(): return lax.ppermute(value, axis, pairs)  4.7 us
  transfers between devices with their start and end apart: 8, of which 5 were waited for; matrix products, arithmetic and copies ran while one was open for 14% of the time, Pallas kernels for 9%

profile of v22, /device:TPU:0, one launch (start us, length us, event | category | flops | bytes accessed | tf_op | source)
XLA Modules:
  0.0 160.3 jit_solution(16441652393594481751)
XLA Ops:
  0.6 3.2 %slice.89 = f32[8,256,256]{2,1,0:T(8,128)} slice(f32[8,256,512]{2,1,0:T(8,128)} %param.6), slice={[0:8], [0:256], [256:512]} | slice | bytes 4194304 | tf_op jit(solution)/shard_map/slice | solution.py:318
  3.8 0.2 fusion.24
  4.1 3.0 %collective-permute-start = (f32[4,256,256]{2,1,0:T(8,128)S(1)}, f32[4,256,256]{2,1,0:T(8,128)S(1)}, u32[]{:S(2)}, u32[]{:S(2)}) collective-permute-start(f32[4,256,256]{2,1,0:T(8,128)S(1)} %get-tuple-element.41.early_ref), channel_id=1, source_target_pairs={{0,16},{8,24},{16,0},{24,8},{1,17},{9,25},{17,1},{25,9},{2,18},{10... | collective-permute-start | bytes 3145736 | tf_op jit(solution)/shard_map/ppermute | solution.py:20
  7.1 0.1 collective-permute-start.1
  7.2 6.2 %all-to-all-start = ((f32[8,256,256]{2,1,0:T(8,128)}), f32[8,256,256]{2,1,0:T(8,128)}, u32[]{:S(2)}, u32[]{:S(2)}) async-start(f32[8,256,256]{2,1,0:T(8,128)} %slice.89), calls=%async_computation | async-start | bytes 4194304 | tf_op jit(solution)/shard_map/all_to_all | solution.py:24
  13.5 1.1 fusion.23
  14.6 0.1 maximum_maximum_fusion
  14.7 1.2 reduce-precision_convert_fusion.2
  16.0 5.2 %fusion.14 = (f32[256,512]{1,0:T(8,128)}, f32[256,512]{1,0:T(8,128)}, f32[256,512]{1,0:T(8,128)S(1)}, f32[256,512]{1,0:T(8,128)S(1)}) fusion(s32[512]{0:T(512)S(1)} %multiply_add_fusion, s32[256]{0:T(256)S(1)} %pad_add_fusion.1, s32[256]{0:T(256)S(1)} %pad_add_fusion), kind=kLoop, calls=%fused_computation.55 | loop fusion | flops 3670016 | bytes 2101248 | tf_op jit(solution)/shard_map/sin | solution.py:77
  21.1 0.8 copy-done.6
  22.0 0.7 fusion.28
  22.7 0.7 log_reduce_fusion
  23.4 0.1 pad_maximum_fusion.13
  23.4 0.1 reshape.446.coef_ref
  23.5 0.0 copy-done.8
  23.5 0.6 log_reduce_fusion.1
  24.1 2.3 %pad_maximum_fusion.1.refs_4_.refs_2_ = bf16[2,512,512]{2,1,0:T(8,128)(2,1)} fusion(bf16[1,512,512]{2,1,0:T(8,128)(2,1)} %get-tuple-element.47, bf16[1,512,512]{2,1,0:T(8,128)(2,1)} %get-tuple-element.46), kind=kLoop, calls=%fused_computation.11 | loop fusion | flops 524288 | bytes 2097152 | tf_op jit(solution)/shard_map/stack | solution.py:89
  26.5 0.1 pad_maximum_fusion.12.coef_ref
  27.9 1.0 slice_negate_fusion.1
  28.9 1.2 pad_maximum_fusion.6
  30.2 0.0 copy-start.5
  30.2 0.2 reduce-precision_convert_fusion.1
  30.3 1.1 pad_maximum_fusion.3.refs_4_
  31.5 0.1 pad_maximum_fusion.8
  31.7 0.2 reduce-precision_convert_fusion
  31.9 1.1 pad_maximum_fusion.5.refs_5_
  32.9 3.2 %fusion.3 = (f32[1,8,256,128]{3,2,1,0:T(8,128)S(1)}, f32[1,8,256,128]{3,2,1,0:T(8,128)S(1)}) fusion(), kind=kLoop, calls=%fused_computation.17 | loop fusion | flops 786432 | bytes 2097152 | tf_op jit(solution)/shard_map/sin | solution.py:337
  36.2 1.5 pad_maximum_fusion.refs_5_.refs_3_
  37.7 15.1 %collective-permute-done.1.late_ref = f32[4,256,256]{2,1,0:T(8,128)} collective-permute-done((f32[4,256,256]{2,1,0:T(8,128)S(1)}, f32[4,256,256]{2,1,0:T(8,128)}, u32[]{:S(2)}, u32[]{:S(2)}) %collective-permute-start.1) | collective-permute-done | bytes 1048608 | tf_op jit(solution)/shard_map/ppermute | solution.py:20
  52.9 2.5 %combine.2.refs_0_ = f32[8,256,256]{2,1,0:T(8,128)} custom-call(f32[1]{0:T(128)} %bitcast.sign_ref, f32[4,256,256]{2,1,0:T(8,128)} %collective-permute-done.1.late_ref, f32[4,256,256]{2,1,0:T(8,128)S(1)} %get-tuple-element.40.early_ref), custom_call_target="tpu_custom_call" | custom-call | flops 524288 | bytes 3145728 | tf_op jit(solution)/shard_map/combine/pallas_call | solution.py:50
  55.4 0.0 collective-permute-done.late_ref
  55.4 1.5 combine.3
  56.9 4.3 %all-to-all-done = f32[8,256,256]{2,1,0:T(8,128)} async-done(((f32[8,256,256]{2,1,0:T(8,128)}), f32[8,256,256]{2,1,0:T(8,128)}, u32[]{:S(2)}, u32[]{:S(2)}) %all-to-all-start) | async-done | bytes 2097184 | tf_op jit(solution)/shard_map/all_to_all | solution.py:24
  61.2 4.8 %all-to-all-start.1 = ((f32[8,256,256]{2,1,0:T(8,128)}), f32[8,256,256]{2,1,0:T(8,128)}, u32[]{:S(2)}, u32[]{:S(2)}) async-start(f32[8,256,256]{2,1,0:T(8,128)} %combine.3), calls=%async_computation.1 | async-start | bytes 4194304 | tf_op jit(solution)/shard_map/all_to_all | solution.py:24
  66.0 1.6 collective-permute-start.2
  67.6 0.0 collective-permute-start.4
  67.6 45.1 %collective-permute-done.2.refs_0_ = f32[2048,256]{1,0:T(8,128)} collective-permute-done((f32[2048,256]{1,0:T(8,128)}, f32[2048,256]{1,0:T(8,128)}, u32[]{:S(2)}, u32[]{:S(2)}) %collective-permute-start.2) | collective-permute-done | bytes 2097184 | tf_op jit(solution)/shard_map/ppermute | solution.py:20
  112.7 0.0 collective-permute-start.3
  112.7 1.0 all-to-all-done.1
  113.8 0.0 collective-permute-start.5
  113.8 0.0 collective-permute-done.4.refs_3_
  113.8 3.5 %collective-permute-done.3.refs_1_ = f32[2048,256]{1,0:T(8,128)} collective-permute-done((f32[2048,256]{1,0:T(8,128)}, f32[2048,256]{1,0:T(8,128)}, u32[]{:S(2)}, u32[]{:S(2)}) %collective-permute-start.3) | collective-permute-done | bytes 2097184 | tf_op jit(solution)/shard_map/ppermute | solution.py:20
  117.2 10.2 %y_dft.2 = (bf16[4,2048,128]{2,1,0:T(8,128)(2,1)S(1)}, bf16[4,2048,128]{2,1,0:T(8,128)(2,1)S(1)}) custom-call(f32[2,4]{1,0:T(2,128)S(1)} %pad_maximum_fusion.12.coef_ref, f32[2048,256]{1,0:T(8,128)} %collective-permute-done.2.refs_0_, f32[2048,256]{1,0:T(8,128)} %collective-permute-done.3.refs_1_, f32[2048,256]{1,0:T(8,128)} %bitcast.1.refs_2_, ...), custom_call_target="tpu_custom_call" | custom-call | flops 10737418240 | bytes 14680064 | tf_op jit(solution)/shard_map/y_dft/pallas_call | solution.py:187
  127.4 0.0 collective-permute-done.5.refs_1_
  127.4 8.0 %y_dft.3 = (bf16[4,2048,128]{2,1,0:T(8,128)(2,1)S(1)}, bf16[4,2048,128]{2,1,0:T(8,128)(2,1)S(1)}) custom-call(f32[2,2]{1,0:T(2,128)S(1)} %reshape.446.coef_ref, f32[2048,256]{1,0:T(8,128)} %bitcast.20.refs_0_, f32[2048,256]{1,0:T(8,128)} %collective-permute-done.5.refs_1_, bf16[2,512,512]{2,1,0:T(8,128)(2,1)S(1)} %copy-done.1, f32[2,8,256,128]{3,2,1,0:T(8,128)S(1)} %copy-done), custom_call_target="tpu_custom_call" | custom-call | flops 10737418240 | bytes 10485760 | tf_op jit(solution)/shard_map/y_dft/pallas_call | solution.py:187
  135.5 9.7 %x_dft.1 = (f32[2,1,2048,512]{3,2,1,0:T(8,128)}, f32[8,128]{1,0:T(8,128)S(1)}) custom-call(bf16[4,2048,128]{2,1,0:T(8,128)(2,1)S(1)} %get-tuple-element.27.refs_0_, bf16[4,2048,128]{2,1,0:T(8,128)(2,1)S(1)} %get-tuple-element.30.refs_1_, bf16[4,2048,128]{2,1,0:T(8,128)(2,1)S(1)} %get-tuple-element.31.refs_2_, ...), custom_call_target="tpu_custom_call" | custom-call | flops 6442450944 | bytes 16777216 | tf_op jit(solution)/shard_map/x_dft/pallas_call | solution.py:279
  145.2 12.7 %all_to_all.23 = f32[32,1,128]{2,1,0:T(1,128)S(1)} all-to-all(f32[32,1,128]{2,1,0:T(1,128)S(1)} %broadcast_in_dim.2), channel_id=1, replica_groups=mesh['gx'=4,'gy'=8] {'gx','gy'}, dimensions={0} | all-to-all | bytes 32768 | tf_op jit(solution)/shard_map/all_to_all | solution.py:310
  157.9 0.6 reduce_sum.39
  (44 shorter events, 0.4 us)
Async XLA Ops:
  0.6 3.2 %copy-start.4 = (f32[8,256,512]{2,1,0:T(8,128)S(1)}, f32[8,256,512]{2,1,0:T(8,128)}, u32[]{:S(2)}) copy-start(f32[8,256,512]{2,1,0:T(8,128)} %param.6) | copy-start | bytes 12582916
  4.1 51.3 %collective-permute-start = (f32[4,256,256]{2,1,0:T(8,128)S(1)}, f32[4,256,256]{2,1,0:T(8,128)S(1)}, u32[]{:S(2)}, u32[]{:S(2)}) collective-permute-start(f32[4,256,256]{2,1,0:T(8,128)S(1)} %get-tuple-element.41.early_ref), channel_id=1, source_target_pairs={{0,16},{8,24},{16,0},{24,8},{1,17},{9,25},{17,1},{25,9},{2,18},{10... | collective-permute-start | bytes 3145736 | tf_op jit(solution)/shard_map/ppermute | solution.py:20
  7.1 45.7 %collective-permute-start.1 = (f32[4,256,256]{2,1,0:T(8,128)S(1)}, f32[4,256,256]{2,1,0:T(8,128)}, u32[]{:S(2)}, u32[]{:S(2)}) collective-permute-start(f32[4,256,256]{2,1,0:T(8,128)S(1)} %get-tuple-element.40.early_ref), channel_id=1, source_target_pairs={{0,16},{8,24},{16,0},{24,8},{1,17},{9,25},{17,1},{25,9},{2,18},{10... | collective-permute-start | bytes 3145736 | tf_op jit(solution)/shard_map/ppermute | solution.py:20
  7.2 54.0 %all-to-all-start = ((f32[8,256,256]{2,1,0:T(8,128)}), f32[8,256,256]{2,1,0:T(8,128)}, u32[]{:S(2)}, u32[]{:S(2)}) async-start(f32[8,256,256]{2,1,0:T(8,128)} %slice.89), calls=%async_computation | async-start | bytes 4194304 | tf_op jit(solution)/shard_map/all_to_all | solution.py:24
  15.9 6.8 %copy-start.9 = (f32[2048]{0:T(1024)S(1)}, f32[2048]{0:T(1024)}, u32[]{:S(2)}) copy-start(f32[2048]{0:T(1024)} %param.7) | copy-start | bytes 24580
  15.9 7.6 %copy-start.8 = (f32[512]{0:T(512)S(1)}, f32[512]{0:T(512)}, u32[]{:S(2)}) copy-start(f32[512]{0:T(512)} %param.8) | copy-start | bytes 6148
  21.1 0.8 copy-start.6
  21.1 5.3 %copy-start.11 = (f32[512]{0:T(512)S(1)}, f32[512]{0:T(512)}, u32[]{:S(2)}) copy-start(f32[512]{0:T(512)} %param.11) | copy-start | bytes 6148
  21.1 5.3 %copy-start.12 = (f32[512]{0:T(512)S(1)}, f32[512]{0:T(512)}, u32[]{:S(2)}) copy-start(f32[512]{0:T(512)} %param.10) | copy-start | bytes 6148
  21.1 6.7 %copy-start.10 = (f32[2048]{0:T(1024)S(1)}, f32[2048]{0:T(1024)}, u32[]{:S(2)}) copy-start(f32[2048]{0:T(1024)} %param.9) | copy-start | bytes 24580
  30.2 1.3 copy-start.5
  30.2 1.3 copy-start.7
  61.2 56.0 %copy-start = (f32[2,8,256,128]{3,2,1,0:T(8,128)S(1)}, f32[2,8,256,128]{3,2,1,0:T(8,128)}, u32[]{:S(2)}) copy-start(f32[2,8,256,128]{3,2,1,0:T(8,128)} %pad_maximum_fusion.refs_5_.refs_3_) | copy-start | bytes 6291460
  61.2 56.0 %copy-start.1 = (bf16[2,512,512]{2,1,0:T(8,128)(2,1)S(1)}, bf16[2,512,512]{2,1,0:T(8,128)(2,1)}, u32[]{:S(2)}) copy-start(bf16[2,512,512]{2,1,0:T(8,128)(2,1)} %pad_maximum_fusion.1.refs_4_.refs_2_) | copy-start | bytes 3145732
  61.2 52.5 %all-to-all-start.1 = ((f32[8,256,256]{2,1,0:T(8,128)}), f32[8,256,256]{2,1,0:T(8,128)}, u32[]{:S(2)}, u32[]{:S(2)}) async-start(f32[8,256,256]{2,1,0:T(8,128)} %combine.3), calls=%async_computation.1 | async-start | bytes 4194304 | tf_op jit(solution)/shard_map/all_to_all | solution.py:24
  66.0 46.7 %collective-permute-start.2 = (f32[2048,256]{1,0:T(8,128)}, f32[2048,256]{1,0:T(8,128)}, u32[]{:S(2)}, u32[]{:S(2)}) collective-permute-start(f32[2048,256]{1,0:T(8,128)} %bitcast.1.refs_2_), channel_id=1, source_target_pairs={{0,16},{8,24},{16,0},{24,8},{1,17},{9,25},{17,1},{25,9},{2,18},{10... | collective-permute-start | bytes 6291464 | tf_op jit(solution)/shard_map/ppermute | solution.py:20
  67.6 46.2 %collective-permute-start.4 = (f32[2048,256]{1,0:T(8,128)}, f32[2048,256]{1,0:T(8,128)}, u32[]{:S(2)}, u32[]{:S(2)}) collective-permute-start(f32[2048,256]{1,0:T(8,128)} %bitcast.1.refs_2_), channel_id=1, source_target_pairs={{0,8},{8,0},{16,24},{24,16},{1,9},{9,1},{17,25},{25,17},{2,10},{10... | collective-permute-start | bytes 6291464 | tf_op jit(solution)/shard_map/ppermute | solution.py:20
  112.7 4.5 %collective-permute-start.3 = (f32[2048,256]{1,0:T(8,128)}, f32[2048,256]{1,0:T(8,128)}, u32[]{:S(2)}, u32[]{:S(2)}) collective-permute-start(f32[2048,256]{1,0:T(8,128)} %collective-permute-done.2.refs_0_), channel_id=1, source_target_pairs={{0,8},{8,0},{16,24},{24,16},{1,9},{9,1},{17,25},{25,17},{2,10},{10... | collective-permute-start | bytes 6291464 | tf_op jit(solution)/shard_map/ppermute | solution.py:20
  113.8 13.7 %collective-permute-start.5 = (f32[2048,256]{1,0:T(8,128)}, f32[2048,256]{1,0:T(8,128)}, u32[]{:S(2)}, u32[]{:S(2)}) collective-permute-start(f32[2048,256]{1,0:T(8,128)} %bitcast.20.refs_0_), channel_id=1, source_target_pairs={{0,8},{8,0},{16,24},{24,16},{1,9},{9,1},{17,25},{25,17},{2,10},{10... | collective-permute-start | bytes 6291464 | tf_op jit(solution)/shard_map/ppermute | solution.py:20
  127.4 8.1 %copy-start.2 = (bf16[2,512,512]{2,1,0:T(8,128)(2,1)S(1)}, bf16[2,512,512]{2,1,0:T(8,128)(2,1)}, u32[]{:S(2)}) copy-start(bf16[2,512,512]{2,1,0:T(8,128)(2,1)} %pad_maximum_fusion.3.refs_4_) | copy-start | bytes 3145732
  127.4 8.1 %copy-start.3 = (bf16[2,512,512]{2,1,0:T(8,128)(2,1)S(1)}, bf16[2,512,512]{2,1,0:T(8,128)(2,1)}, u32[]{:S(2)}) copy-start(bf16[2,512,512]{2,1,0:T(8,128)(2,1)} %pad_maximum_fusion.5.refs_5_) | copy-start | bytes 3145732
